TPU v7x, 128 devices: a whole 4x4x4 slice. The times are simulated.
128 devices in a mesh: wide: 32 (over z, y, core), narrow: 4 (over x).
Axes of the slice: x: 4, y: 4, z: 4, core: 2. Of those that a mesh axis runs over, the one named last changes fastest.
Arguments:
- embeddings: bfloat16 [384, 256, 768], P(('wide', 'narrow'))
- seeds: float32 [384, 256, 64], P(('wide', 'narrow')), may hold values from -6 to 6
- neighbours: int32 [384, 32], P(('wide', 'narrow')), may hold values from -1 to 383, as said below
Outputs:
- scores: float32 [384, 256, 64], P(('wide', 'narrow'))
Inputs may be any that keep to these rules, and one draw needn't show every extreme that they name: `neighbours`: A block's used slots come first and name distinct blocks other than itself, each on a device whose wide index differs from the block's own by at most 2 around the cycle; between 16 and 32 slots of a block are used, all 32 in some block.
All inputs are finite; a program needn't handle non-finite values.
Results may differ from a plain program's by a relative error of at most 0.0013.
Values may be sent and summed in bfloat16 or wider, within the bound.
No kernel may reach another device: no remote copies, remote signals or barrier semaphores. Data moves between devices by JAX's collectives and lax.ppermute only.
A program may use at most 192 MiB of HBM per device.

v0:
```python
import jax
import jax.numpy as jnp
from jax import lax
from jax.sharding import PartitionSpec as P

NBR = 32
ITERS = 3


SHARP = 24.0
ALPHA = 0.8
EPS = 1e-06


def shifted(x, axis, by):
    length = lax.axis_size(axis)
    return lax.ppermute(x, axis, [(i, (i + by) % length) for i in range(length)])


def unit_rows(embeddings):
    values = embeddings.astype(jnp.float32)
    return (values * lax.rsqrt(jnp.sum(values * values, axis=-1, keepdims=True) + EPS)).astype(
        jnp.bfloat16
    )


def fetch_units(units):
    group = lax.all_gather(units[None], "narrow", axis=0, tiled=True)
    pieces = []
    for offset in (-2, -1, 0, 1, 2):
        if offset == 0:
            pieces.append(group)
        else:
            pieces.append(shifted(group, "wide", -offset))
    return jnp.stack(pieces, 0)


def fetch_scores(state):
    group = lax.all_gather(state[None], "narrow", axis=0, tiled=True)
    pieces = []
    for offset in (-2, -1, 0, 1, 2):
        if offset == 0:
            pieces.append(group)
        else:
            pieces.append(shifted(group, "wide", -offset))
    return jnp.stack(pieces, 0)


def tile_weights(own, near_units, usable):
    cosine = jnp.einsum("rd,kqd->krq", own, near_units, preferred_element_type=jnp.float32)
    weight = jnp.where(usable[:, None, None], jnp.exp(SHARP * cosine), 0.0)
    return (weight.astype(jnp.bfloat16), jnp.sum(weight, axis=(0, 2)))


def local(embeddings, seeds, neighbours):
    blocks, rows, width = embeddings.shape
    chans = seeds.shape[2]
    wide_count = lax.axis_size("wide")
    narrow_count = lax.axis_size("narrow")
    cycle_here = lax.axis_index("wide")
    units = unit_rows(embeddings)
    near_all = fetch_units(units).reshape(-1, rows, width)
    reachable = near_all.shape[0]
    valid = neighbours >= 0
    node_ids = jnp.maximum(neighbours, 0)
    device = node_ids // blocks
    cycle_slot = jnp.mod(device // narrow_count - cycle_here + 2, wide_count)
    local_ids = (cycle_slot * narrow_count + device % narrow_count) * blocks + node_ids % blocks
    zero_degree = jnp.zeros((rows,), jnp.float32)

    def build_listed(items):
        own, block_ids, usable = items

        def turn(degree, index):
            picked = lax.dynamic_slice_in_dim(block_ids, index * 8, 8)
            keep = lax.dynamic_slice_in_dim(usable, index * 8, 8)
            tiles, part_degree = tile_weights(own, near_all[picked], keep)
            return (degree + part_degree, tiles)

        degree, tiles = lax.scan(turn, zero_degree, jnp.arange(NBR // 8, dtype=jnp.int32))
        return (tiles.reshape(-1, rows, rows), degree)

    wround, degree = lax.map(build_listed, (units, local_ids, valid))
    state = seeds.astype(jnp.bfloat16)
    scores = seeds
    for step in range(ITERS):
        near_scores = fetch_scores(state.reshape(blocks, rows * chans)).reshape(
            reachable, rows, chans
        )
        picked_scores = near_scores[local_ids]
        spread = jnp.einsum(
            "bkrq,bkqh->brh", wround, picked_scores, preferred_element_type=jnp.float32
        )
        scores = ALPHA * spread / degree[:, :, None] + (1.0 - ALPHA) * seeds
        state = scores.astype(jnp.bfloat16)
    return scores


def solution(mesh):
    return jax.shard_map(
        local,
        mesh=mesh,
        in_specs=(
            P(("wide", "narrow"), None, None),
            P(("wide", "narrow"), None, None),
            P(("wide", "narrow"), None),
        ),
        out_specs=P(("wide", "narrow"), None, None),
        check_vma=False,
    )
```

profile of v0, /device:TPU:0, one launch (start us, length us, event | category | flops | bytes accessed | tf_op | source)
XLA Modules:
  0.0 562.9 jit_solution(2856578459147547198)
XLA Ops:
  7.9 13.2 %all_gather.13 = bf16[4,3,16384]{2,1,0:T(4,128)(2,1)S(1)} all-gather(bf16[1,3,16384]{2,1,0:T(4,128)(2,1)S(1)} %broadcast_in_dim_reshape.9), channel_id=1, replica_groups=mesh['wide'=32,'narrow'=4] {'narrow'}, dimensions={0}, use_global_device_ids=true | all-gather | bytes 491520 | tf_op jit(solution)/shard_map/all_gather | solution.py:39
  22.7 5.1 collective-permute-start.6
  32.5 8.1 %collective-permute-done.4 = bf16[4,3,16384]{2,1,0:T(4,128)(2,1)} collective-permute-done((bf16[4,3,16384]{2,1,0:T(4,128)(2,1)S(1)}, bf16[4,3,16384]{2,1,0:T(4,128)(2,1)}, u32[]{:S(2)}, u32[]{:S(2)}) %collective-permute-start.4) | collective-permute-done | bytes 393248 | tf_op jit(solution)/shard_map/ppermute | solution.py:17
  45.1 38.3 %all-gather.3.cloned.1.call-done = bf16[12,256,768]{2,1,0:T(8,128)(2,1)} async-done(((bf16[3,256,768]{2,1,0:T(8,128)(2,1)}), bf16[12,256,768]{2,1,0:T(8,128)(2,1)}) %all-gather.3.cloned.1.call-update) | async-done | bytes 4718608 | tf_op jit(solution)/shard_map/all_gather | solution.py:28
  86.2 5.1 collective-permute-start.2
  93.2 4.8 reshape.25
  97.9 3.5 copy.17
  103.9 87.8 %collective-permute-done = bf16[4,3,256,768]{3,2,1,0:T(8,128)(2,1)} collective-permute-done((bf16[4,3,256,768]{3,2,1,0:T(8,128)(2,1)}, bf16[4,3,256,768]{3,2,1,0:T(8,128)(2,1)}, u32[]{:S(2)}, u32[]{:S(2)}) %collective-permute-start) | collective-permute-done | bytes 4718624 | tf_op jit(solution)/shard_map/ppermute | solution.py:17
  191.8 2.8 bitcast_dynamic-update-slice_fusion.4
  194.6 46.7 %collective-permute-done.1 = bf16[4,3,256,768]{3,2,1,0:T(8,128)(2,1)} collective-permute-done((bf16[4,3,256,768]{3,2,1,0:T(8,128)(2,1)}, bf16[4,3,256,768]{3,2,1,0:T(8,128)(2,1)}, u32[]{:S(2)}, u32[]{:S(2)}) %collective-permute-start.1) | collective-permute-done | bytes 4718624 | tf_op jit(solution)/shard_map/ppermute | solution.py:17
  241.3 2.7 bitcast_dynamic-update-slice_fusion.3
  244.3 2.7 bitcast_dynamic-update-slice_fusion.2
  247.0 2.7 bitcast_dynamic-update-slice_fusion.1
  249.7 7.8 %copy-done = bf16[5,4,3,256,768]{4,3,2,1,0:T(8,128)(2,1)} copy-done((bf16[5,4,3,256,768]{4,3,2,1,0:T(8,128)(2,1)}, bf16[5,4,3,256,768]{4,3,2,1,0:T(8,128)(2,1)S(1)}, u32[]{:S(2)}) %copy-start) | copy-done | bytes 23592984
  257.6 179.7 %while.26 = (s32[]{:T(128)}, bf16[3,32,256,256]{2,3,1,0:T(8,128)(2,1)}, f32[3,256]{1,0:T(4,128)S(1)}, s32[3,32]{1,0:T(4,128)S(1)}, pred[3,32]{1,0:T(4,128)(4,1)S...) while((s32[]{:T(128)}, ...), condition=%wide.region_5.6_spmd, body=%wide.region_1.5_spmd.sunk | while | flops 808453376 | bytes 24260516 | solution.py:83
  259.4 53.4 %while.27 = (s32[]{:T(128)}, f32[256]{0:T(256)S(1)}, bf16[4,8,256,256]{2,3,1,0:T(8,128)(2,1)}, s32[4]{0:T(128)S(1)}, pred[32]{0:T(512)(128)(4,1)S(1)}, /*index=5...) while((s32[]{:T(128)}, f32[256]{0:T(256)S(1)}, ...), condition=%wide.region_4.4_spmd.clone, body=%wide.region_2.3_spmd.clone.sunk | while | flops 808453376 | bytes 15082337 | solution.py:80
  260.8 8.5 %gather_fusion = bf16[8,256,768]{2,1,0:T(8,128)(2,1)S(1)} fusion(bf16[60,256,768]{2,1,0:T(8,128)(2,1)} %get-tuple-element.296, s32[1024]{0:T(1024)S(1)} %pad_clamp_fusion.3), kind=kCustom, calls=%fused_computation.clone.clone.1 | custom fusion | bytes 6291488 | tf_op jit(solution)/shard_map/while/body/eval_jaxpr/while/body/eval_jaxpr/gather | solution.py:77
  274.1 8.5 %gather_fusion = bf16[8,256,768]{2,1,0:T(8,128)(2,1)S(1)} fusion(bf16[60,256,768]{2,1,0:T(8,128)(2,1)} %get-tuple-element.296, s32[1024]{0:T(1024)S(1)} %pad_clamp_fusion.3), kind=kCustom, calls=%fused_computation.clone.clone.1 | custom fusion | bytes 6291488 | tf_op jit(solution)/shard_map/while/body/eval_jaxpr/while/body/eval_jaxpr/gather | solution.py:77
  287.5 8.5 %gather_fusion = bf16[8,256,768]{2,1,0:T(8,128)(2,1)S(1)} fusion(bf16[60,256,768]{2,1,0:T(8,128)(2,1)} %get-tuple-element.296, s32[1024]{0:T(1024)S(1)} %pad_clamp_fusion.3), kind=kCustom, calls=%fused_computation.clone.clone.1 | custom fusion | bytes 6291488 | tf_op jit(solution)/shard_map/while/body/eval_jaxpr/while/body/eval_jaxpr/gather | solution.py:77
  300.8 8.5 %gather_fusion = bf16[8,256,768]{2,1,0:T(8,128)(2,1)S(1)} fusion(bf16[60,256,768]{2,1,0:T(8,128)(2,1)} %get-tuple-element.296, s32[1024]{0:T(1024)S(1)} %pad_clamp_fusion.3), kind=kCustom, calls=%fused_computation.clone.clone.1 | custom fusion | bytes 6291488 | tf_op jit(solution)/shard_map/while/body/eval_jaxpr/while/body/eval_jaxpr/gather | solution.py:77
  312.8 4.7 bitcast_dynamic-update-slice_fusion.21
  319.4 53.4 %while.27 = (s32[]{:T(128)}, f32[256]{0:T(256)S(1)}, bf16[4,8,256,256]{2,3,1,0:T(8,128)(2,1)}, s32[4]{0:T(128)S(1)}, pred[32]{0:T(512)(128)(4,1)S(1)}, /*index=5...) while((s32[]{:T(128)}, f32[256]{0:T(256)S(1)}, ...), condition=%wide.region_4.4_spmd.clone, body=%wide.region_2.3_spmd.clone.sunk | while | flops 808453376 | bytes 15082337 | solution.py:80
  320.7 8.5 %gather_fusion = bf16[8,256,768]{2,1,0:T(8,128)(2,1)S(1)} fusion(bf16[60,256,768]{2,1,0:T(8,128)(2,1)} %get-tuple-element.296, s32[1024]{0:T(1024)S(1)} %pad_clamp_fusion.3), kind=kCustom, calls=%fused_computation.clone.clone.1 | custom fusion | bytes 6291488 | tf_op jit(solution)/shard_map/while/body/eval_jaxpr/while/body/eval_jaxpr/gather | solution.py:77
  334.1 8.5 %gather_fusion = bf16[8,256,768]{2,1,0:T(8,128)(2,1)S(1)} fusion(bf16[60,256,768]{2,1,0:T(8,128)(2,1)} %get-tuple-element.296, s32[1024]{0:T(1024)S(1)} %pad_clamp_fusion.3), kind=kCustom, calls=%fused_computation.clone.clone.1 | custom fusion | bytes 6291488 | tf_op jit(solution)/shard_map/while/body/eval_jaxpr/while/body/eval_jaxpr/gather | solution.py:77
  347.4 8.5 %gather_fusion = bf16[8,256,768]{2,1,0:T(8,128)(2,1)S(1)} fusion(bf16[60,256,768]{2,1,0:T(8,128)(2,1)} %get-tuple-element.296, s32[1024]{0:T(1024)S(1)} %pad_clamp_fusion.3), kind=kCustom, calls=%fused_computation.clone.clone.1 | custom fusion | bytes 6291488 | tf_op jit(solution)/shard_map/while/body/eval_jaxpr/while/body/eval_jaxpr/gather | solution.py:77
  360.7 8.5 %gather_fusion = bf16[8,256,768]{2,1,0:T(8,128)(2,1)S(1)} fusion(bf16[60,256,768]{2,1,0:T(8,128)(2,1)} %get-tuple-element.296, s32[1024]{0:T(1024)S(1)} %pad_clamp_fusion.3), kind=kCustom, calls=%fused_computation.clone.clone.1 | custom fusion | bytes 6291488 | tf_op jit(solution)/shard_map/while/body/eval_jaxpr/while/body/eval_jaxpr/gather | solution.py:77
  372.8 4.7 bitcast_dynamic-update-slice_fusion.21
  379.3 53.4 %while.27 = (s32[]{:T(128)}, f32[256]{0:T(256)S(1)}, bf16[4,8,256,256]{2,3,1,0:T(8,128)(2,1)}, s32[4]{0:T(128)S(1)}, pred[32]{0:T(512)(128)(4,1)S(1)}, /*index=5...) while((s32[]{:T(128)}, f32[256]{0:T(256)S(1)}, ...), condition=%wide.region_4.4_spmd.clone, body=%wide.region_2.3_spmd.clone.sunk | while | flops 808453376 | bytes 15082337 | solution.py:80
  380.6 8.5 %gather_fusion = bf16[8,256,768]{2,1,0:T(8,128)(2,1)S(1)} fusion(bf16[60,256,768]{2,1,0:T(8,128)(2,1)} %get-tuple-element.296, s32[1024]{0:T(1024)S(1)} %pad_clamp_fusion.3), kind=kCustom, calls=%fused_computation.clone.clone.1 | custom fusion | bytes 6291488 | tf_op jit(solution)/shard_map/while/body/eval_jaxpr/while/body/eval_jaxpr/gather | solution.py:77
  394.0 8.5 %gather_fusion = bf16[8,256,768]{2,1,0:T(8,128)(2,1)S(1)} fusion(bf16[60,256,768]{2,1,0:T(8,128)(2,1)} %get-tuple-element.296, s32[1024]{0:T(1024)S(1)} %pad_clamp_fusion.3), kind=kCustom, calls=%fused_computation.clone.clone.1 | custom fusion | bytes 6291488 | tf_op jit(solution)/shard_map/while/body/eval_jaxpr/while/body/eval_jaxpr/gather | solution.py:77
  407.3 8.5 %gather_fusion = bf16[8,256,768]{2,1,0:T(8,128)(2,1)S(1)} fusion(bf16[60,256,768]{2,1,0:T(8,128)(2,1)} %get-tuple-element.296, s32[1024]{0:T(1024)S(1)} %pad_clamp_fusion.3), kind=kCustom, calls=%fused_computation.clone.clone.1 | custom fusion | bytes 6291488 | tf_op jit(solution)/shard_map/while/body/eval_jaxpr/while/body/eval_jaxpr/gather | solution.py:77
  420.6 8.5 %gather_fusion = bf16[8,256,768]{2,1,0:T(8,128)(2,1)S(1)} fusion(bf16[60,256,768]{2,1,0:T(8,128)(2,1)} %get-tuple-element.296, s32[1024]{0:T(1024)S(1)} %pad_clamp_fusion.3), kind=kCustom, calls=%fused_computation.clone.clone.1 | custom fusion | bytes 6291488 | tf_op jit(solution)/shard_map/while/body/eval_jaxpr/while/body/eval_jaxpr/gather | solution.py:77
  432.7 4.6 bitcast_dynamic-update-slice_fusion.21
  437.3 7.8 %fusion.18 = bf16[3,256,64]{1,2,0:T(8,128)(2,1)S(1)} fusion(bf16[3,32,256,64]{2,3,1,0:T(8,128)(2,1)} %bitcast.124, bf16[3,32,256,256]{2,3,1,0:T(8,128)(2,1)} %get-tuple-element.86, f32[3,256,64]{1,2,0:T(8,128)S(1)} %copy-done.1, f32[3,256]{1,0:T(4,128)S(1)} %get-tuple-element.87), kind=kOutput, calls=%fused_computation.39 | convolution fusion | flops 805552128 | bytes 16026624 | tf_op jit(solution)/shard_map/bkrq,bkqh->brh/dot_general | solution.py:91
  445.5 13.2 %all_gather.14 = bf16[4,3,16384]{2,1,0:T(4,128)(2,1)S(1)} all-gather(bf16[1,3,16384]{2,1,0:T(4,128)(2,1)S(1)} %broadcast_in_dim_reshape.10), channel_id=1, replica_groups=mesh['wide'=32,'narrow'=4] {'narrow'}, dimensions={0}, use_global_device_ids=true | all-gather | bytes 491520 | tf_op jit(solution)/shard_map/all_gather | solution.py:39
  458.7 5.1 collective-permute-start.10
  465.7 10.5 %collective-permute-done.8 = bf16[4,3,16384]{2,1,0:T(4,128)(2,1)S(1)} collective-permute-done((bf16[4,3,16384]{2,1,0:T(4,128)(2,1)S(1)}, bf16[4,3,16384]{2,1,0:T(4,128)(2,1)S(1)}, u32[]{:S(2)}, u32[]{:S(2)}) %collective-permute-start.8) | collective-permute-done | bytes 393248 | tf_op jit(solution)/shard_map/ppermute | solution.py:17
  477.1 4.4 collective-permute-done.11
  481.7 4.7 reshape.26
  486.4 4.7 copy.20
  493.5 6.9 %fusion.19 = bf16[3,256,64]{1,2,0:T(8,128)(2,1)S(1)} fusion(bf16[3,32,256,64]{2,3,1,0:T(8,128)(2,1)S(1)} %bitcast.126, bf16[3,32,256,256]{2,3,1,0:T(8,128)(2,1)} %get-tuple-element.86, f32[3,256,64]{1,2,0:T(8,128)S(1)} %copy-done.1, f32[3,256]{1,0:T(4,128)S(1)} %get-tuple-element.87), kind=kOutput, calls=%fused_computation.40 | convolution fusion | flops 805552128 | bytes 16026624 | tf_op jit(solution)/shard_map/bkrq,bkqh->brh/dot_general | solution.py:91
  500.7 12.8 %all_gather.15 = bf16[4,3,16384]{2,1,0:T(4,128)(2,1)S(1)} all-gather(bf16[1,3,16384]{2,1,0:T(4,128)(2,1)S(1)} %broadcast_in_dim_reshape.11), channel_id=1, replica_groups=mesh['wide'=32,'narrow'=4] {'narrow'}, dimensions={0}, use_global_device_ids=true | all-gather | bytes 491520 | tf_op jit(solution)/shard_map/all_gather | solution.py:39
  513.5 5.1 collective-permute-start.14
  521.1 10.0 %collective-permute-done.12 = bf16[4,3,16384]{2,1,0:T(4,128)(2,1)S(1)} collective-permute-done((bf16[4,3,16384]{2,1,0:T(4,128)(2,1)S(1)}, bf16[4,3,16384]{2,1,0:T(4,128)(2,1)S(1)}, u32[]{:S(2)}, u32[]{:S(2)}) %collective-permute-start.12) | collective-permute-done | bytes 393248 | tf_op jit(solution)/shard_map/ppermute | solution.py:17
  531.9 4.6 collective-permute-done.15
  536.7 4.7 reshape.27
  541.5 4.7 copy.23
  548.5 7.5 %fusion.11 = f32[3,256,64]{1,2,0:T(8,128)} fusion(bf16[3,32,256,64]{2,3,1,0:T(8,128)(2,1)S(1)} %bitcast.125, bf16[3,32,256,256]{2,3,1,0:T(8,128)(2,1)} %get-tuple-element.86, f32[3,256,64]{1,2,0:T(8,128)S(1)} %copy-done.1, f32[3,256]{1,0:T(4,128)S(1)} %get-tuple-element.87), kind=kOutput, calls=%fused_computation.30 | convolution fusion | flops 805502976 | bytes 16124928 | tf_op jit(solution)/shard_map/bkrq,bkqh->brh/dot_general | solution.py:91
  (179 shorter events, 87.8 us)
Async XLA Ops:
  6.5 24.5 %copy-start.2 = (bf16[3,256,768]{2,1,0:T(8,128)(2,1)S(1)}, bf16[3,256,768]{2,1,0:T(8,128)(2,1)}, u32[]{:S(2)}) copy-start(bf16[3,256,768]{2,1,0:T(8,128)(2,1)} %param.7) | copy-start | bytes 3538948
  6.5 25.8 %copy-start.5 = (s32[3,32]{1,0:T(4,128)S(1)}, s32[3,32]{1,0:T(4,128)}, u32[]{:S(2)}) copy-start(s32[3,32]{1,0:T(4,128)} %param.9) | copy-start | bytes 1156
  6.5 76.9 %all-gather.3.cloned.1.call-start = ((), (), s32[]{:S(2)}) async-start(), calls=%async_computation | async-start | bytes 5898240 | tf_op jit(solution)/shard_map/all_gather | solution.py:28
  21.1 19.4 %collective-permute-start.4 = (bf16[4,3,16384]{2,1,0:T(4,128)(2,1)S(1)}, bf16[4,3,16384]{2,1,0:T(4,128)(2,1)}, u32[]{:S(2)}, u32[]{:S(2)}) collective-permute-start(bf16[4,3,16384]{2,1,0:T(4,128)(2,1)S(1)} %all_gather.13), channel_id=1, source_target_pairs={{0,8},{4,12},{8,16},{12,20},{16,24},{20,28},{24,32},{28,36},{32,40... | collective-permute-start | bytes 1179656 | tf_op jit(solution)/shard_map/ppermute | solution.py:17
  22.7 20.9 %collective-permute-start.5 = (bf16[4,3,16384]{2,1,0:T(4,128)(2,1)S(1)}, bf16[4,3,16384]{2,1,0:T(4,128)(2,1)}, u32[]{:S(2)}, u32[]{:S(2)}) collective-permute-start(bf16[4,3,16384]{2,1,0:T(4,128)(2,1)S(1)} %all_gather.13), channel_id=1, source_target_pairs={{0,4},{4,8},{8,12},{12,16},{16,20},{20,24},{24,28},{28,32},{32,36}... | collective-permute-start | bytes 1179656 | tf_op jit(solution)/shard_map/ppermute | solution.py:17
  22.7 62.2 %collective-permute-start.6 = (bf16[4,3,16384]{2,1,0:T(4,128)(2,1)S(1)}, bf16[4,3,16384]{2,1,0:T(4,128)(2,1)}, u32[]{:S(2)}, u32[]{:S(2)}) collective-permute-start(bf16[4,3,16384]{2,1,0:T(4,128)(2,1)S(1)} %all_gather.13), channel_id=1, source_target_pairs={{0,124},{4,0},{8,4},{12,8},{16,12},{20,16},{24,20},{28,24},{32,28}... | collective-permute-start | bytes 1179656 | tf_op jit(solution)/shard_map/ppermute | solution.py:17
  27.8 64.1 %collective-permute-start.7 = (bf16[4,3,16384]{2,1,0:T(4,128)(2,1)S(1)}, bf16[4,3,16384]{2,1,0:T(4,128)(2,1)}, u32[]{:S(2)}, u32[]{:S(2)}) collective-permute-start(bf16[4,3,16384]{2,1,0:T(4,128)(2,1)S(1)} %all_gather.13), channel_id=1, source_target_pairs={{0,120},{4,124},{8,0},{12,4},{16,8},{20,12},{24,16},{28,20},{32,24... | collective-permute-start | bytes 1179656 | tf_op jit(solution)/shard_map/ppermute | solution.py:17
  32.5 68.9 %copy-start.3 = (s32[1024]{0:T(1024)}, s32[1024]{0:T(1024)S(1)}, u32[]{:S(2)}) copy-start(s32[1024]{0:T(1024)S(1)} %pad_clamp_fusion.1) | copy-start | bytes 12292
  83.5 108.3 %collective-permute-start = (bf16[4,3,256,768]{3,2,1,0:T(8,128)(2,1)}, bf16[4,3,256,768]{3,2,1,0:T(8,128)(2,1)}, u32[]{:S(2)}, u32[]{:S(2)}) collective-permute-start(bf16[4,3,256,768]{3,2,1,0:T(8,128)(2,1)} %bitcast.127), channel_id=1, source_target_pairs={{0,8},{4,12},{8,16},{12,20},{16,24},{20,28},{24,32},{28,36},{32,40... | collective-permute-start | bytes 14155784 | tf_op jit(solution)/shard_map/ppermute | solution.py:17
  85.0 156.3 %collective-permute-start.1 = (bf16[4,3,256,768]{3,2,1,0:T(8,128)(2,1)}, bf16[4,3,256,768]{3,2,1,0:T(8,128)(2,1)}, u32[]{:S(2)}, u32[]{:S(2)}) collective-permute-start(bf16[4,3,256,768]{3,2,1,0:T(8,128)(2,1)} %bitcast.128), channel_id=1, source_target_pairs={{0,4},{4,8},{8,12},{12,16},{16,20},{20,24},{24,28},{28,32},{32,36}... | collective-permute-start | bytes 14155784 | tf_op jit(solution)/shard_map/ppermute | solution.py:17
  86.2 158.1 %collective-permute-start.2 = (bf16[4,3,256,768]{3,2,1,0:T(8,128)(2,1)}, bf16[4,3,256,768]{3,2,1,0:T(8,128)(2,1)}, u32[]{:S(2)}, u32[]{:S(2)}) collective-permute-start(bf16[4,3,256,768]{3,2,1,0:T(8,128)(2,1)} %bitcast.129), channel_id=1, source_target_pairs={{0,124},{4,0},{8,4},{12,8},{16,12},{20,16},{24,20},{28,24},{32,28}... | collective-permute-start | bytes 14155784 | tf_op jit(solution)/shard_map/ppermute | solution.py:17
  91.3 155.7 %collective-permute-start.3 = (bf16[4,3,256,768]{3,2,1,0:T(8,128)(2,1)}, bf16[4,3,256,768]{3,2,1,0:T(8,128)(2,1)}, u32[]{:S(2)}, u32[]{:S(2)}) collective-permute-start(bf16[4,3,256,768]{3,2,1,0:T(8,128)(2,1)} %bitcast.130), channel_id=1, source_target_pairs={{0,120},{4,124},{8,0},{12,4},{16,8},{20,12},{24,16},{28,20},{32,24... | collective-permute-start | bytes 14155784 | tf_op jit(solution)/shard_map/ppermute | solution.py:17
  191.8 52.2 %slice-start = ((s8[4718592]{0:T(1024)(128)(4,1)}), s8[4194304]{0:T(1024)(128)(4,1)S(1)}, s32[]{:S(2)}) async-start(s8[4718592]{0:T(1024)(128)(4,1)} %bitcast.131), calls=%async_computation.1 | async-start | bytes 8388608
  194.6 49.4 %slice-start.1 = ((s8[4718592]{0:T(1024)(128)(4,1)}), s8[524288]{0:T(1024)(128)(4,1)S(1)}, s32[]{:S(2)}) async-start(s8[4718592]{0:T(1024)(128)(4,1)} %bitcast.131), calls=%async_computation.2 | async-start | bytes 1048576
  249.7 7.8 %copy-start = (bf16[5,4,3,256,768]{4,3,2,1,0:T(8,128)(2,1)}, bf16[5,4,3,256,768]{4,3,2,1,0:T(8,128)(2,1)S(1)}, u32[]{:S(2)}) copy-start(bf16[5,4,3,256,768]{4,3,2,1,0:T(8,128)(2,1)S(1)} %bitcast_dynamic-update-slice_fusion.1) | copy-start | bytes 70778880
  257.6 179.7 %copy-start.1 = (f32[3,256,64]{1,2,0:T(8,128)S(1)}, f32[3,256,64]{1,2,0:T(8,128)}, u32[]{:S(2)}) copy-start(f32[3,256,64]{1,2,0:T(8,128)} %param.8) | copy-start | bytes 589828
  458.7 17.6 %collective-permute-start.8 = (bf16[4,3,16384]{2,1,0:T(4,128)(2,1)S(1)}, bf16[4,3,16384]{2,1,0:T(4,128)(2,1)S(1)}, u32[]{:S(2)}, u32[]{:S(2)}) collective-permute-start(bf16[4,3,16384]{2,1,0:T(4,128)(2,1)S(1)} %all_gather.14), channel_id=1, source_target_pairs={{0,8},{4,12},{8,16},{12,20},{16,24},{20,28},{24,32},{28,36},{32,40... | collective-permute-start | bytes 1179656 | tf_op jit(solution)/shard_map/ppermute | solution.py:17
  458.7 17.8 %collective-permute-start.9 = (bf16[4,3,16384]{2,1,0:T(4,128)(2,1)S(1)}, bf16[4,3,16384]{2,1,0:T(4,128)(2,1)S(1)}, u32[]{:S(2)}, u32[]{:S(2)}) collective-permute-start(bf16[4,3,16384]{2,1,0:T(4,128)(2,1)S(1)} %all_gather.14), channel_id=1, source_target_pairs={{0,4},{4,8},{8,12},{12,16},{16,20},{20,24},{24,28},{28,32},{32,36}... | collective-permute-start | bytes 1179656 | tf_op jit(solution)/shard_map/ppermute | solution.py:17
  458.7 18.2 %collective-permute-start.10 = (bf16[4,3,16384]{2,1,0:T(4,128)(2,1)S(1)}, bf16[4,3,16384]{2,1,0:T(4,128)(2,1)S(1)}, u32[]{:S(2)}, u32[]{:S(2)}) collective-permute-start(bf16[4,3,16384]{2,1,0:T(4,128)(2,1)S(1)} %all_gather.14), channel_id=1, source_target_pairs={{0,124},{4,0},{8,4},{12,8},{16,12},{20,16},{24,20},{28,24},{32,28}... | collective-permute-start | bytes 1179656 | tf_op jit(solution)/shard_map/ppermute | solution.py:17
  463.8 17.7 %collective-permute-start.11 = (bf16[4,3,16384]{2,1,0:T(4,128)(2,1)S(1)}, bf16[4,3,16384]{2,1,0:T(4,128)(2,1)S(1)}, u32[]{:S(2)}, u32[]{:S(2)}) collective-permute-start(bf16[4,3,16384]{2,1,0:T(4,128)(2,1)S(1)} %all_gather.14), channel_id=1, source_target_pairs={{0,120},{4,124},{8,0},{12,4},{16,8},{20,12},{24,16},{28,20},{32,24... | collective-permute-start | bytes 1179656 | tf_op jit(solution)/shard_map/ppermute | solution.py:17
  486.4 4.7 copy-start.4
  513.5 17.6 %collective-permute-start.12 = (bf16[4,3,16384]{2,1,0:T(4,128)(2,1)S(1)}, bf16[4,3,16384]{2,1,0:T(4,128)(2,1)S(1)}, u32[]{:S(2)}, u32[]{:S(2)}) collective-permute-start(bf16[4,3,16384]{2,1,0:T(4,128)(2,1)S(1)} %all_gather.15), channel_id=1, source_target_pairs={{0,8},{4,12},{8,16},{12,20},{16,24},{20,28},{24,32},{28,36},{32,40... | collective-permute-start | bytes 1179656 | tf_op jit(solution)/shard_map/ppermute | solution.py:17
  513.5 17.8 %collective-permute-start.13 = (bf16[4,3,16384]{2,1,0:T(4,128)(2,1)S(1)}, bf16[4,3,16384]{2,1,0:T(4,128)(2,1)S(1)}, u32[]{:S(2)}, u32[]{:S(2)}) collective-permute-start(bf16[4,3,16384]{2,1,0:T(4,128)(2,1)S(1)} %all_gather.15), channel_id=1, source_target_pairs={{0,4},{4,8},{8,12},{12,16},{16,20},{20,24},{24,28},{28,32},{32,36}... | collective-permute-start | bytes 1179656 | tf_op jit(solution)/shard_map/ppermute | solution.py:17
  513.5 18.2 %collective-permute-start.14 = (bf16[4,3,16384]{2,1,0:T(4,128)(2,1)S(1)}, bf16[4,3,16384]{2,1,0:T(4,128)(2,1)S(1)}, u32[]{:S(2)}, u32[]{:S(2)}) collective-permute-start(bf16[4,3,16384]{2,1,0:T(4,128)(2,1)S(1)} %all_gather.15), channel_id=1, source_target_pairs={{0,124},{4,0},{8,4},{12,8},{16,12},{20,16},{24,20},{28,24},{32,28}... | collective-permute-start | bytes 1179656 | tf_op jit(solution)/shard_map/ppermute | solution.py:17
  518.6 17.9 %collective-permute-start.15 = (bf16[4,3,16384]{2,1,0:T(4,128)(2,1)S(1)}, bf16[4,3,16384]{2,1,0:T(4,128)(2,1)S(1)}, u32[]{:S(2)}, u32[]{:S(2)}) collective-permute-start(bf16[4,3,16384]{2,1,0:T(4,128)(2,1)S(1)} %all_gather.15), channel_id=1, source_target_pairs={{0,120},{4,124},{8,0},{12,4},{16,8},{20,12},{24,16},{28,20},{32,24... | collective-permute-start | bytes 1179656 | tf_op jit(solution)/shard_map/ppermute | solution.py:17
Sparse Core Ops, SparseCore 0:
  32.5 50.9 all-gather.2
where the time goes:
time: 565 us; the launch traced here: 563 us
  waiting for transfers between devices  212 us (38%)
  local copies, waits for them, and re-layouts  191 us (34%)
  matrix products  46.9 us (8%)
  blocking collectives  39.2 us (7%)
  starting transfers between devices  30.1 us (5%)
  other arithmetic  21.8 us (4%)
  between operations  13.7 us (2%)
  loops' own time  8.02 us (1%)
    ppermute x16, waiting for transfers between devices, shifted(): lax.ppermute(x, axis, [(i, (i + by) % length) for i in range(length)])  174 us
    gather x12, local copies, waits for them, and re-layouts, turn(): tiles, part_degree = tile_weights(own, near_all[picked], keep)  101 us
    all_gather x3, blocking collectives, fetch_scores(): group = lax.all_gather(state[None], 'narrow', axis=0, tiled=True)  39.2 us
    all_gather x1, waiting for transfers between devices, fetch_units(): group = lax.all_gather(units[None], 'narrow', axis=0, tiled=True)  38.3 us
    ppermute x16, starting transfers between devices, shifted(): lax.ppermute(x, axis, [(i, (i + by) % length) for i in range(length)])  30.1 us
    reshape x6, local copies, waits for them, and re-layouts, local(): fetch_scores(state.reshape(blocks, rows * chans))  27.1 us
    dot_general x12, matrix products, tile_weights(): jnp.einsum('rd,kqd->krq', own, near_units, preferred_element_type=jnp.flo...  24.7 us
    dot_general x3, matrix products, local(): jnp.einsum('bkrq,bkqh->brh', wround, picked_scores, preferred_element_typ...  22.2 us
  transfers between devices with their start and end apart: 17, of which 9 were waited for; matrix products, arithmetic and copies ran while one was open for 5% of the time, Pallas kernels for 0%

commit v1 on v0

v1 whole, which is shorter than its diff:
```python
import functools
import math

import jax
import jax.numpy as jnp
from jax import lax
from jax.experimental import pallas as pl
from jax.experimental.pallas import tpu as pltpu
from jax.sharding import Mesh, PartitionSpec as P

NBR = 32
ITERS = 3
SHARP = 24.0
ALPHA = 0.8
EPS = 1e-06
ROWS = 256
D = 768
CH = 64
BLK = 3
NX = 4
NW = 32
HALF = BLK * ROWS // 2
SCALE = SHARP * math.log2(math.e)
WIDE = ("z", "y", "c")
VM = pl.BlockSpec(memory_space=pltpu.VMEM)
SM = pl.BlockSpec(memory_space=pltpu.SMEM)
F32 = jnp.float32
BF16 = jnp.bfloat16


def along_x(v, by):
    return lax.ppermute(v, "x", [(i, (i + by) % NX) for i in range(NX)])


def from_wide(v, offset):
    return lax.ppermute(v, WIDE, [((i + offset) % NW, i) for i in range(NW)])


def swap_core(v):
    return lax.ppermute(v, "c", [(0, 1), (1, 0)])


def prep_kernel(emb_ref, seed_ref, low_ref, high_ref, full_ref, state_ref):
    for block in range(BLK):
        values = emb_ref[block].astype(F32)
        total = jnp.sum(values * values, axis=-1, keepdims=True)
        unit = (values * lax.rsqrt(total + EPS)).astype(BF16)
        full_ref[block] = unit
        state_ref[block] = seed_ref[block].astype(BF16)
    low_ref[0:256] = full_ref[0]
    low_ref[256:384] = full_ref[1, 0:128]
    high_ref[0:128] = full_ref[1, 128:256]
    high_ref[128:384] = full_ref[2]


def prepare(embeddings, seeds_t):
    return pl.pallas_call(
        prep_kernel,
        out_shape=(
            jax.ShapeDtypeStruct((HALF, D), BF16),
            jax.ShapeDtypeStruct((HALF, D), BF16),
            jax.ShapeDtypeStruct((BLK, ROWS, D), BF16),
            jax.ShapeDtypeStruct((BLK, CH, ROWS), BF16),
        ),
        in_specs=[VM, VM],
        out_specs=(VM, VM, VM, VM),
        compiler_params=pltpu.CompilerParams(vmem_limit_bytes=16 << 20),
        cost_estimate=pl.CostEstimate(flops=2_000_000, bytes_accessed=5_000_000, transcendentals=768),
        name="prep",
    )(embeddings, seeds_t)


def build_kernel(n_rows, n_cols, has_acc, *refs):
    refs = list(refs)
    mask_ref = refs.pop(0)
    row_refs = [refs.pop(0) for _ in range(n_rows)]
    col_refs = [refs.pop(0) for _ in range(n_cols)]
    state_refs = [refs.pop(0) for _ in range(n_cols)]
    acc_in = [refs.pop(0) for _ in has_acc if _]
    deg_in = [refs.pop(0) for _ in has_acc if _]
    w_ref, acc_ref, deg_ref = refs
    at = 0
    for group in range(n_rows):
        here = pl.ds(group * BLK, BLK)
        if has_acc[group]:
            acc_ref[here] = acc_in[at][...]
            deg_ref[here] = deg_in[at][...]
            at += 1
        else:
            acc_ref[here] = jnp.zeros((BLK, CH, ROWS), F32)
            deg_ref[here] = jnp.zeros((BLK, 8, ROWS), F32)
    width = n_cols * BLK
    for group in range(n_rows):
        for source in range(n_cols):

            @pl.loop(0, BLK * BLK)
            def _(step):
                i = step // BLK
                j = step - i * BLK
                row = group * BLK + i
                slot = row * width + source * BLK + j

                @pl.when(mask_ref[slot] != 0)
                def _():
                    cosine = lax.dot_general(
                        col_refs[source][j],
                        row_refs[group][i],
                        (((1,), (1,)), ((), ())),
                        preferred_element_type=F32,
                    )
                    weight = jnp.exp2(cosine * SCALE)
                    deg_ref[row] += jnp.sum(weight.reshape(ROWS // 8, 8, ROWS), axis=0)
                    rounded = weight.astype(BF16)
                    w_ref[slot] = rounded
                    acc_ref[row] += jnp.dot(
                        state_refs[source][j], rounded, preferred_element_type=F32
                    )


def build(mask, rows, cols, states, accs, degs):
    n_rows, n_cols = len(rows), len(cols)
    has_acc = tuple(a is not None for a in accs)
    slots = n_rows * BLK * n_cols * BLK
    given = [a for a in accs if a is not None] + [d for d in degs if d is not None]
    operands = [mask, *rows, *cols, *states, *given]
    return pl.pallas_call(
        functools.partial(build_kernel, n_rows, n_cols, has_acc),
        out_shape=(
            jax.ShapeDtypeStruct((slots, ROWS, ROWS), BF16),
            jax.ShapeDtypeStruct((n_rows * BLK, CH, ROWS), F32),
            jax.ShapeDtypeStruct((n_rows * BLK, 8, ROWS), F32),
        ),
        in_specs=[SM] + [VM] * (len(operands) - 1),
        out_specs=(VM, VM, VM),
        compiler_params=pltpu.CompilerParams(vmem_limit_bytes=32 << 20),
        cost_estimate=pl.CostEstimate(
            flops=slots * 40_000_000, bytes_accessed=slots * 131072, transcendentals=slots * 26000
        ),
        name=f"build_{n_rows}_{n_cols}",
    )(*operands)


def spread_kernel(plan, n_w, mask_ref, *refs):
    w_refs = refs[:n_w]
    state_refs = refs[n_w:-1]
    acc_ref = refs[-1]

    @pl.loop(0, NX * BLK)
    def _(row):
        acc_ref[row] = jnp.zeros((CH, ROWS), F32)

    for group, pieces in enumerate(plan):
        for which, first_row, width, first_col, source in pieces:

            @pl.loop(0, BLK * BLK)
            def _(step):
                i = step // BLK
                j = step - i * BLK
                row = group * BLK + i

                @pl.when(mask_ref[row * 15 + source * BLK + j] != 0)
                def _():
                    slot = (first_row + i) * width + first_col + j
                    acc_ref[row] += jnp.dot(
                        state_refs[source][j], w_refs[which][slot], preferred_element_type=F32
                    )


def spread(plan, mask, weights, states):
    return pl.pallas_call(
        functools.partial(spread_kernel, plan, len(weights)),
        out_shape=jax.ShapeDtypeStruct((NX * BLK, CH, ROWS), F32),
        in_specs=[SM] + [VM] * (len(weights) + len(states)),
        out_specs=VM,
        compiler_params=pltpu.CompilerParams(vmem_limit_bytes=40 << 20),
        cost_estimate=pl.CostEstimate(flops=75 * 8_400_000, bytes_accessed=10_000_000, transcendentals=0),
        name="spread",
    )(mask, *weights, *states)


def wide_exchange(v, core):
    below = from_wide(v, -2)
    above = from_wide(v, 2)
    partner = swap_core(v)
    across = swap_core(jnp.where(core == 0, above, below))
    return [v, partner, below, above, across]


def local(embeddings, seeds, neighbours):
    core = lax.axis_index("c")
    here_x = lax.axis_index("x")
    here_w = lax.axis_index(WIDE)
    seeds_t = jnp.swapaxes(seeds, 1, 2)
    low, high, units, state = prepare(embeddings, seeds_t)

    left_low = along_x(low, 1)
    right_high = along_x(high, -1)
    below = from_wide(units, -2)
    above = from_wide(units, 2)
    left_high = along_x(high, 1)
    right_low = along_x(low, -1)
    partner = swap_core(units)
    far_low = along_x(left_low, 1)
    far_high = along_x(right_high, -1)
    across = swap_core(jnp.where(core == 0, above, below))
    join = lambda a, b: jnp.concatenate([a, b], 0).reshape(BLK, ROWS, D)
    left = join(left_low, left_high)
    right = join(right_low, right_high)
    far = join(far_low, far_high)

    lists = jnp.concatenate(
        [neighbours, along_x(neighbours, 1), along_x(neighbours, -1), along_x(neighbours, 2)], 0
    )
    wides = jnp.stack(
        [here_w, here_w + 1 - 2 * core, here_w - 2, here_w + 2, here_w - 1 + 2 * core]
    ) % NW
    ids = ((wides[:, None] * NX + here_x) * BLK + jnp.arange(BLK)[None, :]).reshape(-1)
    used = jnp.any(lists[:, :, None] == ids[None, None, :], axis=1).astype(jnp.int32)

    states = wide_exchange(state, core)
    w0, acc0, deg0 = build(
        used[:3, :6].reshape(-1), [units], [units, partner], states[:2], [None], [None]
    )
    w1, acc1, deg1 = build(
        used[3:9, :6].reshape(-1), [left, right], [units, partner], states[:2], [None] * 2, [None] * 2
    )
    w2, acc2, deg2 = build(
        used[:9, 6:].reshape(-1), [units, left, right], [below, above, across], states[2:],
        [acc0, acc1[:3], acc1[3:]], [deg0, deg1[:3], deg1[3:]],
    )
    w3, acc3, deg3 = build(
        used[9:].reshape(-1), [far], [units, partner, below, above, across], states, [None], [None]
    )
    weights = [w0, w1, w2, w3]
    plan = (
        [(0, 0, 6, 0, 0), (0, 0, 6, 3, 1), (2, 0, 9, 0, 2), (2, 0, 9, 3, 3), (2, 0, 9, 6, 4)],
        [(1, 0, 6, 0, 0), (1, 0, 6, 3, 1), (2, 3, 9, 0, 2), (2, 3, 9, 3, 3), (2, 3, 9, 6, 4)],
        [(1, 3, 6, 0, 0), (1, 3, 6, 3, 1), (2, 6, 9, 0, 2), (2, 6, 9, 3, 3), (2, 6, 9, 6, 4)],
        [(3, 0, 15, 0, 0), (3, 0, 15, 3, 1), (3, 0, 15, 6, 2), (3, 0, 15, 9, 3), (3, 0, 15, 12, 4)],
    )

    def reduce_rows(own, to_left, to_right, to_far):
        return own + along_x(to_far, 2) + along_x(to_left, -1) + along_x(to_right, 1)

    wide_acc = jnp.concatenate([acc2, deg2], 1)
    far_acc = jnp.concatenate([acc3, deg3], 1)
    total = reduce_rows(wide_acc[:3], wide_acc[3:6], wide_acc[6:], far_acc)
    degree = jnp.sum(total[:, CH:], axis=1, keepdims=True)
    scale = ALPHA / degree
    prior = (1.0 - ALPHA) * seeds_t
    scores = total[:, :CH] * scale + prior
    flat = used.reshape(-1)
    for _ in range(ITERS - 1):
        states = wide_exchange(scores.astype(BF16), core)
        acc = spread(plan, flat, weights, states)
        total = reduce_rows(acc[:3], acc[3:6], acc[6:9], acc[9:])
        scores = total * scale + prior
    return jnp.swapaxes(scores, 1, 2)


def solution(mesh):
    fine = Mesh(mesh.devices.reshape(4, 4, 2, 4), ("z", "y", "c", "x"))
    everywhere = ("z", "y", "c", "x")
    return jax.shard_map(
        local,
        mesh=fine,
        in_specs=(P(everywhere, None, None), P(everywhere, None, None), P(everywhere, None)),
        out_specs=P(everywhere, None, None),
        check_vma=False,
    )
```

time: 565 us -> 234 us (0.41)
  local copies, waits for them, and re-layouts: 191 us -> 23.6 us
  waiting for transfers between devices: 212 us -> 73.6 us
  Pallas kernels: 0 us -> 69.6 us
  matrix products: 46.9 us -> 0 us
  blocking collectives: 39.2 us -> 0 us
  starting transfers between devices: 30.1 us -> 61.2 us
  other arithmetic: 21.8 us -> 5.84 us
  between operations: 13.7 us -> 0.38 us
  loops' own time: 8.02 us -> 0 us
    gather x15 -> x0, local copies, waits for them, and re-layouts: 109 us -> none  [the longest x12 101 us: turn(): tiles, part_degree = tile_weights(own, near_all[picked], keep)]
    ppermute x16 -> x34, waiting for transfers between devices: 174 us -> 73.6 us  [the longest x18 45.1 us: along_x(): return lax.ppermute(v, 'x', [(i, (i + by) % NX) for i in range(NX)])]
    pallas_call x0 -> x7, Pallas kernels: none -> 69.6 us  [the longest x4 39.6 us: build(): pl.pallas_call(functools.partial(build_kernel, n_rows, n_cols, has_acc),...]
    dot_general x15 -> x0, matrix products: 46.9 us -> none  [the longest x12 24.7 us: tile_weights(): jnp.einsum('rd,kqd->krq', own, near_units, preferred_element_type=jnp.flo...]
    all_gather x3 -> x0, blocking collectives: 39.2 us -> none  [fetch_scores(): group = lax.all_gather(state[None], 'narrow', axis=0, tiled=True)]
    all_gather x1 -> x0, waiting for transfers between devices: 38.3 us -> none  [fetch_units(): group = lax.all_gather(units[None], 'narrow', axis=0, tiled=True)]
    ppermute x16 -> x34, starting transfers between devices: 30.1 us -> 61.2 us  [the longest x18 39.1 us: along_x(): return lax.ppermute(v, 'x', [(i, (i + by) % NX) for i in range(NX)])]
    reshape x6 -> x4, local copies, waits for them, and re-layouts: 27.1 us -> 1.64 us  [the longest x1 0.78 us: local(): used[:9, 6:].reshape(-1)]
  transfers between devices with their start and end apart: 17 -> 34, of which waited for: 9 -> 18; matrix products, arithmetic and copies ran while one was open for 5% -> 4% of each run, Pallas kernels for 0% -> 10%
where the time goes in v1:
time: 234 us
  waiting for transfers between devices  73.6 us (31%)
  Pallas kernels  69.6 us (30%)
  starting transfers between devices  61.2 us (26%)
  local copies, waits for them, and re-layouts  23.6 us (10%)
  other arithmetic  5.84 us (2%)
    ppermute x18, waiting for transfers between devices, along_x(): return lax.ppermute(v, 'x', [(i, (i + by) % NX) for i in range(NX)])  45.1 us
    pallas_call x4, Pallas kernels, build(): pl.pallas_call(functools.partial(build_kernel, n_rows, n_cols, has_acc),...  39.6 us
    ppermute x18, starting transfers between devices, along_x(): return lax.ppermute(v, 'x', [(i, (i + by) % NX) for i in range(NX)])  39.1 us
    pallas_call x2, Pallas kernels, spread(): pl.pallas_call(functools.partial(spread_kernel, plan, len(weights)), out_...  29.6 us
    ppermute x8, waiting for transfers between devices, from_wide(): return lax.ppermute(v, WIDE, [((i + offset) % NW, i) for i in range(NW)])  26.1 us
    ppermute x8, starting transfers between devices, from_wide(): return lax.ppermute(v, WIDE, [((i + offset) % NW, i) for i in range(NW)])  21.2 us
    unnamed x41, local copies, waits for them, and re-layouts  19.2 us
  transfers between devices with their start and end apart: 34, of which 18 were waited for; matrix products, arithmetic and copies ran while one was open for 4% of the time, Pallas kernels for 10%

profile of v1, /device:TPU:0, one launch (start us, length us, event | category | flops | bytes accessed | tf_op | source)
XLA Modules:
  0.0 234.3 jit_solution(6748343194666575297)
XLA Ops:
  0.0 0.9 copy-done.9
  0.9 1.3 copy-done.11
  4.9 1.7 collective-permute-start.9
  6.5 4.9 %collective-permute-start.10 = (bf16[3,256,768]{2,1,0:T(8,128)(2,1)S(1)}, bf16[3,256,768]{2,1,0:T(8,128)(2,1)S(1)}, u32[]{:S(2)}, u32[]{:S(2)}) collective-permute-start(bf16[3,256,768]{2,1,0:T(8,128)(2,1)S(1)} %get-tuple-element.21.refs_1_.refs_2_.refs_3_), channel_id=1, source_target_pairs={{8,0},{12,4},{16,8},{20,12},{24,16},{28,20},{32,24},{36,28},{40,32... | collective-permute-start | bytes 3538952 | tf_op jit(solution)/shard_map/ppermute | solution.py:36
  11.5 3.0 %collective-permute-start.2 = (s32[3,32]{1,0:T(4,128)S(1)}, s32[3,32]{1,0:T(4,128)S(1)}, u32[]{:S(2)}, u32[]{:S(2)}) collective-permute-start(s32[3,32]{1,0:T(4,128)S(1)} %copy-done.18), channel_id=1, source_target_pairs={{0,2},{1,3},{2,0},{3,1},{4,6},{5,7},{6,4},{7,5},{8,10},{9,11},{10,... | collective-permute-start | bytes 1160 | tf_op jit(solution)/shard_map/ppermute | solution.py:32
  14.5 1.1 collective-permute-start.1
  18.1 2.4 %collective-permute-start.8 = (bf16[384,768]{1,0:T(8,128)(2,1)}, bf16[384,768]{1,0:T(8,128)(2,1)}, u32[]{:S(2)}, u32[]{:S(2)}) collective-permute-start(bf16[384,768]{1,0:T(8,128)(2,1)} %copy-done.15), channel_id=1, source_target_pairs={{0,3},{1,0},{2,1},{3,2},{4,7},{5,4},{6,5},{7,6},{8,11},{9,8},{10,9... | collective-permute-start | bytes 1769480 | tf_op jit(solution)/shard_map/ppermute | solution.py:32
  21.6 18.0 %collective-permute-done.12.refs_7_.refs_9_ = bf16[3,64,256]{2,1,0:T(8,128)(2,1)} collective-permute-done((bf16[3,64,256]{2,1,0:T(8,128)(2,1)}, bf16[3,64,256]{2,1,0:T(8,128)(2,1)}, u32[]{:S(2)}, u32[]{:S(2)}) %collective-permute-start.12) | collective-permute-done | bytes 98336 | tf_op jit(solution)/shard_map/ppermute | solution.py:36
  39.6 1.7 collective-permute-start.13
  42.0 2.6 %collective-permute-done.13.refs_8_.refs_10_ = bf16[3,64,256]{2,1,0:T(8,128)(2,1)} collective-permute-done((bf16[3,64,256]{2,1,0:T(8,128)(2,1)}, bf16[3,64,256]{2,1,0:T(8,128)(2,1)}, u32[]{:S(2)}, u32[]{:S(2)}) %collective-permute-start.13) | collective-permute-done | bytes 98336 | tf_op jit(solution)/shard_map/ppermute | solution.py:36
  44.6 2.8 %collective-permute-start.7 = (bf16[384,768]{1,0:T(8,128)(2,1)}, bf16[384,768]{1,0:T(8,128)(2,1)}, u32[]{:S(2)}, u32[]{:S(2)}) collective-permute-start(bf16[384,768]{1,0:T(8,128)(2,1)} %copy-done.14), channel_id=1, source_target_pairs={{0,3},{1,0},{2,1},{3,2},{4,7},{5,4},{6,5},{7,6},{8,11},{9,8},{10,9... | collective-permute-start | bytes 1769480 | tf_op jit(solution)/shard_map/ppermute | solution.py:32
  47.3 1.0 compare_reduce_fusion
  53.5 5.0 %collective-permute-done.7 = bf16[384,768]{1,0:T(8,128)(2,1)} collective-permute-done((bf16[384,768]{1,0:T(8,128)(2,1)}, bf16[384,768]{1,0:T(8,128)(2,1)}, u32[]{:S(2)}, u32[]{:S(2)}) %collective-permute-start.7) | collective-permute-done | bytes 589856 | tf_op jit(solution)/shard_map/ppermute | solution.py:32
  58.5 1.3 pad_maximum_fusion.1
  59.9 9.1 %collective-permute-done.6 = bf16[384,768]{1,0:T(8,128)(2,1)S(1)} collective-permute-done((bf16[384,768]{1,0:T(8,128)(2,1)}, bf16[384,768]{1,0:T(8,128)(2,1)S(1)}, u32[]{:S(2)}, u32[]{:S(2)}) %collective-permute-start.6) | collective-permute-done | bytes 589856 | tf_op jit(solution)/shard_map/ppermute | solution.py:32
  69.0 9.5 %collective-permute-done.5 = bf16[384,768]{1,0:T(8,128)(2,1)S(1)} collective-permute-done((bf16[384,768]{1,0:T(8,128)(2,1)}, bf16[384,768]{1,0:T(8,128)(2,1)S(1)}, u32[]{:S(2)}, u32[]{:S(2)}) %collective-permute-start.5) | collective-permute-done | bytes 589856 | tf_op jit(solution)/shard_map/ppermute | solution.py:32
  78.5 2.1 collective-permute-start.15
  80.6 8.7 %build_2_2.1 = (bf16[36,256,256]{2,1,0:T(8,128)(2,1)S(1)}, f32[6,64,256]{2,1,0:T(8,128)S(1)}, f32[6,8,256]{2,1,0:T(8,128)S(1)}) custom-call(s32[36]{0:T(128)S(1)} %reshape.162.refs_0_, bf16[3,256,768]{2,1,0:T(8,128)(2,1)S(1)} %bitcast.18, bf16[3,256,768]{2,1,0:T(8,128)(2,1)S(1)} %bitcast.16, ...), custom_call_target="tpu_custom_call" | custom-call | flops 1440000000 | bytes 4718592 | tf_op jit(solution)/shard_map/build_2_2/pallas_call | solution.py:126
  89.4 2.1 copy-done.3
  92.0 4.2 %build_1_2.1 = (bf16[18,256,256]{2,1,0:T(8,128)(2,1)S(1)}, f32[3,64,256]{2,1,0:T(8,128)S(1)}, f32[3,8,256]{2,1,0:T(8,128)S(1)}) custom-call(s32[18]{0:T(128)S(1)} %reshape.161.refs_0_, bf16[3,256,768]{2,1,0:T(8,128)(2,1)S(1)} %get-tuple-element.21.refs_1_.refs_2_.refs_3_, bf16[3,256,768]{2,1,0:T(8,128)(2,1)S(1)} %get-tuple-element.21.refs_1_.refs_2_.refs_3_, ...), custom_call_target="tpu_custom_call" | custom-call | flops 720000000 | bytes 2359296 | tf_op jit(solution)/shard_map/build_1_2/pallas_call | solution.py:126
  96.3 16.6 %build_3_3.1 = (bf16[81,256,256]{2,1,0:T(8,128)(2,1)S(1)}, f32[9,64,256]{2,1,0:T(8,128)S(1)}, f32[9,8,256]{2,1,0:T(8,128)S(1)}) custom-call(s32[81]{0:T(128)S(1)} %reshape.165.refs_0_, bf16[3,256,768]{2,1,0:T(8,128)(2,1)S(1)} %get-tuple-element.21.refs_1_.refs_2_.refs_3_, bf16[3,256,768]{2,1,0:T(8,128)(2,1)S(1)} %bitcast.19, ...), custom_call_target="tpu_custom_call" | custom-call | flops 3240000000 | bytes 10616832 | tf_op jit(solution)/shard_map/build_3_3/pallas_call | solution.py:126
  113.0 4.1 %copy-done = bf16[81,256,256]{2,1,0:T(8,128)(2,1)} copy-done((bf16[81,256,256]{2,1,0:T(8,128)(2,1)}, bf16[81,256,256]{2,1,0:T(8,128)(2,1)S(1)}, u32[]{:S(2)}) %copy-start) | copy-done | bytes 10616856
  117.2 7.7 %collective-permute-start.19 = (f32[3,72,256]{2,1,0:T(8,128)S(1)}, f32[3,72,256]{2,1,0:T(8,128)S(1)}, u32[]{:S(2)}, u32[]{:S(2)}) collective-permute-start(f32[3,72,256]{2,1,0:T(8,128)S(1)} %get-tuple-element.44), channel_id=1, source_target_pairs={{0,1},{1,2},{2,3},{3,0},{4,5},{5,6},{6,7},{7,4},{8,9},{9,10},{10,1... | collective-permute-start | bytes 663560 | tf_op jit(solution)/shard_map/ppermute | solution.py:32
  124.8 10.0 %build_1_5.1 = (bf16[45,256,256]{2,1,0:T(8,128)(2,1)S(1)}, f32[3,64,256]{2,1,0:T(8,128)S(1)}, f32[3,8,256]{2,1,0:T(8,128)S(1)}) custom-call(s32[45]{0:T(128)S(1)} %reshape.166.refs_0_, bf16[3,256,768]{2,1,0:T(8,128)(2,1)S(1)} %bitcast.14, bf16[3,256,768]{2,1,0:T(8,128)(2,1)S(1)} %get-tuple-element.21.refs_1_.refs_2_.refs_3_, ...), custom_call_target="tpu_custom_call" | custom-call | flops 1800000000 | bytes 5898240 | tf_op jit(solution)/shard_map/build_1_5/pallas_call | solution.py:126
  134.8 2.5 %copy-done.1 = bf16[45,256,256]{2,1,0:T(8,128)(2,1)} copy-done((bf16[45,256,256]{2,1,0:T(8,128)(2,1)}, bf16[45,256,256]{2,1,0:T(8,128)(2,1)S(1)}, u32[]{:S(2)}) %copy-start.1) | copy-done | bytes 5898264
  137.3 5.7 %collective-permute-start.17 = (f32[3,72,256]{2,1,0:T(8,128)S(1)}, f32[3,72,256]{2,1,0:T(8,128)S(1)}, u32[]{:S(2)}, u32[]{:S(2)}) collective-permute-start(f32[3,72,256]{2,1,0:T(8,128)S(1)} %pad_maximum_fusion.3), channel_id=1, source_target_pairs={{0,2},{1,3},{2,0},{3,1},{4,6},{5,7},{6,4},{7,5},{8,10},{9,11},{10,... | collective-permute-start | bytes 663560 | tf_op jit(solution)/shard_map/ppermute | solution.py:32
  143.0 6.1 %collective-permute-done.17 = f32[3,72,256]{2,1,0:T(8,128)S(1)} collective-permute-done((f32[3,72,256]{2,1,0:T(8,128)S(1)}, f32[3,72,256]{2,1,0:T(8,128)S(1)}, u32[]{:S(2)}, u32[]{:S(2)}) %collective-permute-start.17) | collective-permute-done | bytes 221216 | tf_op jit(solution)/shard_map/ppermute | solution.py:32
  149.4 5.3 %collective-permute-start.22 = (bf16[3,64,256]{2,1,0:T(8,128)(2,1)S(1)}, bf16[3,64,256]{2,1,0:T(8,128)(2,1)S(1)}, u32[]{:S(2)}, u32[]{:S(2)}) collective-permute-start(bf16[3,64,256]{2,1,0:T(8,128)(2,1)S(1)} %fusion.13.refs_4_), channel_id=1, source_target_pairs={{8,0},{12,4},{16,8},{20,12},{24,16},{28,20},{32,24},{36,28},{40,32... | collective-permute-start | bytes 294920 | tf_op jit(solution)/shard_map/ppermute | solution.py:36
  154.7 2.8 %collective-permute-done.21.refs_6_ = bf16[3,64,256]{2,1,0:T(8,128)(2,1)S(1)} collective-permute-done((bf16[3,64,256]{2,1,0:T(8,128)(2,1)S(1)}, bf16[3,64,256]{2,1,0:T(8,128)(2,1)S(1)}, u32[]{:S(2)}, u32[]{:S(2)}) %collective-permute-start.21) | collective-permute-done | bytes 98336 | tf_op jit(solution)/shard_map/ppermute | solution.py:36
  157.7 1.2 collective-permute-done.23.refs_8_
  158.9 2.7 %copy-done.2 = bf16[45,256,256]{2,1,0:T(8,128)(2,1)S(1)} copy-done((bf16[45,256,256]{2,1,0:T(8,128)(2,1)S(1)}, bf16[45,256,256]{2,1,0:T(8,128)(2,1)}, u32[]{:S(2)}) %copy-start.2) | copy-done | bytes 5898264
  161.6 2.3 copy-done.4
  163.9 14.8 %spread.2 = f32[12,64,256]{2,1,0:T(8,128)S(1)} custom-call(s32[180]{0:T(256)S(1)} %reshape.168.mask_ref, bf16[18,256,256]{2,1,0:T(8,128)(2,1)S(1)} %get-tuple-element.23.refs_0_, bf16[36,256,256]{2,1,0:T(8,128)(2,1)S(1)} %copy-done.4, bf16[81,256,256]{2,1,0:T(8,128)(2,1)} %copy-done, bf16[45,256,256]{2,1,0:T(8,128)(2,1)S(1)} %copy-done.2, ...), custom_call_target="tpu_custom_call" | custom-call | flops 630000000 | bytes 10000000 | tf_op jit(solution)/shard_map/spread/pallas_call | solution.py:170
  178.8 1.2 collective-permute-start.26
  179.9 2.1 collective-permute-start.25
  182.1 2.1 collective-permute-start.24
  184.2 1.5 collective-permute-done.26
  186.3 3.1 %collective-permute-done.24 = f32[3,64,256]{2,1,0:T(8,128)S(1)} collective-permute-done((f32[3,64,256]{2,1,0:T(8,128)S(1)}, f32[3,64,256]{2,1,0:T(8,128)S(1)}, u32[]{:S(2)}, u32[]{:S(2)}) %collective-permute-start.24) | collective-permute-done | bytes 196640 | tf_op jit(solution)/shard_map/ppermute | solution.py:32
  190.4 6.5 %collective-permute-start.29 = (bf16[3,64,256]{2,1,0:T(8,128)(2,1)S(1)}, bf16[3,64,256]{2,1,0:T(8,128)(2,1)S(1)}, u32[]{:S(2)}, u32[]{:S(2)}) collective-permute-start(bf16[3,64,256]{2,1,0:T(8,128)(2,1)S(1)} %fusion.11.refs_4_), channel_id=1, source_target_pairs={{8,0},{12,4},{16,8},{20,12},{24,16},{28,20},{32,24},{36,28},{40,32... | collective-permute-start | bytes 294920 | tf_op jit(solution)/shard_map/ppermute | solution.py:36
  197.5 2.8 %collective-permute-done.28.refs_6_ = bf16[3,64,256]{2,1,0:T(8,128)(2,1)S(1)} collective-permute-done((bf16[3,64,256]{2,1,0:T(8,128)(2,1)S(1)}, bf16[3,64,256]{2,1,0:T(8,128)(2,1)S(1)}, u32[]{:S(2)}, u32[]{:S(2)}) %collective-permute-start.28) | collective-permute-done | bytes 98336 | tf_op jit(solution)/shard_map/ppermute | solution.py:36
  200.4 1.2 collective-permute-done.30.refs_8_
  201.6 14.8 %spread.3 = f32[12,64,256]{2,1,0:T(8,128)S(1)} custom-call(s32[180]{0:T(256)S(1)} %reshape.168.mask_ref, bf16[18,256,256]{2,1,0:T(8,128)(2,1)S(1)} %get-tuple-element.23.refs_0_, bf16[36,256,256]{2,1,0:T(8,128)(2,1)S(1)} %copy-done.4, bf16[81,256,256]{2,1,0:T(8,128)(2,1)} %copy-done, bf16[45,256,256]{2,1,0:T(8,128)(2,1)S(1)} %copy-done.2, ...), custom_call_target="tpu_custom_call" | custom-call | flops 630000000 | bytes 10000000 | tf_op jit(solution)/shard_map/spread/pallas_call | solution.py:170
  216.5 3.6 %collective-permute-start.33 = (f32[3,64,256]{2,1,0:T(8,128)S(1)}, f32[3,64,256]{2,1,0:T(8,128)S(1)}, u32[]{:S(2)}, u32[]{:S(2)}) collective-permute-start(f32[3,64,256]{2,1,0:T(8,128)S(1)} %get-tuple-element.38), channel_id=1, source_target_pairs={{0,1},{1,2},{2,3},{3,0},{4,5},{5,6},{6,7},{7,4},{8,9},{9,10},{10,1... | collective-permute-start | bytes 589832 | tf_op jit(solution)/shard_map/ppermute | solution.py:32
  220.1 2.4 %collective-permute-start.32 = (f32[3,64,256]{2,1,0:T(8,128)S(1)}, f32[3,64,256]{2,1,0:T(8,128)S(1)}, u32[]{:S(2)}, u32[]{:S(2)}) collective-permute-start(f32[3,64,256]{2,1,0:T(8,128)S(1)} %get-tuple-element.39), channel_id=1, source_target_pairs={{0,3},{1,0},{2,1},{3,2},{4,7},{5,4},{6,5},{7,6},{8,11},{9,8},{10,9... | collective-permute-start | bytes 589832 | tf_op jit(solution)/shard_map/ppermute | solution.py:32
  222.4 1.4 collective-permute-start.31
  223.8 4.0 %collective-permute-done.33 = f32[3,64,256]{2,1,0:T(8,128)S(1)} collective-permute-done((f32[3,64,256]{2,1,0:T(8,128)S(1)}, f32[3,64,256]{2,1,0:T(8,128)S(1)}, u32[]{:S(2)}, u32[]{:S(2)}) %collective-permute-start.33) | collective-permute-done | bytes 196640 | tf_op jit(solution)/shard_map/ppermute | solution.py:32
  227.9 4.0 %collective-permute-done.32 = f32[3,64,256]{2,1,0:T(8,128)S(1)} collective-permute-done((f32[3,64,256]{2,1,0:T(8,128)S(1)}, f32[3,64,256]{2,1,0:T(8,128)S(1)}, u32[]{:S(2)}, u32[]{:S(2)}) %collective-permute-start.32) | collective-permute-done | bytes 196640 | tf_op jit(solution)/shard_map/ppermute | solution.py:32
  231.8 1.7 collective-permute-done.31
  (104 shorter events, 16.4 us)
Async XLA Ops:
  0.9 1.3 copy-start.11
  2.2 9.3 %copy-start.18 = (s32[3,32]{1,0:T(4,128)S(1)}, s32[3,32]{1,0:T(4,128)}, u32[]{:S(2)}) copy-start(s32[3,32]{1,0:T(4,128)} %param.5) | copy-start | bytes 1156
  4.9 46.3 %collective-permute-start.9 = (bf16[3,256,768]{2,1,0:T(8,128)(2,1)S(1)}, bf16[3,256,768]{2,1,0:T(8,128)(2,1)S(1)}, u32[]{:S(2)}, u32[]{:S(2)}) collective-permute-start(bf16[3,256,768]{2,1,0:T(8,128)(2,1)S(1)} %get-tuple-element.21.refs_1_.refs_2_.refs_3_), channel_id=1, source_target_pairs={{120,0},{124,4},{0,8},{4,12},{8,16},{12,20},{16,24},{20,28},{24,32... | collective-permute-start | bytes 3538952 | tf_op jit(solution)/shard_map/ppermute | solution.py:36
  6.5 44.7 %collective-permute-start.10 = (bf16[3,256,768]{2,1,0:T(8,128)(2,1)S(1)}, bf16[3,256,768]{2,1,0:T(8,128)(2,1)S(1)}, u32[]{:S(2)}, u32[]{:S(2)}) collective-permute-start(bf16[3,256,768]{2,1,0:T(8,128)(2,1)S(1)} %get-tuple-element.21.refs_1_.refs_2_.refs_3_), channel_id=1, source_target_pairs={{8,0},{12,4},{16,8},{20,12},{24,16},{28,20},{32,24},{36,28},{40,32... | collective-permute-start | bytes 3538952 | tf_op jit(solution)/shard_map/ppermute | solution.py:36
  11.5 6.4 %collective-permute-start.2 = (s32[3,32]{1,0:T(4,128)S(1)}, s32[3,32]{1,0:T(4,128)S(1)}, u32[]{:S(2)}, u32[]{:S(2)}) collective-permute-start(s32[3,32]{1,0:T(4,128)S(1)} %copy-done.18), channel_id=1, source_target_pairs={{0,2},{1,3},{2,0},{3,1},{4,6},{5,7},{6,4},{7,5},{8,10},{9,11},{10,... | collective-permute-start | bytes 1160 | tf_op jit(solution)/shard_map/ppermute | solution.py:32
  14.5 3.6 %collective-permute-start.1 = (s32[3,32]{1,0:T(4,128)S(1)}, s32[3,32]{1,0:T(4,128)S(1)}, u32[]{:S(2)}, u32[]{:S(2)}) collective-permute-start(s32[3,32]{1,0:T(4,128)S(1)} %copy-done.18), channel_id=1, source_target_pairs={{0,3},{1,0},{2,1},{3,2},{4,7},{5,4},{6,5},{7,6},{8,11},{9,8},{10,9... | collective-permute-start | bytes 1160 | tf_op jit(solution)/shard_map/ppermute | solution.py:32
  15.6 4.8 %collective-permute-start = (s32[3,32]{1,0:T(4,128)S(1)}, s32[3,32]{1,0:T(4,128)S(1)}, u32[]{:S(2)}, u32[]{:S(2)}) collective-permute-start(s32[3,32]{1,0:T(4,128)S(1)} %copy-done.18), channel_id=1, source_target_pairs={{0,1},{1,2},{2,3},{3,0},{4,5},{5,6},{6,7},{7,4},{8,9},{9,10},{10,1... | collective-permute-start | bytes 1160 | tf_op jit(solution)/shard_map/ppermute | solution.py:32
  17.9 62.7 %collective-permute-start.3 = (bf16[3,256,768]{2,1,0:T(8,128)(2,1)S(1)}, bf16[3,256,768]{2,1,0:T(8,128)(2,1)}, u32[]{:S(2)}, u32[]{:S(2)}) collective-permute-start(bf16[3,256,768]{2,1,0:T(8,128)(2,1)S(1)} %get-tuple-element.21.refs_1_.refs_2_.refs_3_), channel_id=1, source_target_pairs={{0,4},{4,0},{1,5},{5,1},{2,6},{6,2},{3,7},{7,3},{8,12},{12,8},{9,1... | collective-permute-start | bytes 3538952 | tf_op jit(solution)/shard_map/ppermute | solution.py:40
  18.1 34.5 %collective-permute-start.8 = (bf16[384,768]{1,0:T(8,128)(2,1)}, bf16[384,768]{1,0:T(8,128)(2,1)}, u32[]{:S(2)}, u32[]{:S(2)}) collective-permute-start(bf16[384,768]{1,0:T(8,128)(2,1)} %copy-done.15), channel_id=1, source_target_pairs={{0,3},{1,0},{2,1},{3,2},{4,7},{5,4},{6,5},{7,6},{8,11},{9,8},{10,9... | collective-permute-start | bytes 1769480 | tf_op jit(solution)/shard_map/ppermute | solution.py:32
  21.0 18.7 %collective-permute-start.12 = (bf16[3,64,256]{2,1,0:T(8,128)(2,1)}, bf16[3,64,256]{2,1,0:T(8,128)(2,1)}, u32[]{:S(2)}, u32[]{:S(2)}) collective-permute-start(bf16[3,64,256]{2,1,0:T(8,128)(2,1)} %copy-done.12), channel_id=1, source_target_pairs={{120,0},{124,4},{0,8},{4,12},{8,16},{12,20},{16,24},{20,28},{24,32... | collective-permute-start | bytes 294920 | tf_op jit(solution)/shard_map/ppermute | solution.py:36
  39.6 4.9 %collective-permute-start.13 = (bf16[3,64,256]{2,1,0:T(8,128)(2,1)}, bf16[3,64,256]{2,1,0:T(8,128)(2,1)}, u32[]{:S(2)}, u32[]{:S(2)}) collective-permute-start(bf16[3,64,256]{2,1,0:T(8,128)(2,1)} %copy-done.12), channel_id=1, source_target_pairs={{8,0},{12,4},{16,8},{20,12},{24,16},{28,20},{32,24},{36,28},{40,32... | collective-permute-start | bytes 294920 | tf_op jit(solution)/shard_map/ppermute | solution.py:36
  44.6 14.0 %collective-permute-start.7 = (bf16[384,768]{1,0:T(8,128)(2,1)}, bf16[384,768]{1,0:T(8,128)(2,1)}, u32[]{:S(2)}, u32[]{:S(2)}) collective-permute-start(bf16[384,768]{1,0:T(8,128)(2,1)} %copy-done.14), channel_id=1, source_target_pairs={{0,3},{1,0},{2,1},{3,2},{4,7},{5,4},{6,5},{7,6},{8,11},{9,8},{10,9... | collective-permute-start | bytes 1769480 | tf_op jit(solution)/shard_map/ppermute | solution.py:32
  51.2 7.3 %copy-start.13 = (bf16[3,64,256]{2,1,0:T(8,128)(2,1)S(1)}, bf16[3,64,256]{2,1,0:T(8,128)(2,1)}, u32[]{:S(2)}) copy-start(bf16[3,64,256]{2,1,0:T(8,128)(2,1)} %copy-done.12) | copy-start | bytes 294916
  51.2 1.1 copy-start.5
  51.2 17.8 %collective-permute-start.6 = (bf16[384,768]{1,0:T(8,128)(2,1)}, bf16[384,768]{1,0:T(8,128)(2,1)S(1)}, u32[]{:S(2)}, u32[]{:S(2)}) collective-permute-start(bf16[384,768]{1,0:T(8,128)(2,1)} %copy-done.15), channel_id=1, source_target_pairs={{0,1},{1,2},{2,3},{3,0},{4,5},{5,6},{6,7},{7,4},{8,9},{9,10},{10,1... | collective-permute-start | bytes 1769480 | tf_op jit(solution)/shard_map/ppermute | solution.py:32
  51.3 1.3 copy-start.7
  51.3 27.1 %collective-permute-start.5 = (bf16[384,768]{1,0:T(8,128)(2,1)}, bf16[384,768]{1,0:T(8,128)(2,1)S(1)}, u32[]{:S(2)}, u32[]{:S(2)}) collective-permute-start(bf16[384,768]{1,0:T(8,128)(2,1)} %copy-done.14), channel_id=1, source_target_pairs={{0,1},{1,2},{2,3},{3,0},{4,5},{5,6},{6,7},{7,4},{8,9},{9,10},{10,1... | collective-permute-start | bytes 1769480 | tf_op jit(solution)/shard_map/ppermute | solution.py:32
  52.6 43.7 %collective-permute-start.11 = (bf16[3,256,768]{2,1,0:T(8,128)(2,1)S(1)}, bf16[3,256,768]{2,1,0:T(8,128)(2,1)S(1)}, u32[]{:S(2)}, u32[]{:S(2)}) collective-permute-start(bf16[3,256,768]{2,1,0:T(8,128)(2,1)S(1)} %broadcast_select_fusion), channel_id=1, source_target_pairs={{0,4},{4,0},{1,5},{5,1},{2,6},{6,2},{3,7},{7,3},{8,12},{12,8},{9,1... | collective-permute-start | bytes 3538952 | tf_op jit(solution)/shard_map/ppermute | solution.py:40
  58.5 20.0 %collective-permute-start.4 = (bf16[3,64,256]{2,1,0:T(8,128)(2,1)S(1)}, bf16[3,64,256]{2,1,0:T(8,128)(2,1)S(1)}, u32[]{:S(2)}, u32[]{:S(2)}) collective-permute-start(bf16[3,64,256]{2,1,0:T(8,128)(2,1)S(1)} %copy-done.13), channel_id=1, source_target_pairs={{0,4},{4,0},{1,5},{5,1},{2,6},{6,2},{3,7},{7,3},{8,12},{12,8},{9,1... | collective-permute-start | bytes 294920 | tf_op jit(solution)/shard_map/ppermute | solution.py:40
  68.9 27.3 %collective-permute-start.14 = (bf16[3,64,256]{2,1,0:T(8,128)(2,1)S(1)}, bf16[3,64,256]{2,1,0:T(8,128)(2,1)S(1)}, u32[]{:S(2)}, u32[]{:S(2)}) collective-permute-start(bf16[3,64,256]{2,1,0:T(8,128)(2,1)S(1)} %broadcast_select_fusion.3), channel_id=1, source_target_pairs={{0,4},{4,0},{1,5},{5,1},{2,6},{6,2},{3,7},{7,3},{8,12},{12,8},{9,1... | collective-permute-start | bytes 294920 | tf_op jit(solution)/shard_map/ppermute | solution.py:40
  78.4 13.1 %collective-permute-start.16 = (bf16[384,768]{1,0:T(8,128)(2,1)}, bf16[384,768]{1,0:T(8,128)(2,1)S(1)}, u32[]{:S(2)}, u32[]{:S(2)}) collective-permute-start(bf16[384,768]{1,0:T(8,128)(2,1)} %collective-permute-done.8), channel_id=1, source_target_pairs={{0,3},{1,0},{2,1},{3,2},{4,7},{5,4},{6,5},{7,6},{8,11},{9,8},{10,9... | collective-permute-start | bytes 1769480 | tf_op jit(solution)/shard_map/ppermute | solution.py:32
  78.5 13.4 %collective-permute-start.15 = (bf16[384,768]{1,0:T(8,128)(2,1)S(1)}, bf16[384,768]{1,0:T(8,128)(2,1)S(1)}, u32[]{:S(2)}, u32[]{:S(2)}) collective-permute-start(bf16[384,768]{1,0:T(8,128)(2,1)S(1)} %collective-permute-done.5), channel_id=1, source_target_pairs={{0,1},{1,2},{2,3},{3,0},{4,5},{5,6},{6,7},{7,4},{8,9},{9,10},{10,1... | collective-permute-start | bytes 1769480 | tf_op jit(solution)/shard_map/ppermute | solution.py:32
  89.4 2.1 copy-start.3
  92.0 4.3 %copy-start.6 = (bf16[3,256,768]{2,1,0:T(8,128)(2,1)S(1)}, bf16[3,256,768]{2,1,0:T(8,128)(2,1)}, u32[]{:S(2)}) copy-start(bf16[3,256,768]{2,1,0:T(8,128)(2,1)} %copy-done.5) | copy-start | bytes 3538948
  92.0 4.3 %copy-start.8 = (bf16[3,256,768]{2,1,0:T(8,128)(2,1)S(1)}, bf16[3,256,768]{2,1,0:T(8,128)(2,1)}, u32[]{:S(2)}) copy-start(bf16[3,256,768]{2,1,0:T(8,128)(2,1)} %copy-done.7) | copy-start | bytes 3538948
  113.0 4.1 %copy-start = (bf16[81,256,256]{2,1,0:T(8,128)(2,1)}, bf16[81,256,256]{2,1,0:T(8,128)(2,1)S(1)}, u32[]{:S(2)}) copy-start(bf16[81,256,256]{2,1,0:T(8,128)(2,1)S(1)} %get-tuple-element.31.refs_2_) | copy-start | bytes 31850500
  117.2 25.8 %collective-permute-start.19 = (f32[3,72,256]{2,1,0:T(8,128)S(1)}, f32[3,72,256]{2,1,0:T(8,128)S(1)}, u32[]{:S(2)}, u32[]{:S(2)}) collective-permute-start(f32[3,72,256]{2,1,0:T(8,128)S(1)} %get-tuple-element.44), channel_id=1, source_target_pairs={{0,1},{1,2},{2,3},{3,0},{4,5},{5,6},{6,7},{7,4},{8,9},{9,10},{10,1... | collective-permute-start | bytes 663560 | tf_op jit(solution)/shard_map/ppermute | solution.py:32
  124.8 18.2 %collective-permute-start.18 = (f32[3,72,256]{2,1,0:T(8,128)S(1)}, f32[3,72,256]{2,1,0:T(8,128)S(1)}, u32[]{:S(2)}, u32[]{:S(2)}) collective-permute-start(f32[3,72,256]{2,1,0:T(8,128)S(1)} %get-tuple-element.43), channel_id=1, source_target_pairs={{0,3},{1,0},{2,1},{3,2},{4,7},{5,4},{6,5},{7,6},{8,11},{9,8},{10,9... | collective-permute-start | bytes 663560 | tf_op jit(solution)/shard_map/ppermute | solution.py:32
  134.8 2.5 %copy-start.1 = (bf16[45,256,256]{2,1,0:T(8,128)(2,1)}, bf16[45,256,256]{2,1,0:T(8,128)(2,1)S(1)}, u32[]{:S(2)}) copy-start(bf16[45,256,256]{2,1,0:T(8,128)(2,1)S(1)} %get-tuple-element.32.refs_3_) | copy-start | bytes 17694724
  137.3 11.9 %copy-start.10 = (f32[3,256,64]{1,2,0:T(8,128)S(1)}, f32[3,256,64]{1,2,0:T(8,128)}, u32[]{:S(2)}) copy-start(f32[3,256,64]{1,2,0:T(8,128)} %param.4) | copy-start | bytes 589828
  137.3 20.3 %copy-start.17 = (s32[12,15]{1,0:T(8,128)S(1)}, s32[12,15]{1,0:T(8,128)}, u32[]{:S(2)}) copy-start(s32[12,15]{1,0:T(8,128)} %copy-done.16) | copy-start | bytes 2164
  137.3 11.8 %collective-permute-start.17 = (f32[3,72,256]{2,1,0:T(8,128)S(1)}, f32[3,72,256]{2,1,0:T(8,128)S(1)}, u32[]{:S(2)}, u32[]{:S(2)}) collective-permute-start(f32[3,72,256]{2,1,0:T(8,128)S(1)} %pad_maximum_fusion.3), channel_id=1, source_target_pairs={{0,2},{1,3},{2,0},{3,1},{4,6},{5,7},{6,4},{7,5},{8,10},{9,11},{10,... | collective-permute-start | bytes 663560 | tf_op jit(solution)/shard_map/ppermute | solution.py:32
  149.3 8.2 %collective-permute-start.21 = (bf16[3,64,256]{2,1,0:T(8,128)(2,1)S(1)}, bf16[3,64,256]{2,1,0:T(8,128)(2,1)S(1)}, u32[]{:S(2)}, u32[]{:S(2)}) collective-permute-start(bf16[3,64,256]{2,1,0:T(8,128)(2,1)S(1)} %fusion.13.refs_4_), channel_id=1, source_target_pairs={{120,0},{124,4},{0,8},{4,12},{8,16},{12,20},{16,24},{20,28},{24,32... | collective-permute-start | bytes 294920 | tf_op jit(solution)/shard_map/ppermute | solution.py:36
  149.4 8.1 %collective-permute-start.22 = (bf16[3,64,256]{2,1,0:T(8,128)(2,1)S(1)}, bf16[3,64,256]{2,1,0:T(8,128)(2,1)S(1)}, u32[]{:S(2)}, u32[]{:S(2)}) collective-permute-start(bf16[3,64,256]{2,1,0:T(8,128)(2,1)S(1)} %fusion.13.refs_4_), channel_id=1, source_target_pairs={{8,0},{12,4},{16,8},{20,12},{24,16},{28,20},{32,24},{36,28},{40,32... | collective-permute-start | bytes 294920 | tf_op jit(solution)/shard_map/ppermute | solution.py:36
  154.7 3.0 %collective-permute-start.20 = (bf16[3,64,256]{2,1,0:T(8,128)(2,1)S(1)}, bf16[3,64,256]{2,1,0:T(8,128)(2,1)S(1)}, u32[]{:S(2)}, u32[]{:S(2)}) collective-permute-start(bf16[3,64,256]{2,1,0:T(8,128)(2,1)S(1)} %fusion.13.refs_4_), channel_id=1, source_target_pairs={{0,4},{4,0},{1,5},{5,1},{2,6},{6,2},{3,7},{7,3},{8,12},{12,8},{9,1... | collective-permute-start | bytes 294920 | tf_op jit(solution)/shard_map/ppermute | solution.py:40
  157.5 1.4 collective-permute-start.23
  158.9 2.7 %copy-start.2 = (bf16[45,256,256]{2,1,0:T(8,128)(2,1)S(1)}, bf16[45,256,256]{2,1,0:T(8,128)(2,1)}, u32[]{:S(2)}) copy-start(bf16[45,256,256]{2,1,0:T(8,128)(2,1)} %copy-done.1) | copy-start | bytes 17694724
  161.6 2.3 copy-start.4
  178.8 6.9 %collective-permute-start.26 = (f32[3,64,256]{2,1,0:T(8,128)S(1)}, f32[3,64,256]{2,1,0:T(8,128)S(1)}, u32[]{:S(2)}, u32[]{:S(2)}) collective-permute-start(f32[3,64,256]{2,1,0:T(8,128)S(1)} %get-tuple-element.41), channel_id=1, source_target_pairs={{0,1},{1,2},{2,3},{3,0},{4,5},{5,6},{6,7},{7,4},{8,9},{9,10},{10,1... | collective-permute-start | bytes 589832 | tf_op jit(solution)/shard_map/ppermute | solution.py:32
  179.9 6.3 %collective-permute-start.25 = (f32[3,64,256]{2,1,0:T(8,128)S(1)}, f32[3,64,256]{2,1,0:T(8,128)S(1)}, u32[]{:S(2)}, u32[]{:S(2)}) collective-permute-start(f32[3,64,256]{2,1,0:T(8,128)S(1)} %get-tuple-element.42), channel_id=1, source_target_pairs={{0,3},{1,0},{2,1},{3,2},{4,7},{5,4},{6,5},{7,6},{8,11},{9,8},{10,9... | collective-permute-start | bytes 589832 | tf_op jit(solution)/shard_map/ppermute | solution.py:32
  182.1 7.3 %collective-permute-start.24 = (f32[3,64,256]{2,1,0:T(8,128)S(1)}, f32[3,64,256]{2,1,0:T(8,128)S(1)}, u32[]{:S(2)}, u32[]{:S(2)}) collective-permute-start(f32[3,64,256]{2,1,0:T(8,128)S(1)} %get-tuple-element.40), channel_id=1, source_target_pairs={{0,2},{1,3},{2,0},{3,1},{4,6},{5,7},{6,4},{7,5},{8,10},{9,11},{10,... | collective-permute-start | bytes 589832 | tf_op jit(solution)/shard_map/ppermute | solution.py:32
  189.4 10.8 %collective-permute-start.28 = (bf16[3,64,256]{2,1,0:T(8,128)(2,1)S(1)}, bf16[3,64,256]{2,1,0:T(8,128)(2,1)S(1)}, u32[]{:S(2)}, u32[]{:S(2)}) collective-permute-start(bf16[3,64,256]{2,1,0:T(8,128)(2,1)S(1)} %fusion.11.refs_4_), channel_id=1, source_target_pairs={{120,0},{124,4},{0,8},{4,12},{8,16},{12,20},{16,24},{20,28},{24,32... | collective-permute-start | bytes 294920 | tf_op jit(solution)/shard_map/ppermute | solution.py:36
  190.4 9.9 %collective-permute-start.29 = (bf16[3,64,256]{2,1,0:T(8,128)(2,1)S(1)}, bf16[3,64,256]{2,1,0:T(8,128)(2,1)S(1)}, u32[]{:S(2)}, u32[]{:S(2)}) collective-permute-start(bf16[3,64,256]{2,1,0:T(8,128)(2,1)S(1)} %fusion.11.refs_4_), channel_id=1, source_target_pairs={{8,0},{12,4},{16,8},{20,12},{24,16},{28,20},{32,24},{36,28},{40,32... | collective-permute-start | bytes 294920 | tf_op jit(solution)/shard_map/ppermute | solution.py:36
  196.9 3.5 %collective-permute-start.27 = (bf16[3,64,256]{2,1,0:T(8,128)(2,1)S(1)}, bf16[3,64,256]{2,1,0:T(8,128)(2,1)S(1)}, u32[]{:S(2)}, u32[]{:S(2)}) collective-permute-start(bf16[3,64,256]{2,1,0:T(8,128)(2,1)S(1)} %fusion.11.refs_4_), channel_id=1, source_target_pairs={{0,4},{4,0},{1,5},{5,1},{2,6},{6,2},{3,7},{7,3},{8,12},{12,8},{9,1... | collective-permute-start | bytes 294920 | tf_op jit(solution)/shard_map/ppermute | solution.py:40
  200.2 1.4 collective-permute-start.30
  216.5 11.3 %collective-permute-start.33 = (f32[3,64,256]{2,1,0:T(8,128)S(1)}, f32[3,64,256]{2,1,0:T(8,128)S(1)}, u32[]{:S(2)}, u32[]{:S(2)}) collective-permute-start(f32[3,64,256]{2,1,0:T(8,128)S(1)} %get-tuple-element.38), channel_id=1, source_target_pairs={{0,1},{1,2},{2,3},{3,0},{4,5},{5,6},{6,7},{7,4},{8,9},{9,10},{10,1... | collective-permute-start | bytes 589832 | tf_op jit(solution)/shard_map/ppermute | solution.py:32
  220.1 11.8 %collective-permute-start.32 = (f32[3,64,256]{2,1,0:T(8,128)S(1)}, f32[3,64,256]{2,1,0:T(8,128)S(1)}, u32[]{:S(2)}, u32[]{:S(2)}) collective-permute-start(f32[3,64,256]{2,1,0:T(8,128)S(1)} %get-tuple-element.39), channel_id=1, source_target_pairs={{0,3},{1,0},{2,1},{3,2},{4,7},{5,4},{6,5},{7,6},{8,11},{9,8},{10,9... | collective-permute-start | bytes 589832 | tf_op jit(solution)/shard_map/ppermute | solution.py:32
  222.4 11.1 %collective-permute-start.31 = (f32[3,64,256]{2,1,0:T(8,128)S(1)}, f32[3,64,256]{2,1,0:T(8,128)S(1)}, u32[]{:S(2)}, u32[]{:S(2)}) collective-permute-start(f32[3,64,256]{2,1,0:T(8,128)S(1)} %get-tuple-element.37), channel_id=1, source_target_pairs={{0,2},{1,3},{2,0},{3,1},{4,6},{5,7},{6,4},{7,5},{8,10},{9,11},{10,... | collective-permute-start | bytes 589832 | tf_op jit(solution)/shard_map/ppermute | solution.py:32
  (6 other events, 4.5 us)

commit v2 on v0

v2 whole, which is shorter than its diff:
```python
import functools
import math

import jax
import jax.numpy as jnp
from jax import lax
from jax.experimental import pallas as pl
from jax.experimental.pallas import tpu as pltpu
from jax.sharding import Mesh, PartitionSpec as P

NBR = 32
ITERS = 3
SHARP = 24.0
ALPHA = 0.8
EPS = 1e-06
ROWS = 256
D = 768
CH = 64
BLK = 3
NX = 4
NW = 32
SCALE = SHARP * math.log2(math.e)
WIDE = ("z", "y", "c")
VM = pl.BlockSpec(memory_space=pltpu.VMEM)
SM = pl.BlockSpec(memory_space=pltpu.SMEM)
F32 = jnp.float32
BF16 = jnp.bfloat16
FIRST = (0, 48, 96, 176)
CAPS = (36, 36, 64, 48)
CHUNK_ROWS = ((0, 1, 2, 3, 4, 8), (0, 1, 2, 3, 4, 8), (0, 1, 2, 3, 4, 8, 5, 6, 7), (9, 10, 11))
CHUNK_COLS = ((0, 6), (6, 12), (0, 15), (0, 15))
COUNTS = 240
LISTS = 256
SPARE = NX * BLK
SUMS = CH + 8
CHEAP = pl.CostEstimate(flops=1000, bytes_accessed=1000, transcendentals=0)


def along_x(v, sign):
    pairs = []
    for core in range(2):
        by = sign if core == 0 else -sign
        pairs += [(core * NX + x, core * NX + (x + by) % NX) for x in range(NX)]
    return lax.ppermute(v, ("c", "x"), pairs)


def across_x(v):
    return lax.ppermute(v, "x", [(x, (x + 2) % NX) for x in range(NX)])


def from_wide(v, sign):
    return lax.ppermute(
        v, WIDE, [((i + (2 * sign if i % 2 == 0 else -2 * sign)) % NW, i) for i in range(NW)]
    )


def swap_core(v):
    return lax.ppermute(v, "c", [(0, 1), (1, 0)])


def prep_kernel(emb_ref, seed_ref, two_ref, one_ref, full_ref):
    for block in range(BLK):
        values = emb_ref[block].astype(F32)
        total = jnp.sum(values * values, axis=-1, keepdims=True)
        unit = (values * lax.rsqrt(total + EPS)).astype(BF16)
        full_ref[block * ROWS : (block + 1) * ROWS] = unit
        full_ref[BLK * ROWS :, block * ROWS : (block + 1) * ROWS] = seed_ref[block].astype(BF16)
        if block < 2:
            two_ref[block * D : (block + 1) * D] = jnp.transpose(unit)
        else:
            one_ref[...] = jnp.transpose(unit)


def prepare(embeddings, seeds_t):
    return pl.pallas_call(
        prep_kernel,
        out_shape=(
            jax.ShapeDtypeStruct((2 * D, ROWS), BF16),
            jax.ShapeDtypeStruct((D, ROWS), BF16),
            jax.ShapeDtypeStruct((BLK * ROWS + CH, D), BF16),
        ),
        in_specs=[VM, VM],
        out_specs=(VM, VM, VM),
        compiler_params=pltpu.CompilerParams(vmem_limit_bytes=8 << 20),
        cost_estimate=CHEAP,
        name="prep",
    )(embeddings, seeds_t)


def plan_kernel(place_ref, own_ref, back_ref, fore_ref, far_ref, list_ref):
    wide, x = place_ref[0], place_ref[1]
    core = wide & 1
    partner = 3 - 2 * core
    first = 4 - 4 * core
    counts = [jnp.int32(0)] * 4
    for row in range(SPARE):
        ref = (own_ref, back_ref, fore_ref, far_ref)[row // BLK]
        chunks = [c for c in range(4) if row in CHUNK_ROWS[c]]
        code = (row * 16 + CHUNK_ROWS[chunks[0]].index(row)) * 16

        def body(k, carry, ref=ref, i=row % BLK, chunks=chunks, code=code):
            block = ref[i, k]
            device = (block * 43691) >> 17
            step = ((device >> 2) - wide + 2) & (NW - 1)
            source = jnp.where(
                step == 2,
                0,
                jnp.where(
                    step == partner,
                    1,
                    jnp.where(step == first, 2, jnp.where(step == 4 - first, 3, 4)),
                ),
            )
            column = source * BLK + block - BLK * device
            hit = jnp.where((block >= 0) & ((device & (NX - 1)) == x), 1, 0)
            if len(chunks) == 1:
                list_ref[FIRST[chunks[0]] + carry[0]] = code + column
                return (carry[0] + hit,)
            for c in chunks:
                list_ref[FIRST[c] + carry[c]] = code + column
            low = jnp.where(source < 2, hit, 0)
            high = jnp.where(source == 4, hit, 0)
            return (carry[0] + low, carry[1] + hit - low - high, carry[2] + high)

        got = lax.fori_loop(0, NBR, body, tuple(counts[c] for c in chunks))
        for c, n in zip(chunks, got):
            counts[c] = n
    for c in range(4):
        for pad in range(4):
            list_ref[FIRST[c] + counts[c] + pad] = SPARE * 256 + CHUNK_COLS[c][0]
        list_ref[COUNTS + c] = (counts[c] + 3) >> 2


def make_plan(place, own, back, fore, far):
    return pl.pallas_call(
        plan_kernel,
        out_shape=jax.ShapeDtypeStruct((LISTS,), jnp.int32),
        in_specs=[SM] * 5,
        out_specs=SM,
        cost_estimate=CHEAP,
        name="plan",
    )(place, own, back, fore, far)


def build_kernel(chunk, n_rows, n_cols, has_sums, *refs):
    refs = list(refs)
    list_ref = refs.pop(0)
    rows = [refs.pop(0) for _ in range(n_rows)]
    cols = [refs.pop(0) for _ in range(n_cols)]
    given = refs.pop(0) if has_sums else None
    w_ref = refs.pop(0)
    row_buf, col_buf, state_buf, sum_buf = refs[-4:]
    outs = refs[:-4]
    at = 0
    for ref in rows:
        row_buf[at : at + ref.shape[0]] = ref[...]
        at += ref.shape[0]
    for at, ref in enumerate(cols):
        col_buf[at * BLK * ROWS : (at + 1) * BLK * ROWS] = ref[: BLK * ROWS]
        for j in range(BLK):
            state_buf[at * BLK + j] = ref[BLK * ROWS :, j * ROWS : (j + 1) * ROWS]
    if has_sums:
        sum_buf[: given.shape[0]] = given[...]
    else:
        sum_buf[...] = jnp.zeros_like(sum_buf)
    base = CHUNK_COLS[chunk][0]
    steps = list_ref[COUNTS + chunk]

    def four_tiles(step, _):
        for k in range(4):
            n = 4 * step + k
            named = list_ref[FIRST[chunk] + n]
            col = (named & 15) - base
            cosine = jnp.dot(
                col_buf[pl.ds(pl.multiple_of(col * ROWS, ROWS), ROWS), :],
                row_buf[pl.ds(pl.multiple_of(((named >> 4) & 15) * D, D), D), :],
                preferred_element_type=F32,
            )
            weight = jnp.exp2(cosine * SCALE)
            w_ref[n] = weight.astype(BF16)
            sum_buf[named >> 8, CH:] += jnp.sum(weight.reshape(ROWS // 8, 8, ROWS), axis=0)
        return 0

    def four_spreads(step, _):
        for k in range(4):
            n = 4 * step + k
            named = list_ref[FIRST[chunk] + n]
            sum_buf[named >> 8, :CH] += jnp.dot(
                state_buf[(named & 15) - base], w_ref[n], preferred_element_type=F32
            )
        return 0

    lax.fori_loop(0, steps, four_tiles, 0)
    lax.fori_loop(0, steps, four_spreads, 0)
    at = BLK * (NX - 1) if chunk == 3 else 0
    for ref in outs:
        ref[...] = sum_buf[at : at + ref.shape[0]]
        at += ref.shape[0]


def build(chunk, lists, rows, cols, sums, out_rows):
    n_cols = len(cols)
    operands = [lists, *rows, *cols] + ([sums] if sums is not None else [])
    return pl.pallas_call(
        functools.partial(build_kernel, chunk, len(rows), n_cols, sums is not None),
        out_shape=(
            jax.ShapeDtypeStruct((CAPS[chunk], ROWS, ROWS), BF16),
            *[jax.ShapeDtypeStruct((n, SUMS, ROWS), F32) for n in out_rows],
        ),
        in_specs=[SM] + [VM] * (len(operands) - 1),
        out_specs=(VM,) * (len(out_rows) + 1),
        scratch_shapes=[
            pltpu.VMEM((sum(r.shape[0] for r in rows), ROWS), BF16),
            pltpu.VMEM((n_cols * BLK * ROWS, D), BF16),
            pltpu.VMEM((n_cols * BLK, CH, ROWS), BF16),
            pltpu.VMEM((SPARE + 1, SUMS, ROWS), F32),
        ],
        compiler_params=pltpu.CompilerParams(vmem_limit_bytes=(20 if chunk == 2 else 14) << 20),
        cost_estimate=CHEAP,
        name=f"build_{chunk}",
    )(*operands)


def spread_kernel(list_ref, *refs):
    w_refs, state_refs, outs, (sum_buf, state_buf) = refs[:4], refs[4:9], refs[9:13], refs[13:]
    sum_buf[...] = jnp.zeros_like(sum_buf)
    for at, ref in enumerate(state_refs):
        state_buf[at * BLK : (at + 1) * BLK] = ref[...]
    for chunk, w_ref in enumerate(w_refs):

        def four(step, _, chunk=chunk, w_ref=w_ref):
            for k in range(4):
                n = 4 * step + k
                named = list_ref[FIRST[chunk] + n]
                sum_buf[named >> 8] += jnp.dot(
                    state_buf[named & 15], w_ref[n], preferred_element_type=F32
                )
            return 0

        lax.fori_loop(0, list_ref[COUNTS + chunk], four, 0)
    for at, ref in enumerate(outs):
        ref[...] = sum_buf[at * BLK : (at + 1) * BLK]


def spread(lists, weights, states):
    return pl.pallas_call(
        spread_kernel,
        out_shape=(jax.ShapeDtypeStruct((BLK, CH, ROWS), F32),) * NX,
        in_specs=[SM] + [VM] * (len(weights) + len(states)),
        out_specs=(VM,) * NX,
        scratch_shapes=[
            pltpu.VMEM((SPARE + 1, CH, ROWS), F32),
            pltpu.VMEM((5 * BLK, CH, ROWS), BF16),
        ],
        compiler_params=pltpu.CompilerParams(vmem_limit_bytes=4 << 20),
        cost_estimate=CHEAP,
        name="spread",
    )(lists, *weights, *states)


def wide_exchange(v):
    one = from_wide(v, 1)
    partner = swap_core(v)
    other = from_wide(v, -1)
    across = swap_core(one)
    return [v, partner, one, other, across]


def reduce_rows(own, back, fore, far):
    return own + along_x(back, -1) + along_x(fore, 1) + across_x(far)


def local(embeddings, seeds, neighbours):
    place = jnp.stack([lax.axis_index(WIDE), lax.axis_index("x")]).astype(jnp.int32)
    seeds_t = jnp.swapaxes(seeds, 1, 2)
    listed = [along_x(neighbours, 1), along_x(neighbours, -1), across_x(neighbours)]
    two, one, full = prepare(embeddings, seeds_t)
    two, one, full, *listed = lax.optimization_barrier((two, one, full, *listed))
    after = lambda v, *done: lax.optimization_barrier((v, *done))[0]
    partner = swap_core(full)
    back_two = along_x(two, 1)
    fore_one = along_x(one, -1)
    above = from_wide(full, 1)
    below = from_wide(after(full, partner), -1)
    lists = make_plan(place, neighbours, *listed)
    far_two = along_x(after(back_two, lists), 1)
    far_one = along_x(after(fore_one, lists), -1)
    fore_two = along_x(after(two, fore_one, lists), -1)
    back_one = along_x(after(one, back_two, lists), 1)

    near = [two, one, back_two, fore_one]
    w0, sums = build(0, lists, near, [full, partner], None, (9,))
    beside = swap_core(after(above, back_one))
    cols = [full, partner, above, below, beside]
    w1, sums = build(1, lists, near, [above, below], sums, (9,))
    w2, own, back, fore = build(2, lists, [*near, back_one, fore_two], cols, sums, (BLK, BLK, BLK))
    w3, far = build(3, after(lists, own), [far_two, far_one], cols, None, (BLK,))
    weights = [w0, w1, w2, w3]

    total = reduce_rows(own, back, fore, far)
    scale = ALPHA / jnp.sum(total[:, CH:], axis=1, keepdims=True)
    prior = (1.0 - ALPHA) * seeds_t
    scores = total[:, :CH] * scale + prior
    for _ in range(ITERS - 1):
        states = wide_exchange(scores.astype(BF16))
        total = reduce_rows(*spread(lists, weights, states))
        scores = total * scale + prior
    return jnp.swapaxes(scores, 1, 2)


def solution(mesh):
    fine = Mesh(mesh.devices.reshape(4, 4, 2, 4), ("z", "y", "c", "x"))
    everywhere = ("z", "y", "c", "x")
    return jax.shard_map(
        local,
        mesh=fine,
        in_specs=(P(everywhere, None, None), P(everywhere, None, None), P(everywhere, None)),
        out_specs=P(everywhere, None, None),
        check_vma=False,
    )
```

time: 565 us -> 148 us (0.26)
  local copies, waits for them, and re-layouts: 191 us -> 4.63 us
  waiting for transfers between devices: 212 us -> 59.9 us
  matrix products: 46.9 us -> 0 us
  Pallas kernels: 0 us -> 42.9 us
  blocking collectives: 39.2 us -> 0 us
  other arithmetic: 21.8 us -> 1.6 us
  between operations: 13.7 us -> 0.23 us
  loops' own time: 8.02 us -> 0 us
  starting transfers between devices: 30.1 us -> 37.9 us
    ppermute x16 -> x30, waiting for transfers between devices: 174 us -> 59.9 us  [the longest x14 44.8 us: along_x(): return lax.ppermute(v, ('c', 'x'), pairs)]
    gather x15 -> x0, local copies, waits for them, and re-layouts: 109 us -> none  [the longest x12 101 us: turn(): tiles, part_degree = tile_weights(own, near_all[picked], keep)]
    dot_general x15 -> x0, matrix products: 46.9 us -> none  [the longest x12 24.7 us: tile_weights(): jnp.einsum('rd,kqd->krq', own, near_units, preferred_element_type=jnp.flo...]
    pallas_call x0 -> x8, Pallas kernels: none -> 42.9 us  [the longest x4 24 us: build(): pl.pallas_call(functools.partial(build_kernel, chunk, len(rows), n_cols,...]
    all_gather x3 -> x0, blocking collectives: 39.2 us -> none  [fetch_scores(): group = lax.all_gather(state[None], 'narrow', axis=0, tiled=True)]
    all_gather x1 -> x0, waiting for transfers between devices: 38.3 us -> none  [fetch_units(): group = lax.all_gather(units[None], 'narrow', axis=0, tiled=True)]
    reshape x6 -> x0, local copies, waits for them, and re-layouts: 27.1 us -> none  [local(): fetch_scores(state.reshape(blocks, rows * chans))]
    unnamed x32 -> x20, local copies, waits for them, and re-layouts: 22 us -> 4.63 us
  transfers between devices with their start and end apart: 17 -> 30, of which waited for: 9 -> 14; matrix products, arithmetic and copies ran while one was open for 5% -> 0% of each run, Pallas kernels for 0% -> 18%
where the time goes in v2:
time: 148 us; the launch traced here: 147 us
  waiting for transfers between devices  59.9 us (40%)
  Pallas kernels  42.9 us (29%)
  starting transfers between devices  37.9 us (26%)
  local copies, waits for them, and re-layouts  4.63 us (3%)
  other arithmetic  1.6 us (1%)
    ppermute x14, waiting for transfers between devices, along_x(): return lax.ppermute(v, ('c', 'x'), pairs)  44.8 us
    pallas_call x4, Pallas kernels, build(): pl.pallas_call(functools.partial(build_kernel, chunk, len(rows), n_cols,...  24 us
    ppermute x14, starting transfers between devices, along_x(): return lax.ppermute(v, ('c', 'x'), pairs)  16 us
    ppermute x6, starting transfers between devices, from_wide(): lax.ppermute(v, WIDE, [((i + (2 * sign if i % 2 == 0 else -2 * sign)) % N...  10.7 us
    pallas_call x2, Pallas kernels, spread(): pl.pallas_call(spread_kernel, out_shape=(jax.ShapeDtypeStruct((BLK, CH, R...  10 us
    pallas_call x1, Pallas kernels, make_plan(): pl.pallas_call(plan_kernel, out_shape=jax.ShapeDtypeStruct((LISTS,), jnp....  8.14 us
    ppermute x4, waiting for transfers between devices, across_x(): return lax.ppermute(v, 'x', [(x, (x + 2) % NX) for x in range(NX)])  7.74 us
    ppermute x6, waiting for transfers between devices, from_wide(): lax.ppermute(v, WIDE, [((i + (2 * sign if i % 2 == 0 else -2 * sign)) % N...  7.36 us
  transfers between devices with their start and end apart: 30, of which 14 were waited for; matrix products, arithmetic and copies ran while one was open for 0% of the time, Pallas kernels for 18%

profile of v2, /device:TPU:0, one launch (start us, length us, event | category | flops | bytes accessed | tf_op | source)
XLA Modules:
  0.0 147.2 jit_solution(8926501112275526134)
XLA Ops:
  0.0 2.8 %collective-permute-start.1 = (s32[3,32]{1,0:T(4,128)}, s32[3,32]{1,0:T(4,128)S(1)}, u32[]{:S(2)}, u32[]{:S(2)}) collective-permute-start(s32[3,32]{1,0:T(4,128)} %own_ref.1), channel_id=1, source_target_pairs={{0,3},{1,0},{2,1},{3,2},{4,5},{5,6},{6,7},{7,4},{8,11},{9,8},{10,9... | collective-permute-start | bytes 1160 | tf_op jit(solution)/shard_map/ppermute | solution.py:44
  2.8 2.3 %collective-permute-start.2 = (s32[3,32]{1,0:T(4,128)}, s32[3,32]{1,0:T(4,128)S(1)}, u32[]{:S(2)}, u32[]{:S(2)}) collective-permute-start(s32[3,32]{1,0:T(4,128)} %own_ref.1), channel_id=1, source_target_pairs={{0,2},{1,3},{2,0},{3,1},{4,6},{5,7},{6,4},{7,5},{8,10},{9,11},{10,... | collective-permute-start | bytes 1160 | tf_op jit(solution)/shard_map/ppermute | solution.py:48
  5.1 0.9 copy-done.3
  6.1 1.3 copy-done.5
  7.3 0.7 prep.1
  8.0 0.7 copy-done
  8.9 6.6 %collective-permute-start.6 = (bf16[832,768]{1,0:T(8,128)(2,1)S(1)}, bf16[832,768]{1,0:T(8,128)(2,1)}, u32[]{:S(2)}, u32[]{:S(2)}) collective-permute-start(bf16[832,768]{1,0:T(8,128)(2,1)S(1)} %get-tuple-element.49.refs_5_.refs_7_.refs_3_), channel_id=1, source_target_pairs={{8,0},{124,4},{16,8},{4,12},{24,16},{12,20},{32,24},{20,28},{40,32... | collective-permute-start | bytes 3833864 | tf_op jit(solution)/shard_map/ppermute | solution.py:52
  15.5 1.8 %collective-permute-start.3 = (bf16[1536,256]{1,0:T(8,128)(2,1)S(1)}, bf16[1536,256]{1,0:T(8,128)(2,1)}, u32[]{:S(2)}, u32[]{:S(2)}) collective-permute-start(bf16[1536,256]{1,0:T(8,128)(2,1)S(1)} %get-tuple-element.53.refs_1_), channel_id=1, source_target_pairs={{0,1},{1,2},{2,3},{3,0},{4,7},{5,4},{6,5},{7,6},{8,9},{9,10},{10,1... | collective-permute-start | bytes 2359304 | tf_op jit(solution)/shard_map/ppermute | solution.py:44
  17.3 0.7 pad_add_fusion.place_ref
  17.9 8.1 %plan.1.refs_0_.list_ref = s32[256]{0:T(256)} custom-call(s32[2]{0:T(128)} %pad_add_fusion.place_ref, s32[3,32]{1,0:T(4,128)} %own_ref.1, s32[3,32]{1,0:T(4,128)} %copy-done.8, s32[3,32]{1,0:T(4,128)} %copy-done.7, s32[3,32]{1,0:T(4,128)} %copy-done.9), custom_call_target="tpu_custom_call" | custom-call | flops 1000 | bytes 1000 | tf_op jit(solution)/shard_map/plan/pallas_call | solution.py:135
  26.1 2.7 %collective-permute-done.3.refs_3_ = bf16[1536,256]{1,0:T(8,128)(2,1)} collective-permute-done((bf16[1536,256]{1,0:T(8,128)(2,1)S(1)}, bf16[1536,256]{1,0:T(8,128)(2,1)}, u32[]{:S(2)}, u32[]{:S(2)}) %collective-permute-start.3) | collective-permute-done | bytes 786464 | tf_op jit(solution)/shard_map/ppermute | solution.py:44
  28.8 0.6 collective-permute-start.8
  29.4 8.6 %collective-permute-done.8.refs_5_ = bf16[768,256]{1,0:T(8,128)(2,1)S(1)} collective-permute-done((bf16[768,256]{1,0:T(8,128)(2,1)}, bf16[768,256]{1,0:T(8,128)(2,1)S(1)}, u32[]{:S(2)}, u32[]{:S(2)}) %collective-permute-start.8) | collective-permute-done | bytes 393248 | tf_op jit(solution)/shard_map/ppermute | solution.py:44
  38.0 8.0 %collective-permute-done.4.refs_4_ = bf16[768,256]{1,0:T(8,128)(2,1)S(1)} collective-permute-done((bf16[768,256]{1,0:T(8,128)(2,1)}, bf16[768,256]{1,0:T(8,128)(2,1)S(1)}, u32[]{:S(2)}, u32[]{:S(2)}) %collective-permute-start.4) | collective-permute-done | bytes 393248 | tf_op jit(solution)/shard_map/ppermute | solution.py:44
  46.0 1.2 collective-permute-start.9
  47.2 0.8 collective-permute-start.11
  48.0 2.4 %collective-permute-start.12 = (bf16[768,256]{1,0:T(8,128)(2,1)S(1)}, bf16[768,256]{1,0:T(8,128)(2,1)S(1)}, u32[]{:S(2)}, u32[]{:S(2)}) collective-permute-start(bf16[768,256]{1,0:T(8,128)(2,1)S(1)} %collective-permute-done.4.refs_4_), channel_id=1, source_target_pairs={{0,3},{1,0},{2,1},{3,2},{4,5},{5,6},{6,7},{7,4},{8,11},{9,8},{10,9... | collective-permute-start | bytes 1179656 | tf_op jit(solution)/shard_map/ppermute | solution.py:44
  50.4 1.0 copy-done.1
  51.4 0.7 copy-done.6
  52.1 4.8 %build_0.1 = (bf16[36,256,256]{2,1,0:T(8,128)(2,1)S(1)}, f32[9,72,256]{2,1,0:T(8,128)S(1)}) custom-call(s32[256]{0:T(256)S(1)} %copy-done.6, bf16[1536,256]{1,0:T(8,128)(2,1)S(1)} %get-tuple-element.53.refs_1_, bf16[768,256]{1,0:T(8,128)(2,1)S(1)} %copy-done.1, bf16[1536,256]{1,0:T(8,128)(2,1)} %collective-permute-done.3.refs_3_, ...), custom_call_target="tpu_custom_call" | custom-call | flops 1000 | bytes 1000 | tf_op jit(solution)/shard_map/build_0/pallas_call | solution.py:204
  57.0 4.4 %build_1.1 = (bf16[36,256,256]{2,1,0:T(8,128)(2,1)S(1)}, f32[9,72,256]{2,1,0:T(8,128)S(1)}) custom-call(s32[256]{0:T(256)S(1)} %copy-done.6, bf16[1536,256]{1,0:T(8,128)(2,1)S(1)} %get-tuple-element.53.refs_1_, bf16[768,256]{1,0:T(8,128)(2,1)S(1)} %copy-done.2, bf16[1536,256]{1,0:T(8,128)(2,1)} %collective-permute-done.3.refs_3_, ...), custom_call_target="tpu_custom_call" | custom-call | flops 1000 | bytes 1000 | tf_op jit(solution)/shard_map/build_1/pallas_call | solution.py:204
  61.4 4.9 %collective-permute-done.9.refs_6_ = bf16[1536,256]{1,0:T(8,128)(2,1)S(1)} collective-permute-done((bf16[1536,256]{1,0:T(8,128)(2,1)S(1)}, bf16[1536,256]{1,0:T(8,128)(2,1)S(1)}, u32[]{:S(2)}, u32[]{:S(2)}) %collective-permute-start.9) | collective-permute-done | bytes 786464 | tf_op jit(solution)/shard_map/ppermute | solution.py:44
  66.3 8.0 %build_2.1 = (bf16[64,256,256]{2,1,0:T(8,128)(2,1)S(1)}, f32[3,72,256]{2,1,0:T(8,128)S(1)}, f32[3,72,256]{2,1,0:T(8,128)S(1)}, f32[3,72,256]{2,1,0:T(8,128)S(1)}) custom-call(s32[256]{0:T(256)S(1)} %copy-done.6, bf16[1536,256]{1,0:T(8,128)(2,1)S(1)} %get-tuple-element.53.refs_1_, bf16[768,256]{1,0:T(8,128)(2,1)S(1)} %copy-done.2, ...), custom_call_target="tpu_custom_call" | custom-call | flops 1000 | bytes 1000 | tf_op jit(solution)/shard_map/build_2/pallas_call | solution.py:204
  74.3 6.8 %build_3.1 = (bf16[48,256,256]{2,1,0:T(8,128)(2,1)S(1)}, f32[3,72,256]{2,1,0:T(8,128)S(1)}) custom-call(s32[256]{0:T(256)S(1)} %copy-done.6, bf16[1536,256]{1,0:T(8,128)(2,1)S(1)} %collective-permute-done.11.refs_1_, bf16[768,256]{1,0:T(8,128)(2,1)S(1)} %collective-permute-done.12.refs_2_, bf16[832,768]{1,0:T(8,128)(2,1)S(1)} %get-tuple-element.49.refs_5_.refs_7_.refs_3_, ...), custom_call_target="tpu_custom_call" | custom-call | flops 1000 | bytes 1000 | tf_op jit(solution)/shard_map/build_3/pallas_call | solution.py:204
  81.8 1.5 %collective-permute-start.14 = (f32[3,72,256]{2,1,0:T(8,128)S(1)}, f32[3,72,256]{2,1,0:T(8,128)S(1)}, u32[]{:S(2)}, u32[]{:S(2)}) collective-permute-start(f32[3,72,256]{2,1,0:T(8,128)S(1)} %get-tuple-element.63), channel_id=1, source_target_pairs={{0,1},{1,2},{2,3},{3,0},{4,7},{5,4},{6,5},{7,6},{8,9},{9,10},{10,1... | collective-permute-start | bytes 663560 | tf_op jit(solution)/shard_map/ppermute | solution.py:44
  83.3 7.7 %collective-permute-done.15 = f32[3,72,256]{2,1,0:T(8,128)S(1)} collective-permute-done((f32[3,72,256]{2,1,0:T(8,128)S(1)}, f32[3,72,256]{2,1,0:T(8,128)S(1)}, u32[]{:S(2)}, u32[]{:S(2)}) %collective-permute-start.15) | collective-permute-done | bytes 221216 | tf_op jit(solution)/shard_map/ppermute | solution.py:48
  91.0 3.3 %collective-permute-done.14 = f32[3,72,256]{2,1,0:T(8,128)S(1)} collective-permute-done((f32[3,72,256]{2,1,0:T(8,128)S(1)}, f32[3,72,256]{2,1,0:T(8,128)S(1)}, u32[]{:S(2)}, u32[]{:S(2)}) %collective-permute-start.14) | collective-permute-done | bytes 221216 | tf_op jit(solution)/shard_map/ppermute | solution.py:44
  94.5 2.0 %collective-permute-start.18 = (bf16[3,64,256]{2,1,0:T(8,128)(2,1)S(1)}, bf16[3,64,256]{2,1,0:T(8,128)(2,1)S(1)}, u32[]{:S(2)}, u32[]{:S(2)}) collective-permute-start(bf16[3,64,256]{2,1,0:T(8,128)(2,1)S(1)} %fusion.1.refs_4_), channel_id=1, source_target_pairs={{120,0},{12,4},{0,8},{20,12},{8,16},{28,20},{16,24},{36,28},{24,32... | collective-permute-start | bytes 294920 | tf_op jit(solution)/shard_map/ppermute | solution.py:52
  96.5 2.6 %collective-permute-start.16 = (bf16[3,64,256]{2,1,0:T(8,128)(2,1)S(1)}, bf16[3,64,256]{2,1,0:T(8,128)(2,1)S(1)}, u32[]{:S(2)}, u32[]{:S(2)}) collective-permute-start(bf16[3,64,256]{2,1,0:T(8,128)(2,1)S(1)} %fusion.1.refs_4_), channel_id=1, source_target_pairs={{0,4},{4,0},{1,5},{5,1},{2,6},{6,2},{3,7},{7,3},{8,12},{12,8},{9,1... | collective-permute-start | bytes 294920 | tf_op jit(solution)/shard_map/ppermute | solution.py:58
  99.3 1.8 %collective-permute-start.19 = (bf16[3,64,256]{2,1,0:T(8,128)(2,1)S(1)}, bf16[3,64,256]{2,1,0:T(8,128)(2,1)S(1)}, u32[]{:S(2)}, u32[]{:S(2)}) collective-permute-start(bf16[3,64,256]{2,1,0:T(8,128)(2,1)S(1)} %collective-permute-done.17.refs_6_), channel_id=1, source_target_pairs={{0,4},{4,0},{1,5},{5,1},{2,6},{6,2},{3,7},{7,3},{8,12},{12,8},{9,1... | collective-permute-start | bytes 294920 | tf_op jit(solution)/shard_map/ppermute | solution.py:58
  101.1 1.6 %collective-permute-done.18.refs_7_ = bf16[3,64,256]{2,1,0:T(8,128)(2,1)S(1)} collective-permute-done((bf16[3,64,256]{2,1,0:T(8,128)(2,1)S(1)}, bf16[3,64,256]{2,1,0:T(8,128)(2,1)S(1)}, u32[]{:S(2)}, u32[]{:S(2)}) %collective-permute-start.18) | collective-permute-done | bytes 98336 | tf_op jit(solution)/shard_map/ppermute | solution.py:52
  102.7 5.0 %spread.2 = (f32[3,64,256]{2,1,0:T(8,128)S(1)}, f32[3,64,256]{2,1,0:T(8,128)S(1)}, f32[3,64,256]{2,1,0:T(8,128)S(1)}, f32[3,64,256]{2,1,0:T(8,128)S(1)}) custom-call(s32[256]{0:T(256)S(1)} %copy-done.6, bf16[36,256,256]{2,1,0:T(8,128)(2,1)S(1)} %get-tuple-element.48.refs_0_, bf16[36,256,256]{2,1,0:T(8,128)(2,1)S(1)} %get-tuple-element.51.refs_1_, ...), custom_call_target="tpu_custom_call" | custom-call | flops 1000 | bytes 1000 | tf_op jit(solution)/shard_map/spread/pallas_call | solution.py:246
  107.7 1.1 collective-permute-start.20
  108.8 1.0 collective-permute-start.21
  110.4 7.5 %collective-permute-done.20 = f32[3,64,256]{2,1,0:T(8,128)S(1)} collective-permute-done((f32[3,64,256]{2,1,0:T(8,128)S(1)}, f32[3,64,256]{2,1,0:T(8,128)S(1)}, u32[]{:S(2)}, u32[]{:S(2)}) %collective-permute-start.20) | collective-permute-done | bytes 196640 | tf_op jit(solution)/shard_map/ppermute | solution.py:44
  117.9 2.1 %collective-permute-done.21 = f32[3,64,256]{2,1,0:T(8,128)S(1)} collective-permute-done((f32[3,64,256]{2,1,0:T(8,128)S(1)}, f32[3,64,256]{2,1,0:T(8,128)S(1)}, u32[]{:S(2)}, u32[]{:S(2)}) %collective-permute-start.21) | collective-permute-done | bytes 196640 | tf_op jit(solution)/shard_map/ppermute | solution.py:44
  120.0 1.7 %collective-permute-start.24 = (bf16[3,64,256]{2,1,0:T(8,128)(2,1)S(1)}, bf16[3,64,256]{2,1,0:T(8,128)(2,1)S(1)}, u32[]{:S(2)}, u32[]{:S(2)}) collective-permute-start(bf16[3,64,256]{2,1,0:T(8,128)(2,1)S(1)} %add_convert_fusion.refs_4_), channel_id=1, source_target_pairs={{8,0},{124,4},{16,8},{4,12},{24,16},{12,20},{32,24},{20,28},{40,32... | collective-permute-start | bytes 294920 | tf_op jit(solution)/shard_map/ppermute | solution.py:52
  122.1 1.3 collective-permute-start.23
  123.4 1.3 collective-permute-done.24.refs_6_
  124.7 0.7 collective-permute-start.26
  125.4 4.3 %collective-permute-done.25.refs_7_ = bf16[3,64,256]{2,1,0:T(8,128)(2,1)S(1)} collective-permute-done((bf16[3,64,256]{2,1,0:T(8,128)(2,1)S(1)}, bf16[3,64,256]{2,1,0:T(8,128)(2,1)S(1)}, u32[]{:S(2)}, u32[]{:S(2)}) %collective-permute-start.25) | collective-permute-done | bytes 98336 | tf_op jit(solution)/shard_map/ppermute | solution.py:52
  129.7 5.0 %spread.3 = (f32[3,64,256]{2,1,0:T(8,128)S(1)}, f32[3,64,256]{2,1,0:T(8,128)S(1)}, f32[3,64,256]{2,1,0:T(8,128)S(1)}, f32[3,64,256]{2,1,0:T(8,128)S(1)}) custom-call(s32[256]{0:T(256)S(1)} %copy-done.6, bf16[36,256,256]{2,1,0:T(8,128)(2,1)S(1)} %get-tuple-element.48.refs_0_, bf16[36,256,256]{2,1,0:T(8,128)(2,1)S(1)} %get-tuple-element.51.refs_1_, ...), custom_call_target="tpu_custom_call" | custom-call | flops 1000 | bytes 1000 | tf_op jit(solution)/shard_map/spread/pallas_call | solution.py:246
  134.7 1.4 collective-permute-start.27
  136.1 0.7 collective-permute-start.28
  136.8 1.8 %collective-permute-start.29 = (f32[3,64,256]{2,1,0:T(8,128)S(1)}, f32[3,64,256]{2,1,0:T(8,128)S(1)}, u32[]{:S(2)}, u32[]{:S(2)}) collective-permute-start(f32[3,64,256]{2,1,0:T(8,128)S(1)} %get-tuple-element.72), channel_id=1, source_target_pairs={{0,2},{1,3},{2,0},{3,1},{4,6},{5,7},{6,4},{7,5},{8,10},{9,11},{10,... | collective-permute-start | bytes 589832 | tf_op jit(solution)/shard_map/ppermute | solution.py:48
  138.6 5.7 %collective-permute-done.27 = f32[3,64,256]{2,1,0:T(8,128)S(1)} collective-permute-done((f32[3,64,256]{2,1,0:T(8,128)S(1)}, f32[3,64,256]{2,1,0:T(8,128)S(1)}, u32[]{:S(2)}, u32[]{:S(2)}) %collective-permute-start.27) | collective-permute-done | bytes 196640 | tf_op jit(solution)/shard_map/ppermute | solution.py:44
  144.3 2.1 %collective-permute-done.28 = f32[3,64,256]{2,1,0:T(8,128)S(1)} collective-permute-done((f32[3,64,256]{2,1,0:T(8,128)S(1)}, f32[3,64,256]{2,1,0:T(8,128)S(1)}, u32[]{:S(2)}, u32[]{:S(2)}) %collective-permute-start.28) | collective-permute-done | bytes 196640 | tf_op jit(solution)/shard_map/ppermute | solution.py:44
  146.4 0.7 add_bitcast_fusion
  (47 shorter events, 2.2 us)
Async XLA Ops:
  0.0 8.8 %collective-permute-start.1 = (s32[3,32]{1,0:T(4,128)}, s32[3,32]{1,0:T(4,128)S(1)}, u32[]{:S(2)}, u32[]{:S(2)}) collective-permute-start(s32[3,32]{1,0:T(4,128)} %own_ref.1), channel_id=1, source_target_pairs={{0,3},{1,0},{2,1},{3,2},{4,5},{5,6},{6,7},{7,4},{8,11},{9,8},{10,9... | collective-permute-start | bytes 1160 | tf_op jit(solution)/shard_map/ppermute | solution.py:44
  2.8 5.9 %collective-permute-start = (s32[3,32]{1,0:T(4,128)}, s32[3,32]{1,0:T(4,128)S(1)}, u32[]{:S(2)}, u32[]{:S(2)}) collective-permute-start(s32[3,32]{1,0:T(4,128)} %own_ref.1), channel_id=1, source_target_pairs={{0,1},{1,2},{2,3},{3,0},{4,7},{5,4},{6,5},{7,6},{8,9},{9,10},{10,1... | collective-permute-start | bytes 1160 | tf_op jit(solution)/shard_map/ppermute | solution.py:44
  2.8 6.0 %collective-permute-start.2 = (s32[3,32]{1,0:T(4,128)}, s32[3,32]{1,0:T(4,128)S(1)}, u32[]{:S(2)}, u32[]{:S(2)}) collective-permute-start(s32[3,32]{1,0:T(4,128)} %own_ref.1), channel_id=1, source_target_pairs={{0,2},{1,3},{2,0},{3,1},{4,6},{5,7},{6,4},{7,5},{8,10},{9,11},{10,... | collective-permute-start | bytes 1160 | tf_op jit(solution)/shard_map/ppermute | solution.py:48
  5.1 0.9 copy-start.3
  6.1 1.3 copy-start.5
  8.0 0.8 copy-start
  8.8 9.2 %copy-start.7 = (s32[3,32]{1,0:T(4,128)}, s32[3,32]{1,0:T(4,128)S(1)}, u32[]{:S(2)}) copy-start(s32[3,32]{1,0:T(4,128)S(1)} %collective-permute-done.1.fore_ref) | copy-start | bytes 1156
  8.8 9.1 %copy-start.8 = (s32[3,32]{1,0:T(4,128)}, s32[3,32]{1,0:T(4,128)S(1)}, u32[]{:S(2)}) copy-start(s32[3,32]{1,0:T(4,128)S(1)} %collective-permute-done.back_ref) | copy-start | bytes 1156
  8.8 9.1 %copy-start.9 = (s32[3,32]{1,0:T(4,128)}, s32[3,32]{1,0:T(4,128)S(1)}, u32[]{:S(2)}) copy-start(s32[3,32]{1,0:T(4,128)S(1)} %collective-permute-done.2.far_ref) | copy-start | bytes 1156
  8.8 20.6 %collective-permute-start.5 = (bf16[832,768]{1,0:T(8,128)(2,1)S(1)}, bf16[832,768]{1,0:T(8,128)(2,1)S(1)}, u32[]{:S(2)}, u32[]{:S(2)}) collective-permute-start(bf16[832,768]{1,0:T(8,128)(2,1)S(1)} %get-tuple-element.49.refs_5_.refs_7_.refs_3_), channel_id=1, source_target_pairs={{0,4},{4,0},{1,5},{5,1},{2,6},{6,2},{3,7},{7,3},{8,12},{12,8},{9,1... | collective-permute-start | bytes 3833864 | tf_op jit(solution)/shard_map/ppermute | solution.py:58
  8.9 29.1 %collective-permute-start.6 = (bf16[832,768]{1,0:T(8,128)(2,1)S(1)}, bf16[832,768]{1,0:T(8,128)(2,1)}, u32[]{:S(2)}, u32[]{:S(2)}) collective-permute-start(bf16[832,768]{1,0:T(8,128)(2,1)S(1)} %get-tuple-element.49.refs_5_.refs_7_.refs_3_), channel_id=1, source_target_pairs={{8,0},{124,4},{16,8},{4,12},{24,16},{12,20},{32,24},{20,28},{40,32... | collective-permute-start | bytes 3833864 | tf_op jit(solution)/shard_map/ppermute | solution.py:52
  15.5 13.3 %collective-permute-start.3 = (bf16[1536,256]{1,0:T(8,128)(2,1)S(1)}, bf16[1536,256]{1,0:T(8,128)(2,1)}, u32[]{:S(2)}, u32[]{:S(2)}) collective-permute-start(bf16[1536,256]{1,0:T(8,128)(2,1)S(1)} %get-tuple-element.53.refs_1_), channel_id=1, source_target_pairs={{0,1},{1,2},{2,3},{3,0},{4,7},{5,4},{6,5},{7,6},{8,9},{9,10},{10,1... | collective-permute-start | bytes 2359304 | tf_op jit(solution)/shard_map/ppermute | solution.py:44
  28.8 9.2 %collective-permute-start.8 = (bf16[768,256]{1,0:T(8,128)(2,1)}, bf16[768,256]{1,0:T(8,128)(2,1)S(1)}, u32[]{:S(2)}, u32[]{:S(2)}) collective-permute-start(bf16[768,256]{1,0:T(8,128)(2,1)} %copy-done), channel_id=1, source_target_pairs={{0,1},{1,2},{2,3},{3,0},{4,7},{5,4},{6,5},{7,6},{8,9},{9,10},{10,1... | collective-permute-start | bytes 1179656 | tf_op jit(solution)/shard_map/ppermute | solution.py:44
  29.4 27.6 %collective-permute-start.7 = (bf16[832,768]{1,0:T(8,128)(2,1)S(1)}, bf16[832,768]{1,0:T(8,128)(2,1)S(1)}, u32[]{:S(2)}, u32[]{:S(2)}) collective-permute-start(bf16[832,768]{1,0:T(8,128)(2,1)S(1)} %get-tuple-element.49.refs_5_.refs_7_.refs_3_), channel_id=1, source_target_pairs={{120,0},{12,4},{0,8},{20,12},{8,16},{28,20},{16,24},{36,28},{24,32... | collective-permute-start | bytes 3833864 | tf_op jit(solution)/shard_map/ppermute | solution.py:52
  38.0 28.3 %collective-permute-start.10 = (bf16[832,768]{1,0:T(8,128)(2,1)}, bf16[832,768]{1,0:T(8,128)(2,1)S(1)}, u32[]{:S(2)}, u32[]{:S(2)}) collective-permute-start(bf16[832,768]{1,0:T(8,128)(2,1)} %collective-permute-done.6.refs_5_.refs_9_), channel_id=1, source_target_pairs={{0,4},{4,0},{1,5},{5,1},{2,6},{6,2},{3,7},{7,3},{8,12},{12,8},{9,1... | collective-permute-start | bytes 3833864 | tf_op jit(solution)/shard_map/ppermute | solution.py:58
  38.0 8.0 %collective-permute-start.4 = (bf16[768,256]{1,0:T(8,128)(2,1)}, bf16[768,256]{1,0:T(8,128)(2,1)S(1)}, u32[]{:S(2)}, u32[]{:S(2)}) collective-permute-start(bf16[768,256]{1,0:T(8,128)(2,1)} %copy-done), channel_id=1, source_target_pairs={{0,3},{1,0},{2,1},{3,2},{4,5},{5,6},{6,7},{7,4},{8,11},{9,8},{10,9... | collective-permute-start | bytes 1179656 | tf_op jit(solution)/shard_map/ppermute | solution.py:44
  46.0 20.3 %collective-permute-start.9 = (bf16[1536,256]{1,0:T(8,128)(2,1)S(1)}, bf16[1536,256]{1,0:T(8,128)(2,1)S(1)}, u32[]{:S(2)}, u32[]{:S(2)}) collective-permute-start(bf16[1536,256]{1,0:T(8,128)(2,1)S(1)} %get-tuple-element.53.refs_1_), channel_id=1, source_target_pairs={{0,3},{1,0},{2,1},{3,2},{4,5},{5,6},{6,7},{7,4},{8,11},{9,8},{10,9... | collective-permute-start | bytes 2359304 | tf_op jit(solution)/shard_map/ppermute | solution.py:44
  47.2 27.1 %collective-permute-start.11 = (bf16[1536,256]{1,0:T(8,128)(2,1)}, bf16[1536,256]{1,0:T(8,128)(2,1)S(1)}, u32[]{:S(2)}, u32[]{:S(2)}) collective-permute-start(bf16[1536,256]{1,0:T(8,128)(2,1)} %collective-permute-done.3.refs_3_), channel_id=1, source_target_pairs={{0,1},{1,2},{2,3},{3,0},{4,7},{5,4},{6,5},{7,6},{8,9},{9,10},{10,1... | collective-permute-start | bytes 2359304 | tf_op jit(solution)/shard_map/ppermute | solution.py:44
  48.0 26.3 %collective-permute-start.12 = (bf16[768,256]{1,0:T(8,128)(2,1)S(1)}, bf16[768,256]{1,0:T(8,128)(2,1)S(1)}, u32[]{:S(2)}, u32[]{:S(2)}) collective-permute-start(bf16[768,256]{1,0:T(8,128)(2,1)S(1)} %collective-permute-done.4.refs_4_), channel_id=1, source_target_pairs={{0,3},{1,0},{2,1},{3,2},{4,5},{5,6},{6,7},{7,4},{8,11},{9,8},{10,9... | collective-permute-start | bytes 1179656 | tf_op jit(solution)/shard_map/ppermute | solution.py:44
  50.4 1.0 copy-start.1
  51.4 0.7 copy-start.6
  52.1 4.9 %copy-start.2 = (bf16[768,256]{1,0:T(8,128)(2,1)S(1)}, bf16[768,256]{1,0:T(8,128)(2,1)}, u32[]{:S(2)}) copy-start(bf16[768,256]{1,0:T(8,128)(2,1)} %copy-done) | copy-start | bytes 1179652
  81.1 13.3 %copy-start.4 = (f32[3,256,64]{1,2,0:T(8,128)S(1)}, f32[3,256,64]{1,2,0:T(8,128)}, u32[]{:S(2)}) copy-start(f32[3,256,64]{1,2,0:T(8,128)} %param.4) | copy-start | bytes 589828
  81.1 9.9 %collective-permute-start.15 = (f32[3,72,256]{2,1,0:T(8,128)S(1)}, f32[3,72,256]{2,1,0:T(8,128)S(1)}, u32[]{:S(2)}, u32[]{:S(2)}) collective-permute-start(f32[3,72,256]{2,1,0:T(8,128)S(1)} %get-tuple-element.64), channel_id=1, source_target_pairs={{0,2},{1,3},{2,0},{3,1},{4,6},{5,7},{6,4},{7,5},{8,10},{9,11},{10,... | collective-permute-start | bytes 663560 | tf_op jit(solution)/shard_map/ppermute | solution.py:48
  81.2 9.8 %collective-permute-start.13 = (f32[3,72,256]{2,1,0:T(8,128)S(1)}, f32[3,72,256]{2,1,0:T(8,128)S(1)}, u32[]{:S(2)}, u32[]{:S(2)}) collective-permute-start(f32[3,72,256]{2,1,0:T(8,128)S(1)} %get-tuple-element.62), channel_id=1, source_target_pairs={{0,3},{1,0},{2,1},{3,2},{4,5},{5,6},{6,7},{7,4},{8,11},{9,8},{10,9... | collective-permute-start | bytes 663560 | tf_op jit(solution)/shard_map/ppermute | solution.py:44
  81.8 12.5 %collective-permute-start.14 = (f32[3,72,256]{2,1,0:T(8,128)S(1)}, f32[3,72,256]{2,1,0:T(8,128)S(1)}, u32[]{:S(2)}, u32[]{:S(2)}) collective-permute-start(f32[3,72,256]{2,1,0:T(8,128)S(1)} %get-tuple-element.63), channel_id=1, source_target_pairs={{0,1},{1,2},{2,3},{3,0},{4,7},{5,4},{6,5},{7,6},{8,9},{9,10},{10,1... | collective-permute-start | bytes 663560 | tf_op jit(solution)/shard_map/ppermute | solution.py:44
  94.4 4.8 %collective-permute-start.17 = (bf16[3,64,256]{2,1,0:T(8,128)(2,1)S(1)}, bf16[3,64,256]{2,1,0:T(8,128)(2,1)S(1)}, u32[]{:S(2)}, u32[]{:S(2)}) collective-permute-start(bf16[3,64,256]{2,1,0:T(8,128)(2,1)S(1)} %fusion.1.refs_4_), channel_id=1, source_target_pairs={{8,0},{124,4},{16,8},{4,12},{24,16},{12,20},{32,24},{20,28},{40,32... | collective-permute-start | bytes 294920 | tf_op jit(solution)/shard_map/ppermute | solution.py:52
  94.5 8.2 %collective-permute-start.18 = (bf16[3,64,256]{2,1,0:T(8,128)(2,1)S(1)}, bf16[3,64,256]{2,1,0:T(8,128)(2,1)S(1)}, u32[]{:S(2)}, u32[]{:S(2)}) collective-permute-start(bf16[3,64,256]{2,1,0:T(8,128)(2,1)S(1)} %fusion.1.refs_4_), channel_id=1, source_target_pairs={{120,0},{12,4},{0,8},{20,12},{8,16},{28,20},{16,24},{36,28},{24,32... | collective-permute-start | bytes 294920 | tf_op jit(solution)/shard_map/ppermute | solution.py:52
  96.5 6.2 %collective-permute-start.16 = (bf16[3,64,256]{2,1,0:T(8,128)(2,1)S(1)}, bf16[3,64,256]{2,1,0:T(8,128)(2,1)S(1)}, u32[]{:S(2)}, u32[]{:S(2)}) collective-permute-start(bf16[3,64,256]{2,1,0:T(8,128)(2,1)S(1)} %fusion.1.refs_4_), channel_id=1, source_target_pairs={{0,4},{4,0},{1,5},{5,1},{2,6},{6,2},{3,7},{7,3},{8,12},{12,8},{9,1... | collective-permute-start | bytes 294920 | tf_op jit(solution)/shard_map/ppermute | solution.py:58
  99.3 3.4 %collective-permute-start.19 = (bf16[3,64,256]{2,1,0:T(8,128)(2,1)S(1)}, bf16[3,64,256]{2,1,0:T(8,128)(2,1)S(1)}, u32[]{:S(2)}, u32[]{:S(2)}) collective-permute-start(bf16[3,64,256]{2,1,0:T(8,128)(2,1)S(1)} %collective-permute-done.17.refs_6_), channel_id=1, source_target_pairs={{0,4},{4,0},{1,5},{5,1},{2,6},{6,2},{3,7},{7,3},{8,12},{12,8},{9,1... | collective-permute-start | bytes 294920 | tf_op jit(solution)/shard_map/ppermute | solution.py:58
  107.7 10.1 %collective-permute-start.20 = (f32[3,64,256]{2,1,0:T(8,128)S(1)}, f32[3,64,256]{2,1,0:T(8,128)S(1)}, u32[]{:S(2)}, u32[]{:S(2)}) collective-permute-start(f32[3,64,256]{2,1,0:T(8,128)S(1)} %get-tuple-element.66), channel_id=1, source_target_pairs={{0,3},{1,0},{2,1},{3,2},{4,5},{5,6},{6,7},{7,4},{8,11},{9,8},{10,9... | collective-permute-start | bytes 589832 | tf_op jit(solution)/shard_map/ppermute | solution.py:44
  108.8 11.1 %collective-permute-start.21 = (f32[3,64,256]{2,1,0:T(8,128)S(1)}, f32[3,64,256]{2,1,0:T(8,128)S(1)}, u32[]{:S(2)}, u32[]{:S(2)}) collective-permute-start(f32[3,64,256]{2,1,0:T(8,128)S(1)} %get-tuple-element.67), channel_id=1, source_target_pairs={{0,1},{1,2},{2,3},{3,0},{4,7},{5,4},{6,5},{7,6},{8,9},{9,10},{10,1... | collective-permute-start | bytes 589832 | tf_op jit(solution)/shard_map/ppermute | solution.py:44
  109.8 10.1 %collective-permute-start.22 = (f32[3,64,256]{2,1,0:T(8,128)S(1)}, f32[3,64,256]{2,1,0:T(8,128)S(1)}, u32[]{:S(2)}, u32[]{:S(2)}) collective-permute-start(f32[3,64,256]{2,1,0:T(8,128)S(1)} %get-tuple-element.68), channel_id=1, source_target_pairs={{0,2},{1,3},{2,0},{3,1},{4,6},{5,7},{6,4},{7,5},{8,10},{9,11},{10,... | collective-permute-start | bytes 589832 | tf_op jit(solution)/shard_map/ppermute | solution.py:48
  120.0 4.7 %collective-permute-start.24 = (bf16[3,64,256]{2,1,0:T(8,128)(2,1)S(1)}, bf16[3,64,256]{2,1,0:T(8,128)(2,1)S(1)}, u32[]{:S(2)}, u32[]{:S(2)}) collective-permute-start(bf16[3,64,256]{2,1,0:T(8,128)(2,1)S(1)} %add_convert_fusion.refs_4_), channel_id=1, source_target_pairs={{8,0},{124,4},{16,8},{4,12},{24,16},{12,20},{32,24},{20,28},{40,32... | collective-permute-start | bytes 294920 | tf_op jit(solution)/shard_map/ppermute | solution.py:52
  121.7 7.9 %collective-permute-start.25 = (bf16[3,64,256]{2,1,0:T(8,128)(2,1)S(1)}, bf16[3,64,256]{2,1,0:T(8,128)(2,1)S(1)}, u32[]{:S(2)}, u32[]{:S(2)}) collective-permute-start(bf16[3,64,256]{2,1,0:T(8,128)(2,1)S(1)} %add_convert_fusion.refs_4_), channel_id=1, source_target_pairs={{120,0},{12,4},{0,8},{20,12},{8,16},{28,20},{16,24},{36,28},{24,32... | collective-permute-start | bytes 294920 | tf_op jit(solution)/shard_map/ppermute | solution.py:52
  122.1 7.6 %collective-permute-start.23 = (bf16[3,64,256]{2,1,0:T(8,128)(2,1)S(1)}, bf16[3,64,256]{2,1,0:T(8,128)(2,1)S(1)}, u32[]{:S(2)}, u32[]{:S(2)}) collective-permute-start(bf16[3,64,256]{2,1,0:T(8,128)(2,1)S(1)} %add_convert_fusion.refs_4_), channel_id=1, source_target_pairs={{0,4},{4,0},{1,5},{5,1},{2,6},{6,2},{3,7},{7,3},{8,12},{12,8},{9,1... | collective-permute-start | bytes 294920 | tf_op jit(solution)/shard_map/ppermute | solution.py:58
  124.7 5.0 %collective-permute-start.26 = (bf16[3,64,256]{2,1,0:T(8,128)(2,1)S(1)}, bf16[3,64,256]{2,1,0:T(8,128)(2,1)S(1)}, u32[]{:S(2)}, u32[]{:S(2)}) collective-permute-start(bf16[3,64,256]{2,1,0:T(8,128)(2,1)S(1)} %collective-permute-done.24.refs_6_), channel_id=1, source_target_pairs={{0,4},{4,0},{1,5},{5,1},{2,6},{6,2},{3,7},{7,3},{8,12},{12,8},{9,1... | collective-permute-start | bytes 294920 | tf_op jit(solution)/shard_map/ppermute | solution.py:58
  134.7 9.6 %collective-permute-start.27 = (f32[3,64,256]{2,1,0:T(8,128)S(1)}, f32[3,64,256]{2,1,0:T(8,128)S(1)}, u32[]{:S(2)}, u32[]{:S(2)}) collective-permute-start(f32[3,64,256]{2,1,0:T(8,128)S(1)} %get-tuple-element.70), channel_id=1, source_target_pairs={{0,3},{1,0},{2,1},{3,2},{4,5},{5,6},{6,7},{7,4},{8,11},{9,8},{10,9... | collective-permute-start | bytes 589832 | tf_op jit(solution)/shard_map/ppermute | solution.py:44
  136.1 10.3 %collective-permute-start.28 = (f32[3,64,256]{2,1,0:T(8,128)S(1)}, f32[3,64,256]{2,1,0:T(8,128)S(1)}, u32[]{:S(2)}, u32[]{:S(2)}) collective-permute-start(f32[3,64,256]{2,1,0:T(8,128)S(1)} %get-tuple-element.71), channel_id=1, source_target_pairs={{0,1},{1,2},{2,3},{3,0},{4,7},{5,4},{6,5},{7,6},{8,9},{9,10},{10,1... | collective-permute-start | bytes 589832 | tf_op jit(solution)/shard_map/ppermute | solution.py:44
  136.8 9.6 %collective-permute-start.29 = (f32[3,64,256]{2,1,0:T(8,128)S(1)}, f32[3,64,256]{2,1,0:T(8,128)S(1)}, u32[]{:S(2)}, u32[]{:S(2)}) collective-permute-start(f32[3,64,256]{2,1,0:T(8,128)S(1)} %get-tuple-element.72), channel_id=1, source_target_pairs={{0,2},{1,3},{2,0},{3,1},{4,6},{5,7},{6,4},{7,5},{8,10},{9,11},{10,... | collective-permute-start | bytes 589832 | tf_op jit(solution)/shard_map/ppermute | solution.py:48

commit v3 on v2

v3 whole, which is shorter than its diff:
```python
import functools
import math

import jax
import jax.numpy as jnp
from jax import lax
from jax.experimental import pallas as pl
from jax.experimental.pallas import tpu as pltpu
from jax.sharding import Mesh, PartitionSpec as P

NBR = 32
ITERS = 3
SHARP = 24.0
ALPHA = 0.8
EPS = 1e-06
ROWS = 256
D = 768
CH = 64
BLK = 3
NX = 4
NW = 32
SCALE = SHARP * math.log2(math.e)
WIDE = ("z", "y", "c")
VM = pl.BlockSpec(memory_space=pltpu.VMEM)
SM = pl.BlockSpec(memory_space=pltpu.SMEM)
F32 = jnp.float32
BF16 = jnp.bfloat16
FIRST = (0, 48, 96, 144, 192)
CAP = 36
BASE = (0, 6, 0, 6, 12)
CHUNKS = 5
SOON = (0, 1, 2, 3, 4, 8)
COUNTS = 240
TOTALS = 248
LISTS = 256
SPARE = NX * BLK
SUMS = CH + 8
IDS = 16
CHEAP = pl.CostEstimate(flops=1000, bytes_accessed=1000, transcendentals=0)
LONG = pl.CostEstimate(flops=30_000_000_000, bytes_accessed=1000, transcendentals=0)


def along_x(v, sign):
    pairs = []
    for core in range(2):
        by = sign if core == 0 else -sign
        pairs += [(core * NX + x, core * NX + (x + by) % NX) for x in range(NX)]
    return lax.ppermute(v, ("c", "x"), pairs)


def across_x(v):
    return lax.ppermute(v, "x", [(x, (x + 2) % NX) for x in range(NX)])


def from_wide(v, sign):
    return lax.ppermute(
        v, WIDE, [((i + (2 * sign if i % 2 == 0 else -2 * sign)) % NW, i) for i in range(NW)]
    )


def swap_core(v):
    return lax.ppermute(v, "c", [(0, 1), (1, 0)])


def prep_kernel(emb_ref, seed_ref, ids_ref, two_ref, one_ref, full_ref):
    for block in range(BLK):
        values = emb_ref[block].astype(F32)
        total = jnp.sum(values * values, axis=-1, keepdims=True)
        unit = (values * lax.rsqrt(total + EPS)).astype(BF16)
        full_ref[block * ROWS : (block + 1) * ROWS] = unit
        full_ref[BLK * ROWS :, block * ROWS : (block + 1) * ROWS] = seed_ref[block].astype(BF16)
        if block < 2:
            two_ref[block * D : (block + 1) * D] = jnp.transpose(unit)
        else:
            one_ref[:D] = jnp.transpose(unit)
    two_ref[2 * D :] = ids_ref[...]
    one_ref[D:] = ids_ref[...]


def prepare(embeddings, seeds_t, ids):
    return pl.pallas_call(
        prep_kernel,
        out_shape=(
            jax.ShapeDtypeStruct((2 * D + IDS, ROWS), BF16),
            jax.ShapeDtypeStruct((D + IDS, ROWS), BF16),
            jax.ShapeDtypeStruct((BLK * ROWS + CH, D), BF16),
        ),
        in_specs=[VM, VM, VM],
        out_specs=(VM, VM, VM),
        compiler_params=pltpu.CompilerParams(vmem_limit_bytes=8 << 20),
        cost_estimate=CHEAP,
        name="prep",
    )(embeddings, seeds_t, ids)


def split_ids(neighbours):
    shown = neighbours + 1
    parts = jnp.concatenate([shown >> 4, shown & 15], axis=1).astype(BF16)
    return jnp.pad(parts, ((0, IDS - BLK), (0, ROWS - 2 * NBR)))


def joined_ids(rows):
    parts = rows[-IDS:][:BLK].astype(jnp.int32)
    return parts[:, :NBR] * 16 + parts[:, NBR : 2 * NBR] - 1


def plan_kernel(groups, place_ref, *refs):
    id_refs = refs[: len(groups)]
    old_ref, list_ref = (refs[-2], refs[-1]) if len(refs) > len(groups) + 1 else (None, refs[-1])
    wide, x = place_ref[0], place_ref[1]
    core = wide & 1
    partner = 3 - 2 * core
    first = 4 - 4 * core
    if old_ref is None:
        counts = [jnp.int32(0)] * CHUNKS
    else:

        def copy(k, _):
            list_ref[k] = old_ref[k]
            return 0

        counts = [old_ref[TOTALS + c] for c in range(CHUNKS)]
        for c in range(2, CHUNKS):
            lax.fori_loop(FIRST[c], FIRST[c] + counts[c], copy, 0)
    for ref, group in zip(id_refs, groups):
        for i in range(BLK):
            row = group * BLK + i
            chunks = (0, 1, 4) if row in SOON else (2, 3, 4)

            def body(k, carry, ref=ref, i=i, row=row, chunks=chunks):
                block = ref[i, k]
                device = (block * 43691) >> 17
                step = ((device >> 2) - wide + 2) & (NW - 1)
                source = jnp.where(
                    step == 2,
                    0,
                    jnp.where(
                        step == partner,
                        1,
                        jnp.where(step == first, 2, jnp.where(step == 4 - first, 3, 4)),
                    ),
                )
                code = row * 16 + source * BLK + block - BLK * device
                hit = jnp.where((block >= 0) & ((device & (NX - 1)) == x), 1, 0)
                for c, n in zip(chunks, carry):
                    list_ref[FIRST[c] + n] = code
                low = jnp.where(source < 2, hit, 0)
                high = jnp.where(source == 4, hit, 0)
                return (carry[0] + low, carry[1] + hit - low - high, carry[2] + high)

            got = lax.fori_loop(0, NBR, body, tuple(counts[c] for c in chunks), unroll=4)
            for c, n in zip(chunks, got):
                counts[c] = n
    for c in range(CHUNKS):
        for pad in range(4):
            list_ref[FIRST[c] + counts[c] + pad] = SPARE * 16 + BASE[c]
        list_ref[COUNTS + c] = (counts[c] + 3) >> 2
        list_ref[TOTALS + c] = counts[c]


def make_plan(groups, place, ids, old=None):
    operands = [place, *ids] + ([old] if old is not None else [])
    return pl.pallas_call(
        functools.partial(plan_kernel, groups),
        out_shape=jax.ShapeDtypeStruct((LISTS,), jnp.int32),
        in_specs=[SM] * len(operands),
        out_specs=SM,
        compiler_params=pltpu.CompilerParams(vmem_limit_bytes=1 << 20),
        cost_estimate=LONG,
        name="plan",
    )(*operands)


def tiles(chunk, list_ref, row_ref, col_ref, state_ref, w_ref, sum_ref, base=0):
    steps = list_ref[COUNTS + chunk]

    def four_tiles(step, _):
        for k in range(4):
            n = 4 * step + k
            named = list_ref[FIRST[chunk] + n]
            row, col = named >> 4, (named & 15) - base
            place = jnp.where(row == SPARE, 0, row) * D
            cosine = jnp.dot(
                col_ref[pl.ds(pl.multiple_of(col * ROWS, ROWS), ROWS), :],
                row_ref[pl.ds(pl.multiple_of(place, D), D), :],
                preferred_element_type=F32,
            )
            weight = jnp.exp2(cosine * SCALE)
            w_ref[n] = weight.astype(BF16)
            sum_ref[row, CH:] += jnp.sum(weight.reshape(ROWS // 8, 8, ROWS), axis=0)
        return 0

    def four_spreads(step, _):
        for k in range(4):
            n = 4 * step + k
            named = list_ref[FIRST[chunk] + n]
            sum_ref[named >> 4, :CH] += jnp.dot(
                state_ref[(named & 15) - base], w_ref[n], preferred_element_type=F32
            )
        return 0

    lax.fori_loop(0, steps, four_tiles, 0)
    lax.fori_loop(0, steps, four_spreads, 0)


def put_rows(buf, refs, places):
    for ref, (at, n) in zip(refs, places):
        buf[at * D : (at + n) * D] = ref[: n * D]


def put_cols(buf, states, refs):
    for at, ref in enumerate(refs):
        buf[at * BLK * ROWS : (at + 1) * BLK * ROWS] = ref[: BLK * ROWS]
        for j in range(BLK):
            states[at * BLK + j] = ref[BLK * ROWS :, j * ROWS : (j + 1) * ROWS]


def build_0(list_ref, r0, r1, r2, r3, c0, c1, w_ref, sum_ref, rows, cols, states):
    put_rows(rows, (r0, r1, r2, r3), ((0, 2), (2, 1), (3, 2), (8, 1)))
    put_cols(cols, states, (c0, c1))
    sum_ref[...] = jnp.zeros_like(sum_ref)
    tiles(0, list_ref, rows, cols, states, w_ref, sum_ref)


def build_1(list_ref, rows, c0, c1, c2, c3, given, w_ref, sum_ref, cols, states):
    put_cols(cols, states, (c0, c1, c2, c3))
    sum_ref[...] = given[...]
    tiles(1, list_ref, rows, cols, states, w_ref, sum_ref)


def build_2(list_ref, old_rows, r0, r1, r2, r3, cols, states, given, w2_ref, w3_ref, sum_ref, rows):
    rows[: 5 * D] = old_rows[: 5 * D]
    rows[8 * D : 9 * D] = old_rows[8 * D :]
    put_rows(rows, (r0, r1, r2, r3), ((5, 1), (6, 2), (9, 2), (11, 1)))
    sum_ref[...] = given[...]
    tiles(2, list_ref, rows, cols, states, w2_ref, sum_ref)
    tiles(3, list_ref, rows, cols, states, w3_ref, sum_ref)


def build_3(list_ref, rows, c4, given, w_ref, *refs):
    outs, (sums, states) = refs[:NX], refs[NX:]
    sums[...] = given[...]
    for j in range(BLK):
        states[j] = c4[BLK * ROWS :, j * ROWS : (j + 1) * ROWS]
    tiles(4, list_ref, rows, c4, states, w_ref, sums, base=BASE[4])
    for at, ref in enumerate(outs):
        ref[...] = sums[at * BLK : (at + 1) * BLK]


def build(kernel, room, outs, scratch, *operands):
    return pl.pallas_call(
        kernel,
        out_shape=[jax.ShapeDtypeStruct(*o) for o in outs],
        in_specs=[SM if o.dtype == jnp.int32 else VM for o in operands],
        out_specs=[VM] * len(outs),
        scratch_shapes=[pltpu.VMEM(*s) for s in scratch],
        compiler_params=pltpu.CompilerParams(vmem_limit_bytes=room << 20),
        cost_estimate=LONG,
        name=kernel.__name__,
    )(*operands)


WEIGHTS = ((CAP, ROWS, ROWS), BF16)


def rows_of(n):
    return ((n * D, ROWS), BF16)


def columns(n):
    return [((n * BLK * ROWS, D), BF16), ((n * BLK, CH, ROWS), BF16)]


SUM_BUF = ((SPARE + 1, SUMS, ROWS), F32)


def add_spread(chunk, list_ref, w_ref, state_ref, sum_ref):
    def four(step, _):
        for k in range(4):
            n = 4 * step + k
            named = list_ref[FIRST[chunk] + n]
            sum_ref[named >> 4] += jnp.dot(
                state_ref[named & 15], w_ref[n], preferred_element_type=F32
            )
        return 0

    lax.fori_loop(0, list_ref[COUNTS + chunk], four, 0)


def spread_near(near_ref, list_ref, w0, w2, s0, s1, sum_ref, states):
    sum_ref[...] = jnp.zeros_like(sum_ref)
    for at, ref in enumerate((s0, s1)):
        states[at * BLK : (at + 1) * BLK] = ref[...]
    add_spread(0, near_ref, w0, states, sum_ref)
    add_spread(2, list_ref, w2, states, sum_ref)


def spread_rest(near_ref, list_ref, w1, w3, w4, s2, s3, s4, given, own, back, fore, far, sums, states):
    sums[...] = given[...]
    for at, ref in enumerate((s2, s3, s4)):
        states[(at + 2) * BLK : (at + 3) * BLK] = ref[...]
    add_spread(1, near_ref, w1, states, sums)
    add_spread(3, list_ref, w3, states, sums)
    add_spread(4, list_ref, w4, states, sums)
    for at, ref in enumerate((own, back, fore, far)):
        ref[...] = sums[at * BLK : (at + 1) * BLK]


def spread(lists, weights, states):
    sums = ((SPARE + 1, CH, ROWS), F32)
    held = ((5 * BLK, CH, ROWS), BF16)
    w0, w1, w2, w3, w4 = weights
    (near,) = build(spread_near, 3, [sums], [held], *lists, w0, w2, *states[:2])
    return build(
        spread_rest, 4, [((BLK, CH, ROWS), F32)] * NX, [sums, held], *lists, w1, w3, w4, *states[2:], near
    )


def wide_exchange(v):
    one = from_wide(v, 1)
    partner = swap_core(v)
    other = from_wide(v, -1)
    across = swap_core(one)
    return [v, partner, one, other, across]


def reduce_rows(own, back, fore, far):
    return own + along_x(back, -1) + along_x(fore, 1) + across_x(far)


def local(embeddings, seeds, neighbours):
    place = jnp.stack([lax.axis_index(WIDE), lax.axis_index("x")]).astype(jnp.int32)
    seeds_t = jnp.swapaxes(seeds, 1, 2)
    after = lambda v, *done: lax.optimization_barrier((v, *done))[0]
    two, one, full = prepare(embeddings, seeds_t, split_ids(neighbours))
    back_two = along_x(two, 1)
    fore_one = along_x(one, -1)
    above = from_wide(full, 1)
    below = from_wide(full, -1)
    back_one = along_x(one, 1)
    back_two, fore_one, back_one, late_full, late_two = lax.optimization_barrier(
        (back_two, fore_one, back_one, full, two)
    )
    partner = swap_core(late_full)
    far_two = along_x(back_two, 1)
    fore_two = along_x(late_two, -1)
    far_one = along_x(after(fore_one, partner), -1)

    near = make_plan((0, 1, 2), place, [neighbours, joined_ids(back_two), joined_ids(fore_one)])
    w0, sums, rows = build(
        build_0, 6, [WEIGHTS, SUM_BUF, rows_of(9)], columns(2),
        near, two, one, back_two, fore_one, full, partner,
    )
    beside = swap_core(after(above, sums))
    w1, sums, cols, states = build(
        build_1, 4, [WEIGHTS, SUM_BUF, *columns(4)], [], near, rows, full, partner, above, below, sums
    )
    lists = make_plan((3,), place, [joined_ids(after(far_two, sums))], near)
    w2, w3, sums, rows = build(
        build_2, 4, [WEIGHTS, WEIGHTS, SUM_BUF, rows_of(12)], [],
        lists, rows, back_one, fore_two, far_two, far_one, cols, states, sums,
    )
    w4, own, back, fore, far = build(
        build_3, 4, [WEIGHTS] + [((BLK, SUMS, ROWS), F32)] * NX, [SUM_BUF, ((BLK, CH, ROWS), BF16)],
        lists, rows, beside, sums,
    )
    lists = [near, lists]
    weights = [w0, w1, w2, w3, w4]

    total = reduce_rows(own, back, fore, far)
    scale = ALPHA / jnp.sum(total[:, CH:], axis=1, keepdims=True)
    prior = (1.0 - ALPHA) * seeds_t
    scores = total[:, :CH] * scale + prior
    for _ in range(ITERS - 1):
        states = wide_exchange(scores.astype(BF16))
        total = reduce_rows(*spread(lists, weights, states))
        scores = total * scale + prior
    return jnp.swapaxes(scores, 1, 2)


def solution(mesh):
    fine = Mesh(mesh.devices.reshape(4, 4, 2, 4), ("z", "y", "c", "x"))
    everywhere = ("z", "y", "c", "x")
    return jax.shard_map(
        local,
        mesh=fine,
        in_specs=(P(everywhere, None, None), P(everywhere, None, None), P(everywhere, None)),
        out_specs=P(everywhere, None, None),
        check_vma=False,
    )
```

time: 148 us -> 138 us (0.932)
  waiting for transfers between devices: 59.9 us -> 46.9 us
  Pallas kernels: 42.9 us -> 46.1 us
  starting transfers between devices: 37.9 us -> 40.3 us
  local copies, waits for them, and re-layouts: 4.63 us -> 2.88 us
    ppermute x6, starting transfers between devices: 10.7 us -> 20 us  [from_wide(): lax.ppermute(v, WIDE, [((i + (2 * sign if i % 2 == 0 else -2 * sign)) % N...]
    ppermute x14 -> x12, waiting for transfers between devices: 44.8 us -> 36.4 us  [along_x(): return lax.ppermute(v, ('c', 'x'), pairs)]
    ppermute x4 -> x3, waiting for transfers between devices: 7.74 us -> 0.01 us  [across_x(): return lax.ppermute(v, 'x', [(x, (x + 2) % NX) for x in range(NX)])]
    ppermute x6, starting transfers between devices: 6.47 us -> 2.11 us  [swap_core(): return lax.ppermute(v, 'c', [(0, 1), (1, 0)])]
    pallas_call x8 -> x11, Pallas kernels: 42.9 us -> 46.1 us  [the longest x8 36.3 us: build(): pl.pallas_call(kernel, out_shape=[jax.ShapeDtypeStruct(*o) for o in outs]...]
    ppermute x6, waiting for transfers between devices: 7.36 us -> 10.5 us  [from_wide(): lax.ppermute(v, WIDE, [((i + (2 * sign if i % 2 == 0 else -2 * sign)) % N...]
    ppermute x4 -> x3, starting transfers between devices: 4.75 us -> 2.55 us  [across_x(): return lax.ppermute(v, 'x', [(x, (x + 2) % NX) for x in range(NX)])]
    unnamed x20 -> x8, local copies, waits for them, and re-layouts: 4.63 us -> 2.88 us
  transfers between devices with their start and end apart: 30 -> 27, of which waited for: 14 -> 12; matrix products, arithmetic and copies ran while one was open for 0% -> 0% of each run, Pallas kernels for 18% -> 24%
where the time goes in v3:
time: 138 us; the launch traced here: 139 us
  waiting for transfers between devices  46.9 us (34%)
  Pallas kernels  46.1 us (33%)
  starting transfers between devices  40.3 us (29%)
  local copies, waits for them, and re-layouts  2.88 us (2%)
  other arithmetic  2.02 us (1%)
    ppermute x12, waiting for transfers between devices, along_x(): return lax.ppermute(v, ('c', 'x'), pairs)  36.4 us
    pallas_call x8, Pallas kernels, build(): pl.pallas_call(kernel, out_shape=[jax.ShapeDtypeStruct(*o) for o in outs]...  36.3 us
    ppermute x6, starting transfers between devices, from_wide(): lax.ppermute(v, WIDE, [((i + (2 * sign if i % 2 == 0 else -2 * sign)) % N...  20 us
    ppermute x12, starting transfers between devices, along_x(): return lax.ppermute(v, ('c', 'x'), pairs)  15.7 us
    ppermute x6, waiting for transfers between devices, from_wide(): lax.ppermute(v, WIDE, [((i + (2 * sign if i % 2 == 0 else -2 * sign)) % N...  10.5 us
    pallas_call x2, Pallas kernels, make_plan(): pl.pallas_call(functools.partial(plan_kernel, groups), out_shape=jax.Shap...  8.02 us
    unnamed x8, local copies, waits for them, and re-layouts  2.88 us
  transfers between devices with their start and end apart: 27, of which 12 were waited for; matrix products, arithmetic and copies ran while one was open for 0% of the time, Pallas kernels for 24%

profile of v3, /device:TPU:0, one launch (start us, length us, event | category | flops | bytes accessed | tf_op | source)
XLA Modules:
  0.0 138.5 jit_solution(755248960979629058)
XLA Ops:
  0.0 0.7 shift-right-arithmetic_convert_fusion
  0.7 0.1 fusion.7.ids_ref
  0.8 0.9 copy-done
  1.7 1.3 copy-done.2
  3.0 1.8 %prep.1 = (bf16[1552,256]{1,0:T(8,128)(2,1)S(1)}, bf16[784,256]{1,0:T(8,128)(2,1)}, bf16[832,768]{1,0:T(8,128)(2,1)}) custom-call(bf16[3,256,768]{2,1,0:T(8,128)(2,1)S(1)} %copy-done.2, f32[3,64,256]{2,1,0:T(8,128)S(1)} %bitcast.8, bf16[16,256]{1,0:T(8,128)(2,1)S(1)} %fusion.7.ids_ref), custom_call_target="tpu_custom_call" | custom-call | flops 1000 | bytes 1000 | tf_op jit(solution)/shard_map/prep/pallas_call | solution.py:81
  4.8 1.6 %collective-permute-start = (bf16[1552,256]{1,0:T(8,128)(2,1)S(1)}, bf16[1552,256]{1,0:T(8,128)(2,1)S(1)}, u32[]{:S(2)}, u32[]{:S(2)}) collective-permute-start(bf16[1552,256]{1,0:T(8,128)(2,1)S(1)} %get-tuple-element.52.r0), channel_id=1, source_target_pairs={{0,1},{1,2},{2,3},{3,0},{4,7},{5,4},{6,5},{7,6},{8,9},{9,10},{10,1... | collective-permute-start | bytes 2383880 | tf_op jit(solution)/shard_map/ppermute | solution.py:48
  6.4 1.5 %collective-permute-start.2 = (bf16[784,256]{1,0:T(8,128)(2,1)}, bf16[784,256]{1,0:T(8,128)(2,1)}, u32[]{:S(2)}, u32[]{:S(2)}) collective-permute-start(bf16[784,256]{1,0:T(8,128)(2,1)} %get-tuple-element.41.r1), channel_id=1, source_target_pairs={{0,1},{1,2},{2,3},{3,0},{4,7},{5,4},{6,5},{7,6},{8,9},{9,10},{10,1... | collective-permute-start | bytes 1204232 | tf_op jit(solution)/shard_map/ppermute | solution.py:48
  7.9 1.7 %collective-permute-start.1 = (bf16[784,256]{1,0:T(8,128)(2,1)}, bf16[784,256]{1,0:T(8,128)(2,1)S(1)}, u32[]{:S(2)}, u32[]{:S(2)}) collective-permute-start(bf16[784,256]{1,0:T(8,128)(2,1)} %get-tuple-element.41.r1), channel_id=1, source_target_pairs={{0,3},{1,0},{2,1},{3,2},{4,5},{5,6},{6,7},{7,4},{8,11},{9,8},{10,9... | collective-permute-start | bytes 1204232 | tf_op jit(solution)/shard_map/ppermute | solution.py:48
  9.6 1.6 %collective-permute-start.6 = (bf16[832,768]{1,0:T(8,128)(2,1)}, bf16[832,768]{1,0:T(8,128)(2,1)}, u32[]{:S(2)}, u32[]{:S(2)}) collective-permute-start(bf16[832,768]{1,0:T(8,128)(2,1)} %get-tuple-element.45.c0), channel_id=1, source_target_pairs={{120,0},{12,4},{0,8},{20,12},{8,16},{28,20},{16,24},{36,28},{24,32... | collective-permute-start | bytes 3833864 | tf_op jit(solution)/shard_map/ppermute | solution.py:56
  11.2 4.9 %collective-permute-start.5 = (bf16[832,768]{1,0:T(8,128)(2,1)}, bf16[832,768]{1,0:T(8,128)(2,1)S(1)}, u32[]{:S(2)}, u32[]{:S(2)}) collective-permute-start(bf16[832,768]{1,0:T(8,128)(2,1)} %get-tuple-element.45.c0), channel_id=1, source_target_pairs={{8,0},{124,4},{16,8},{4,12},{24,16},{12,20},{32,24},{20,28},{40,32... | collective-permute-start | bytes 3833864 | tf_op jit(solution)/shard_map/ppermute | solution.py:56
  16.2 10.6 %collective-permute-done.2.r0 = bf16[784,256]{1,0:T(8,128)(2,1)} collective-permute-done((bf16[784,256]{1,0:T(8,128)(2,1)}, bf16[784,256]{1,0:T(8,128)(2,1)}, u32[]{:S(2)}, u32[]{:S(2)}) %collective-permute-start.2) | collective-permute-done | bytes 401440 | tf_op jit(solution)/shard_map/ppermute | solution.py:48
  26.8 0.4 collective-permute-start.3
  27.3 2.9 %collective-permute-start.7 = (bf16[1552,256]{1,0:T(8,128)(2,1)S(1)}, bf16[1552,256]{1,0:T(8,128)(2,1)S(1)}, u32[]{:S(2)}, u32[]{:S(2)}) collective-permute-start(bf16[1552,256]{1,0:T(8,128)(2,1)S(1)} %get-tuple-element.52.r0), channel_id=1, source_target_pairs={{0,3},{1,0},{2,1},{3,2},{4,5},{5,6},{6,7},{7,4},{8,11},{9,8},{10,9... | collective-permute-start | bytes 2383880 | tf_op jit(solution)/shard_map/ppermute | solution.py:48
  30.2 0.7 copy-done.3
  30.9 5.3 %plan.2.list_ref.refs_1_.near_ref = s32[256]{0:T(256)S(1)} custom-call(s32[2]{0:T(128)S(1)} %pad_add_fusion.place_ref, s32[3,32]{1,0:T(4,128)S(1)} %copy-done.3, s32[3,32]{1,0:T(4,128)S(1)} %fusion.10.refs_1_, s32[3,32]{1,0:T(4,128)S(1)} %fusion.9.refs_2_), custom_call_target="tpu_custom_call" | custom-call | flops 30000001024 | bytes 1000 | tf_op jit(solution)/shard_map/plan/pallas_call | solution.py:163
  36.2 1.3 collective-permute-start.8
  37.5 5.1 %build_0.1 = (bf16[36,256,256]{2,1,0:T(8,128)(2,1)S(1)}, f32[13,72,256]{2,1,0:T(8,128)S(1)}, bf16[6912,256]{1,0:T(8,128)(2,1)S(1)}) custom-call(s32[256]{0:T(256)S(1)} %plan.2.list_ref.refs_1_.near_ref, bf16[1552,256]{1,0:T(8,128)(2,1)S(1)} %get-tuple-element.52.r0, bf16[784,256]{1,0:T(8,128)(2,1)} %get-tuple-element.41.r1, ...), custom_call_target="tpu_custom_call" | custom-call | flops 30000001024 | bytes 1000 | tf_op jit(solution)/shard_map/build_0/pallas_call | solution.py:251
  42.6 0.3 collective-permute-done.5.c2
  43.0 2.1 %collective-permute-start.9 = (bf16[832,768]{1,0:T(8,128)(2,1)S(1)}, bf16[832,768]{1,0:T(8,128)(2,1)S(1)}, u32[]{:S(2)}, u32[]{:S(2)}) collective-permute-start(bf16[832,768]{1,0:T(8,128)(2,1)S(1)} %collective-permute-done.5.c2), channel_id=1, source_target_pairs={{0,4},{4,0},{1,5},{5,1},{2,6},{6,2},{3,7},{7,3},{8,12},{12,8},{9,1... | collective-permute-start | bytes 3833864 | tf_op jit(solution)/shard_map/ppermute | solution.py:62
  45.1 4.6 %build_1.1 = (bf16[36,256,256]{2,1,0:T(8,128)(2,1)S(1)}, f32[13,72,256]{2,1,0:T(8,128)S(1)}, bf16[3072,768]{1,0:T(8,128)(2,1)S(1)}, bf16[12,64,256]{2,1,0:T(8,128)(2,1)S(1)}) custom-call(s32[256]{0:T(256)S(1)} %plan.2.list_ref.refs_1_.near_ref, bf16[6912,256]{1,0:T(8,128)(2,1)S(1)} %get-tuple-element.46.rows.old_rows, ...), custom_call_target="tpu_custom_call" | custom-call | flops 30000001024 | bytes 1000 | tf_op jit(solution)/shard_map/build_1/pallas_call | solution.py:251
  49.7 2.7 %plan.3.list_ref = s32[256]{0:T(256)S(1)} custom-call(s32[2]{0:T(128)S(1)} %pad_add_fusion.place_ref, s32[3,32]{1,0:T(4,128)S(1)} %fusion.8.refs_0_, s32[256]{0:T(256)S(1)} %plan.2.list_ref.refs_1_.near_ref), custom_call_target="tpu_custom_call" | custom-call | flops 30000001024 | bytes 1000 | tf_op jit(solution)/shard_map/plan/pallas_call | solution.py:163
  52.5 10.4 %build_2.1 = (bf16[36,256,256]{2,1,0:T(8,128)(2,1)S(1)}, bf16[36,256,256]{2,1,0:T(8,128)(2,1)S(1)}, f32[13,72,256]{2,1,0:T(8,128)S(1)}, bf16[9216,256]{1,0:T(8,128)(2,1)S(1)}) custom-call(s32[256]{0:T(256)S(1)} %plan.3.list_ref, bf16[6912,256]{1,0:T(8,128)(2,1)S(1)} %get-tuple-element.46.rows.old_rows, bf16[784,256]{1,0:T(8,128)(2,1)} %collective-permute-done.2.r0, ...), custom_call_target="tpu_custom_call" | custom-call | flops 30000001024 | bytes 1000 | tf_op jit(solution)/shard_map/build_2/pallas_call | solution.py:251
  62.9 3.9 %build_3.1 = (bf16[36,256,256]{2,1,0:T(8,128)(2,1)S(1)}, f32[3,72,256]{2,1,0:T(8,128)S(1)}, f32[3,72,256]{2,1,0:T(8,128)S(1)}, f32[3,72,256]{2,1,0:T(8,128)S(1)}, f32[3,72,256]{2,1,0:T(8,128)S(1)}) custom-call(s32[256]{0:T(256)S(1)} %plan.3.list_ref, bf16[9216,256]{1,0:T(8,128)(2,1)S(1)} %get-tuple-element.57.rows, ...), custom_call_target="tpu_custom_call" | custom-call | flops 30000001024 | bytes 1000 | tf_op jit(solution)/shard_map/build_3/pallas_call | solution.py:251
  66.9 0.7 collective-permute-start.10
  67.5 1.4 %collective-permute-start.11 = (f32[3,72,256]{2,1,0:T(8,128)S(1)}, f32[3,72,256]{2,1,0:T(8,128)S(1)}, u32[]{:S(2)}, u32[]{:S(2)}) collective-permute-start(f32[3,72,256]{2,1,0:T(8,128)S(1)} %get-tuple-element.63), channel_id=1, source_target_pairs={{0,1},{1,2},{2,3},{3,0},{4,7},{5,4},{6,5},{7,6},{8,9},{9,10},{10,1... | collective-permute-start | bytes 663560 | tf_op jit(solution)/shard_map/ppermute | solution.py:48
  69.0 0.1 collective-permute-start.12
  69.1 7.1 %collective-permute-done.10 = f32[3,72,256]{2,1,0:T(8,128)S(1)} collective-permute-done((f32[3,72,256]{2,1,0:T(8,128)S(1)}, f32[3,72,256]{2,1,0:T(8,128)S(1)}, u32[]{:S(2)}, u32[]{:S(2)}) %collective-permute-start.10) | collective-permute-done | bytes 221216 | tf_op jit(solution)/shard_map/ppermute | solution.py:48
  76.2 2.2 %collective-permute-done.11 = f32[3,72,256]{2,1,0:T(8,128)S(1)} collective-permute-done((f32[3,72,256]{2,1,0:T(8,128)S(1)}, f32[3,72,256]{2,1,0:T(8,128)S(1)}, u32[]{:S(2)}, u32[]{:S(2)}) %collective-permute-start.11) | collective-permute-done | bytes 221216 | tf_op jit(solution)/shard_map/ppermute | solution.py:48
  78.5 8.3 %collective-permute-start.13 = (bf16[3,64,256]{2,1,0:T(8,128)(2,1)S(1)}, bf16[3,64,256]{2,1,0:T(8,128)(2,1)S(1)}, u32[]{:S(2)}, u32[]{:S(2)}) collective-permute-start(bf16[3,64,256]{2,1,0:T(8,128)(2,1)S(1)} %fusion.1.s0), channel_id=1, source_target_pairs={{8,0},{124,4},{16,8},{4,12},{24,16},{12,20},{32,24},{20,28},{40,32... | collective-permute-start | bytes 294920 | tf_op jit(solution)/shard_map/ppermute | solution.py:56
  86.8 3.0 %collective-permute-done.13.s2 = bf16[3,64,256]{2,1,0:T(8,128)(2,1)S(1)} collective-permute-done((bf16[3,64,256]{2,1,0:T(8,128)(2,1)S(1)}, bf16[3,64,256]{2,1,0:T(8,128)(2,1)S(1)}, u32[]{:S(2)}, u32[]{:S(2)}) %collective-permute-start.13) | collective-permute-done | bytes 98336 | tf_op jit(solution)/shard_map/ppermute | solution.py:56
  89.8 2.8 %spread_near.2.given = f32[13,64,256]{2,1,0:T(8,128)S(1)} custom-call(s32[256]{0:T(256)S(1)} %plan.2.list_ref.refs_1_.near_ref, s32[256]{0:T(256)S(1)} %plan.3.list_ref, bf16[36,256,256]{2,1,0:T(8,128)(2,1)S(1)} %get-tuple-element.65.w0, bf16[36,256,256]{2,1,0:T(8,128)(2,1)S(1)} %get-tuple-element.66.w2, bf16[3,64,256]{2,1,0:T(8,128)(2,1)S(1)} %fusion.1.s0, ...), custom_call_target="tpu_custom_call" | custom-call | flops 30000001024 | bytes 1000 | tf_op jit(solution)/shard_map/spread_near/pallas_call | solution.py:251
  92.7 2.1 %collective-permute-done.14.s3 = bf16[3,64,256]{2,1,0:T(8,128)(2,1)S(1)} collective-permute-done((bf16[3,64,256]{2,1,0:T(8,128)(2,1)S(1)}, bf16[3,64,256]{2,1,0:T(8,128)(2,1)S(1)}, u32[]{:S(2)}, u32[]{:S(2)}) %collective-permute-start.14) | collective-permute-done | bytes 98336 | tf_op jit(solution)/shard_map/ppermute | solution.py:56
  94.7 3.3 %spread_rest.2 = (f32[3,64,256]{2,1,0:T(8,128)S(1)}, f32[3,64,256]{2,1,0:T(8,128)S(1)}, f32[3,64,256]{2,1,0:T(8,128)S(1)}, f32[3,64,256]{2,1,0:T(8,128)S(1)}) custom-call(s32[256]{0:T(256)S(1)} %plan.2.list_ref.refs_1_.near_ref, s32[256]{0:T(256)S(1)} %plan.3.list_ref, bf16[36,256,256]{2,1,0:T(8,128)(2,1)S(1)} %get-tuple-element.50.w1, ...), custom_call_target="tpu_custom_call" | custom-call | flops 30000001024 | bytes 1000 | tf_op jit(solution)/shard_map/spread_rest/pallas_call | solution.py:251
  98.1 1.4 %collective-permute-start.17 = (f32[3,64,256]{2,1,0:T(8,128)S(1)}, f32[3,64,256]{2,1,0:T(8,128)S(1)}, u32[]{:S(2)}, u32[]{:S(2)}) collective-permute-start(f32[3,64,256]{2,1,0:T(8,128)S(1)} %get-tuple-element.68), channel_id=1, source_target_pairs={{0,3},{1,0},{2,1},{3,2},{4,5},{5,6},{6,7},{7,4},{8,11},{9,8},{10,9... | collective-permute-start | bytes 589832 | tf_op jit(solution)/shard_map/ppermute | solution.py:48
  99.5 0.7 collective-permute-start.18
  100.2 0.9 collective-permute-start.19
  101.1 6.2 %collective-permute-done.17 = f32[3,64,256]{2,1,0:T(8,128)S(1)} collective-permute-done((f32[3,64,256]{2,1,0:T(8,128)S(1)}, f32[3,64,256]{2,1,0:T(8,128)S(1)}, u32[]{:S(2)}, u32[]{:S(2)}) %collective-permute-start.17) | collective-permute-done | bytes 196640 | tf_op jit(solution)/shard_map/ppermute | solution.py:48
  107.2 2.4 %collective-permute-done.18 = f32[3,64,256]{2,1,0:T(8,128)S(1)} collective-permute-done((f32[3,64,256]{2,1,0:T(8,128)S(1)}, f32[3,64,256]{2,1,0:T(8,128)S(1)}, u32[]{:S(2)}, u32[]{:S(2)}) %collective-permute-start.18) | collective-permute-done | bytes 196640 | tf_op jit(solution)/shard_map/ppermute | solution.py:48
  109.7 5.2 %collective-permute-start.20 = (bf16[3,64,256]{2,1,0:T(8,128)(2,1)S(1)}, bf16[3,64,256]{2,1,0:T(8,128)(2,1)S(1)}, u32[]{:S(2)}, u32[]{:S(2)}) collective-permute-start(bf16[3,64,256]{2,1,0:T(8,128)(2,1)S(1)} %add_convert_fusion.s0), channel_id=1, source_target_pairs={{8,0},{124,4},{16,8},{4,12},{24,16},{12,20},{32,24},{20,28},{40,32... | collective-permute-start | bytes 294920 | tf_op jit(solution)/shard_map/ppermute | solution.py:56
  114.9 3.0 %collective-permute-done.20.s2 = bf16[3,64,256]{2,1,0:T(8,128)(2,1)S(1)} collective-permute-done((bf16[3,64,256]{2,1,0:T(8,128)(2,1)S(1)}, bf16[3,64,256]{2,1,0:T(8,128)(2,1)S(1)}, u32[]{:S(2)}, u32[]{:S(2)}) %collective-permute-start.20) | collective-permute-done | bytes 98336 | tf_op jit(solution)/shard_map/ppermute | solution.py:56
  117.9 2.8 %spread_near.3.given = f32[13,64,256]{2,1,0:T(8,128)S(1)} custom-call(s32[256]{0:T(256)S(1)} %plan.2.list_ref.refs_1_.near_ref, s32[256]{0:T(256)S(1)} %plan.3.list_ref, bf16[36,256,256]{2,1,0:T(8,128)(2,1)S(1)} %get-tuple-element.65.w0, bf16[36,256,256]{2,1,0:T(8,128)(2,1)S(1)} %get-tuple-element.66.w2, bf16[3,64,256]{2,1,0:T(8,128)(2,1)S(1)} %add_convert_fusion.s0, ...), custom_call_target="tpu_custom_call" | custom-call | flops 30000001024 | bytes 1000 | tf_op jit(solution)/shard_map/spread_near/pallas_call | solution.py:251
  120.8 2.1 %collective-permute-done.21.s3 = bf16[3,64,256]{2,1,0:T(8,128)(2,1)S(1)} collective-permute-done((bf16[3,64,256]{2,1,0:T(8,128)(2,1)S(1)}, bf16[3,64,256]{2,1,0:T(8,128)(2,1)S(1)}, u32[]{:S(2)}, u32[]{:S(2)}) %collective-permute-start.21) | collective-permute-done | bytes 98336 | tf_op jit(solution)/shard_map/ppermute | solution.py:56
  122.9 3.3 %spread_rest.3 = (f32[3,64,256]{2,1,0:T(8,128)S(1)}, f32[3,64,256]{2,1,0:T(8,128)S(1)}, f32[3,64,256]{2,1,0:T(8,128)S(1)}, f32[3,64,256]{2,1,0:T(8,128)S(1)}) custom-call(s32[256]{0:T(256)S(1)} %plan.2.list_ref.refs_1_.near_ref, s32[256]{0:T(256)S(1)} %plan.3.list_ref, bf16[36,256,256]{2,1,0:T(8,128)(2,1)S(1)} %get-tuple-element.50.w1, ...), custom_call_target="tpu_custom_call" | custom-call | flops 30000001024 | bytes 1000 | tf_op jit(solution)/shard_map/spread_rest/pallas_call | solution.py:251
  126.2 2.2 %collective-permute-start.24 = (f32[3,64,256]{2,1,0:T(8,128)S(1)}, f32[3,64,256]{2,1,0:T(8,128)S(1)}, u32[]{:S(2)}, u32[]{:S(2)}) collective-permute-start(f32[3,64,256]{2,1,0:T(8,128)S(1)} %get-tuple-element.72), channel_id=1, source_target_pairs={{0,3},{1,0},{2,1},{3,2},{4,5},{5,6},{6,7},{7,4},{8,11},{9,8},{10,9... | collective-permute-start | bytes 589832 | tf_op jit(solution)/shard_map/ppermute | solution.py:48
  128.3 1.5 %collective-permute-start.26 = (f32[3,64,256]{2,1,0:T(8,128)S(1)}, f32[3,64,256]{2,1,0:T(8,128)S(1)}, u32[]{:S(2)}, u32[]{:S(2)}) collective-permute-start(f32[3,64,256]{2,1,0:T(8,128)S(1)} %get-tuple-element.74), channel_id=1, source_target_pairs={{0,2},{1,3},{2,0},{3,1},{4,6},{5,7},{6,4},{7,5},{8,10},{9,11},{10,... | collective-permute-start | bytes 589832 | tf_op jit(solution)/shard_map/ppermute | solution.py:52
  129.9 3.4 %collective-permute-done.24 = f32[3,64,256]{2,1,0:T(8,128)S(1)} collective-permute-done((f32[3,64,256]{2,1,0:T(8,128)S(1)}, f32[3,64,256]{2,1,0:T(8,128)S(1)}, u32[]{:S(2)}, u32[]{:S(2)}) %collective-permute-start.24) | collective-permute-done | bytes 196640 | tf_op jit(solution)/shard_map/ppermute | solution.py:48
  133.2 4.5 %collective-permute-done.25 = f32[3,64,256]{2,1,0:T(8,128)S(1)} collective-permute-done((f32[3,64,256]{2,1,0:T(8,128)S(1)}, f32[3,64,256]{2,1,0:T(8,128)S(1)}, u32[]{:S(2)}, u32[]{:S(2)}) %collective-permute-start.25) | collective-permute-done | bytes 196640 | tf_op jit(solution)/shard_map/ppermute | solution.py:48
  137.8 0.7 add_bitcast_fusion
  (39 shorter events, 0.6 us)
Async XLA Ops:
  0.8 0.9 copy-start
  1.7 1.3 copy-start.2
  4.8 22.0 %collective-permute-start = (bf16[1552,256]{1,0:T(8,128)(2,1)S(1)}, bf16[1552,256]{1,0:T(8,128)(2,1)S(1)}, u32[]{:S(2)}, u32[]{:S(2)}) collective-permute-start(bf16[1552,256]{1,0:T(8,128)(2,1)S(1)} %get-tuple-element.52.r0), channel_id=1, source_target_pairs={{0,1},{1,2},{2,3},{3,0},{4,7},{5,4},{6,5},{7,6},{8,9},{9,10},{10,1... | collective-permute-start | bytes 2383880 | tf_op jit(solution)/shard_map/ppermute | solution.py:48
  6.4 20.4 %collective-permute-start.2 = (bf16[784,256]{1,0:T(8,128)(2,1)}, bf16[784,256]{1,0:T(8,128)(2,1)}, u32[]{:S(2)}, u32[]{:S(2)}) collective-permute-start(bf16[784,256]{1,0:T(8,128)(2,1)} %get-tuple-element.41.r1), channel_id=1, source_target_pairs={{0,1},{1,2},{2,3},{3,0},{4,7},{5,4},{6,5},{7,6},{8,9},{9,10},{10,1... | collective-permute-start | bytes 1204232 | tf_op jit(solution)/shard_map/ppermute | solution.py:48
  7.9 18.9 %collective-permute-start.1 = (bf16[784,256]{1,0:T(8,128)(2,1)}, bf16[784,256]{1,0:T(8,128)(2,1)S(1)}, u32[]{:S(2)}, u32[]{:S(2)}) collective-permute-start(bf16[784,256]{1,0:T(8,128)(2,1)} %get-tuple-element.41.r1), channel_id=1, source_target_pairs={{0,3},{1,0},{2,1},{3,2},{4,5},{5,6},{6,7},{7,4},{8,11},{9,8},{10,9... | collective-permute-start | bytes 1204232 | tf_op jit(solution)/shard_map/ppermute | solution.py:48
  9.6 35.4 %collective-permute-start.6 = (bf16[832,768]{1,0:T(8,128)(2,1)}, bf16[832,768]{1,0:T(8,128)(2,1)}, u32[]{:S(2)}, u32[]{:S(2)}) collective-permute-start(bf16[832,768]{1,0:T(8,128)(2,1)} %get-tuple-element.45.c0), channel_id=1, source_target_pairs={{120,0},{12,4},{0,8},{20,12},{8,16},{28,20},{16,24},{36,28},{24,32... | collective-permute-start | bytes 3833864 | tf_op jit(solution)/shard_map/ppermute | solution.py:56
  11.2 31.8 %collective-permute-start.5 = (bf16[832,768]{1,0:T(8,128)(2,1)}, bf16[832,768]{1,0:T(8,128)(2,1)S(1)}, u32[]{:S(2)}, u32[]{:S(2)}) collective-permute-start(bf16[832,768]{1,0:T(8,128)(2,1)} %get-tuple-element.45.c0), channel_id=1, source_target_pairs={{8,0},{124,4},{16,8},{4,12},{24,16},{12,20},{32,24},{20,28},{40,32... | collective-permute-start | bytes 3833864 | tf_op jit(solution)/shard_map/ppermute | solution.py:56
  26.8 22.8 %collective-permute-start.3 = (bf16[1552,256]{1,0:T(8,128)(2,1)S(1)}, bf16[1552,256]{1,0:T(8,128)(2,1)S(1)}, u32[]{:S(2)}, u32[]{:S(2)}) collective-permute-start(bf16[1552,256]{1,0:T(8,128)(2,1)S(1)} %collective-permute-done.r2), channel_id=1, source_target_pairs={{0,1},{1,2},{2,3},{3,0},{4,7},{5,4},{6,5},{7,6},{8,9},{9,10},{10,1... | collective-permute-start | bytes 2383880 | tf_op jit(solution)/shard_map/ppermute | solution.py:48
  27.3 25.1 %collective-permute-start.7 = (bf16[1552,256]{1,0:T(8,128)(2,1)S(1)}, bf16[1552,256]{1,0:T(8,128)(2,1)S(1)}, u32[]{:S(2)}, u32[]{:S(2)}) collective-permute-start(bf16[1552,256]{1,0:T(8,128)(2,1)S(1)} %get-tuple-element.52.r0), channel_id=1, source_target_pairs={{0,3},{1,0},{2,1},{3,2},{4,5},{5,6},{6,7},{7,4},{8,11},{9,8},{10,9... | collective-permute-start | bytes 2383880 | tf_op jit(solution)/shard_map/ppermute | solution.py:48
  30.2 6.0 %collective-permute-start.4 = (bf16[832,768]{1,0:T(8,128)(2,1)}, bf16[832,768]{1,0:T(8,128)(2,1)S(1)}, u32[]{:S(2)}, u32[]{:S(2)}) collective-permute-start(bf16[832,768]{1,0:T(8,128)(2,1)} %get-tuple-element.45.c0), channel_id=1, source_target_pairs={{0,4},{4,0},{1,5},{5,1},{2,6},{6,2},{3,7},{7,3},{8,12},{12,8},{9,1... | collective-permute-start | bytes 3833864 | tf_op jit(solution)/shard_map/ppermute | solution.py:62
  30.2 0.7 copy-start.3
  36.2 16.3 %collective-permute-start.8 = (bf16[784,256]{1,0:T(8,128)(2,1)S(1)}, bf16[784,256]{1,0:T(8,128)(2,1)S(1)}, u32[]{:S(2)}, u32[]{:S(2)}) collective-permute-start(bf16[784,256]{1,0:T(8,128)(2,1)S(1)} %collective-permute-done.1.r3), channel_id=1, source_target_pairs={{0,3},{1,0},{2,1},{3,2},{4,5},{5,6},{6,7},{7,4},{8,11},{9,8},{10,9... | collective-permute-start | bytes 1204232 | tf_op jit(solution)/shard_map/ppermute | solution.py:48
  43.0 19.9 %collective-permute-start.9 = (bf16[832,768]{1,0:T(8,128)(2,1)S(1)}, bf16[832,768]{1,0:T(8,128)(2,1)S(1)}, u32[]{:S(2)}, u32[]{:S(2)}) collective-permute-start(bf16[832,768]{1,0:T(8,128)(2,1)S(1)} %collective-permute-done.5.c2), channel_id=1, source_target_pairs={{0,4},{4,0},{1,5},{5,1},{2,6},{6,2},{3,7},{7,3},{8,12},{12,8},{9,1... | collective-permute-start | bytes 3833864 | tf_op jit(solution)/shard_map/ppermute | solution.py:62
  62.9 15.6 %copy-start.1 = (f32[3,256,64]{1,2,0:T(8,128)S(1)}, f32[3,256,64]{1,2,0:T(8,128)}, u32[]{:S(2)}) copy-start(f32[3,256,64]{1,2,0:T(8,128)} %param.4) | copy-start | bytes 589828
  66.9 9.3 %collective-permute-start.10 = (f32[3,72,256]{2,1,0:T(8,128)S(1)}, f32[3,72,256]{2,1,0:T(8,128)S(1)}, u32[]{:S(2)}, u32[]{:S(2)}) collective-permute-start(f32[3,72,256]{2,1,0:T(8,128)S(1)} %get-tuple-element.62), channel_id=1, source_target_pairs={{0,3},{1,0},{2,1},{3,2},{4,5},{5,6},{6,7},{7,4},{8,11},{9,8},{10,9... | collective-permute-start | bytes 663560 | tf_op jit(solution)/shard_map/ppermute | solution.py:48
  67.5 10.9 %collective-permute-start.11 = (f32[3,72,256]{2,1,0:T(8,128)S(1)}, f32[3,72,256]{2,1,0:T(8,128)S(1)}, u32[]{:S(2)}, u32[]{:S(2)}) collective-permute-start(f32[3,72,256]{2,1,0:T(8,128)S(1)} %get-tuple-element.63), channel_id=1, source_target_pairs={{0,1},{1,2},{2,3},{3,0},{4,7},{5,4},{6,5},{7,6},{8,9},{9,10},{10,1... | collective-permute-start | bytes 663560 | tf_op jit(solution)/shard_map/ppermute | solution.py:48
  69.0 9.4 %collective-permute-start.12 = (f32[3,72,256]{2,1,0:T(8,128)S(1)}, f32[3,72,256]{2,1,0:T(8,128)S(1)}, u32[]{:S(2)}, u32[]{:S(2)}) collective-permute-start(f32[3,72,256]{2,1,0:T(8,128)S(1)} %get-tuple-element.64), channel_id=1, source_target_pairs={{0,2},{1,3},{2,0},{3,1},{4,6},{5,7},{6,4},{7,5},{8,10},{9,11},{10,... | collective-permute-start | bytes 663560 | tf_op jit(solution)/shard_map/ppermute | solution.py:52
  78.5 11.3 %collective-permute-start.13 = (bf16[3,64,256]{2,1,0:T(8,128)(2,1)S(1)}, bf16[3,64,256]{2,1,0:T(8,128)(2,1)S(1)}, u32[]{:S(2)}, u32[]{:S(2)}) collective-permute-start(bf16[3,64,256]{2,1,0:T(8,128)(2,1)S(1)} %fusion.1.s0), channel_id=1, source_target_pairs={{8,0},{124,4},{16,8},{4,12},{24,16},{12,20},{32,24},{20,28},{40,32... | collective-permute-start | bytes 294920 | tf_op jit(solution)/shard_map/ppermute | solution.py:56
  86.8 3.0 %collective-permute-start.16 = (bf16[3,64,256]{2,1,0:T(8,128)(2,1)S(1)}, bf16[3,64,256]{2,1,0:T(8,128)(2,1)S(1)}, u32[]{:S(2)}, u32[]{:S(2)}) collective-permute-start(bf16[3,64,256]{2,1,0:T(8,128)(2,1)S(1)} %fusion.1.s0), channel_id=1, source_target_pairs={{0,4},{4,0},{1,5},{5,1},{2,6},{6,2},{3,7},{7,3},{8,12},{12,8},{9,1... | collective-permute-start | bytes 294920 | tf_op jit(solution)/shard_map/ppermute | solution.py:62
  86.8 7.9 %collective-permute-start.14 = (bf16[3,64,256]{2,1,0:T(8,128)(2,1)S(1)}, bf16[3,64,256]{2,1,0:T(8,128)(2,1)S(1)}, u32[]{:S(2)}, u32[]{:S(2)}) collective-permute-start(bf16[3,64,256]{2,1,0:T(8,128)(2,1)S(1)} %fusion.1.s0), channel_id=1, source_target_pairs={{120,0},{12,4},{0,8},{20,12},{8,16},{28,20},{16,24},{36,28},{24,32... | collective-permute-start | bytes 294920 | tf_op jit(solution)/shard_map/ppermute | solution.py:56
  89.8 4.9 %collective-permute-start.15 = (bf16[3,64,256]{2,1,0:T(8,128)(2,1)S(1)}, bf16[3,64,256]{2,1,0:T(8,128)(2,1)S(1)}, u32[]{:S(2)}, u32[]{:S(2)}) collective-permute-start(bf16[3,64,256]{2,1,0:T(8,128)(2,1)S(1)} %collective-permute-done.13.s2), channel_id=1, source_target_pairs={{0,4},{4,0},{1,5},{5,1},{2,6},{6,2},{3,7},{7,3},{8,12},{12,8},{9,1... | collective-permute-start | bytes 294920 | tf_op jit(solution)/shard_map/ppermute | solution.py:62
  98.1 9.2 %collective-permute-start.17 = (f32[3,64,256]{2,1,0:T(8,128)S(1)}, f32[3,64,256]{2,1,0:T(8,128)S(1)}, u32[]{:S(2)}, u32[]{:S(2)}) collective-permute-start(f32[3,64,256]{2,1,0:T(8,128)S(1)} %get-tuple-element.68), channel_id=1, source_target_pairs={{0,3},{1,0},{2,1},{3,2},{4,5},{5,6},{6,7},{7,4},{8,11},{9,8},{10,9... | collective-permute-start | bytes 589832 | tf_op jit(solution)/shard_map/ppermute | solution.py:48
  99.5 10.1 %collective-permute-start.18 = (f32[3,64,256]{2,1,0:T(8,128)S(1)}, f32[3,64,256]{2,1,0:T(8,128)S(1)}, u32[]{:S(2)}, u32[]{:S(2)}) collective-permute-start(f32[3,64,256]{2,1,0:T(8,128)S(1)} %get-tuple-element.69), channel_id=1, source_target_pairs={{0,1},{1,2},{2,3},{3,0},{4,7},{5,4},{6,5},{7,6},{8,9},{9,10},{10,1... | collective-permute-start | bytes 589832 | tf_op jit(solution)/shard_map/ppermute | solution.py:48
  100.2 9.5 %collective-permute-start.19 = (f32[3,64,256]{2,1,0:T(8,128)S(1)}, f32[3,64,256]{2,1,0:T(8,128)S(1)}, u32[]{:S(2)}, u32[]{:S(2)}) collective-permute-start(f32[3,64,256]{2,1,0:T(8,128)S(1)} %get-tuple-element.70), channel_id=1, source_target_pairs={{0,2},{1,3},{2,0},{3,1},{4,6},{5,7},{6,4},{7,5},{8,10},{9,11},{10,... | collective-permute-start | bytes 589832 | tf_op jit(solution)/shard_map/ppermute | solution.py:52
  109.7 8.2 %collective-permute-start.20 = (bf16[3,64,256]{2,1,0:T(8,128)(2,1)S(1)}, bf16[3,64,256]{2,1,0:T(8,128)(2,1)S(1)}, u32[]{:S(2)}, u32[]{:S(2)}) collective-permute-start(bf16[3,64,256]{2,1,0:T(8,128)(2,1)S(1)} %add_convert_fusion.s0), channel_id=1, source_target_pairs={{8,0},{124,4},{16,8},{4,12},{24,16},{12,20},{32,24},{20,28},{40,32... | collective-permute-start | bytes 294920 | tf_op jit(solution)/shard_map/ppermute | solution.py:56
  114.9 3.0 %collective-permute-start.23 = (bf16[3,64,256]{2,1,0:T(8,128)(2,1)S(1)}, bf16[3,64,256]{2,1,0:T(8,128)(2,1)S(1)}, u32[]{:S(2)}, u32[]{:S(2)}) collective-permute-start(bf16[3,64,256]{2,1,0:T(8,128)(2,1)S(1)} %add_convert_fusion.s0), channel_id=1, source_target_pairs={{0,4},{4,0},{1,5},{5,1},{2,6},{6,2},{3,7},{7,3},{8,12},{12,8},{9,1... | collective-permute-start | bytes 294920 | tf_op jit(solution)/shard_map/ppermute | solution.py:62
  114.9 7.9 %collective-permute-start.21 = (bf16[3,64,256]{2,1,0:T(8,128)(2,1)S(1)}, bf16[3,64,256]{2,1,0:T(8,128)(2,1)S(1)}, u32[]{:S(2)}, u32[]{:S(2)}) collective-permute-start(bf16[3,64,256]{2,1,0:T(8,128)(2,1)S(1)} %add_convert_fusion.s0), channel_id=1, source_target_pairs={{120,0},{12,4},{0,8},{20,12},{8,16},{28,20},{16,24},{36,28},{24,32... | collective-permute-start | bytes 294920 | tf_op jit(solution)/shard_map/ppermute | solution.py:56
  117.9 4.9 %collective-permute-start.22 = (bf16[3,64,256]{2,1,0:T(8,128)(2,1)S(1)}, bf16[3,64,256]{2,1,0:T(8,128)(2,1)S(1)}, u32[]{:S(2)}, u32[]{:S(2)}) collective-permute-start(bf16[3,64,256]{2,1,0:T(8,128)(2,1)S(1)} %collective-permute-done.20.s2), channel_id=1, source_target_pairs={{0,4},{4,0},{1,5},{5,1},{2,6},{6,2},{3,7},{7,3},{8,12},{12,8},{9,1... | collective-permute-start | bytes 294920 | tf_op jit(solution)/shard_map/ppermute | solution.py:62
  126.2 7.1 %collective-permute-start.24 = (f32[3,64,256]{2,1,0:T(8,128)S(1)}, f32[3,64,256]{2,1,0:T(8,128)S(1)}, u32[]{:S(2)}, u32[]{:S(2)}) collective-permute-start(f32[3,64,256]{2,1,0:T(8,128)S(1)} %get-tuple-element.72), channel_id=1, source_target_pairs={{0,3},{1,0},{2,1},{3,2},{4,5},{5,6},{6,7},{7,4},{8,11},{9,8},{10,9... | collective-permute-start | bytes 589832 | tf_op jit(solution)/shard_map/ppermute | solution.py:48
  128.3 9.4 %collective-permute-start.25 = (f32[3,64,256]{2,1,0:T(8,128)S(1)}, f32[3,64,256]{2,1,0:T(8,128)S(1)}, u32[]{:S(2)}, u32[]{:S(2)}) collective-permute-start(f32[3,64,256]{2,1,0:T(8,128)S(1)} %get-tuple-element.73), channel_id=1, source_target_pairs={{0,1},{1,2},{2,3},{3,0},{4,7},{5,4},{6,5},{7,6},{8,9},{9,10},{10,1... | collective-permute-start | bytes 589832 | tf_op jit(solution)/shard_map/ppermute | solution.py:48
  128.3 9.4 %collective-permute-start.26 = (f32[3,64,256]{2,1,0:T(8,128)S(1)}, f32[3,64,256]{2,1,0:T(8,128)S(1)}, u32[]{:S(2)}, u32[]{:S(2)}) collective-permute-start(f32[3,64,256]{2,1,0:T(8,128)S(1)} %get-tuple-element.74), channel_id=1, source_target_pairs={{0,2},{1,3},{2,0},{3,1},{4,6},{5,7},{6,4},{7,5},{8,10},{9,11},{10,... | collective-permute-start | bytes 589832 | tf_op jit(solution)/shard_map/ppermute | solution.py:52

commit v4 on v3

--- a/solution.py
+++ b/solution.py
@@ -26,13 +26,15 @@
 F32 = jnp.float32
 BF16 = jnp.bfloat16
 FIRST = (0, 48, 96, 144, 192)
-CAP = 36
+CAP = 40
 BASE = (0, 6, 0, 6, 12)
 CHUNKS = 5
 SOON = (0, 1, 2, 3, 4, 8)
 COUNTS = 240
-TOTALS = 248
+TOTALS = 245
+BEFORE = 250
 LISTS = 256
+STEP = 9
 SPARE = NX * BLK
 SUMS = CH + 8
 IDS = 16
@@ -104,16 +106,26 @@
     return parts[:, :NBR] * 16 + parts[:, NBR : 2 * NBR] - 1
 
 
-def plan_kernel(groups, place_ref, *refs):
-    id_refs = refs[: len(groups)]
+def coded(ids, wide, x):
+    core = wide & 1
+    device = ids // BLK
+    step = (device // NX - wide + 2) & (NW - 1)
+    first = 4 - 4 * core
+    source = jnp.where(
+        step == 2,
+        0,
+        jnp.where(step == 3 - 2 * core, 1, jnp.where(step == first, 2, jnp.where(step == 4 - first, 3, 4))),
+    )
+    adds = jnp.where(source < 2, 1, jnp.where(source < 4, 1 << STEP, 1 << (2 * STEP)))
+    hit = (ids >= 0) & (device % NX == x)
+    return jnp.where(hit, source * BLK + ids % BLK + 16 * adds, 0)
+
+
+def plan_kernel(groups, *refs):
+    code_refs = refs[: len(groups)]
     old_ref, list_ref = (refs[-2], refs[-1]) if len(refs) > len(groups) + 1 else (None, refs[-1])
-    wide, x = place_ref[0], place_ref[1]
-    core = wide & 1
-    partner = 3 - 2 * core
-    first = 4 - 4 * core
-    if old_ref is None:
-        counts = [jnp.int32(0)] * CHUNKS
-    else:
+    counts = [jnp.int32(0)] * CHUNKS
+    if old_ref is not None:
 
         def copy(k, _):
             list_ref[k] = old_ref[k]
@@ -122,35 +134,25 @@
         counts = [old_ref[TOTALS + c] for c in range(CHUNKS)]
         for c in range(2, CHUNKS):
             lax.fori_loop(FIRST[c], FIRST[c] + counts[c], copy, 0)
-    for ref, group in zip(id_refs, groups):
+    for c in range(CHUNKS):
+        list_ref[BEFORE + c] = counts[c]
+    for ref, group in zip(code_refs, groups):
         for i in range(BLK):
             row = group * BLK + i
             chunks = (0, 1, 4) if row in SOON else (2, 3, 4)
 
-            def body(k, carry, ref=ref, i=i, row=row, chunks=chunks):
-                block = ref[i, k]
-                device = (block * 43691) >> 17
-                step = ((device >> 2) - wide + 2) & (NW - 1)
-                source = jnp.where(
-                    step == 2,
-                    0,
-                    jnp.where(
-                        step == partner,
-                        1,
-                        jnp.where(step == first, 2, jnp.where(step == 4 - first, 3, 4)),
-                    ),
-                )
-                code = row * 16 + source * BLK + block - BLK * device
-                hit = jnp.where((block >= 0) & ((device & (NX - 1)) == x), 1, 0)
-                for c, n in zip(chunks, carry):
-                    list_ref[FIRST[c] + n] = code
-                low = jnp.where(source < 2, hit, 0)
-                high = jnp.where(source == 4, hit, 0)
-                return (carry[0] + low, carry[1] + hit - low - high, carry[2] + high)
-
-            got = lax.fori_loop(0, NBR, body, tuple(counts[c] for c in chunks), unroll=4)
-            for c, n in zip(chunks, got):
-                counts[c] = n
+            def body(k, packed, ref=ref, i=i, row=row, chunks=chunks):
+                value = ref[i, k]
+                entry = row * 16 + (value & 15)
+                list_ref[FIRST[chunks[0]] + (packed & ((1 << STEP) - 1))] = entry
+                list_ref[FIRST[chunks[1]] + ((packed >> STEP) & ((1 << STEP) - 1))] = entry
+                list_ref[FIRST[chunks[2]] + (packed >> (2 * STEP))] = entry
+                return packed + (value >> 4)
+
+            packed = sum(counts[c] << (at * STEP) for at, c in enumerate(chunks))
+            packed = lax.fori_loop(0, NBR, body, packed, unroll=8)
+            for at, c in enumerate(chunks):
+                counts[c] = (packed >> (at * STEP)) & ((1 << STEP) - 1)
     for c in range(CHUNKS):
         for pad in range(4):
             list_ref[FIRST[c] + counts[c] + pad] = SPARE * 16 + BASE[c]
@@ -158,8 +160,8 @@
         list_ref[TOTALS + c] = counts[c]
 
 
-def make_plan(groups, place, ids, old=None):
-    operands = [place, *ids] + ([old] if old is not None else [])
+def make_plan(groups, codes, old=None):
+    operands = [*codes] + ([old] if old is not None else [])
     return pl.pallas_call(
         functools.partial(plan_kernel, groups),
         out_shape=jax.ShapeDtypeStruct((LISTS,), jnp.int32),
@@ -274,46 +276,57 @@
 SUM_BUF = ((SPARE + 1, SUMS, ROWS), F32)
 
 
-def add_spread(chunk, list_ref, w_ref, state_ref, sum_ref):
+def add_spread(chunk, list_ref, w_ref, state_ref, sum_ref, low, high):
     def four(step, _):
         for k in range(4):
-            n = 4 * step + k
+            n = low + 4 * step + k
             named = list_ref[FIRST[chunk] + n]
-            sum_ref[named >> 4] += jnp.dot(
-                state_ref[named & 15], w_ref[n], preferred_element_type=F32
-            )
+            row = jnp.where(n < high, named >> 4, SPARE)
+            sum_ref[row] += jnp.dot(state_ref[named & 15], w_ref[n], preferred_element_type=F32)
         return 0
 
-    lax.fori_loop(0, list_ref[COUNTS + chunk], four, 0)
+    lax.fori_loop(0, (high - low + 3) >> 2, four, 0)
 
 
 def spread_near(near_ref, list_ref, w0, w2, s0, s1, sum_ref, states):
     sum_ref[...] = jnp.zeros_like(sum_ref)
     for at, ref in enumerate((s0, s1)):
         states[at * BLK : (at + 1) * BLK] = ref[...]
-    add_spread(0, near_ref, w0, states, sum_ref)
-    add_spread(2, list_ref, w2, states, sum_ref)
-
-
-def spread_rest(near_ref, list_ref, w1, w3, w4, s2, s3, s4, given, own, back, fore, far, sums, states):
+    add_spread(0, near_ref, w0, states, sum_ref, 0, near_ref[TOTALS])
+    add_spread(2, list_ref, w2, states, sum_ref, 0, list_ref[TOTALS + 2])
+
+
+def spread_far(list_ref, w3, w4, s2, s3, s4, given, far, sums, states):
     sums[...] = given[...]
     for at, ref in enumerate((s2, s3, s4)):
         states[(at + 2) * BLK : (at + 3) * BLK] = ref[...]
-    add_spread(1, near_ref, w1, states, sums)
-    add_spread(3, list_ref, w3, states, sums)
-    add_spread(4, list_ref, w4, states, sums)
-    for at, ref in enumerate((own, back, fore, far)):
+    for chunk, w_ref in ((3, w3), (4, w4)):
+        add_spread(chunk, list_ref, w_ref, states, sums, list_ref[BEFORE + chunk], list_ref[TOTALS + chunk])
+    far[...] = sums[3 * BLK : SPARE]
+
+
+def spread_rest(near_ref, list_ref, w1, w3, w4, s2, s3, s4, given, own, back, fore, sums, states):
+    sums[...] = given[...]
+    for at, ref in enumerate((s2, s3, s4)):
+        states[(at + 2) * BLK : (at + 3) * BLK] = ref[...]
+    add_spread(1, near_ref, w1, states, sums, 0, near_ref[TOTALS + 1])
+    for chunk, w_ref in ((3, w3), (4, w4)):
+        add_spread(chunk, list_ref, w_ref, states, sums, 0, list_ref[BEFORE + chunk])
+    for at, ref in enumerate((own, back, fore)):
         ref[...] = sums[at * BLK : (at + 1) * BLK]
 
 
 def spread(lists, weights, states):
     sums = ((SPARE + 1, CH, ROWS), F32)
     held = ((5 * BLK, CH, ROWS), BF16)
+    part = ((BLK, CH, ROWS), F32)
     w0, w1, w2, w3, w4 = weights
     (near,) = build(spread_near, 3, [sums], [held], *lists, w0, w2, *states[:2])
-    return build(
-        spread_rest, 4, [((BLK, CH, ROWS), F32)] * NX, [sums, held], *lists, w1, w3, w4, *states[2:], near
-    )
+    (far,) = build(spread_far, 4, [part], [sums, held], lists[1], w3, w4, *states[2:], near)
+    near, _ = lax.optimization_barrier((near, far))
+    return *build(
+        spread_rest, 4, [part] * (NX - 1), [sums, held], *lists, w1, w3, w4, *states[2:], near
+    ), far
 
 
 def wide_exchange(v):
@@ -325,11 +338,12 @@
 
 
 def reduce_rows(own, back, fore, far):
-    return own + along_x(back, -1) + along_x(fore, 1) + across_x(far)
+    first = lax.optimization_barrier(own + across_x(far))
+    return first + along_x(back, -1) + along_x(fore, 1)
 
 
 def local(embeddings, seeds, neighbours):
-    place = jnp.stack([lax.axis_index(WIDE), lax.axis_index("x")]).astype(jnp.int32)
+    code = functools.partial(coded, wide=lax.axis_index(WIDE), x=lax.axis_index("x"))
     seeds_t = jnp.swapaxes(seeds, 1, 2)
     after = lambda v, *done: lax.optimization_barrier((v, *done))[0]
     two, one, full = prepare(embeddings, seeds_t, split_ids(neighbours))
@@ -346,7 +360,9 @@
     fore_two = along_x(late_two, -1)
     far_one = along_x(after(fore_one, partner), -1)
 
-    near = make_plan((0, 1, 2), place, [neighbours, joined_ids(back_two), joined_ids(fore_one)])
+    near = make_plan(
+        (0, 1, 2), [code(neighbours), code(joined_ids(back_two)), code(joined_ids(fore_one))]
+    )
     w0, sums, rows = build(
         build_0, 6, [WEIGHTS, SUM_BUF, rows_of(9)], columns(2),
         near, two, one, back_two, fore_one, full, partner,
@@ -355,7 +371,7 @@
     w1, sums, cols, states = build(
         build_1, 4, [WEIGHTS, SUM_BUF, *columns(4)], [], near, rows, full, partner, above, below, sums
     )
-    lists = make_plan((3,), place, [joined_ids(after(far_two, sums))], near)
+    lists = make_plan((3,), [code(joined_ids(after(far_two, sums)))], near)
     w2, w3, sums, rows = build(
         build_2, 4, [WEIGHTS, WEIGHTS, SUM_BUF, rows_of(12)], [],
         lists, rows, back_one, fore_two, far_two, far_one, cols, states, sums,

time: 138 us -> 131 us (0.949); the launches traced: 139 us -> 130 us
  Pallas kernels: 46.1 us -> 38.2 us
    ppermute x12, waiting for transfers between devices: 36.4 us -> 26.6 us  [along_x(): return lax.ppermute(v, ('c', 'x'), pairs)]
    ppermute x3, starting transfers between devices: 2.55 us -> 8.46 us  [across_x(): return lax.ppermute(v, 'x', [(x, (x + 2) % NX) for x in range(NX)])]
    ppermute x6, starting transfers between devices: 20 us -> 14.1 us  [from_wide(): lax.ppermute(v, WIDE, [((i + (2 * sign if i % 2 == 0 else -2 * sign)) % N...]
    ppermute x3, waiting for transfers between devices: 0.01 us -> 5.15 us  [across_x(): return lax.ppermute(v, 'x', [(x, (x + 2) % NX) for x in range(NX)])]
    ppermute x6, waiting for transfers between devices: 10.5 us -> 14.5 us  [from_wide(): lax.ppermute(v, WIDE, [((i + (2 * sign if i % 2 == 0 else -2 * sign)) % N...]
    pallas_call x8 -> x10, Pallas kernels: 36.3 us -> 32.4 us  [build(): pl.pallas_call(kernel, out_shape=[jax.ShapeDtypeStruct(*o) for o in outs]...]
    pallas_call x2, Pallas kernels: 8.02 us -> 5.03 us  [make_plan(): pl.pallas_call(functools.partial(plan_kernel, groups), out_shape=jax.Shap...]
    unnamed x8 -> x6, local copies, waits for them, and re-layouts: 2.88 us -> 2.2 us
  transfers between devices with their start and end apart: 27 -> 27, of which waited for: 12 -> 15; matrix products, arithmetic and copies ran while one was open for 0% -> 0% of each run, Pallas kernels for 24% -> 24%
where the time goes in v4:
time: 131 us; the launch traced here: 130 us
  waiting for transfers between devices  46.2 us (35%)
  starting transfers between devices  41 us (31%)
  Pallas kernels  38.2 us (29%)
  local copies, waits for them, and re-layouts  2.2 us (2%)
  other arithmetic  2 us (2%)
    pallas_call x10, Pallas kernels, build(): pl.pallas_call(kernel, out_shape=[jax.ShapeDtypeStruct(*o) for o in outs]...  32.4 us
    ppermute x12, waiting for transfers between devices, along_x(): return lax.ppermute(v, ('c', 'x'), pairs)  26.6 us
    ppermute x12, starting transfers between devices, along_x(): return lax.ppermute(v, ('c', 'x'), pairs)  15.7 us
    ppermute x6, waiting for transfers between devices, from_wide(): lax.ppermute(v, WIDE, [((i + (2 * sign if i % 2 == 0 else -2 * sign)) % N...  14.5 us
    ppermute x6, starting transfers between devices, from_wide(): lax.ppermute(v, WIDE, [((i + (2 * sign if i % 2 == 0 else -2 * sign)) % N...  14.1 us
    ppermute x3, starting transfers between devices, across_x(): return lax.ppermute(v, 'x', [(x, (x + 2) % NX) for x in range(NX)])  8.46 us
    ppermute x3, waiting for transfers between devices, across_x(): return lax.ppermute(v, 'x', [(x, (x + 2) % NX) for x in range(NX)])  5.15 us
    pallas_call x2, Pallas kernels, make_plan(): pl.pallas_call(functools.partial(plan_kernel, groups), out_shape=jax.Shap...  5.03 us
  transfers between devices with their start and end apart: 27, of which 15 were waited for; matrix products, arithmetic and copies ran while one was open for 0% of the time, Pallas kernels for 24%

profile of v4, /device:TPU:0, one launch (start us, length us, event | category | flops | bytes accessed | tf_op | source)
XLA Modules:
  0.0 129.8 jit_solution(765285168541839742)
XLA Ops:
  0.0 0.7 shift-right-arithmetic_convert_fusion
  0.8 0.9 copy-done
  1.7 1.3 copy-done.2
  3.0 0.7 prep.1
  3.7 1.6 %collective-permute-start = (bf16[1552,256]{1,0:T(8,128)(2,1)S(1)}, bf16[1552,256]{1,0:T(8,128)(2,1)S(1)}, u32[]{:S(2)}, u32[]{:S(2)}) collective-permute-start(bf16[1552,256]{1,0:T(8,128)(2,1)S(1)} %get-tuple-element.52.r0), channel_id=1, source_target_pairs={{0,1},{1,2},{2,3},{3,0},{4,7},{5,4},{6,5},{7,6},{8,9},{9,10},{10,1... | collective-permute-start | bytes 2383880 | tf_op jit(solution)/shard_map/ppermute | solution.py:50
  5.3 1.5 %collective-permute-start.2 = (bf16[784,256]{1,0:T(8,128)(2,1)S(1)}, bf16[784,256]{1,0:T(8,128)(2,1)S(1)}, u32[]{:S(2)}, u32[]{:S(2)}) collective-permute-start(bf16[784,256]{1,0:T(8,128)(2,1)S(1)} %get-tuple-element.41.r1), channel_id=1, source_target_pairs={{0,1},{1,2},{2,3},{3,0},{4,7},{5,4},{6,5},{7,6},{8,9},{9,10},{10,1... | collective-permute-start | bytes 1204232 | tf_op jit(solution)/shard_map/ppermute | solution.py:50
  6.8 1.7 %collective-permute-start.1 = (bf16[784,256]{1,0:T(8,128)(2,1)S(1)}, bf16[784,256]{1,0:T(8,128)(2,1)S(1)}, u32[]{:S(2)}, u32[]{:S(2)}) collective-permute-start(bf16[784,256]{1,0:T(8,128)(2,1)S(1)} %get-tuple-element.41.r1), channel_id=1, source_target_pairs={{0,3},{1,0},{2,1},{3,2},{4,5},{5,6},{6,7},{7,4},{8,11},{9,8},{10,9... | collective-permute-start | bytes 1204232 | tf_op jit(solution)/shard_map/ppermute | solution.py:50
  8.6 1.6 %collective-permute-start.6 = (bf16[832,768]{1,0:T(8,128)(2,1)S(1)}, bf16[832,768]{1,0:T(8,128)(2,1)S(1)}, u32[]{:S(2)}, u32[]{:S(2)}) collective-permute-start(bf16[832,768]{1,0:T(8,128)(2,1)S(1)} %get-tuple-element.45.c0), channel_id=1, source_target_pairs={{120,0},{12,4},{0,8},{20,12},{8,16},{28,20},{16,24},{36,28},{24,32... | collective-permute-start | bytes 3833864 | tf_op jit(solution)/shard_map/ppermute | solution.py:58
  10.1 4.9 %collective-permute-start.5 = (bf16[832,768]{1,0:T(8,128)(2,1)S(1)}, bf16[832,768]{1,0:T(8,128)(2,1)S(1)}, u32[]{:S(2)}, u32[]{:S(2)}) collective-permute-start(bf16[832,768]{1,0:T(8,128)(2,1)S(1)} %get-tuple-element.45.c0), channel_id=1, source_target_pairs={{8,0},{124,4},{16,8},{4,12},{24,16},{12,20},{32,24},{20,28},{40,32... | collective-permute-start | bytes 3833864 | tf_op jit(solution)/shard_map/ppermute | solution.py:58
  15.1 10.6 %collective-permute-done.2.r0 = bf16[784,256]{1,0:T(8,128)(2,1)S(1)} collective-permute-done((bf16[784,256]{1,0:T(8,128)(2,1)S(1)}, bf16[784,256]{1,0:T(8,128)(2,1)S(1)}, u32[]{:S(2)}, u32[]{:S(2)}) %collective-permute-start.2) | collective-permute-done | bytes 401440 | tf_op jit(solution)/shard_map/ppermute | solution.py:50
  26.1 2.9 %collective-permute-start.7 = (bf16[1552,256]{1,0:T(8,128)(2,1)S(1)}, bf16[1552,256]{1,0:T(8,128)(2,1)S(1)}, u32[]{:S(2)}, u32[]{:S(2)}) collective-permute-start(bf16[1552,256]{1,0:T(8,128)(2,1)S(1)} %get-tuple-element.52.r0), channel_id=1, source_target_pairs={{0,3},{1,0},{2,1},{3,2},{4,5},{5,6},{6,7},{7,4},{8,11},{9,8},{10,9... | collective-permute-start | bytes 2383880 | tf_op jit(solution)/shard_map/ppermute | solution.py:50
  29.1 3.0 %plan.2.list_ref.refs_1_.near_ref = s32[256]{0:T(256)S(1)} custom-call(s32[3,32]{1,0:T(4,128)S(1)} %get-tuple-element.77.refs_0_, s32[3,32]{1,0:T(4,128)S(1)} %get-tuple-element.78.refs_1_, s32[3,32]{1,0:T(4,128)S(1)} %get-tuple-element.79.refs_2_), custom_call_target="tpu_custom_call" | custom-call | flops 30000001024 | bytes 1000 | tf_op jit(solution)/shard_map/plan/pallas_call | solution.py:165
  32.1 1.3 %collective-permute-start.8 = (bf16[784,256]{1,0:T(8,128)(2,1)S(1)}, bf16[784,256]{1,0:T(8,128)(2,1)S(1)}, u32[]{:S(2)}, u32[]{:S(2)}) collective-permute-start(bf16[784,256]{1,0:T(8,128)(2,1)S(1)} %collective-permute-done.1.r3), channel_id=1, source_target_pairs={{0,3},{1,0},{2,1},{3,2},{4,5},{5,6},{6,7},{7,4},{8,11},{9,8},{10,9... | collective-permute-start | bytes 1204232 | tf_op jit(solution)/shard_map/ppermute | solution.py:50
  33.5 4.2 %build_0.1 = (bf16[40,256,256]{2,1,0:T(8,128)(2,1)S(1)}, f32[13,72,256]{2,1,0:T(8,128)S(1)}, bf16[6912,256]{1,0:T(8,128)(2,1)S(1)}) custom-call(s32[256]{0:T(256)S(1)} %plan.2.list_ref.refs_1_.near_ref, bf16[1552,256]{1,0:T(8,128)(2,1)S(1)} %get-tuple-element.52.r0, bf16[784,256]{1,0:T(8,128)(2,1)S(1)} %get-tuple-element.41.r1, ...), custom_call_target="tpu_custom_call" | custom-call | flops 30000001024 | bytes 1000 | tf_op jit(solution)/shard_map/build_0/pallas_call | solution.py:253
  37.7 3.9 %collective-permute-done.5.c2 = bf16[832,768]{1,0:T(8,128)(2,1)S(1)} collective-permute-done((bf16[832,768]{1,0:T(8,128)(2,1)S(1)}, bf16[832,768]{1,0:T(8,128)(2,1)S(1)}, u32[]{:S(2)}, u32[]{:S(2)}) %collective-permute-start.5) | collective-permute-done | bytes 1277984 | tf_op jit(solution)/shard_map/ppermute | solution.py:58
  41.6 2.2 %collective-permute-start.9 = (bf16[832,768]{1,0:T(8,128)(2,1)S(1)}, bf16[832,768]{1,0:T(8,128)(2,1)S(1)}, u32[]{:S(2)}, u32[]{:S(2)}) collective-permute-start(bf16[832,768]{1,0:T(8,128)(2,1)S(1)} %collective-permute-done.5.c2), channel_id=1, source_target_pairs={{0,4},{4,0},{1,5},{5,1},{2,6},{6,2},{3,7},{7,3},{8,12},{12,8},{9,1... | collective-permute-start | bytes 3833864 | tf_op jit(solution)/shard_map/ppermute | solution.py:64
  43.8 4.2 %build_1.1 = (bf16[40,256,256]{2,1,0:T(8,128)(2,1)S(1)}, f32[13,72,256]{2,1,0:T(8,128)S(1)}, bf16[3072,768]{1,0:T(8,128)(2,1)S(1)}, bf16[12,64,256]{2,1,0:T(8,128)(2,1)S(1)}) custom-call(s32[256]{0:T(256)S(1)} %plan.2.list_ref.refs_1_.near_ref, bf16[6912,256]{1,0:T(8,128)(2,1)S(1)} %get-tuple-element.46.rows.old_rows, ...), custom_call_target="tpu_custom_call" | custom-call | flops 30000001024 | bytes 1000 | tf_op jit(solution)/shard_map/build_1/pallas_call | solution.py:253
  48.1 2.0 %plan.3.list_ref = s32[256]{0:T(256)S(1)} custom-call(s32[3,32]{1,0:T(4,128)S(1)} %fusion.35.refs_0_, s32[256]{0:T(256)S(1)} %plan.2.list_ref.refs_1_.near_ref), custom_call_target="tpu_custom_call" | custom-call | flops 30000001024 | bytes 1000 | tf_op jit(solution)/shard_map/plan/pallas_call | solution.py:165
  50.1 7.4 %build_2.1 = (bf16[40,256,256]{2,1,0:T(8,128)(2,1)S(1)}, bf16[40,256,256]{2,1,0:T(8,128)(2,1)S(1)}, f32[13,72,256]{2,1,0:T(8,128)S(1)}, bf16[9216,256]{1,0:T(8,128)(2,1)S(1)}) custom-call(s32[256]{0:T(256)S(1)} %plan.3.list_ref, bf16[6912,256]{1,0:T(8,128)(2,1)S(1)} %get-tuple-element.46.rows.old_rows, bf16[784,256]{1,0:T(8,128)(2,1)S(1)} %collective-permute-done.2.r0, ...), custom_call_target="tpu_custom_call" | custom-call | flops 30000001024 | bytes 1000 | tf_op jit(solution)/shard_map/build_2/pallas_call | solution.py:253
  57.6 3.9 %build_3.1 = (bf16[40,256,256]{2,1,0:T(8,128)(2,1)S(1)}, f32[3,72,256]{2,1,0:T(8,128)S(1)}, f32[3,72,256]{2,1,0:T(8,128)S(1)}, f32[3,72,256]{2,1,0:T(8,128)S(1)}, f32[3,72,256]{2,1,0:T(8,128)S(1)}) custom-call(s32[256]{0:T(256)S(1)} %plan.3.list_ref, bf16[9216,256]{1,0:T(8,128)(2,1)S(1)} %get-tuple-element.57.rows, ...), custom_call_target="tpu_custom_call" | custom-call | flops 30000001024 | bytes 1000 | tf_op jit(solution)/shard_map/build_3/pallas_call | solution.py:253
  61.6 2.4 %collective-permute-start.10 = (f32[3,72,256]{2,1,0:T(8,128)S(1)}, f32[3,72,256]{2,1,0:T(8,128)S(1)}, u32[]{:S(2)}, u32[]{:S(2)}) collective-permute-start(f32[3,72,256]{2,1,0:T(8,128)S(1)} %get-tuple-element.62), channel_id=1, source_target_pairs={{0,2},{1,3},{2,0},{3,1},{4,6},{5,7},{6,4},{7,5},{8,10},{9,11},{10,... | collective-permute-start | bytes 663560 | tf_op jit(solution)/shard_map/ppermute | solution.py:54
  64.2 1.8 %collective-permute-start.12 = (f32[3,72,256]{2,1,0:T(8,128)S(1)}, f32[3,72,256]{2,1,0:T(8,128)S(1)}, u32[]{:S(2)}, u32[]{:S(2)}) collective-permute-start(f32[3,72,256]{2,1,0:T(8,128)S(1)} %get-tuple-element.64), channel_id=1, source_target_pairs={{0,1},{1,2},{2,3},{3,0},{4,7},{5,4},{6,5},{7,6},{8,9},{9,10},{10,1... | collective-permute-start | bytes 663560 | tf_op jit(solution)/shard_map/ppermute | solution.py:50
  66.0 4.1 %collective-permute-done.10 = f32[3,72,256]{2,1,0:T(8,128)S(1)} collective-permute-done((f32[3,72,256]{2,1,0:T(8,128)S(1)}, f32[3,72,256]{2,1,0:T(8,128)S(1)}, u32[]{:S(2)}, u32[]{:S(2)}) %collective-permute-start.10) | collective-permute-done | bytes 221216 | tf_op jit(solution)/shard_map/ppermute | solution.py:54
  70.2 5.6 %collective-permute-done.11 = f32[3,72,256]{2,1,0:T(8,128)S(1)} collective-permute-done((f32[3,72,256]{2,1,0:T(8,128)S(1)}, f32[3,72,256]{2,1,0:T(8,128)S(1)}, u32[]{:S(2)}, u32[]{:S(2)}) %collective-permute-start.11) | collective-permute-done | bytes 221216 | tf_op jit(solution)/shard_map/ppermute | solution.py:50
  76.3 4.1 %collective-permute-start.13 = (bf16[3,64,256]{2,1,0:T(8,128)(2,1)S(1)}, bf16[3,64,256]{2,1,0:T(8,128)(2,1)S(1)}, u32[]{:S(2)}, u32[]{:S(2)}) collective-permute-start(bf16[3,64,256]{2,1,0:T(8,128)(2,1)S(1)} %fusion.1.s0), channel_id=1, source_target_pairs={{8,0},{124,4},{16,8},{4,12},{24,16},{12,20},{32,24},{20,28},{40,32... | collective-permute-start | bytes 294920 | tf_op jit(solution)/shard_map/ppermute | solution.py:58
  80.5 2.2 %collective-permute-done.13.s2 = bf16[3,64,256]{2,1,0:T(8,128)(2,1)S(1)} collective-permute-done((bf16[3,64,256]{2,1,0:T(8,128)(2,1)S(1)}, bf16[3,64,256]{2,1,0:T(8,128)(2,1)S(1)}, u32[]{:S(2)}, u32[]{:S(2)}) %collective-permute-start.13) | collective-permute-done | bytes 98336 | tf_op jit(solution)/shard_map/ppermute | solution.py:58
  83.2 2.4 %spread_near.2.given = f32[13,64,256]{2,1,0:T(8,128)S(1)} custom-call(s32[256]{0:T(256)S(1)} %plan.2.list_ref.refs_1_.near_ref, s32[256]{0:T(256)S(1)} %plan.3.list_ref, bf16[40,256,256]{2,1,0:T(8,128)(2,1)S(1)} %get-tuple-element.65.w0, bf16[40,256,256]{2,1,0:T(8,128)(2,1)S(1)} %get-tuple-element.66.w2, bf16[3,64,256]{2,1,0:T(8,128)(2,1)S(1)} %fusion.1.s0, ...), custom_call_target="tpu_custom_call" | custom-call | flops 30000001024 | bytes 1000 | tf_op jit(solution)/shard_map/spread_near/pallas_call | solution.py:253
  85.6 2.8 %collective-permute-done.14.s3 = bf16[3,64,256]{2,1,0:T(8,128)(2,1)S(1)} collective-permute-done((bf16[3,64,256]{2,1,0:T(8,128)(2,1)S(1)}, bf16[3,64,256]{2,1,0:T(8,128)(2,1)S(1)}, u32[]{:S(2)}, u32[]{:S(2)}) %collective-permute-start.14) | collective-permute-done | bytes 98336 | tf_op jit(solution)/shard_map/ppermute | solution.py:58
  88.4 1.3 spread_far.2
  89.7 3.5 %collective-permute-start.17 = (f32[3,64,256]{2,1,0:T(8,128)S(1)}, f32[3,64,256]{2,1,0:T(8,128)S(1)}, u32[]{:S(2)}, u32[]{:S(2)}) collective-permute-start(f32[3,64,256]{2,1,0:T(8,128)S(1)} %spread_far.2), channel_id=1, source_target_pairs={{0,2},{1,3},{2,0},{3,1},{4,6},{5,7},{6,4},{7,5},{8,10},{9,11},{10,... | collective-permute-start | bytes 589832 | tf_op jit(solution)/shard_map/ppermute | solution.py:54
  93.2 2.6 %spread_rest.2 = (f32[3,64,256]{2,1,0:T(8,128)S(1)}, f32[3,64,256]{2,1,0:T(8,128)S(1)}, f32[3,64,256]{2,1,0:T(8,128)S(1)}) custom-call(s32[256]{0:T(256)S(1)} %plan.2.list_ref.refs_1_.near_ref, s32[256]{0:T(256)S(1)} %plan.3.list_ref, bf16[40,256,256]{2,1,0:T(8,128)(2,1)S(1)} %get-tuple-element.50.w1, bf16[40,256,256]{2,1,0:T(8,128)(2,1)S(1)} %get-tuple-element.56.w3, ...), custom_call_target="tpu_custom_call" | custom-call | flops 30000001024 | bytes 1000 | tf_op jit(solution)/shard_map/spread_rest/pallas_call | solution.py:253
  95.8 0.6 collective-permute-start.18
  96.5 1.4 %collective-permute-start.19 = (f32[3,64,256]{2,1,0:T(8,128)S(1)}, f32[3,64,256]{2,1,0:T(8,128)S(1)}, u32[]{:S(2)}, u32[]{:S(2)}) collective-permute-start(f32[3,64,256]{2,1,0:T(8,128)S(1)} %get-tuple-element.70), channel_id=1, source_target_pairs={{0,1},{1,2},{2,3},{3,0},{4,7},{5,4},{6,5},{7,6},{8,9},{9,10},{10,1... | collective-permute-start | bytes 589832 | tf_op jit(solution)/shard_map/ppermute | solution.py:50
  98.3 3.2 %collective-permute-done.18 = f32[3,64,256]{2,1,0:T(8,128)S(1)} collective-permute-done((f32[3,64,256]{2,1,0:T(8,128)S(1)}, f32[3,64,256]{2,1,0:T(8,128)S(1)}, u32[]{:S(2)}, u32[]{:S(2)}) %collective-permute-start.18) | collective-permute-done | bytes 196640 | tf_op jit(solution)/shard_map/ppermute | solution.py:50
  101.5 1.8 %collective-permute-done.19 = f32[3,64,256]{2,1,0:T(8,128)S(1)} collective-permute-done((f32[3,64,256]{2,1,0:T(8,128)S(1)}, f32[3,64,256]{2,1,0:T(8,128)S(1)}, u32[]{:S(2)}, u32[]{:S(2)}) %collective-permute-start.19) | collective-permute-done | bytes 196640 | tf_op jit(solution)/shard_map/ppermute | solution.py:50
  103.4 3.5 %collective-permute-start.20 = (bf16[3,64,256]{2,1,0:T(8,128)(2,1)S(1)}, bf16[3,64,256]{2,1,0:T(8,128)(2,1)S(1)}, u32[]{:S(2)}, u32[]{:S(2)}) collective-permute-start(bf16[3,64,256]{2,1,0:T(8,128)(2,1)S(1)} %add_convert_fusion.s0), channel_id=1, source_target_pairs={{8,0},{124,4},{16,8},{4,12},{24,16},{12,20},{32,24},{20,28},{40,32... | collective-permute-start | bytes 294920 | tf_op jit(solution)/shard_map/ppermute | solution.py:58
  106.9 3.0 %collective-permute-done.20.s2 = bf16[3,64,256]{2,1,0:T(8,128)(2,1)S(1)} collective-permute-done((bf16[3,64,256]{2,1,0:T(8,128)(2,1)S(1)}, bf16[3,64,256]{2,1,0:T(8,128)(2,1)S(1)}, u32[]{:S(2)}, u32[]{:S(2)}) %collective-permute-start.20) | collective-permute-done | bytes 98336 | tf_op jit(solution)/shard_map/ppermute | solution.py:58
  109.9 2.4 %spread_near.3.given = f32[13,64,256]{2,1,0:T(8,128)S(1)} custom-call(s32[256]{0:T(256)S(1)} %plan.2.list_ref.refs_1_.near_ref, s32[256]{0:T(256)S(1)} %plan.3.list_ref, bf16[40,256,256]{2,1,0:T(8,128)(2,1)S(1)} %get-tuple-element.65.w0, bf16[40,256,256]{2,1,0:T(8,128)(2,1)S(1)} %get-tuple-element.66.w2, bf16[3,64,256]{2,1,0:T(8,128)(2,1)S(1)} %add_convert_fusion.s0, ...), custom_call_target="tpu_custom_call" | custom-call | flops 30000001024 | bytes 1000 | tf_op jit(solution)/shard_map/spread_near/pallas_call | solution.py:253
  112.3 2.5 %collective-permute-done.21.s3 = bf16[3,64,256]{2,1,0:T(8,128)(2,1)S(1)} collective-permute-done((bf16[3,64,256]{2,1,0:T(8,128)(2,1)S(1)}, bf16[3,64,256]{2,1,0:T(8,128)(2,1)S(1)}, u32[]{:S(2)}, u32[]{:S(2)}) %collective-permute-start.21) | collective-permute-done | bytes 98336 | tf_op jit(solution)/shard_map/ppermute | solution.py:58
  114.8 1.3 spread_far.3
  116.1 2.6 %collective-permute-start.24 = (f32[3,64,256]{2,1,0:T(8,128)S(1)}, f32[3,64,256]{2,1,0:T(8,128)S(1)}, u32[]{:S(2)}, u32[]{:S(2)}) collective-permute-start(f32[3,64,256]{2,1,0:T(8,128)S(1)} %spread_far.3), channel_id=1, source_target_pairs={{0,2},{1,3},{2,0},{3,1},{4,6},{5,7},{6,4},{7,5},{8,10},{9,11},{10,... | collective-permute-start | bytes 589832 | tf_op jit(solution)/shard_map/ppermute | solution.py:54
  118.7 2.6 %spread_rest.3 = (f32[3,64,256]{2,1,0:T(8,128)S(1)}, f32[3,64,256]{2,1,0:T(8,128)S(1)}, f32[3,64,256]{2,1,0:T(8,128)S(1)}) custom-call(s32[256]{0:T(256)S(1)} %plan.2.list_ref.refs_1_.near_ref, s32[256]{0:T(256)S(1)} %plan.3.list_ref, bf16[40,256,256]{2,1,0:T(8,128)(2,1)S(1)} %get-tuple-element.50.w1, bf16[40,256,256]{2,1,0:T(8,128)(2,1)S(1)} %get-tuple-element.56.w3, ...), custom_call_target="tpu_custom_call" | custom-call | flops 30000001024 | bytes 1000 | tf_op jit(solution)/shard_map/spread_rest/pallas_call | solution.py:253
  121.4 0.9 collective-permute-start.25
  122.2 1.2 collective-permute-start.26
  123.5 0.6 collective-permute-done.24
  124.1 3.0 %collective-permute-done.25 = f32[3,64,256]{2,1,0:T(8,128)S(1)} collective-permute-done((f32[3,64,256]{2,1,0:T(8,128)S(1)}, f32[3,64,256]{2,1,0:T(8,128)S(1)}, u32[]{:S(2)}, u32[]{:S(2)}) %collective-permute-start.25) | collective-permute-done | bytes 196640 | tf_op jit(solution)/shard_map/ppermute | solution.py:50
  127.1 2.0 %collective-permute-done.26 = f32[3,64,256]{2,1,0:T(8,128)S(1)} collective-permute-done((f32[3,64,256]{2,1,0:T(8,128)S(1)}, f32[3,64,256]{2,1,0:T(8,128)S(1)}, u32[]{:S(2)}, u32[]{:S(2)}) %collective-permute-start.26) | collective-permute-done | bytes 196640 | tf_op jit(solution)/shard_map/ppermute | solution.py:50
  129.1 0.7 add_bitcast_fusion
  (41 shorter events, 2.7 us)
Async XLA Ops:
  0.8 0.9 copy-start
  1.7 1.3 copy-start.2
  3.7 22.0 %collective-permute-start = (bf16[1552,256]{1,0:T(8,128)(2,1)S(1)}, bf16[1552,256]{1,0:T(8,128)(2,1)S(1)}, u32[]{:S(2)}, u32[]{:S(2)}) collective-permute-start(bf16[1552,256]{1,0:T(8,128)(2,1)S(1)} %get-tuple-element.52.r0), channel_id=1, source_target_pairs={{0,1},{1,2},{2,3},{3,0},{4,7},{5,4},{6,5},{7,6},{8,9},{9,10},{10,1... | collective-permute-start | bytes 2383880 | tf_op jit(solution)/shard_map/ppermute | solution.py:50
  5.3 20.3 %collective-permute-start.2 = (bf16[784,256]{1,0:T(8,128)(2,1)S(1)}, bf16[784,256]{1,0:T(8,128)(2,1)S(1)}, u32[]{:S(2)}, u32[]{:S(2)}) collective-permute-start(bf16[784,256]{1,0:T(8,128)(2,1)S(1)} %get-tuple-element.41.r1), channel_id=1, source_target_pairs={{0,1},{1,2},{2,3},{3,0},{4,7},{5,4},{6,5},{7,6},{8,9},{9,10},{10,1... | collective-permute-start | bytes 1204232 | tf_op jit(solution)/shard_map/ppermute | solution.py:50
  6.8 18.8 %collective-permute-start.1 = (bf16[784,256]{1,0:T(8,128)(2,1)S(1)}, bf16[784,256]{1,0:T(8,128)(2,1)S(1)}, u32[]{:S(2)}, u32[]{:S(2)}) collective-permute-start(bf16[784,256]{1,0:T(8,128)(2,1)S(1)} %get-tuple-element.41.r1), channel_id=1, source_target_pairs={{0,3},{1,0},{2,1},{3,2},{4,5},{5,6},{6,7},{7,4},{8,11},{9,8},{10,9... | collective-permute-start | bytes 1204232 | tf_op jit(solution)/shard_map/ppermute | solution.py:50
  8.6 35.2 %collective-permute-start.6 = (bf16[832,768]{1,0:T(8,128)(2,1)S(1)}, bf16[832,768]{1,0:T(8,128)(2,1)S(1)}, u32[]{:S(2)}, u32[]{:S(2)}) collective-permute-start(bf16[832,768]{1,0:T(8,128)(2,1)S(1)} %get-tuple-element.45.c0), channel_id=1, source_target_pairs={{120,0},{12,4},{0,8},{20,12},{8,16},{28,20},{16,24},{36,28},{24,32... | collective-permute-start | bytes 3833864 | tf_op jit(solution)/shard_map/ppermute | solution.py:58
  10.1 31.5 %collective-permute-start.5 = (bf16[832,768]{1,0:T(8,128)(2,1)S(1)}, bf16[832,768]{1,0:T(8,128)(2,1)S(1)}, u32[]{:S(2)}, u32[]{:S(2)}) collective-permute-start(bf16[832,768]{1,0:T(8,128)(2,1)S(1)} %get-tuple-element.45.c0), channel_id=1, source_target_pairs={{8,0},{124,4},{16,8},{4,12},{24,16},{12,20},{32,24},{20,28},{40,32... | collective-permute-start | bytes 3833864 | tf_op jit(solution)/shard_map/ppermute | solution.py:58
  25.7 22.4 %collective-permute-start.3 = (bf16[1552,256]{1,0:T(8,128)(2,1)S(1)}, bf16[1552,256]{1,0:T(8,128)(2,1)S(1)}, u32[]{:S(2)}, u32[]{:S(2)}) collective-permute-start(bf16[1552,256]{1,0:T(8,128)(2,1)S(1)} %collective-permute-done.r2), channel_id=1, source_target_pairs={{0,1},{1,2},{2,3},{3,0},{4,7},{5,4},{6,5},{7,6},{8,9},{9,10},{10,1... | collective-permute-start | bytes 2383880 | tf_op jit(solution)/shard_map/ppermute | solution.py:50
  26.1 24.0 %collective-permute-start.7 = (bf16[1552,256]{1,0:T(8,128)(2,1)S(1)}, bf16[1552,256]{1,0:T(8,128)(2,1)S(1)}, u32[]{:S(2)}, u32[]{:S(2)}) collective-permute-start(bf16[1552,256]{1,0:T(8,128)(2,1)S(1)} %get-tuple-element.52.r0), channel_id=1, source_target_pairs={{0,3},{1,0},{2,1},{3,2},{4,5},{5,6},{6,7},{7,4},{8,11},{9,8},{10,9... | collective-permute-start | bytes 2383880 | tf_op jit(solution)/shard_map/ppermute | solution.py:50
  29.0 3.2 %collective-permute-start.4 = (bf16[832,768]{1,0:T(8,128)(2,1)S(1)}, bf16[832,768]{1,0:T(8,128)(2,1)S(1)}, u32[]{:S(2)}, u32[]{:S(2)}) collective-permute-start(bf16[832,768]{1,0:T(8,128)(2,1)S(1)} %get-tuple-element.45.c0), channel_id=1, source_target_pairs={{0,4},{4,0},{1,5},{5,1},{2,6},{6,2},{3,7},{7,3},{8,12},{12,8},{9,1... | collective-permute-start | bytes 3833864 | tf_op jit(solution)/shard_map/ppermute | solution.py:64
  32.1 18.0 %collective-permute-start.8 = (bf16[784,256]{1,0:T(8,128)(2,1)S(1)}, bf16[784,256]{1,0:T(8,128)(2,1)S(1)}, u32[]{:S(2)}, u32[]{:S(2)}) collective-permute-start(bf16[784,256]{1,0:T(8,128)(2,1)S(1)} %collective-permute-done.1.r3), channel_id=1, source_target_pairs={{0,3},{1,0},{2,1},{3,2},{4,5},{5,6},{6,7},{7,4},{8,11},{9,8},{10,9... | collective-permute-start | bytes 1204232 | tf_op jit(solution)/shard_map/ppermute | solution.py:50
  41.6 16.0 %collective-permute-start.9 = (bf16[832,768]{1,0:T(8,128)(2,1)S(1)}, bf16[832,768]{1,0:T(8,128)(2,1)S(1)}, u32[]{:S(2)}, u32[]{:S(2)}) collective-permute-start(bf16[832,768]{1,0:T(8,128)(2,1)S(1)} %collective-permute-done.5.c2), channel_id=1, source_target_pairs={{0,4},{4,0},{1,5},{5,1},{2,6},{6,2},{3,7},{7,3},{8,12},{12,8},{9,1... | collective-permute-start | bytes 3833864 | tf_op jit(solution)/shard_map/ppermute | solution.py:64
  57.6 18.7 %copy-start.1 = (f32[3,256,64]{1,2,0:T(8,128)S(1)}, f32[3,256,64]{1,2,0:T(8,128)}, u32[]{:S(2)}) copy-start(f32[3,256,64]{1,2,0:T(8,128)} %param.4) | copy-start | bytes 589828
  61.6 8.6 %collective-permute-start.10 = (f32[3,72,256]{2,1,0:T(8,128)S(1)}, f32[3,72,256]{2,1,0:T(8,128)S(1)}, u32[]{:S(2)}, u32[]{:S(2)}) collective-permute-start(f32[3,72,256]{2,1,0:T(8,128)S(1)} %get-tuple-element.62), channel_id=1, source_target_pairs={{0,2},{1,3},{2,0},{3,1},{4,6},{5,7},{6,4},{7,5},{8,10},{9,11},{10,... | collective-permute-start | bytes 663560 | tf_op jit(solution)/shard_map/ppermute | solution.py:54
  64.0 11.8 %collective-permute-start.11 = (f32[3,72,256]{2,1,0:T(8,128)S(1)}, f32[3,72,256]{2,1,0:T(8,128)S(1)}, u32[]{:S(2)}, u32[]{:S(2)}) collective-permute-start(f32[3,72,256]{2,1,0:T(8,128)S(1)} %get-tuple-element.63), channel_id=1, source_target_pairs={{0,3},{1,0},{2,1},{3,2},{4,5},{5,6},{6,7},{7,4},{8,11},{9,8},{10,9... | collective-permute-start | bytes 663560 | tf_op jit(solution)/shard_map/ppermute | solution.py:50
  64.2 11.9 %collective-permute-start.12 = (f32[3,72,256]{2,1,0:T(8,128)S(1)}, f32[3,72,256]{2,1,0:T(8,128)S(1)}, u32[]{:S(2)}, u32[]{:S(2)}) collective-permute-start(f32[3,72,256]{2,1,0:T(8,128)S(1)} %get-tuple-element.64), channel_id=1, source_target_pairs={{0,1},{1,2},{2,3},{3,0},{4,7},{5,4},{6,5},{7,6},{8,9},{9,10},{10,1... | collective-permute-start | bytes 663560 | tf_op jit(solution)/shard_map/ppermute | solution.py:50
  76.3 6.4 %collective-permute-start.13 = (bf16[3,64,256]{2,1,0:T(8,128)(2,1)S(1)}, bf16[3,64,256]{2,1,0:T(8,128)(2,1)S(1)}, u32[]{:S(2)}, u32[]{:S(2)}) collective-permute-start(bf16[3,64,256]{2,1,0:T(8,128)(2,1)S(1)} %fusion.1.s0), channel_id=1, source_target_pairs={{8,0},{124,4},{16,8},{4,12},{24,16},{12,20},{32,24},{20,28},{40,32... | collective-permute-start | bytes 294920 | tf_op jit(solution)/shard_map/ppermute | solution.py:58
  80.5 2.7 %collective-permute-start.16 = (bf16[3,64,256]{2,1,0:T(8,128)(2,1)S(1)}, bf16[3,64,256]{2,1,0:T(8,128)(2,1)S(1)}, u32[]{:S(2)}, u32[]{:S(2)}) collective-permute-start(bf16[3,64,256]{2,1,0:T(8,128)(2,1)S(1)} %fusion.1.s0), channel_id=1, source_target_pairs={{0,4},{4,0},{1,5},{5,1},{2,6},{6,2},{3,7},{7,3},{8,12},{12,8},{9,1... | collective-permute-start | bytes 294920 | tf_op jit(solution)/shard_map/ppermute | solution.py:64
  80.5 7.9 %collective-permute-start.14 = (bf16[3,64,256]{2,1,0:T(8,128)(2,1)S(1)}, bf16[3,64,256]{2,1,0:T(8,128)(2,1)S(1)}, u32[]{:S(2)}, u32[]{:S(2)}) collective-permute-start(bf16[3,64,256]{2,1,0:T(8,128)(2,1)S(1)} %fusion.1.s0), channel_id=1, source_target_pairs={{120,0},{12,4},{0,8},{20,12},{8,16},{28,20},{16,24},{36,28},{24,32... | collective-permute-start | bytes 294920 | tf_op jit(solution)/shard_map/ppermute | solution.py:58
  82.7 5.7 %collective-permute-start.15 = (bf16[3,64,256]{2,1,0:T(8,128)(2,1)S(1)}, bf16[3,64,256]{2,1,0:T(8,128)(2,1)S(1)}, u32[]{:S(2)}, u32[]{:S(2)}) collective-permute-start(bf16[3,64,256]{2,1,0:T(8,128)(2,1)S(1)} %collective-permute-done.13.s2), channel_id=1, source_target_pairs={{0,4},{4,0},{1,5},{5,1},{2,6},{6,2},{3,7},{7,3},{8,12},{12,8},{9,1... | collective-permute-start | bytes 294920 | tf_op jit(solution)/shard_map/ppermute | solution.py:64
  89.7 8.6 %collective-permute-start.17 = (f32[3,64,256]{2,1,0:T(8,128)S(1)}, f32[3,64,256]{2,1,0:T(8,128)S(1)}, u32[]{:S(2)}, u32[]{:S(2)}) collective-permute-start(f32[3,64,256]{2,1,0:T(8,128)S(1)} %spread_far.2), channel_id=1, source_target_pairs={{0,2},{1,3},{2,0},{3,1},{4,6},{5,7},{6,4},{7,5},{8,10},{9,11},{10,... | collective-permute-start | bytes 589832 | tf_op jit(solution)/shard_map/ppermute | solution.py:54
  95.8 5.7 %collective-permute-start.18 = (f32[3,64,256]{2,1,0:T(8,128)S(1)}, f32[3,64,256]{2,1,0:T(8,128)S(1)}, u32[]{:S(2)}, u32[]{:S(2)}) collective-permute-start(f32[3,64,256]{2,1,0:T(8,128)S(1)} %get-tuple-element.69), channel_id=1, source_target_pairs={{0,3},{1,0},{2,1},{3,2},{4,5},{5,6},{6,7},{7,4},{8,11},{9,8},{10,9... | collective-permute-start | bytes 589832 | tf_op jit(solution)/shard_map/ppermute | solution.py:50
  96.5 6.9 %collective-permute-start.19 = (f32[3,64,256]{2,1,0:T(8,128)S(1)}, f32[3,64,256]{2,1,0:T(8,128)S(1)}, u32[]{:S(2)}, u32[]{:S(2)}) collective-permute-start(f32[3,64,256]{2,1,0:T(8,128)S(1)} %get-tuple-element.70), channel_id=1, source_target_pairs={{0,1},{1,2},{2,3},{3,0},{4,7},{5,4},{6,5},{7,6},{8,9},{9,10},{10,1... | collective-permute-start | bytes 589832 | tf_op jit(solution)/shard_map/ppermute | solution.py:50
  103.4 6.5 %collective-permute-start.20 = (bf16[3,64,256]{2,1,0:T(8,128)(2,1)S(1)}, bf16[3,64,256]{2,1,0:T(8,128)(2,1)S(1)}, u32[]{:S(2)}, u32[]{:S(2)}) collective-permute-start(bf16[3,64,256]{2,1,0:T(8,128)(2,1)S(1)} %add_convert_fusion.s0), channel_id=1, source_target_pairs={{8,0},{124,4},{16,8},{4,12},{24,16},{12,20},{32,24},{20,28},{40,32... | collective-permute-start | bytes 294920 | tf_op jit(solution)/shard_map/ppermute | solution.py:58
  106.9 3.0 %collective-permute-start.23 = (bf16[3,64,256]{2,1,0:T(8,128)(2,1)S(1)}, bf16[3,64,256]{2,1,0:T(8,128)(2,1)S(1)}, u32[]{:S(2)}, u32[]{:S(2)}) collective-permute-start(bf16[3,64,256]{2,1,0:T(8,128)(2,1)S(1)} %add_convert_fusion.s0), channel_id=1, source_target_pairs={{0,4},{4,0},{1,5},{5,1},{2,6},{6,2},{3,7},{7,3},{8,12},{12,8},{9,1... | collective-permute-start | bytes 294920 | tf_op jit(solution)/shard_map/ppermute | solution.py:64
  106.9 7.9 %collective-permute-start.21 = (bf16[3,64,256]{2,1,0:T(8,128)(2,1)S(1)}, bf16[3,64,256]{2,1,0:T(8,128)(2,1)S(1)}, u32[]{:S(2)}, u32[]{:S(2)}) collective-permute-start(bf16[3,64,256]{2,1,0:T(8,128)(2,1)S(1)} %add_convert_fusion.s0), channel_id=1, source_target_pairs={{120,0},{12,4},{0,8},{20,12},{8,16},{28,20},{16,24},{36,28},{24,32... | collective-permute-start | bytes 294920 | tf_op jit(solution)/shard_map/ppermute | solution.py:58
  109.9 4.9 %collective-permute-start.22 = (bf16[3,64,256]{2,1,0:T(8,128)(2,1)S(1)}, bf16[3,64,256]{2,1,0:T(8,128)(2,1)S(1)}, u32[]{:S(2)}, u32[]{:S(2)}) collective-permute-start(bf16[3,64,256]{2,1,0:T(8,128)(2,1)S(1)} %collective-permute-done.20.s2), channel_id=1, source_target_pairs={{0,4},{4,0},{1,5},{5,1},{2,6},{6,2},{3,7},{7,3},{8,12},{12,8},{9,1... | collective-permute-start | bytes 294920 | tf_op jit(solution)/shard_map/ppermute | solution.py:64
  116.1 8.0 %collective-permute-start.24 = (f32[3,64,256]{2,1,0:T(8,128)S(1)}, f32[3,64,256]{2,1,0:T(8,128)S(1)}, u32[]{:S(2)}, u32[]{:S(2)}) collective-permute-start(f32[3,64,256]{2,1,0:T(8,128)S(1)} %spread_far.3), channel_id=1, source_target_pairs={{0,2},{1,3},{2,0},{3,1},{4,6},{5,7},{6,4},{7,5},{8,10},{9,11},{10,... | collective-permute-start | bytes 589832 | tf_op jit(solution)/shard_map/ppermute | solution.py:54
  121.4 5.7 %collective-permute-start.25 = (f32[3,64,256]{2,1,0:T(8,128)S(1)}, f32[3,64,256]{2,1,0:T(8,128)S(1)}, u32[]{:S(2)}, u32[]{:S(2)}) collective-permute-start(f32[3,64,256]{2,1,0:T(8,128)S(1)} %get-tuple-element.73), channel_id=1, source_target_pairs={{0,3},{1,0},{2,1},{3,2},{4,5},{5,6},{6,7},{7,4},{8,11},{9,8},{10,9... | collective-permute-start | bytes 589832 | tf_op jit(solution)/shard_map/ppermute | solution.py:50
  122.2 6.9 %collective-permute-start.26 = (f32[3,64,256]{2,1,0:T(8,128)S(1)}, f32[3,64,256]{2,1,0:T(8,128)S(1)}, u32[]{:S(2)}, u32[]{:S(2)}) collective-permute-start(f32[3,64,256]{2,1,0:T(8,128)S(1)} %get-tuple-element.74), channel_id=1, source_target_pairs={{0,1},{1,2},{2,3},{3,0},{4,7},{5,4},{6,5},{7,6},{8,9},{9,10},{10,1... | collective-permute-start | bytes 589832 | tf_op jit(solution)/shard_map/ppermute | solution.py:50

commit v5 on v4

--- a/solution.py
+++ b/solution.py
@@ -26,11 +26,10 @@
 F32 = jnp.float32
 BF16 = jnp.bfloat16
 FIRST = (0, 48, 96, 144, 192)
-CAP = 40
+CAPS = (44, 44, 36, 36, 40)
 BASE = (0, 6, 0, 6, 12)
 CHUNKS = 5
-SOON = (0, 1, 2, 3, 4, 8)
-COUNTS = 240
+SOON = (0, 1, 2, 3, 4, 5, 8)
 TOTALS = 245
 BEFORE = 250
 LISTS = 256
@@ -64,35 +63,65 @@
     return lax.ppermute(v, "c", [(0, 1), (1, 0)])
 
 
-def prep_kernel(emb_ref, seed_ref, ids_ref, two_ref, one_ref, full_ref):
+def prep_kernel(emb_hbm, seed_hbm, ids_ref, two_ref, full_ref, emb_buf, seed_buf, sems):
+    copies = [pltpu.make_async_copy(emb_hbm.at[b], emb_buf.at[b], sems.at[b]) for b in range(BLK)]
+    copies.append(pltpu.make_async_copy(seed_hbm, seed_buf, sems.at[BLK]))
+    for copy in copies:
+        copy.start()
     for block in range(BLK):
-        values = emb_ref[block].astype(F32)
+        copies[block].wait()
+        values = emb_buf[block].astype(F32)
         total = jnp.sum(values * values, axis=-1, keepdims=True)
         unit = (values * lax.rsqrt(total + EPS)).astype(BF16)
         full_ref[block * ROWS : (block + 1) * ROWS] = unit
-        full_ref[BLK * ROWS :, block * ROWS : (block + 1) * ROWS] = seed_ref[block].astype(BF16)
         if block < 2:
             two_ref[block * D : (block + 1) * D] = jnp.transpose(unit)
-        else:
-            one_ref[:D] = jnp.transpose(unit)
     two_ref[2 * D :] = ids_ref[...]
-    one_ref[D:] = ids_ref[...]
+    copies[BLK].wait()
+    for block in range(BLK):
+        full_ref[BLK * ROWS :, block * ROWS : (block + 1) * ROWS] = seed_buf[block].astype(BF16)
 
 
 def prepare(embeddings, seeds_t, ids):
+    far = pl.BlockSpec(memory_space=pltpu.HBM)
     return pl.pallas_call(
         prep_kernel,
         out_shape=(
             jax.ShapeDtypeStruct((2 * D + IDS, ROWS), BF16),
-            jax.ShapeDtypeStruct((D + IDS, ROWS), BF16),
             jax.ShapeDtypeStruct((BLK * ROWS + CH, D), BF16),
         ),
-        in_specs=[VM, VM, VM],
-        out_specs=(VM, VM, VM),
+        in_specs=[far, far, VM],
+        out_specs=(VM, VM),
+        scratch_shapes=[
+            pltpu.VMEM((BLK, ROWS, D), BF16),
+            pltpu.VMEM((BLK, CH, ROWS), F32),
+            pltpu.SemaphoreType.DMA((BLK + 1,)),
+        ],
         compiler_params=pltpu.CompilerParams(vmem_limit_bytes=8 << 20),
         cost_estimate=CHEAP,
         name="prep",
-    )(embeddings, seeds_t, ids)
+    )(
+        pltpu.with_memory_space_constraint(embeddings, pltpu.HBM),
+        pltpu.with_memory_space_constraint(seeds_t, pltpu.HBM),
+        ids,
+    )
+
+
+def third_kernel(full_ref, ids_ref, one_ref):
+    one_ref[:D] = jnp.transpose(full_ref[2 * ROWS : BLK * ROWS])
+    one_ref[D:] = ids_ref[...]
+
+
+def third_turned(full, ids):
+    return pl.pallas_call(
+        third_kernel,
+        out_shape=jax.ShapeDtypeStruct((D + IDS, ROWS), BF16),
+        in_specs=[VM, VM],
+        out_specs=VM,
+        compiler_params=pltpu.CompilerParams(vmem_limit_bytes=2 << 20),
+        cost_estimate=LONG,
+        name="third",
+    )(full, ids)
 
 
 def split_ids(neighbours):
@@ -156,7 +185,6 @@
     for c in range(CHUNKS):
         for pad in range(4):
             list_ref[FIRST[c] + counts[c] + pad] = SPARE * 16 + BASE[c]
-        list_ref[COUNTS + c] = (counts[c] + 3) >> 2
         list_ref[TOTALS + c] = counts[c]
 
 
@@ -173,14 +201,25 @@
     )(*operands)
 
 
-def tiles(chunk, list_ref, row_ref, col_ref, state_ref, w_ref, sum_ref, base=0):
-    steps = list_ref[COUNTS + chunk]
+def tiles(chunk, list_ref, row_ref, col_ref, state_ref, w_ref, sum_ref, low=0, high=None, base=0):
+    high = list_ref[TOTALS + chunk] if high is None else high
+    steps = (high - low + 3) >> 2
+
+    def spread_four(step, live):
+        for k in range(4):
+            n = low + 4 * step + k
+            named = list_ref[FIRST[chunk] + n]
+            row = jnp.where(live & (n < high), named >> 4, SPARE)
+            sum_ref[row, :CH] += jnp.dot(
+                state_ref[(named & 15) - base], w_ref[n], preferred_element_type=F32
+            )
 
     def four_tiles(step, _):
+        spread_four(jnp.maximum(step - 1, 0), step > 0)
         for k in range(4):
-            n = 4 * step + k
+            n = low + 4 * step + k
             named = list_ref[FIRST[chunk] + n]
-            row, col = named >> 4, (named & 15) - base
+            row, col = jnp.where(n < high, named >> 4, SPARE), (named & 15) - base
             place = jnp.where(row == SPARE, 0, row) * D
             cosine = jnp.dot(
                 col_ref[pl.ds(pl.multiple_of(col * ROWS, ROWS), ROWS), :],
@@ -192,17 +231,8 @@
             sum_ref[row, CH:] += jnp.sum(weight.reshape(ROWS // 8, 8, ROWS), axis=0)
         return 0
 
-    def four_spreads(step, _):
-        for k in range(4):
-            n = 4 * step + k
-            named = list_ref[FIRST[chunk] + n]
-            sum_ref[named >> 4, :CH] += jnp.dot(
-                state_ref[(named & 15) - base], w_ref[n], preferred_element_type=F32
-            )
-        return 0
-
     lax.fori_loop(0, steps, four_tiles, 0)
-    lax.fori_loop(0, steps, four_spreads, 0)
+    spread_four(jnp.maximum(steps - 1, 0), steps > 0)
 
 
 def put_rows(buf, refs, places):
@@ -217,8 +247,8 @@
             states[at * BLK + j] = ref[BLK * ROWS :, j * ROWS : (j + 1) * ROWS]
 
 
-def build_0(list_ref, r0, r1, r2, r3, c0, c1, w_ref, sum_ref, rows, cols, states):
-    put_rows(rows, (r0, r1, r2, r3), ((0, 2), (2, 1), (3, 2), (8, 1)))
+def build_0(list_ref, r0, r1, r2, r3, r4, c0, c1, w_ref, sum_ref, rows, cols, states):
+    put_rows(rows, (r0, r1, r2, r3, r4), ((0, 2), (2, 1), (3, 2), (5, 1), (8, 1)))
     put_cols(cols, states, (c0, c1))
     sum_ref[...] = jnp.zeros_like(sum_ref)
     tiles(0, list_ref, rows, cols, states, w_ref, sum_ref)
@@ -230,26 +260,37 @@
     tiles(1, list_ref, rows, cols, states, w_ref, sum_ref)
 
 
-def build_2(list_ref, old_rows, r0, r1, r2, r3, cols, states, given, w2_ref, w3_ref, sum_ref, rows):
-    rows[: 5 * D] = old_rows[: 5 * D]
+def build_2(list_ref, old_rows, r0, r1, r2, cols, states, given, w2_ref, w3_ref, sum_ref, rows):
+    rows[: 6 * D] = old_rows[: 6 * D]
     rows[8 * D : 9 * D] = old_rows[8 * D :]
-    put_rows(rows, (r0, r1, r2, r3), ((5, 1), (6, 2), (9, 2), (11, 1)))
+    put_rows(rows, (r0, r1, r2), ((6, 2), (9, 2), (11, 1)))
     sum_ref[...] = given[...]
     tiles(2, list_ref, rows, cols, states, w2_ref, sum_ref)
     tiles(3, list_ref, rows, cols, states, w3_ref, sum_ref)
 
 
-def build_3(list_ref, rows, c4, given, w_ref, *refs):
-    outs, (sums, states) = refs[:NX], refs[NX:]
+def last_columns(list_ref, rows, c4, given, w_ref, outs, sums, states, first, low, high):
     sums[...] = given[...]
     for j in range(BLK):
         states[j] = c4[BLK * ROWS :, j * ROWS : (j + 1) * ROWS]
-    tiles(4, list_ref, rows, c4, states, w_ref, sums, base=BASE[4])
+    tiles(4, list_ref, rows, c4, states, w_ref, sums, low, high, BASE[4])
     for at, ref in enumerate(outs):
-        ref[...] = sums[at * BLK : (at + 1) * BLK]
-
-
-def build(kernel, room, outs, scratch, *operands):
+        ref[...] = sums[(first + at) * BLK : (first + at + 1) * BLK]
+
+
+def build_far(list_ref, rows, c4, given, w_ref, far, sums, states):
+    last_columns(
+        list_ref, rows, c4, given, w_ref, (far,), sums, states, 3, list_ref[BEFORE + 4], list_ref[TOTALS + 4]
+    )
+
+
+def build_rest(list_ref, rows, c4, given, w_ref, own, back, fore, sums, states):
+    last_columns(
+        list_ref, rows, c4, given, w_ref, (own, back, fore), sums, states, 0, 0, list_ref[BEFORE + 4]
+    )
+
+
+def build(kernel, room, outs, scratch, *operands, cost=None):
     return pl.pallas_call(
         kernel,
         out_shape=[jax.ShapeDtypeStruct(*o) for o in outs],
@@ -257,12 +298,13 @@
         out_specs=[VM] * len(outs),
         scratch_shapes=[pltpu.VMEM(*s) for s in scratch],
         compiler_params=pltpu.CompilerParams(vmem_limit_bytes=room << 20),
-        cost_estimate=LONG,
+        cost_estimate=cost or LONG,
         name=kernel.__name__,
     )(*operands)
 
 
-WEIGHTS = ((CAP, ROWS, ROWS), BF16)
+def weights_of(chunk):
+    return ((CAPS[chunk], ROWS, ROWS), BF16)
 
 
 def rows_of(n):
@@ -320,9 +362,9 @@
     sums = ((SPARE + 1, CH, ROWS), F32)
     held = ((5 * BLK, CH, ROWS), BF16)
     part = ((BLK, CH, ROWS), F32)
-    w0, w1, w2, w3, w4 = weights
+    w0, w1, w2, w3, w4_far, w4 = weights
     (near,) = build(spread_near, 3, [sums], [held], *lists, w0, w2, *states[:2])
-    (far,) = build(spread_far, 4, [part], [sums, held], lists[1], w3, w4, *states[2:], near)
+    (far,) = build(spread_far, 4, [part], [sums, held], lists[1], w3, w4_far, *states[2:], near)
     near, _ = lax.optimization_barrier((near, far))
     return *build(
         spread_rest, 4, [part] * (NX - 1), [sums, held], *lists, w1, w3, w4, *states[2:], near
@@ -346,11 +388,13 @@
     code = functools.partial(coded, wide=lax.axis_index(WIDE), x=lax.axis_index("x"))
     seeds_t = jnp.swapaxes(seeds, 1, 2)
     after = lambda v, *done: lax.optimization_barrier((v, *done))[0]
-    two, one, full = prepare(embeddings, seeds_t, split_ids(neighbours))
+    ids = split_ids(neighbours)
+    two, full = prepare(embeddings, seeds_t, ids)
+    one = third_turned(full, ids)
     back_two = along_x(two, 1)
-    fore_one = along_x(one, -1)
     above = from_wide(full, 1)
     below = from_wide(full, -1)
+    fore_one = along_x(one, -1)
     back_one = along_x(one, 1)
     back_two, fore_one, back_one, late_full, late_two = lax.optimization_barrier(
         (back_two, fore_one, back_one, full, two)
@@ -364,24 +408,28 @@
         (0, 1, 2), [code(neighbours), code(joined_ids(back_two)), code(joined_ids(fore_one))]
     )
     w0, sums, rows = build(
-        build_0, 6, [WEIGHTS, SUM_BUF, rows_of(9)], columns(2),
-        near, two, one, back_two, fore_one, full, partner,
+        build_0, 6, [weights_of(0), SUM_BUF, rows_of(9)], columns(2),
+        near, two, one, back_two, back_one, fore_one, full, partner,
     )
     beside = swap_core(after(above, sums))
     w1, sums, cols, states = build(
-        build_1, 4, [WEIGHTS, SUM_BUF, *columns(4)], [], near, rows, full, partner, above, below, sums
+        build_1, 4, [weights_of(1), SUM_BUF, *columns(4)], [],
+        near, rows, full, partner, above, below, sums,
     )
     lists = make_plan((3,), [code(joined_ids(after(far_two, sums)))], near)
     w2, w3, sums, rows = build(
-        build_2, 4, [WEIGHTS, WEIGHTS, SUM_BUF, rows_of(12)], [],
-        lists, rows, back_one, fore_two, far_two, far_one, cols, states, sums,
-    )
-    w4, own, back, fore, far = build(
-        build_3, 4, [WEIGHTS] + [((BLK, SUMS, ROWS), F32)] * NX, [SUM_BUF, ((BLK, CH, ROWS), BF16)],
-        lists, rows, beside, sums,
+        build_2, 4, [weights_of(2), weights_of(3), SUM_BUF, rows_of(12)], [],
+        lists, rows, fore_two, far_two, far_one, cols, states, sums,
+    )
+    part = ((BLK, SUMS, ROWS), F32)
+    scratch = [SUM_BUF, ((BLK, CH, ROWS), BF16)]
+    w4_far, far = build(build_far, 4, [weights_of(4), part], scratch, lists, rows, beside, sums)
+    w4, own, back, fore = build(
+        build_rest, 4, [weights_of(4)] + [part] * (NX - 1), scratch,
+        lists, rows, beside, after(sums, far),
     )
     lists = [near, lists]
-    weights = [w0, w1, w2, w3, w4]
+    weights = [w0, w1, w2, w3, w4_far, w4]
 
     total = reduce_rows(own, back, fore, far)
     scale = ALPHA / jnp.sum(total[:, CH:], axis=1, keepdims=True)

time: 131 us -> 127 us (0.969); the launches traced: 130 us -> 127 us
  waiting for transfers between devices: 46.2 us -> 42.8 us
  starting transfers between devices: 41 us -> 43.3 us
  local copies, waits for them, and re-layouts: 2.2 us -> 0.01 us
    ppermute x6, starting transfers between devices: 14.1 us -> 18 us  [from_wide(): lax.ppermute(v, WIDE, [((i + (2 * sign if i % 2 == 0 else -2 * sign)) % N...]
    ppermute x12, waiting for transfers between devices: 26.6 us -> 23 us  [along_x(): return lax.ppermute(v, ('c', 'x'), pairs)]
    unnamed x6 -> x2, local copies, waits for them, and re-layouts: 2.2 us -> 0.01 us
    pallas_call x10 -> x11, Pallas kernels: 32.4 us -> 32 us  [build(): pl.pallas_call(kernel, out_shape=[jax.ShapeDtypeStruct(*o) for o in outs]...]
  transfers between devices with their start and end apart: 27 -> 27, of which waited for: 15 -> 15; matrix products, arithmetic and copies ran while one was open for 0% -> 0% of each run, Pallas kernels for 24% -> 26%
where the time goes in v5:
time: 127 us
  starting transfers between devices  43.3 us (34%)
  waiting for transfers between devices  42.8 us (34%)
  Pallas kernels  38.9 us (31%)
  other arithmetic  1.99 us (2%)
    pallas_call x11, Pallas kernels, build(): pl.pallas_call(kernel, out_shape=[jax.ShapeDtypeStruct(*o) for o in outs]...  32 us
    ppermute x12, waiting for transfers between devices, along_x(): return lax.ppermute(v, ('c', 'x'), pairs)  23 us
    ppermute x6, starting transfers between devices, from_wide(): lax.ppermute(v, WIDE, [((i + (2 * sign if i % 2 == 0 else -2 * sign)) % N...  18 us
    ppermute x12, starting transfers between devices, along_x(): return lax.ppermute(v, ('c', 'x'), pairs)  15.9 us
    ppermute x6, waiting for transfers between devices, from_wide(): lax.ppermute(v, WIDE, [((i + (2 * sign if i % 2 == 0 else -2 * sign)) % N...  15.2 us
    ppermute x3, starting transfers between devices, across_x(): return lax.ppermute(v, 'x', [(x, (x + 2) % NX) for x in range(NX)])  7.22 us
    pallas_call x2, Pallas kernels, make_plan(): pl.pallas_call(functools.partial(plan_kernel, groups), out_shape=jax.Shap...  4.99 us
    ppermute x3, waiting for transfers between devices, across_x(): return lax.ppermute(v, 'x', [(x, (x + 2) % NX) for x in range(NX)])  4.61 us
  transfers between devices with their start and end apart: 27, of which 15 were waited for; matrix products, arithmetic and copies ran while one was open for 0% of the time, Pallas kernels for 26%

profile of v5, /device:TPU:0, one launch (start us, length us, event | category | flops | bytes accessed | tf_op | source)
XLA Modules:
  0.0 127.2 jit_solution(14270199175772712989)
XLA Ops:
  0.0 0.7 shift-right-arithmetic_convert_fusion
  0.8 1.7 %prep.1 = (bf16[1552,256]{1,0:T(8,128)(2,1)S(1)}, bf16[832,768]{1,0:T(8,128)(2,1)S(1)}) custom-call(bf16[3,256,768]{2,1,0:T(8,128)(2,1)} %emb_hbm.1, f32[3,64,256]{2,1,0:T(8,128)} %bitcast.6, bf16[16,256]{1,0:T(8,128)(2,1)S(1)} %fusion.7.ids_ref), custom_call_target="tpu_custom_call" | custom-call | flops 1000 | bytes 1000 | tf_op jit(solution)/shard_map/prep/pallas_call | solution.py:87
  2.5 1.6 %collective-permute-start = (bf16[1552,256]{1,0:T(8,128)(2,1)S(1)}, bf16[1552,256]{1,0:T(8,128)(2,1)S(1)}, u32[]{:S(2)}, u32[]{:S(2)}) collective-permute-start(bf16[1552,256]{1,0:T(8,128)(2,1)S(1)} %get-tuple-element.52.r0), channel_id=1, source_target_pairs={{0,1},{1,2},{2,3},{3,0},{4,7},{5,4},{6,5},{7,6},{8,9},{9,10},{10,1... | collective-permute-start | bytes 2383880 | tf_op jit(solution)/shard_map/ppermute | solution.py:49
  4.3 1.6 %collective-permute-start.2 = (bf16[784,256]{1,0:T(8,128)(2,1)S(1)}, bf16[784,256]{1,0:T(8,128)(2,1)S(1)}, u32[]{:S(2)}, u32[]{:S(2)}) collective-permute-start(bf16[784,256]{1,0:T(8,128)(2,1)S(1)} %third.1.r1), channel_id=1, source_target_pairs={{0,1},{1,2},{2,3},{3,0},{4,7},{5,4},{6,5},{7,6},{8,9},{9,10},{10,1... | collective-permute-start | bytes 1204232 | tf_op jit(solution)/shard_map/ppermute | solution.py:49
  5.9 1.7 %collective-permute-start.1 = (bf16[784,256]{1,0:T(8,128)(2,1)S(1)}, bf16[784,256]{1,0:T(8,128)(2,1)S(1)}, u32[]{:S(2)}, u32[]{:S(2)}) collective-permute-start(bf16[784,256]{1,0:T(8,128)(2,1)S(1)} %third.1.r1), channel_id=1, source_target_pairs={{0,3},{1,0},{2,1},{3,2},{4,5},{5,6},{6,7},{7,4},{8,11},{9,8},{10,9... | collective-permute-start | bytes 1204232 | tf_op jit(solution)/shard_map/ppermute | solution.py:49
  7.6 1.6 %collective-permute-start.6 = (bf16[832,768]{1,0:T(8,128)(2,1)S(1)}, bf16[832,768]{1,0:T(8,128)(2,1)S(1)}, u32[]{:S(2)}, u32[]{:S(2)}) collective-permute-start(bf16[832,768]{1,0:T(8,128)(2,1)S(1)} %get-tuple-element.46.full_ref.c0), channel_id=1, source_target_pairs={{120,0},{12,4},{0,8},{20,12},{8,16},{28,20},{16,24},{36,28},{24,32... | collective-permute-start | bytes 3833864 | tf_op jit(solution)/shard_map/ppermute | solution.py:57
  9.2 4.9 %collective-permute-start.5 = (bf16[832,768]{1,0:T(8,128)(2,1)S(1)}, bf16[832,768]{1,0:T(8,128)(2,1)S(1)}, u32[]{:S(2)}, u32[]{:S(2)}) collective-permute-start(bf16[832,768]{1,0:T(8,128)(2,1)S(1)} %get-tuple-element.46.full_ref.c0), channel_id=1, source_target_pairs={{8,0},{124,4},{16,8},{4,12},{24,16},{12,20},{32,24},{20,28},{40,32... | collective-permute-start | bytes 3833864 | tf_op jit(solution)/shard_map/ppermute | solution.py:57
  14.1 10.4 %collective-permute-done.2.r3 = bf16[784,256]{1,0:T(8,128)(2,1)S(1)} collective-permute-done((bf16[784,256]{1,0:T(8,128)(2,1)S(1)}, bf16[784,256]{1,0:T(8,128)(2,1)S(1)}, u32[]{:S(2)}, u32[]{:S(2)}) %collective-permute-start.2) | collective-permute-done | bytes 401440 | tf_op jit(solution)/shard_map/ppermute | solution.py:49
  24.9 2.9 %collective-permute-start.7 = (bf16[1552,256]{1,0:T(8,128)(2,1)S(1)}, bf16[1552,256]{1,0:T(8,128)(2,1)S(1)}, u32[]{:S(2)}, u32[]{:S(2)}) collective-permute-start(bf16[1552,256]{1,0:T(8,128)(2,1)S(1)} %get-tuple-element.52.r0), channel_id=1, source_target_pairs={{0,3},{1,0},{2,1},{3,2},{4,5},{5,6},{6,7},{7,4},{8,11},{9,8},{10,9... | collective-permute-start | bytes 2383880 | tf_op jit(solution)/shard_map/ppermute | solution.py:49
  27.9 3.0 %plan.2.list_ref.refs_1_.near_ref = s32[256]{0:T(256)S(1)} custom-call(s32[3,32]{1,0:T(4,128)S(1)} %get-tuple-element.79.refs_0_, s32[3,32]{1,0:T(4,128)S(1)} %get-tuple-element.80.refs_1_, s32[3,32]{1,0:T(4,128)S(1)} %get-tuple-element.81.refs_2_), custom_call_target="tpu_custom_call" | custom-call | flops 30000001024 | bytes 1000 | tf_op jit(solution)/shard_map/plan/pallas_call | solution.py:193
  31.0 1.3 %collective-permute-start.8 = (bf16[784,256]{1,0:T(8,128)(2,1)S(1)}, bf16[784,256]{1,0:T(8,128)(2,1)S(1)}, u32[]{:S(2)}, u32[]{:S(2)}) collective-permute-start(bf16[784,256]{1,0:T(8,128)(2,1)S(1)} %collective-permute-done.1.r4), channel_id=1, source_target_pairs={{0,3},{1,0},{2,1},{3,2},{4,5},{5,6},{6,7},{7,4},{8,11},{9,8},{10,9... | collective-permute-start | bytes 1204232 | tf_op jit(solution)/shard_map/ppermute | solution.py:49
  32.3 4.7 %build_0.1 = (bf16[44,256,256]{2,1,0:T(8,128)(2,1)S(1)}, f32[13,72,256]{2,1,0:T(8,128)S(1)}, bf16[6912,256]{1,0:T(8,128)(2,1)S(1)}) custom-call(s32[256]{0:T(256)S(1)} %plan.2.list_ref.refs_1_.near_ref, bf16[1552,256]{1,0:T(8,128)(2,1)S(1)} %get-tuple-element.52.r0, bf16[784,256]{1,0:T(8,128)(2,1)S(1)} %third.1.r1, ...), custom_call_target="tpu_custom_call" | custom-call | flops 30000001024 | bytes 1000 | tf_op jit(solution)/shard_map/build_0/pallas_call | solution.py:294
  37.0 3.7 %collective-permute-done.5.c2 = bf16[832,768]{1,0:T(8,128)(2,1)S(1)} collective-permute-done((bf16[832,768]{1,0:T(8,128)(2,1)S(1)}, bf16[832,768]{1,0:T(8,128)(2,1)S(1)}, u32[]{:S(2)}, u32[]{:S(2)}) %collective-permute-start.5) | collective-permute-done | bytes 1277984 | tf_op jit(solution)/shard_map/ppermute | solution.py:57
  40.7 2.2 %collective-permute-start.9 = (bf16[832,768]{1,0:T(8,128)(2,1)S(1)}, bf16[832,768]{1,0:T(8,128)(2,1)S(1)}, u32[]{:S(2)}, u32[]{:S(2)}) collective-permute-start(bf16[832,768]{1,0:T(8,128)(2,1)S(1)} %collective-permute-done.5.c2), channel_id=1, source_target_pairs={{0,4},{4,0},{1,5},{5,1},{2,6},{6,2},{3,7},{7,3},{8,12},{12,8},{9,1... | collective-permute-start | bytes 3833864 | tf_op jit(solution)/shard_map/ppermute | solution.py:63
  42.9 4.0 %build_1.1 = (bf16[44,256,256]{2,1,0:T(8,128)(2,1)S(1)}, f32[13,72,256]{2,1,0:T(8,128)S(1)}, bf16[3072,768]{1,0:T(8,128)(2,1)S(1)}, bf16[12,64,256]{2,1,0:T(8,128)(2,1)S(1)}) custom-call(s32[256]{0:T(256)S(1)} %plan.2.list_ref.refs_1_.near_ref, bf16[6912,256]{1,0:T(8,128)(2,1)S(1)} %get-tuple-element.47.rows.old_rows, ...), custom_call_target="tpu_custom_call" | custom-call | flops 30000001024 | bytes 1000 | tf_op jit(solution)/shard_map/build_1/pallas_call | solution.py:294
  47.0 2.0 %plan.3.list_ref = s32[256]{0:T(256)S(1)} custom-call(s32[3,32]{1,0:T(4,128)S(1)} %fusion.35.refs_0_, s32[256]{0:T(256)S(1)} %plan.2.list_ref.refs_1_.near_ref), custom_call_target="tpu_custom_call" | custom-call | flops 30000001024 | bytes 1000 | tf_op jit(solution)/shard_map/plan/pallas_call | solution.py:193
  49.0 5.5 %build_2.1 = (bf16[36,256,256]{2,1,0:T(8,128)(2,1)S(1)}, bf16[36,256,256]{2,1,0:T(8,128)(2,1)S(1)}, f32[13,72,256]{2,1,0:T(8,128)S(1)}, bf16[9216,256]{1,0:T(8,128)(2,1)S(1)}) custom-call(s32[256]{0:T(256)S(1)} %plan.3.list_ref, bf16[6912,256]{1,0:T(8,128)(2,1)S(1)} %get-tuple-element.47.rows.old_rows, bf16[1552,256]{1,0:T(8,128)(2,1)S(1)} %collective-permute-done.7.r0, ...), custom_call_target="tpu_custom_call" | custom-call | flops 30000001024 | bytes 1000 | tf_op jit(solution)/shard_map/build_2/pallas_call | solution.py:294
  54.5 1.5 %build_far.1 = (bf16[40,256,256]{2,1,0:T(8,128)(2,1)S(1)}, f32[3,72,256]{2,1,0:T(8,128)S(1)}) custom-call(s32[256]{0:T(256)S(1)} %plan.3.list_ref, bf16[9216,256]{1,0:T(8,128)(2,1)S(1)} %get-tuple-element.57.rows, bf16[832,768]{1,0:T(8,128)(2,1)S(1)} %collective-permute-done.9.c4, f32[13,72,256]{2,1,0:T(8,128)S(1)} %get-tuple-element.61.given), custom_call_target="tpu_custom_call" | custom-call | flops 30000001024 | bytes 1000 | tf_op jit(solution)/shard_map/build_far/pallas_call | solution.py:294
  56.1 3.0 %collective-permute-start.10 = (f32[3,72,256]{2,1,0:T(8,128)S(1)}, f32[3,72,256]{2,1,0:T(8,128)S(1)}, u32[]{:S(2)}, u32[]{:S(2)}) collective-permute-start(f32[3,72,256]{2,1,0:T(8,128)S(1)} %get-tuple-element.60), channel_id=1, source_target_pairs={{0,2},{1,3},{2,0},{3,1},{4,6},{5,7},{6,4},{7,5},{8,10},{9,11},{10,... | collective-permute-start | bytes 663560 | tf_op jit(solution)/shard_map/ppermute | solution.py:53
  59.1 3.7 %build_rest.1 = (bf16[40,256,256]{2,1,0:T(8,128)(2,1)S(1)}, f32[3,72,256]{2,1,0:T(8,128)S(1)}, f32[3,72,256]{2,1,0:T(8,128)S(1)}, f32[3,72,256]{2,1,0:T(8,128)S(1)}) custom-call(s32[256]{0:T(256)S(1)} %plan.3.list_ref, bf16[9216,256]{1,0:T(8,128)(2,1)S(1)} %get-tuple-element.57.rows, bf16[832,768]{1,0:T(8,128)(2,1)S(1)} %collective-permute-done.9.c4, ...), custom_call_target="tpu_custom_call" | custom-call | flops 30000001024 | bytes 1000 | tf_op jit(solution)/shard_map/build_rest/pallas_call | solution.py:294
  62.7 1.1 collective-permute-start.11
  63.9 1.0 collective-permute-start.12
  64.8 0.7 collective-permute-done.10
  65.5 5.0 %collective-permute-done.11 = f32[3,72,256]{2,1,0:T(8,128)S(1)} collective-permute-done((f32[3,72,256]{2,1,0:T(8,128)S(1)}, f32[3,72,256]{2,1,0:T(8,128)S(1)}, u32[]{:S(2)}, u32[]{:S(2)}) %collective-permute-start.11) | collective-permute-done | bytes 221216 | tf_op jit(solution)/shard_map/ppermute | solution.py:49
  71.1 7.2 %collective-permute-start.13 = (bf16[3,64,256]{2,1,0:T(8,128)(2,1)S(1)}, bf16[3,64,256]{2,1,0:T(8,128)(2,1)S(1)}, u32[]{:S(2)}, u32[]{:S(2)}) collective-permute-start(bf16[3,64,256]{2,1,0:T(8,128)(2,1)S(1)} %fusion.1.s0), channel_id=1, source_target_pairs={{8,0},{124,4},{16,8},{4,12},{24,16},{12,20},{32,24},{20,28},{40,32... | collective-permute-start | bytes 294920 | tf_op jit(solution)/shard_map/ppermute | solution.py:57
  78.3 3.0 %collective-permute-done.13.s2 = bf16[3,64,256]{2,1,0:T(8,128)(2,1)S(1)} collective-permute-done((bf16[3,64,256]{2,1,0:T(8,128)(2,1)S(1)}, bf16[3,64,256]{2,1,0:T(8,128)(2,1)S(1)}, u32[]{:S(2)}, u32[]{:S(2)}) %collective-permute-start.13) | collective-permute-done | bytes 98336 | tf_op jit(solution)/shard_map/ppermute | solution.py:57
  81.3 2.2 %spread_near.2.given = f32[13,64,256]{2,1,0:T(8,128)S(1)} custom-call(s32[256]{0:T(256)S(1)} %plan.2.list_ref.refs_1_.near_ref, s32[256]{0:T(256)S(1)} %plan.3.list_ref, bf16[44,256,256]{2,1,0:T(8,128)(2,1)S(1)} %get-tuple-element.66.w0, bf16[36,256,256]{2,1,0:T(8,128)(2,1)S(1)} %get-tuple-element.67.w2, bf16[3,64,256]{2,1,0:T(8,128)(2,1)S(1)} %fusion.1.s0, ...), custom_call_target="tpu_custom_call" | custom-call | flops 30000001024 | bytes 1000 | tf_op jit(solution)/shard_map/spread_near/pallas_call | solution.py:294
  83.5 2.7 %collective-permute-done.14.s3 = bf16[3,64,256]{2,1,0:T(8,128)(2,1)S(1)} collective-permute-done((bf16[3,64,256]{2,1,0:T(8,128)(2,1)S(1)}, bf16[3,64,256]{2,1,0:T(8,128)(2,1)S(1)}, u32[]{:S(2)}, u32[]{:S(2)}) %collective-permute-start.14) | collective-permute-done | bytes 98336 | tf_op jit(solution)/shard_map/ppermute | solution.py:57
  86.3 1.3 %spread_far.2 = f32[3,64,256]{2,1,0:T(8,128)S(1)} custom-call(s32[256]{0:T(256)S(1)} %plan.3.list_ref, bf16[36,256,256]{2,1,0:T(8,128)(2,1)S(1)} %get-tuple-element.56.w3, bf16[40,256,256]{2,1,0:T(8,128)(2,1)S(1)} %get-tuple-element.68.w4, bf16[3,64,256]{2,1,0:T(8,128)(2,1)S(1)} %collective-permute-done.13.s2, ...), custom_call_target="tpu_custom_call" | custom-call | flops 30000001024 | bytes 1000 | tf_op jit(solution)/shard_map/spread_far/pallas_call | solution.py:294
  87.6 2.3 %collective-permute-start.17 = (f32[3,64,256]{2,1,0:T(8,128)S(1)}, f32[3,64,256]{2,1,0:T(8,128)S(1)}, u32[]{:S(2)}, u32[]{:S(2)}) collective-permute-start(f32[3,64,256]{2,1,0:T(8,128)S(1)} %spread_far.2), channel_id=1, source_target_pairs={{0,2},{1,3},{2,0},{3,1},{4,6},{5,7},{6,4},{7,5},{8,10},{9,11},{10,... | collective-permute-start | bytes 589832 | tf_op jit(solution)/shard_map/ppermute | solution.py:53
  89.9 2.9 %spread_rest.2 = (f32[3,64,256]{2,1,0:T(8,128)S(1)}, f32[3,64,256]{2,1,0:T(8,128)S(1)}, f32[3,64,256]{2,1,0:T(8,128)S(1)}) custom-call(s32[256]{0:T(256)S(1)} %plan.2.list_ref.refs_1_.near_ref, s32[256]{0:T(256)S(1)} %plan.3.list_ref, bf16[44,256,256]{2,1,0:T(8,128)(2,1)S(1)} %get-tuple-element.51.w1, bf16[36,256,256]{2,1,0:T(8,128)(2,1)S(1)} %get-tuple-element.56.w3, ...), custom_call_target="tpu_custom_call" | custom-call | flops 30000001024 | bytes 1000 | tf_op jit(solution)/shard_map/spread_rest/pallas_call | solution.py:294
  93.3 1.6 %collective-permute-start.19 = (f32[3,64,256]{2,1,0:T(8,128)S(1)}, f32[3,64,256]{2,1,0:T(8,128)S(1)}, u32[]{:S(2)}, u32[]{:S(2)}) collective-permute-start(f32[3,64,256]{2,1,0:T(8,128)S(1)} %get-tuple-element.72), channel_id=1, source_target_pairs={{0,1},{1,2},{2,3},{3,0},{4,7},{5,4},{6,5},{7,6},{8,9},{9,10},{10,1... | collective-permute-start | bytes 589832 | tf_op jit(solution)/shard_map/ppermute | solution.py:49
  94.9 1.8 %collective-permute-done.17 = f32[3,64,256]{2,1,0:T(8,128)S(1)} collective-permute-done((f32[3,64,256]{2,1,0:T(8,128)S(1)}, f32[3,64,256]{2,1,0:T(8,128)S(1)}, u32[]{:S(2)}, u32[]{:S(2)}) %collective-permute-start.17) | collective-permute-done | bytes 196640 | tf_op jit(solution)/shard_map/ppermute | solution.py:53
  96.7 1.8 %collective-permute-done.18 = f32[3,64,256]{2,1,0:T(8,128)S(1)} collective-permute-done((f32[3,64,256]{2,1,0:T(8,128)S(1)}, f32[3,64,256]{2,1,0:T(8,128)S(1)}, u32[]{:S(2)}, u32[]{:S(2)}) %collective-permute-start.18) | collective-permute-done | bytes 196640 | tf_op jit(solution)/shard_map/ppermute | solution.py:49
  98.5 1.7 %collective-permute-done.19 = f32[3,64,256]{2,1,0:T(8,128)S(1)} collective-permute-done((f32[3,64,256]{2,1,0:T(8,128)S(1)}, f32[3,64,256]{2,1,0:T(8,128)S(1)}, u32[]{:S(2)}, u32[]{:S(2)}) %collective-permute-start.19) | collective-permute-done | bytes 196640 | tf_op jit(solution)/shard_map/ppermute | solution.py:49
  100.2 4.3 %collective-permute-start.20 = (bf16[3,64,256]{2,1,0:T(8,128)(2,1)S(1)}, bf16[3,64,256]{2,1,0:T(8,128)(2,1)S(1)}, u32[]{:S(2)}, u32[]{:S(2)}) collective-permute-start(bf16[3,64,256]{2,1,0:T(8,128)(2,1)S(1)} %add_convert_fusion.s0), channel_id=1, source_target_pairs={{8,0},{124,4},{16,8},{4,12},{24,16},{12,20},{32,24},{20,28},{40,32... | collective-permute-start | bytes 294920 | tf_op jit(solution)/shard_map/ppermute | solution.py:57
  104.5 3.0 %collective-permute-done.20.s2 = bf16[3,64,256]{2,1,0:T(8,128)(2,1)S(1)} collective-permute-done((bf16[3,64,256]{2,1,0:T(8,128)(2,1)S(1)}, bf16[3,64,256]{2,1,0:T(8,128)(2,1)S(1)}, u32[]{:S(2)}, u32[]{:S(2)}) %collective-permute-start.20) | collective-permute-done | bytes 98336 | tf_op jit(solution)/shard_map/ppermute | solution.py:57
  107.5 2.2 %spread_near.3.given = f32[13,64,256]{2,1,0:T(8,128)S(1)} custom-call(s32[256]{0:T(256)S(1)} %plan.2.list_ref.refs_1_.near_ref, s32[256]{0:T(256)S(1)} %plan.3.list_ref, bf16[44,256,256]{2,1,0:T(8,128)(2,1)S(1)} %get-tuple-element.66.w0, bf16[36,256,256]{2,1,0:T(8,128)(2,1)S(1)} %get-tuple-element.67.w2, bf16[3,64,256]{2,1,0:T(8,128)(2,1)S(1)} %add_convert_fusion.s0, ...), custom_call_target="tpu_custom_call" | custom-call | flops 30000001024 | bytes 1000 | tf_op jit(solution)/shard_map/spread_near/pallas_call | solution.py:294
  109.7 2.7 %collective-permute-done.21.s3 = bf16[3,64,256]{2,1,0:T(8,128)(2,1)S(1)} collective-permute-done((bf16[3,64,256]{2,1,0:T(8,128)(2,1)S(1)}, bf16[3,64,256]{2,1,0:T(8,128)(2,1)S(1)}, u32[]{:S(2)}, u32[]{:S(2)}) %collective-permute-start.21) | collective-permute-done | bytes 98336 | tf_op jit(solution)/shard_map/ppermute | solution.py:57
  112.5 1.3 %spread_far.3 = f32[3,64,256]{2,1,0:T(8,128)S(1)} custom-call(s32[256]{0:T(256)S(1)} %plan.3.list_ref, bf16[36,256,256]{2,1,0:T(8,128)(2,1)S(1)} %get-tuple-element.56.w3, bf16[40,256,256]{2,1,0:T(8,128)(2,1)S(1)} %get-tuple-element.68.w4, bf16[3,64,256]{2,1,0:T(8,128)(2,1)S(1)} %collective-permute-done.20.s2, ...), custom_call_target="tpu_custom_call" | custom-call | flops 30000001024 | bytes 1000 | tf_op jit(solution)/shard_map/spread_far/pallas_call | solution.py:294
  113.8 1.9 %collective-permute-start.24 = (f32[3,64,256]{2,1,0:T(8,128)S(1)}, f32[3,64,256]{2,1,0:T(8,128)S(1)}, u32[]{:S(2)}, u32[]{:S(2)}) collective-permute-start(f32[3,64,256]{2,1,0:T(8,128)S(1)} %spread_far.3), channel_id=1, source_target_pairs={{0,2},{1,3},{2,0},{3,1},{4,6},{5,7},{6,4},{7,5},{8,10},{9,11},{10,... | collective-permute-start | bytes 589832 | tf_op jit(solution)/shard_map/ppermute | solution.py:53
  115.7 2.9 %spread_rest.3 = (f32[3,64,256]{2,1,0:T(8,128)S(1)}, f32[3,64,256]{2,1,0:T(8,128)S(1)}, f32[3,64,256]{2,1,0:T(8,128)S(1)}) custom-call(s32[256]{0:T(256)S(1)} %plan.2.list_ref.refs_1_.near_ref, s32[256]{0:T(256)S(1)} %plan.3.list_ref, bf16[44,256,256]{2,1,0:T(8,128)(2,1)S(1)} %get-tuple-element.51.w1, bf16[36,256,256]{2,1,0:T(8,128)(2,1)S(1)} %get-tuple-element.56.w3, ...), custom_call_target="tpu_custom_call" | custom-call | flops 30000001024 | bytes 1000 | tf_op jit(solution)/shard_map/spread_rest/pallas_call | solution.py:294
  118.5 1.0 collective-permute-start.25
  119.6 1.1 collective-permute-start.26
  120.6 2.2 %collective-permute-done.24 = f32[3,64,256]{2,1,0:T(8,128)S(1)} collective-permute-done((f32[3,64,256]{2,1,0:T(8,128)S(1)}, f32[3,64,256]{2,1,0:T(8,128)S(1)}, u32[]{:S(2)}, u32[]{:S(2)}) %collective-permute-start.24) | collective-permute-done | bytes 196640 | tf_op jit(solution)/shard_map/ppermute | solution.py:53
  122.8 1.5 %collective-permute-done.25 = f32[3,64,256]{2,1,0:T(8,128)S(1)} collective-permute-done((f32[3,64,256]{2,1,0:T(8,128)S(1)}, f32[3,64,256]{2,1,0:T(8,128)S(1)}, u32[]{:S(2)}, u32[]{:S(2)}) %collective-permute-start.25) | collective-permute-done | bytes 196640 | tf_op jit(solution)/shard_map/ppermute | solution.py:49
  124.3 2.2 %collective-permute-done.26 = f32[3,64,256]{2,1,0:T(8,128)S(1)} collective-permute-done((f32[3,64,256]{2,1,0:T(8,128)S(1)}, f32[3,64,256]{2,1,0:T(8,128)S(1)}, u32[]{:S(2)}, u32[]{:S(2)}) %collective-permute-start.26) | collective-permute-done | bytes 196640 | tf_op jit(solution)/shard_map/ppermute | solution.py:49
  126.5 0.7 add_bitcast_fusion
  (39 shorter events, 2.2 us)
Async XLA Ops:
  2.5 22.0 %collective-permute-start = (bf16[1552,256]{1,0:T(8,128)(2,1)S(1)}, bf16[1552,256]{1,0:T(8,128)(2,1)S(1)}, u32[]{:S(2)}, u32[]{:S(2)}) collective-permute-start(bf16[1552,256]{1,0:T(8,128)(2,1)S(1)} %get-tuple-element.52.r0), channel_id=1, source_target_pairs={{0,1},{1,2},{2,3},{3,0},{4,7},{5,4},{6,5},{7,6},{8,9},{9,10},{10,1... | collective-permute-start | bytes 2383880 | tf_op jit(solution)/shard_map/ppermute | solution.py:49
  4.3 20.2 %collective-permute-start.2 = (bf16[784,256]{1,0:T(8,128)(2,1)S(1)}, bf16[784,256]{1,0:T(8,128)(2,1)S(1)}, u32[]{:S(2)}, u32[]{:S(2)}) collective-permute-start(bf16[784,256]{1,0:T(8,128)(2,1)S(1)} %third.1.r1), channel_id=1, source_target_pairs={{0,1},{1,2},{2,3},{3,0},{4,7},{5,4},{6,5},{7,6},{8,9},{9,10},{10,1... | collective-permute-start | bytes 1204232 | tf_op jit(solution)/shard_map/ppermute | solution.py:49
  5.9 18.6 %collective-permute-start.1 = (bf16[784,256]{1,0:T(8,128)(2,1)S(1)}, bf16[784,256]{1,0:T(8,128)(2,1)S(1)}, u32[]{:S(2)}, u32[]{:S(2)}) collective-permute-start(bf16[784,256]{1,0:T(8,128)(2,1)S(1)} %third.1.r1), channel_id=1, source_target_pairs={{0,3},{1,0},{2,1},{3,2},{4,5},{5,6},{6,7},{7,4},{8,11},{9,8},{10,9... | collective-permute-start | bytes 1204232 | tf_op jit(solution)/shard_map/ppermute | solution.py:49
  7.6 35.2 %collective-permute-start.6 = (bf16[832,768]{1,0:T(8,128)(2,1)S(1)}, bf16[832,768]{1,0:T(8,128)(2,1)S(1)}, u32[]{:S(2)}, u32[]{:S(2)}) collective-permute-start(bf16[832,768]{1,0:T(8,128)(2,1)S(1)} %get-tuple-element.46.full_ref.c0), channel_id=1, source_target_pairs={{120,0},{12,4},{0,8},{20,12},{8,16},{28,20},{16,24},{36,28},{24,32... | collective-permute-start | bytes 3833864 | tf_op jit(solution)/shard_map/ppermute | solution.py:57
  9.2 31.5 %collective-permute-start.5 = (bf16[832,768]{1,0:T(8,128)(2,1)S(1)}, bf16[832,768]{1,0:T(8,128)(2,1)S(1)}, u32[]{:S(2)}, u32[]{:S(2)}) collective-permute-start(bf16[832,768]{1,0:T(8,128)(2,1)S(1)} %get-tuple-element.46.full_ref.c0), channel_id=1, source_target_pairs={{8,0},{124,4},{16,8},{4,12},{24,16},{12,20},{32,24},{20,28},{40,32... | collective-permute-start | bytes 3833864 | tf_op jit(solution)/shard_map/ppermute | solution.py:57
  24.5 22.3 %collective-permute-start.3 = (bf16[1552,256]{1,0:T(8,128)(2,1)S(1)}, bf16[1552,256]{1,0:T(8,128)(2,1)S(1)}, u32[]{:S(2)}, u32[]{:S(2)}) collective-permute-start(bf16[1552,256]{1,0:T(8,128)(2,1)S(1)} %collective-permute-done.r2), channel_id=1, source_target_pairs={{0,1},{1,2},{2,3},{3,0},{4,7},{5,4},{6,5},{7,6},{8,9},{9,10},{10,1... | collective-permute-start | bytes 2383880 | tf_op jit(solution)/shard_map/ppermute | solution.py:49
  24.9 24.0 %collective-permute-start.7 = (bf16[1552,256]{1,0:T(8,128)(2,1)S(1)}, bf16[1552,256]{1,0:T(8,128)(2,1)S(1)}, u32[]{:S(2)}, u32[]{:S(2)}) collective-permute-start(bf16[1552,256]{1,0:T(8,128)(2,1)S(1)} %get-tuple-element.52.r0), channel_id=1, source_target_pairs={{0,3},{1,0},{2,1},{3,2},{4,5},{5,6},{6,7},{7,4},{8,11},{9,8},{10,9... | collective-permute-start | bytes 2383880 | tf_op jit(solution)/shard_map/ppermute | solution.py:49
  27.8 3.2 %collective-permute-start.4 = (bf16[832,768]{1,0:T(8,128)(2,1)S(1)}, bf16[832,768]{1,0:T(8,128)(2,1)S(1)}, u32[]{:S(2)}, u32[]{:S(2)}) collective-permute-start(bf16[832,768]{1,0:T(8,128)(2,1)S(1)} %get-tuple-element.46.full_ref.c0), channel_id=1, source_target_pairs={{0,4},{4,0},{1,5},{5,1},{2,6},{6,2},{3,7},{7,3},{8,12},{12,8},{9,1... | collective-permute-start | bytes 3833864 | tf_op jit(solution)/shard_map/ppermute | solution.py:63
  31.0 18.0 %collective-permute-start.8 = (bf16[784,256]{1,0:T(8,128)(2,1)S(1)}, bf16[784,256]{1,0:T(8,128)(2,1)S(1)}, u32[]{:S(2)}, u32[]{:S(2)}) collective-permute-start(bf16[784,256]{1,0:T(8,128)(2,1)S(1)} %collective-permute-done.1.r4), channel_id=1, source_target_pairs={{0,3},{1,0},{2,1},{3,2},{4,5},{5,6},{6,7},{7,4},{8,11},{9,8},{10,9... | collective-permute-start | bytes 1204232 | tf_op jit(solution)/shard_map/ppermute | solution.py:49
  40.7 13.8 %collective-permute-start.9 = (bf16[832,768]{1,0:T(8,128)(2,1)S(1)}, bf16[832,768]{1,0:T(8,128)(2,1)S(1)}, u32[]{:S(2)}, u32[]{:S(2)}) collective-permute-start(bf16[832,768]{1,0:T(8,128)(2,1)S(1)} %collective-permute-done.5.c2), channel_id=1, source_target_pairs={{0,4},{4,0},{1,5},{5,1},{2,6},{6,2},{3,7},{7,3},{8,12},{12,8},{9,1... | collective-permute-start | bytes 3833864 | tf_op jit(solution)/shard_map/ppermute | solution.py:63
  56.1 15.0 %copy-start = (f32[3,256,64]{1,2,0:T(8,128)S(1)}, f32[3,256,64]{1,2,0:T(8,128)}, u32[]{:S(2)}) copy-start(f32[3,256,64]{1,2,0:T(8,128)} %param.4) | copy-start | bytes 589828
  56.1 9.4 %collective-permute-start.10 = (f32[3,72,256]{2,1,0:T(8,128)S(1)}, f32[3,72,256]{2,1,0:T(8,128)S(1)}, u32[]{:S(2)}, u32[]{:S(2)}) collective-permute-start(f32[3,72,256]{2,1,0:T(8,128)S(1)} %get-tuple-element.60), channel_id=1, source_target_pairs={{0,2},{1,3},{2,0},{3,1},{4,6},{5,7},{6,4},{7,5},{8,10},{9,11},{10,... | collective-permute-start | bytes 663560 | tf_op jit(solution)/shard_map/ppermute | solution.py:53
  62.7 7.7 %collective-permute-start.11 = (f32[3,72,256]{2,1,0:T(8,128)S(1)}, f32[3,72,256]{2,1,0:T(8,128)S(1)}, u32[]{:S(2)}, u32[]{:S(2)}) collective-permute-start(f32[3,72,256]{2,1,0:T(8,128)S(1)} %get-tuple-element.64), channel_id=1, source_target_pairs={{0,3},{1,0},{2,1},{3,2},{4,5},{5,6},{6,7},{7,4},{8,11},{9,8},{10,9... | collective-permute-start | bytes 663560 | tf_op jit(solution)/shard_map/ppermute | solution.py:49
  63.9 7.1 %collective-permute-start.12 = (f32[3,72,256]{2,1,0:T(8,128)S(1)}, f32[3,72,256]{2,1,0:T(8,128)S(1)}, u32[]{:S(2)}, u32[]{:S(2)}) collective-permute-start(f32[3,72,256]{2,1,0:T(8,128)S(1)} %get-tuple-element.65), channel_id=1, source_target_pairs={{0,1},{1,2},{2,3},{3,0},{4,7},{5,4},{6,5},{7,6},{8,9},{9,10},{10,1... | collective-permute-start | bytes 663560 | tf_op jit(solution)/shard_map/ppermute | solution.py:49
  71.1 10.2 %collective-permute-start.13 = (bf16[3,64,256]{2,1,0:T(8,128)(2,1)S(1)}, bf16[3,64,256]{2,1,0:T(8,128)(2,1)S(1)}, u32[]{:S(2)}, u32[]{:S(2)}) collective-permute-start(bf16[3,64,256]{2,1,0:T(8,128)(2,1)S(1)} %fusion.1.s0), channel_id=1, source_target_pairs={{8,0},{124,4},{16,8},{4,12},{24,16},{12,20},{32,24},{20,28},{40,32... | collective-permute-start | bytes 294920 | tf_op jit(solution)/shard_map/ppermute | solution.py:57
  78.3 3.0 %collective-permute-start.16 = (bf16[3,64,256]{2,1,0:T(8,128)(2,1)S(1)}, bf16[3,64,256]{2,1,0:T(8,128)(2,1)S(1)}, u32[]{:S(2)}, u32[]{:S(2)}) collective-permute-start(bf16[3,64,256]{2,1,0:T(8,128)(2,1)S(1)} %fusion.1.s0), channel_id=1, source_target_pairs={{0,4},{4,0},{1,5},{5,1},{2,6},{6,2},{3,7},{7,3},{8,12},{12,8},{9,1... | collective-permute-start | bytes 294920 | tf_op jit(solution)/shard_map/ppermute | solution.py:63
  78.3 7.9 %collective-permute-start.14 = (bf16[3,64,256]{2,1,0:T(8,128)(2,1)S(1)}, bf16[3,64,256]{2,1,0:T(8,128)(2,1)S(1)}, u32[]{:S(2)}, u32[]{:S(2)}) collective-permute-start(bf16[3,64,256]{2,1,0:T(8,128)(2,1)S(1)} %fusion.1.s0), channel_id=1, source_target_pairs={{120,0},{12,4},{0,8},{20,12},{8,16},{28,20},{16,24},{36,28},{24,32... | collective-permute-start | bytes 294920 | tf_op jit(solution)/shard_map/ppermute | solution.py:57
  81.3 4.9 %collective-permute-start.15 = (bf16[3,64,256]{2,1,0:T(8,128)(2,1)S(1)}, bf16[3,64,256]{2,1,0:T(8,128)(2,1)S(1)}, u32[]{:S(2)}, u32[]{:S(2)}) collective-permute-start(bf16[3,64,256]{2,1,0:T(8,128)(2,1)S(1)} %collective-permute-done.13.s2), channel_id=1, source_target_pairs={{0,4},{4,0},{1,5},{5,1},{2,6},{6,2},{3,7},{7,3},{8,12},{12,8},{9,1... | collective-permute-start | bytes 294920 | tf_op jit(solution)/shard_map/ppermute | solution.py:63
  87.6 9.1 %collective-permute-start.17 = (f32[3,64,256]{2,1,0:T(8,128)S(1)}, f32[3,64,256]{2,1,0:T(8,128)S(1)}, u32[]{:S(2)}, u32[]{:S(2)}) collective-permute-start(f32[3,64,256]{2,1,0:T(8,128)S(1)} %spread_far.2), channel_id=1, source_target_pairs={{0,2},{1,3},{2,0},{3,1},{4,6},{5,7},{6,4},{7,5},{8,10},{9,11},{10,... | collective-permute-start | bytes 589832 | tf_op jit(solution)/shard_map/ppermute | solution.py:53
  92.8 5.7 %collective-permute-start.18 = (f32[3,64,256]{2,1,0:T(8,128)S(1)}, f32[3,64,256]{2,1,0:T(8,128)S(1)}, u32[]{:S(2)}, u32[]{:S(2)}) collective-permute-start(f32[3,64,256]{2,1,0:T(8,128)S(1)} %get-tuple-element.71), channel_id=1, source_target_pairs={{0,3},{1,0},{2,1},{3,2},{4,5},{5,6},{6,7},{7,4},{8,11},{9,8},{10,9... | collective-permute-start | bytes 589832 | tf_op jit(solution)/shard_map/ppermute | solution.py:49
  93.3 6.9 %collective-permute-start.19 = (f32[3,64,256]{2,1,0:T(8,128)S(1)}, f32[3,64,256]{2,1,0:T(8,128)S(1)}, u32[]{:S(2)}, u32[]{:S(2)}) collective-permute-start(f32[3,64,256]{2,1,0:T(8,128)S(1)} %get-tuple-element.72), channel_id=1, source_target_pairs={{0,1},{1,2},{2,3},{3,0},{4,7},{5,4},{6,5},{7,6},{8,9},{9,10},{10,1... | collective-permute-start | bytes 589832 | tf_op jit(solution)/shard_map/ppermute | solution.py:49
  100.2 7.3 %collective-permute-start.20 = (bf16[3,64,256]{2,1,0:T(8,128)(2,1)S(1)}, bf16[3,64,256]{2,1,0:T(8,128)(2,1)S(1)}, u32[]{:S(2)}, u32[]{:S(2)}) collective-permute-start(bf16[3,64,256]{2,1,0:T(8,128)(2,1)S(1)} %add_convert_fusion.s0), channel_id=1, source_target_pairs={{8,0},{124,4},{16,8},{4,12},{24,16},{12,20},{32,24},{20,28},{40,32... | collective-permute-start | bytes 294920 | tf_op jit(solution)/shard_map/ppermute | solution.py:57
  104.5 3.0 %collective-permute-start.23 = (bf16[3,64,256]{2,1,0:T(8,128)(2,1)S(1)}, bf16[3,64,256]{2,1,0:T(8,128)(2,1)S(1)}, u32[]{:S(2)}, u32[]{:S(2)}) collective-permute-start(bf16[3,64,256]{2,1,0:T(8,128)(2,1)S(1)} %add_convert_fusion.s0), channel_id=1, source_target_pairs={{0,4},{4,0},{1,5},{5,1},{2,6},{6,2},{3,7},{7,3},{8,12},{12,8},{9,1... | collective-permute-start | bytes 294920 | tf_op jit(solution)/shard_map/ppermute | solution.py:63
  104.5 7.9 %collective-permute-start.21 = (bf16[3,64,256]{2,1,0:T(8,128)(2,1)S(1)}, bf16[3,64,256]{2,1,0:T(8,128)(2,1)S(1)}, u32[]{:S(2)}, u32[]{:S(2)}) collective-permute-start(bf16[3,64,256]{2,1,0:T(8,128)(2,1)S(1)} %add_convert_fusion.s0), channel_id=1, source_target_pairs={{120,0},{12,4},{0,8},{20,12},{8,16},{28,20},{16,24},{36,28},{24,32... | collective-permute-start | bytes 294920 | tf_op jit(solution)/shard_map/ppermute | solution.py:57
  107.5 4.9 %collective-permute-start.22 = (bf16[3,64,256]{2,1,0:T(8,128)(2,1)S(1)}, bf16[3,64,256]{2,1,0:T(8,128)(2,1)S(1)}, u32[]{:S(2)}, u32[]{:S(2)}) collective-permute-start(bf16[3,64,256]{2,1,0:T(8,128)(2,1)S(1)} %collective-permute-done.20.s2), channel_id=1, source_target_pairs={{0,4},{4,0},{1,5},{5,1},{2,6},{6,2},{3,7},{7,3},{8,12},{12,8},{9,1... | collective-permute-start | bytes 294920 | tf_op jit(solution)/shard_map/ppermute | solution.py:63
  113.8 9.0 %collective-permute-start.24 = (f32[3,64,256]{2,1,0:T(8,128)S(1)}, f32[3,64,256]{2,1,0:T(8,128)S(1)}, u32[]{:S(2)}, u32[]{:S(2)}) collective-permute-start(f32[3,64,256]{2,1,0:T(8,128)S(1)} %spread_far.3), channel_id=1, source_target_pairs={{0,2},{1,3},{2,0},{3,1},{4,6},{5,7},{6,4},{7,5},{8,10},{9,11},{10,... | collective-permute-start | bytes 589832 | tf_op jit(solution)/shard_map/ppermute | solution.py:53
  118.5 5.7 %collective-permute-start.25 = (f32[3,64,256]{2,1,0:T(8,128)S(1)}, f32[3,64,256]{2,1,0:T(8,128)S(1)}, u32[]{:S(2)}, u32[]{:S(2)}) collective-permute-start(f32[3,64,256]{2,1,0:T(8,128)S(1)} %get-tuple-element.75), channel_id=1, source_target_pairs={{0,3},{1,0},{2,1},{3,2},{4,5},{5,6},{6,7},{7,4},{8,11},{9,8},{10,9... | collective-permute-start | bytes 589832 | tf_op jit(solution)/shard_map/ppermute | solution.py:49
  119.6 6.9 %collective-permute-start.26 = (f32[3,64,256]{2,1,0:T(8,128)S(1)}, f32[3,64,256]{2,1,0:T(8,128)S(1)}, u32[]{:S(2)}, u32[]{:S(2)}) collective-permute-start(f32[3,64,256]{2,1,0:T(8,128)S(1)} %get-tuple-element.76), channel_id=1, source_target_pairs={{0,1},{1,2},{2,3},{3,0},{4,7},{5,4},{6,5},{7,6},{8,9},{9,10},{10,1... | collective-permute-start | bytes 589832 | tf_op jit(solution)/shard_map/ppermute | solution.py:49

commit v6 on v5

--- a/solution.py
+++ b/solution.py
@@ -34,6 +34,7 @@
 BEFORE = 250
 LISTS = 256
 STEP = 9
+CODED = 32000.0
 SPARE = NX * BLK
 SUMS = CH + 8
 IDS = 16
@@ -338,13 +339,32 @@
     add_spread(2, list_ref, w2, states, sum_ref, 0, list_ref[TOTALS + 2])
 
 
+def put_coded(ref, sums, first):
+    row = lax.broadcasted_iota(jnp.int32, (16, ROWS), 0)
+    powers = jnp.zeros((16, ROWS), F32)
+    for i in range(BLK):
+        values = sums[first + i]
+        largest = jnp.maximum(jnp.max(jnp.abs(values), axis=0, keepdims=True), 1e-30)
+        power = jnp.ceil(jnp.log2(largest))
+        coded = jnp.floor(values * (jnp.exp2(-power) * CODED) + 0.5)
+        ref[i * CH : (i + 1) * CH] = coded.astype(jnp.int32).astype(jnp.int16)
+        powers = jnp.where(row == i, power, powers)
+    ref[BLK * CH :] = powers.astype(jnp.int32).astype(jnp.int16)
+
+
+def uncoded(v):
+    values = v[: BLK * CH].astype(F32).reshape(BLK, CH, ROWS)
+    powers = v[BLK * CH : BLK * CH + BLK].astype(F32)
+    return values * (jnp.exp2(powers) * (1.0 / CODED))[:, None, :]
+
+
 def spread_far(list_ref, w3, w4, s2, s3, s4, given, far, sums, states):
     sums[...] = given[...]
     for at, ref in enumerate((s2, s3, s4)):
         states[(at + 2) * BLK : (at + 3) * BLK] = ref[...]
     for chunk, w_ref in ((3, w3), (4, w4)):
         add_spread(chunk, list_ref, w_ref, states, sums, list_ref[BEFORE + chunk], list_ref[TOTALS + chunk])
-    far[...] = sums[3 * BLK : SPARE]
+    put_coded(far, sums, 3 * BLK)
 
 
 def spread_rest(near_ref, list_ref, w1, w3, w4, s2, s3, s4, given, own, back, fore, sums, states):
@@ -354,20 +374,22 @@
     add_spread(1, near_ref, w1, states, sums, 0, near_ref[TOTALS + 1])
     for chunk, w_ref in ((3, w3), (4, w4)):
         add_spread(chunk, list_ref, w_ref, states, sums, 0, list_ref[BEFORE + chunk])
-    for at, ref in enumerate((own, back, fore)):
-        ref[...] = sums[at * BLK : (at + 1) * BLK]
+    own[...] = sums[:BLK]
+    put_coded(back, sums, BLK)
+    put_coded(fore, sums, 2 * BLK)
 
 
 def spread(lists, weights, states):
     sums = ((SPARE + 1, CH, ROWS), F32)
     held = ((5 * BLK, CH, ROWS), BF16)
-    part = ((BLK, CH, ROWS), F32)
+    part = ((BLK * CH + 16, ROWS), jnp.int16)
     w0, w1, w2, w3, w4_far, w4 = weights
     (near,) = build(spread_near, 3, [sums], [held], *lists, w0, w2, *states[:2])
     (far,) = build(spread_far, 4, [part], [sums, held], lists[1], w3, w4_far, *states[2:], near)
     near, _ = lax.optimization_barrier((near, far))
     return *build(
-        spread_rest, 4, [part] * (NX - 1), [sums, held], *lists, w1, w3, w4, *states[2:], near
+        spread_rest, 4, [((BLK, CH, ROWS), F32), part, part], [sums, held],
+        *lists, w1, w3, w4, *states[2:], near,
     ), far
 
 
@@ -379,9 +401,9 @@
     return [v, partner, one, other, across]
 
 
-def reduce_rows(own, back, fore, far):
-    first = lax.optimization_barrier(own + across_x(far))
-    return first + along_x(back, -1) + along_x(fore, 1)
+def reduce_rows(own, back, fore, far, read=lambda v: v):
+    first = lax.optimization_barrier(own + read(across_x(far)))
+    return first + read(along_x(back, -1)) + read(along_x(fore, 1))
 
 
 def local(embeddings, seeds, neighbours):
@@ -437,7 +459,7 @@
     scores = total[:, :CH] * scale + prior
     for _ in range(ITERS - 1):
         states = wide_exchange(scores.astype(BF16))
-        total = reduce_rows(*spread(lists, weights, states))
+        total = reduce_rows(*spread(lists, weights, states), uncoded)
         scores = total * scale + prior
     return jnp.swapaxes(scores, 1, 2)
 

time: 127 us -> 124 us (0.976)
  starting transfers between devices: 43.3 us -> 39.3 us
  waiting for transfers between devices: 42.8 us -> 44.9 us
  Pallas kernels: 38.9 us -> 36.9 us
    ppermute x12, waiting for transfers between devices: 23 us -> 26.1 us  [along_x(): return lax.ppermute(v, ('c', 'x'), pairs)]
    ppermute x6, starting transfers between devices: 18 us -> 15 us  [from_wide(): lax.ppermute(v, WIDE, [((i + (2 * sign if i % 2 == 0 else -2 * sign)) % N...]
    ppermute x3, starting transfers between devices: 7.22 us -> 4.26 us  [across_x(): return lax.ppermute(v, 'x', [(x, (x + 2) % NX) for x in range(NX)])]
    ppermute x3, waiting for transfers between devices: 4.61 us -> 2.16 us  [across_x(): return lax.ppermute(v, 'x', [(x, (x + 2) % NX) for x in range(NX)])]
    ppermute x12, starting transfers between devices: 15.9 us -> 17.9 us  [along_x(): return lax.ppermute(v, ('c', 'x'), pairs)]
    pallas_call x11, Pallas kernels: 32 us -> 30 us  [build(): pl.pallas_call(kernel, out_shape=[jax.ShapeDtypeStruct(*o) for o in outs]...]
    ppermute x6, waiting for transfers between devices: 15.2 us -> 16.6 us  [from_wide(): lax.ppermute(v, WIDE, [((i + (2 * sign if i % 2 == 0 else -2 * sign)) % N...]
  transfers between devices with their start and end apart: 27 -> 27, of which waited for: 15 -> 14; matrix products, arithmetic and copies ran while one was open for 0% -> 0% of each run, Pallas kernels for 26% -> 25%
where the time goes in v6:
time: 124 us
  waiting for transfers between devices  44.9 us (36%)
  starting transfers between devices  39.3 us (32%)
  Pallas kernels  36.9 us (30%)
  other arithmetic  2.2 us (2%)
    pallas_call x11, Pallas kernels, build(): pl.pallas_call(kernel, out_shape=[jax.ShapeDtypeStruct(*o) for o in outs]...  30 us
    ppermute x12, waiting for transfers between devices, along_x(): return lax.ppermute(v, ('c', 'x'), pairs)  26.1 us
    ppermute x12, starting transfers between devices, along_x(): return lax.ppermute(v, ('c', 'x'), pairs)  17.9 us
    ppermute x6, waiting for transfers between devices, from_wide(): lax.ppermute(v, WIDE, [((i + (2 * sign if i % 2 == 0 else -2 * sign)) % N...  16.6 us
    ppermute x6, starting transfers between devices, from_wide(): lax.ppermute(v, WIDE, [((i + (2 * sign if i % 2 == 0 else -2 * sign)) % N...  15 us
    pallas_call x2, Pallas kernels, make_plan(): pl.pallas_call(functools.partial(plan_kernel, groups), out_shape=jax.Shap...  4.97 us
    ppermute x3, starting transfers between devices, across_x(): return lax.ppermute(v, 'x', [(x, (x + 2) % NX) for x in range(NX)])  4.26 us
  transfers between devices with their start and end apart: 27, of which 14 were waited for; matrix products, arithmetic and copies ran while one was open for 0% of the time, Pallas kernels for 25%

profile of v6, /device:TPU:0, one launch (start us, length us, event | category | flops | bytes accessed | tf_op | source)
XLA Modules:
  0.0 123.7 jit_solution(10350836141255168529)
XLA Ops:
  0.0 0.7 shift-right-arithmetic_convert_fusion
  0.8 1.7 %prep.1 = (bf16[1552,256]{1,0:T(8,128)(2,1)S(1)}, bf16[832,768]{1,0:T(8,128)(2,1)S(1)}) custom-call(bf16[3,256,768]{2,1,0:T(8,128)(2,1)} %emb_hbm.1, f32[3,64,256]{2,1,0:T(8,128)} %bitcast.18, bf16[16,256]{1,0:T(8,128)(2,1)S(1)} %fusion.19.ids_ref), custom_call_target="tpu_custom_call" | custom-call | flops 1000 | bytes 1000 | tf_op jit(solution)/shard_map/prep/pallas_call | solution.py:88
  2.5 1.6 %collective-permute-start = (bf16[1552,256]{1,0:T(8,128)(2,1)S(1)}, bf16[1552,256]{1,0:T(8,128)(2,1)S(1)}, u32[]{:S(2)}, u32[]{:S(2)}) collective-permute-start(bf16[1552,256]{1,0:T(8,128)(2,1)S(1)} %get-tuple-element.52.r0), channel_id=1, source_target_pairs={{0,1},{1,2},{2,3},{3,0},{4,7},{5,4},{6,5},{7,6},{8,9},{9,10},{10,1... | collective-permute-start | bytes 2383880 | tf_op jit(solution)/shard_map/ppermute | solution.py:50
  4.3 1.6 %collective-permute-start.2 = (bf16[784,256]{1,0:T(8,128)(2,1)S(1)}, bf16[784,256]{1,0:T(8,128)(2,1)S(1)}, u32[]{:S(2)}, u32[]{:S(2)}) collective-permute-start(bf16[784,256]{1,0:T(8,128)(2,1)S(1)} %third.1.r1), channel_id=1, source_target_pairs={{0,1},{1,2},{2,3},{3,0},{4,7},{5,4},{6,5},{7,6},{8,9},{9,10},{10,1... | collective-permute-start | bytes 1204232 | tf_op jit(solution)/shard_map/ppermute | solution.py:50
  5.9 1.7 %collective-permute-start.1 = (bf16[784,256]{1,0:T(8,128)(2,1)S(1)}, bf16[784,256]{1,0:T(8,128)(2,1)S(1)}, u32[]{:S(2)}, u32[]{:S(2)}) collective-permute-start(bf16[784,256]{1,0:T(8,128)(2,1)S(1)} %third.1.r1), channel_id=1, source_target_pairs={{0,3},{1,0},{2,1},{3,2},{4,5},{5,6},{6,7},{7,4},{8,11},{9,8},{10,9... | collective-permute-start | bytes 1204232 | tf_op jit(solution)/shard_map/ppermute | solution.py:50
  7.6 1.6 %collective-permute-start.6 = (bf16[832,768]{1,0:T(8,128)(2,1)S(1)}, bf16[832,768]{1,0:T(8,128)(2,1)S(1)}, u32[]{:S(2)}, u32[]{:S(2)}) collective-permute-start(bf16[832,768]{1,0:T(8,128)(2,1)S(1)} %get-tuple-element.46.full_ref.c0), channel_id=1, source_target_pairs={{120,0},{12,4},{0,8},{20,12},{8,16},{28,20},{16,24},{36,28},{24,32... | collective-permute-start | bytes 3833864 | tf_op jit(solution)/shard_map/ppermute | solution.py:58
  9.2 4.9 %collective-permute-start.5 = (bf16[832,768]{1,0:T(8,128)(2,1)S(1)}, bf16[832,768]{1,0:T(8,128)(2,1)S(1)}, u32[]{:S(2)}, u32[]{:S(2)}) collective-permute-start(bf16[832,768]{1,0:T(8,128)(2,1)S(1)} %get-tuple-element.46.full_ref.c0), channel_id=1, source_target_pairs={{8,0},{124,4},{16,8},{4,12},{24,16},{12,20},{32,24},{20,28},{40,32... | collective-permute-start | bytes 3833864 | tf_op jit(solution)/shard_map/ppermute | solution.py:58
  14.1 10.4 %collective-permute-done.2.r3 = bf16[784,256]{1,0:T(8,128)(2,1)S(1)} collective-permute-done((bf16[784,256]{1,0:T(8,128)(2,1)S(1)}, bf16[784,256]{1,0:T(8,128)(2,1)S(1)}, u32[]{:S(2)}, u32[]{:S(2)}) %collective-permute-start.2) | collective-permute-done | bytes 401440 | tf_op jit(solution)/shard_map/ppermute | solution.py:50
  24.5 0.4 collective-permute-start.3
  24.9 2.9 %collective-permute-start.7 = (bf16[1552,256]{1,0:T(8,128)(2,1)S(1)}, bf16[1552,256]{1,0:T(8,128)(2,1)S(1)}, u32[]{:S(2)}, u32[]{:S(2)}) collective-permute-start(bf16[1552,256]{1,0:T(8,128)(2,1)S(1)} %get-tuple-element.52.r0), channel_id=1, source_target_pairs={{0,3},{1,0},{2,1},{3,2},{4,5},{5,6},{6,7},{7,4},{8,11},{9,8},{10,9... | collective-permute-start | bytes 2383880 | tf_op jit(solution)/shard_map/ppermute | solution.py:50
  27.9 3.0 %plan.2.list_ref.refs_1_.near_ref = s32[256]{0:T(256)S(1)} custom-call(s32[3,32]{1,0:T(4,128)S(1)} %get-tuple-element.79.refs_0_, s32[3,32]{1,0:T(4,128)S(1)} %get-tuple-element.80.refs_1_, s32[3,32]{1,0:T(4,128)S(1)} %get-tuple-element.81.refs_2_), custom_call_target="tpu_custom_call" | custom-call | flops 30000001024 | bytes 1000 | tf_op jit(solution)/shard_map/plan/pallas_call | solution.py:194
  31.0 1.3 %collective-permute-start.8 = (bf16[784,256]{1,0:T(8,128)(2,1)S(1)}, bf16[784,256]{1,0:T(8,128)(2,1)S(1)}, u32[]{:S(2)}, u32[]{:S(2)}) collective-permute-start(bf16[784,256]{1,0:T(8,128)(2,1)S(1)} %collective-permute-done.1.r4), channel_id=1, source_target_pairs={{0,3},{1,0},{2,1},{3,2},{4,5},{5,6},{6,7},{7,4},{8,11},{9,8},{10,9... | collective-permute-start | bytes 1204232 | tf_op jit(solution)/shard_map/ppermute | solution.py:50
  32.3 3.3 %build_0.1 = (bf16[44,256,256]{2,1,0:T(8,128)(2,1)S(1)}, f32[13,72,256]{2,1,0:T(8,128)S(1)}, bf16[6912,256]{1,0:T(8,128)(2,1)S(1)}) custom-call(s32[256]{0:T(256)S(1)} %plan.2.list_ref.refs_1_.near_ref, bf16[1552,256]{1,0:T(8,128)(2,1)S(1)} %get-tuple-element.52.r0, bf16[784,256]{1,0:T(8,128)(2,1)S(1)} %third.1.r1, ...), custom_call_target="tpu_custom_call" | custom-call | flops 30000001024 | bytes 1000 | tf_op jit(solution)/shard_map/build_0/pallas_call | solution.py:295
  35.6 5.1 %collective-permute-done.5.c2 = bf16[832,768]{1,0:T(8,128)(2,1)S(1)} collective-permute-done((bf16[832,768]{1,0:T(8,128)(2,1)S(1)}, bf16[832,768]{1,0:T(8,128)(2,1)S(1)}, u32[]{:S(2)}, u32[]{:S(2)}) %collective-permute-start.5) | collective-permute-done | bytes 1277984 | tf_op jit(solution)/shard_map/ppermute | solution.py:58
  40.7 2.2 %collective-permute-start.9 = (bf16[832,768]{1,0:T(8,128)(2,1)S(1)}, bf16[832,768]{1,0:T(8,128)(2,1)S(1)}, u32[]{:S(2)}, u32[]{:S(2)}) collective-permute-start(bf16[832,768]{1,0:T(8,128)(2,1)S(1)} %collective-permute-done.5.c2), channel_id=1, source_target_pairs={{0,4},{4,0},{1,5},{5,1},{2,6},{6,2},{3,7},{7,3},{8,12},{12,8},{9,1... | collective-permute-start | bytes 3833864 | tf_op jit(solution)/shard_map/ppermute | solution.py:64
  42.9 4.0 %build_1.1 = (bf16[44,256,256]{2,1,0:T(8,128)(2,1)S(1)}, f32[13,72,256]{2,1,0:T(8,128)S(1)}, bf16[3072,768]{1,0:T(8,128)(2,1)S(1)}, bf16[12,64,256]{2,1,0:T(8,128)(2,1)S(1)}) custom-call(s32[256]{0:T(256)S(1)} %plan.2.list_ref.refs_1_.near_ref, bf16[6912,256]{1,0:T(8,128)(2,1)S(1)} %get-tuple-element.47.rows.old_rows, ...), custom_call_target="tpu_custom_call" | custom-call | flops 30000001024 | bytes 1000 | tf_op jit(solution)/shard_map/build_1/pallas_call | solution.py:295
  47.0 1.9 %plan.3.list_ref = s32[256]{0:T(256)S(1)} custom-call(s32[3,32]{1,0:T(4,128)S(1)} %fusion.47.refs_0_, s32[256]{0:T(256)S(1)} %plan.2.list_ref.refs_1_.near_ref), custom_call_target="tpu_custom_call" | custom-call | flops 30000001024 | bytes 1000 | tf_op jit(solution)/shard_map/plan/pallas_call | solution.py:194
  48.9 6.2 %build_2.1 = (bf16[36,256,256]{2,1,0:T(8,128)(2,1)S(1)}, bf16[36,256,256]{2,1,0:T(8,128)(2,1)S(1)}, f32[13,72,256]{2,1,0:T(8,128)S(1)}, bf16[9216,256]{1,0:T(8,128)(2,1)S(1)}) custom-call(s32[256]{0:T(256)S(1)} %plan.3.list_ref, bf16[6912,256]{1,0:T(8,128)(2,1)S(1)} %get-tuple-element.47.rows.old_rows, bf16[1552,256]{1,0:T(8,128)(2,1)S(1)} %collective-permute-done.7.r0, ...), custom_call_target="tpu_custom_call" | custom-call | flops 30000001024 | bytes 1000 | tf_op jit(solution)/shard_map/build_2/pallas_call | solution.py:295
  55.2 1.6 %build_far.1 = (bf16[40,256,256]{2,1,0:T(8,128)(2,1)S(1)}, f32[3,72,256]{2,1,0:T(8,128)S(1)}) custom-call(s32[256]{0:T(256)S(1)} %plan.3.list_ref, bf16[9216,256]{1,0:T(8,128)(2,1)S(1)} %get-tuple-element.57.rows, bf16[832,768]{1,0:T(8,128)(2,1)S(1)} %collective-permute-done.9.c4, f32[13,72,256]{2,1,0:T(8,128)S(1)} %get-tuple-element.61.given), custom_call_target="tpu_custom_call" | custom-call | flops 30000001024 | bytes 1000 | tf_op jit(solution)/shard_map/build_far/pallas_call | solution.py:295
  56.7 1.6 %collective-permute-start.10 = (f32[3,72,256]{2,1,0:T(8,128)S(1)}, f32[3,72,256]{2,1,0:T(8,128)S(1)}, u32[]{:S(2)}, u32[]{:S(2)}) collective-permute-start(f32[3,72,256]{2,1,0:T(8,128)S(1)} %get-tuple-element.60), channel_id=1, source_target_pairs={{0,2},{1,3},{2,0},{3,1},{4,6},{5,7},{6,4},{7,5},{8,10},{9,11},{10,... | collective-permute-start | bytes 663560 | tf_op jit(solution)/shard_map/ppermute | solution.py:54
  58.4 3.0 %build_rest.1 = (bf16[40,256,256]{2,1,0:T(8,128)(2,1)S(1)}, f32[3,72,256]{2,1,0:T(8,128)S(1)}, f32[3,72,256]{2,1,0:T(8,128)S(1)}, f32[3,72,256]{2,1,0:T(8,128)S(1)}) custom-call(s32[256]{0:T(256)S(1)} %plan.3.list_ref, bf16[9216,256]{1,0:T(8,128)(2,1)S(1)} %get-tuple-element.57.rows, bf16[832,768]{1,0:T(8,128)(2,1)S(1)} %collective-permute-done.9.c4, ...), custom_call_target="tpu_custom_call" | custom-call | flops 30000001024 | bytes 1000 | tf_op jit(solution)/shard_map/build_rest/pallas_call | solution.py:295
  61.4 3.6 %collective-permute-start.11 = (f32[3,72,256]{2,1,0:T(8,128)S(1)}, f32[3,72,256]{2,1,0:T(8,128)S(1)}, u32[]{:S(2)}, u32[]{:S(2)}) collective-permute-start(f32[3,72,256]{2,1,0:T(8,128)S(1)} %get-tuple-element.64), channel_id=1, source_target_pairs={{0,3},{1,0},{2,1},{3,2},{4,5},{5,6},{6,7},{7,4},{8,11},{9,8},{10,9... | collective-permute-start | bytes 663560 | tf_op jit(solution)/shard_map/ppermute | solution.py:50
  65.0 0.9 collective-permute-done.10
  65.9 3.7 %collective-permute-done.11 = f32[3,72,256]{2,1,0:T(8,128)S(1)} collective-permute-done((f32[3,72,256]{2,1,0:T(8,128)S(1)}, f32[3,72,256]{2,1,0:T(8,128)S(1)}, u32[]{:S(2)}, u32[]{:S(2)}) %collective-permute-start.11) | collective-permute-done | bytes 221216 | tf_op jit(solution)/shard_map/ppermute | solution.py:50
  69.6 2.5 %collective-permute-done.12 = f32[3,72,256]{2,1,0:T(8,128)S(1)} collective-permute-done((f32[3,72,256]{2,1,0:T(8,128)S(1)}, f32[3,72,256]{2,1,0:T(8,128)S(1)}, u32[]{:S(2)}, u32[]{:S(2)}) %collective-permute-start.12) | collective-permute-done | bytes 221216 | tf_op jit(solution)/shard_map/ppermute | solution.py:50
  72.3 5.2 %collective-permute-start.13 = (bf16[3,64,256]{2,1,0:T(8,128)(2,1)S(1)}, bf16[3,64,256]{2,1,0:T(8,128)(2,1)S(1)}, u32[]{:S(2)}, u32[]{:S(2)}) collective-permute-start(bf16[3,64,256]{2,1,0:T(8,128)(2,1)S(1)} %fusion.1.s0), channel_id=1, source_target_pairs={{8,0},{124,4},{16,8},{4,12},{24,16},{12,20},{32,24},{20,28},{40,32... | collective-permute-start | bytes 294920 | tf_op jit(solution)/shard_map/ppermute | solution.py:58
  77.4 2.2 %collective-permute-done.13.s2 = bf16[3,64,256]{2,1,0:T(8,128)(2,1)S(1)} collective-permute-done((bf16[3,64,256]{2,1,0:T(8,128)(2,1)S(1)}, bf16[3,64,256]{2,1,0:T(8,128)(2,1)S(1)}, u32[]{:S(2)}, u32[]{:S(2)}) %collective-permute-start.13) | collective-permute-done | bytes 98336 | tf_op jit(solution)/shard_map/ppermute | solution.py:58
  79.7 2.2 %spread_near.2.given = f32[13,64,256]{2,1,0:T(8,128)S(1)} custom-call(s32[256]{0:T(256)S(1)} %plan.2.list_ref.refs_1_.near_ref, s32[256]{0:T(256)S(1)} %plan.3.list_ref, bf16[44,256,256]{2,1,0:T(8,128)(2,1)S(1)} %get-tuple-element.66.w0, bf16[36,256,256]{2,1,0:T(8,128)(2,1)S(1)} %get-tuple-element.67.w2, bf16[3,64,256]{2,1,0:T(8,128)(2,1)S(1)} %fusion.1.s0, ...), custom_call_target="tpu_custom_call" | custom-call | flops 30000001024 | bytes 1000 | tf_op jit(solution)/shard_map/spread_near/pallas_call | solution.py:295
  81.8 3.5 %collective-permute-done.14.s3 = bf16[3,64,256]{2,1,0:T(8,128)(2,1)S(1)} collective-permute-done((bf16[3,64,256]{2,1,0:T(8,128)(2,1)S(1)}, bf16[3,64,256]{2,1,0:T(8,128)(2,1)S(1)}, u32[]{:S(2)}, u32[]{:S(2)}) %collective-permute-start.14) | collective-permute-done | bytes 98336 | tf_op jit(solution)/shard_map/ppermute | solution.py:58
  85.4 1.3 %spread_far.2 = s16[208,256]{1,0:T(8,128)(2,1)S(1)} custom-call(s32[256]{0:T(256)S(1)} %plan.3.list_ref, bf16[36,256,256]{2,1,0:T(8,128)(2,1)S(1)} %get-tuple-element.56.w3, bf16[40,256,256]{2,1,0:T(8,128)(2,1)S(1)} %get-tuple-element.68.w4, bf16[3,64,256]{2,1,0:T(8,128)(2,1)S(1)} %collective-permute-done.13.s2, ...), custom_call_target="tpu_custom_call" | custom-call | flops 30000001024 | bytes 1000 | tf_op jit(solution)/shard_map/spread_far/pallas_call | solution.py:295
  86.7 2.6 %collective-permute-start.17 = (s16[208,256]{1,0:T(8,128)(2,1)S(1)}, s16[208,256]{1,0:T(8,128)(2,1)S(1)}, u32[]{:S(2)}, u32[]{:S(2)}) collective-permute-start(s16[208,256]{1,0:T(8,128)(2,1)S(1)} %spread_far.2), channel_id=1, source_target_pairs={{0,2},{1,3},{2,0},{3,1},{4,6},{5,7},{6,4},{7,5},{8,10},{9,11},{10,... | collective-permute-start | bytes 319496 | tf_op jit(solution)/shard_map/ppermute | solution.py:54
  89.3 2.5 %spread_rest.2 = (f32[3,64,256]{2,1,0:T(8,128)S(1)}, s16[208,256]{1,0:T(8,128)(2,1)S(1)}, s16[208,256]{1,0:T(8,128)(2,1)S(1)}) custom-call(s32[256]{0:T(256)S(1)} %plan.2.list_ref.refs_1_.near_ref, s32[256]{0:T(256)S(1)} %plan.3.list_ref, bf16[44,256,256]{2,1,0:T(8,128)(2,1)S(1)} %get-tuple-element.51.w1, bf16[36,256,256]{2,1,0:T(8,128)(2,1)S(1)} %get-tuple-element.56.w3, ...), custom_call_target="tpu_custom_call" | custom-call | flops 30000001024 | bytes 1000 | tf_op jit(solution)/shard_map/spread_rest/pallas_call | solution.py:295
  91.8 1.9 %collective-permute-start.18 = (s16[208,256]{1,0:T(8,128)(2,1)S(1)}, s16[208,256]{1,0:T(8,128)(2,1)S(1)}, u32[]{:S(2)}, u32[]{:S(2)}) collective-permute-start(s16[208,256]{1,0:T(8,128)(2,1)S(1)} %get-tuple-element.71), channel_id=1, source_target_pairs={{0,3},{1,0},{2,1},{3,2},{4,5},{5,6},{6,7},{7,4},{8,11},{9,8},{10,9... | collective-permute-start | bytes 319496 | tf_op jit(solution)/shard_map/ppermute | solution.py:50
  93.7 0.2 collective-permute-start.19
  94.0 2.6 %collective-permute-done.18 = s16[208,256]{1,0:T(8,128)(2,1)S(1)} collective-permute-done((s16[208,256]{1,0:T(8,128)(2,1)S(1)}, s16[208,256]{1,0:T(8,128)(2,1)S(1)}, u32[]{:S(2)}, u32[]{:S(2)}) %collective-permute-start.18) | collective-permute-done | bytes 106528 | tf_op jit(solution)/shard_map/ppermute | solution.py:50
  96.6 3.0 %collective-permute-done.19 = s16[208,256]{1,0:T(8,128)(2,1)S(1)} collective-permute-done((s16[208,256]{1,0:T(8,128)(2,1)S(1)}, s16[208,256]{1,0:T(8,128)(2,1)S(1)}, u32[]{:S(2)}, u32[]{:S(2)}) %collective-permute-start.19) | collective-permute-done | bytes 106528 | tf_op jit(solution)/shard_map/ppermute | solution.py:50
  99.8 3.3 %collective-permute-start.20 = (bf16[3,64,256]{2,1,0:T(8,128)(2,1)S(1)}, bf16[3,64,256]{2,1,0:T(8,128)(2,1)S(1)}, u32[]{:S(2)}, u32[]{:S(2)}) collective-permute-start(bf16[3,64,256]{2,1,0:T(8,128)(2,1)S(1)} %fusion.11.s0), channel_id=1, source_target_pairs={{8,0},{124,4},{16,8},{4,12},{24,16},{12,20},{32,24},{20,28},{40,32... | collective-permute-start | bytes 294920 | tf_op jit(solution)/shard_map/ppermute | solution.py:58
  103.1 3.0 %collective-permute-done.20.s2 = bf16[3,64,256]{2,1,0:T(8,128)(2,1)S(1)} collective-permute-done((bf16[3,64,256]{2,1,0:T(8,128)(2,1)S(1)}, bf16[3,64,256]{2,1,0:T(8,128)(2,1)S(1)}, u32[]{:S(2)}, u32[]{:S(2)}) %collective-permute-start.20) | collective-permute-done | bytes 98336 | tf_op jit(solution)/shard_map/ppermute | solution.py:58
  106.1 2.2 %spread_near.3.given = f32[13,64,256]{2,1,0:T(8,128)S(1)} custom-call(s32[256]{0:T(256)S(1)} %plan.2.list_ref.refs_1_.near_ref, s32[256]{0:T(256)S(1)} %plan.3.list_ref, bf16[44,256,256]{2,1,0:T(8,128)(2,1)S(1)} %get-tuple-element.66.w0, bf16[36,256,256]{2,1,0:T(8,128)(2,1)S(1)} %get-tuple-element.67.w2, bf16[3,64,256]{2,1,0:T(8,128)(2,1)S(1)} %fusion.11.s0, ...), custom_call_target="tpu_custom_call" | custom-call | flops 30000001024 | bytes 1000 | tf_op jit(solution)/shard_map/spread_near/pallas_call | solution.py:295
  108.3 2.8 %collective-permute-done.21.s3 = bf16[3,64,256]{2,1,0:T(8,128)(2,1)S(1)} collective-permute-done((bf16[3,64,256]{2,1,0:T(8,128)(2,1)S(1)}, bf16[3,64,256]{2,1,0:T(8,128)(2,1)S(1)}, u32[]{:S(2)}, u32[]{:S(2)}) %collective-permute-start.21) | collective-permute-done | bytes 98336 | tf_op jit(solution)/shard_map/ppermute | solution.py:58
  111.0 1.3 %spread_far.3 = s16[208,256]{1,0:T(8,128)(2,1)S(1)} custom-call(s32[256]{0:T(256)S(1)} %plan.3.list_ref, bf16[36,256,256]{2,1,0:T(8,128)(2,1)S(1)} %get-tuple-element.56.w3, bf16[40,256,256]{2,1,0:T(8,128)(2,1)S(1)} %get-tuple-element.68.w4, bf16[3,64,256]{2,1,0:T(8,128)(2,1)S(1)} %collective-permute-done.20.s2, ...), custom_call_target="tpu_custom_call" | custom-call | flops 30000001024 | bytes 1000 | tf_op jit(solution)/shard_map/spread_far/pallas_call | solution.py:295
  112.5 2.5 %spread_rest.3 = (f32[3,64,256]{2,1,0:T(8,128)S(1)}, s16[208,256]{1,0:T(8,128)(2,1)S(1)}, s16[208,256]{1,0:T(8,128)(2,1)S(1)}) custom-call(s32[256]{0:T(256)S(1)} %plan.2.list_ref.refs_1_.near_ref, s32[256]{0:T(256)S(1)} %plan.3.list_ref, bf16[44,256,256]{2,1,0:T(8,128)(2,1)S(1)} %get-tuple-element.51.w1, bf16[36,256,256]{2,1,0:T(8,128)(2,1)S(1)} %get-tuple-element.56.w3, ...), custom_call_target="tpu_custom_call" | custom-call | flops 30000001024 | bytes 1000 | tf_op jit(solution)/shard_map/spread_rest/pallas_call | solution.py:295
  115.0 2.0 %collective-permute-start.25 = (s16[208,256]{1,0:T(8,128)(2,1)S(1)}, s16[208,256]{1,0:T(8,128)(2,1)S(1)}, u32[]{:S(2)}, u32[]{:S(2)}) collective-permute-start(s16[208,256]{1,0:T(8,128)(2,1)S(1)} %get-tuple-element.75), channel_id=1, source_target_pairs={{0,3},{1,0},{2,1},{3,2},{4,5},{5,6},{6,7},{7,4},{8,11},{9,8},{10,9... | collective-permute-start | bytes 319496 | tf_op jit(solution)/shard_map/ppermute | solution.py:50
  117.0 0.6 collective-permute-start.26
  117.6 1.3 %collective-permute-done.24 = s16[208,256]{1,0:T(8,128)(2,1)S(1)} collective-permute-done((s16[208,256]{1,0:T(8,128)(2,1)S(1)}, s16[208,256]{1,0:T(8,128)(2,1)S(1)}, u32[]{:S(2)}, u32[]{:S(2)}) %collective-permute-start.24) | collective-permute-done | bytes 106528 | tf_op jit(solution)/shard_map/ppermute | solution.py:54
  119.0 1.2 %collective-permute-done.25 = s16[208,256]{1,0:T(8,128)(2,1)S(1)} collective-permute-done((s16[208,256]{1,0:T(8,128)(2,1)S(1)}, s16[208,256]{1,0:T(8,128)(2,1)S(1)}, u32[]{:S(2)}, u32[]{:S(2)}) %collective-permute-start.25) | collective-permute-done | bytes 106528 | tf_op jit(solution)/shard_map/ppermute | solution.py:50
  120.2 2.6 %collective-permute-done.26 = s16[208,256]{1,0:T(8,128)(2,1)S(1)} collective-permute-done((s16[208,256]{1,0:T(8,128)(2,1)S(1)}, s16[208,256]{1,0:T(8,128)(2,1)S(1)}, u32[]{:S(2)}, u32[]{:S(2)}) %collective-permute-start.26) | collective-permute-done | bytes 106528 | tf_op jit(solution)/shard_map/ppermute | solution.py:50
  122.9 0.8 fusion.5
  (51 shorter events, 1.1 us)
Async XLA Ops:
  2.5 22.0 %collective-permute-start = (bf16[1552,256]{1,0:T(8,128)(2,1)S(1)}, bf16[1552,256]{1,0:T(8,128)(2,1)S(1)}, u32[]{:S(2)}, u32[]{:S(2)}) collective-permute-start(bf16[1552,256]{1,0:T(8,128)(2,1)S(1)} %get-tuple-element.52.r0), channel_id=1, source_target_pairs={{0,1},{1,2},{2,3},{3,0},{4,7},{5,4},{6,5},{7,6},{8,9},{9,10},{10,1... | collective-permute-start | bytes 2383880 | tf_op jit(solution)/shard_map/ppermute | solution.py:50
  4.3 20.2 %collective-permute-start.2 = (bf16[784,256]{1,0:T(8,128)(2,1)S(1)}, bf16[784,256]{1,0:T(8,128)(2,1)S(1)}, u32[]{:S(2)}, u32[]{:S(2)}) collective-permute-start(bf16[784,256]{1,0:T(8,128)(2,1)S(1)} %third.1.r1), channel_id=1, source_target_pairs={{0,1},{1,2},{2,3},{3,0},{4,7},{5,4},{6,5},{7,6},{8,9},{9,10},{10,1... | collective-permute-start | bytes 1204232 | tf_op jit(solution)/shard_map/ppermute | solution.py:50
  5.9 18.6 %collective-permute-start.1 = (bf16[784,256]{1,0:T(8,128)(2,1)S(1)}, bf16[784,256]{1,0:T(8,128)(2,1)S(1)}, u32[]{:S(2)}, u32[]{:S(2)}) collective-permute-start(bf16[784,256]{1,0:T(8,128)(2,1)S(1)} %third.1.r1), channel_id=1, source_target_pairs={{0,3},{1,0},{2,1},{3,2},{4,5},{5,6},{6,7},{7,4},{8,11},{9,8},{10,9... | collective-permute-start | bytes 1204232 | tf_op jit(solution)/shard_map/ppermute | solution.py:50
  7.6 35.2 %collective-permute-start.6 = (bf16[832,768]{1,0:T(8,128)(2,1)S(1)}, bf16[832,768]{1,0:T(8,128)(2,1)S(1)}, u32[]{:S(2)}, u32[]{:S(2)}) collective-permute-start(bf16[832,768]{1,0:T(8,128)(2,1)S(1)} %get-tuple-element.46.full_ref.c0), channel_id=1, source_target_pairs={{120,0},{12,4},{0,8},{20,12},{8,16},{28,20},{16,24},{36,28},{24,32... | collective-permute-start | bytes 3833864 | tf_op jit(solution)/shard_map/ppermute | solution.py:58
  9.2 31.5 %collective-permute-start.5 = (bf16[832,768]{1,0:T(8,128)(2,1)S(1)}, bf16[832,768]{1,0:T(8,128)(2,1)S(1)}, u32[]{:S(2)}, u32[]{:S(2)}) collective-permute-start(bf16[832,768]{1,0:T(8,128)(2,1)S(1)} %get-tuple-element.46.full_ref.c0), channel_id=1, source_target_pairs={{8,0},{124,4},{16,8},{4,12},{24,16},{12,20},{32,24},{20,28},{40,32... | collective-permute-start | bytes 3833864 | tf_op jit(solution)/shard_map/ppermute | solution.py:58
  24.5 22.3 %collective-permute-start.3 = (bf16[1552,256]{1,0:T(8,128)(2,1)S(1)}, bf16[1552,256]{1,0:T(8,128)(2,1)S(1)}, u32[]{:S(2)}, u32[]{:S(2)}) collective-permute-start(bf16[1552,256]{1,0:T(8,128)(2,1)S(1)} %collective-permute-done.r2), channel_id=1, source_target_pairs={{0,1},{1,2},{2,3},{3,0},{4,7},{5,4},{6,5},{7,6},{8,9},{9,10},{10,1... | collective-permute-start | bytes 2383880 | tf_op jit(solution)/shard_map/ppermute | solution.py:50
  24.9 24.0 %collective-permute-start.7 = (bf16[1552,256]{1,0:T(8,128)(2,1)S(1)}, bf16[1552,256]{1,0:T(8,128)(2,1)S(1)}, u32[]{:S(2)}, u32[]{:S(2)}) collective-permute-start(bf16[1552,256]{1,0:T(8,128)(2,1)S(1)} %get-tuple-element.52.r0), channel_id=1, source_target_pairs={{0,3},{1,0},{2,1},{3,2},{4,5},{5,6},{6,7},{7,4},{8,11},{9,8},{10,9... | collective-permute-start | bytes 2383880 | tf_op jit(solution)/shard_map/ppermute | solution.py:50
  27.8 3.2 %collective-permute-start.4 = (bf16[832,768]{1,0:T(8,128)(2,1)S(1)}, bf16[832,768]{1,0:T(8,128)(2,1)S(1)}, u32[]{:S(2)}, u32[]{:S(2)}) collective-permute-start(bf16[832,768]{1,0:T(8,128)(2,1)S(1)} %get-tuple-element.46.full_ref.c0), channel_id=1, source_target_pairs={{0,4},{4,0},{1,5},{5,1},{2,6},{6,2},{3,7},{7,3},{8,12},{12,8},{9,1... | collective-permute-start | bytes 3833864 | tf_op jit(solution)/shard_map/ppermute | solution.py:64
  31.0 17.9 %collective-permute-start.8 = (bf16[784,256]{1,0:T(8,128)(2,1)S(1)}, bf16[784,256]{1,0:T(8,128)(2,1)S(1)}, u32[]{:S(2)}, u32[]{:S(2)}) collective-permute-start(bf16[784,256]{1,0:T(8,128)(2,1)S(1)} %collective-permute-done.1.r4), channel_id=1, source_target_pairs={{0,3},{1,0},{2,1},{3,2},{4,5},{5,6},{6,7},{7,4},{8,11},{9,8},{10,9... | collective-permute-start | bytes 1204232 | tf_op jit(solution)/shard_map/ppermute | solution.py:50
  40.7 14.5 %collective-permute-start.9 = (bf16[832,768]{1,0:T(8,128)(2,1)S(1)}, bf16[832,768]{1,0:T(8,128)(2,1)S(1)}, u32[]{:S(2)}, u32[]{:S(2)}) collective-permute-start(bf16[832,768]{1,0:T(8,128)(2,1)S(1)} %collective-permute-done.5.c2), channel_id=1, source_target_pairs={{0,4},{4,0},{1,5},{5,1},{2,6},{6,2},{3,7},{7,3},{8,12},{12,8},{9,1... | collective-permute-start | bytes 3833864 | tf_op jit(solution)/shard_map/ppermute | solution.py:64
  56.7 15.5 %copy-start = (f32[3,256,64]{1,2,0:T(8,128)S(1)}, f32[3,256,64]{1,2,0:T(8,128)}, u32[]{:S(2)}) copy-start(f32[3,256,64]{1,2,0:T(8,128)} %param.4) | copy-start | bytes 589828
  56.7 9.1 %collective-permute-start.10 = (f32[3,72,256]{2,1,0:T(8,128)S(1)}, f32[3,72,256]{2,1,0:T(8,128)S(1)}, u32[]{:S(2)}, u32[]{:S(2)}) collective-permute-start(f32[3,72,256]{2,1,0:T(8,128)S(1)} %get-tuple-element.60), channel_id=1, source_target_pairs={{0,2},{1,3},{2,0},{3,1},{4,6},{5,7},{6,4},{7,5},{8,10},{9,11},{10,... | collective-permute-start | bytes 663560 | tf_op jit(solution)/shard_map/ppermute | solution.py:54
  61.4 8.3 %collective-permute-start.11 = (f32[3,72,256]{2,1,0:T(8,128)S(1)}, f32[3,72,256]{2,1,0:T(8,128)S(1)}, u32[]{:S(2)}, u32[]{:S(2)}) collective-permute-start(f32[3,72,256]{2,1,0:T(8,128)S(1)} %get-tuple-element.64), channel_id=1, source_target_pairs={{0,3},{1,0},{2,1},{3,2},{4,5},{5,6},{6,7},{7,4},{8,11},{9,8},{10,9... | collective-permute-start | bytes 663560 | tf_op jit(solution)/shard_map/ppermute | solution.py:50
  65.0 7.1 %collective-permute-start.12 = (f32[3,72,256]{2,1,0:T(8,128)S(1)}, f32[3,72,256]{2,1,0:T(8,128)S(1)}, u32[]{:S(2)}, u32[]{:S(2)}) collective-permute-start(f32[3,72,256]{2,1,0:T(8,128)S(1)} %get-tuple-element.65), channel_id=1, source_target_pairs={{0,1},{1,2},{2,3},{3,0},{4,7},{5,4},{6,5},{7,6},{8,9},{9,10},{10,1... | collective-permute-start | bytes 663560 | tf_op jit(solution)/shard_map/ppermute | solution.py:50
  72.3 7.4 %collective-permute-start.13 = (bf16[3,64,256]{2,1,0:T(8,128)(2,1)S(1)}, bf16[3,64,256]{2,1,0:T(8,128)(2,1)S(1)}, u32[]{:S(2)}, u32[]{:S(2)}) collective-permute-start(bf16[3,64,256]{2,1,0:T(8,128)(2,1)S(1)} %fusion.1.s0), channel_id=1, source_target_pairs={{8,0},{124,4},{16,8},{4,12},{24,16},{12,20},{32,24},{20,28},{40,32... | collective-permute-start | bytes 294920 | tf_op jit(solution)/shard_map/ppermute | solution.py:58
  77.4 2.2 %collective-permute-start.16 = (bf16[3,64,256]{2,1,0:T(8,128)(2,1)S(1)}, bf16[3,64,256]{2,1,0:T(8,128)(2,1)S(1)}, u32[]{:S(2)}, u32[]{:S(2)}) collective-permute-start(bf16[3,64,256]{2,1,0:T(8,128)(2,1)S(1)} %fusion.1.s0), channel_id=1, source_target_pairs={{0,4},{4,0},{1,5},{5,1},{2,6},{6,2},{3,7},{7,3},{8,12},{12,8},{9,1... | collective-permute-start | bytes 294920 | tf_op jit(solution)/shard_map/ppermute | solution.py:64
  77.4 7.9 %collective-permute-start.14 = (bf16[3,64,256]{2,1,0:T(8,128)(2,1)S(1)}, bf16[3,64,256]{2,1,0:T(8,128)(2,1)S(1)}, u32[]{:S(2)}, u32[]{:S(2)}) collective-permute-start(bf16[3,64,256]{2,1,0:T(8,128)(2,1)S(1)} %fusion.1.s0), channel_id=1, source_target_pairs={{120,0},{12,4},{0,8},{20,12},{8,16},{28,20},{16,24},{36,28},{24,32... | collective-permute-start | bytes 294920 | tf_op jit(solution)/shard_map/ppermute | solution.py:58
  79.7 5.7 %collective-permute-start.15 = (bf16[3,64,256]{2,1,0:T(8,128)(2,1)S(1)}, bf16[3,64,256]{2,1,0:T(8,128)(2,1)S(1)}, u32[]{:S(2)}, u32[]{:S(2)}) collective-permute-start(bf16[3,64,256]{2,1,0:T(8,128)(2,1)S(1)} %collective-permute-done.13.s2), channel_id=1, source_target_pairs={{0,4},{4,0},{1,5},{5,1},{2,6},{6,2},{3,7},{7,3},{8,12},{12,8},{9,1... | collective-permute-start | bytes 294920 | tf_op jit(solution)/shard_map/ppermute | solution.py:64
  86.7 7.2 %collective-permute-start.17 = (s16[208,256]{1,0:T(8,128)(2,1)S(1)}, s16[208,256]{1,0:T(8,128)(2,1)S(1)}, u32[]{:S(2)}, u32[]{:S(2)}) collective-permute-start(s16[208,256]{1,0:T(8,128)(2,1)S(1)} %spread_far.2), channel_id=1, source_target_pairs={{0,2},{1,3},{2,0},{3,1},{4,6},{5,7},{6,4},{7,5},{8,10},{9,11},{10,... | collective-permute-start | bytes 319496 | tf_op jit(solution)/shard_map/ppermute | solution.py:54
  91.8 4.8 %collective-permute-start.18 = (s16[208,256]{1,0:T(8,128)(2,1)S(1)}, s16[208,256]{1,0:T(8,128)(2,1)S(1)}, u32[]{:S(2)}, u32[]{:S(2)}) collective-permute-start(s16[208,256]{1,0:T(8,128)(2,1)S(1)} %get-tuple-element.71), channel_id=1, source_target_pairs={{0,3},{1,0},{2,1},{3,2},{4,5},{5,6},{6,7},{7,4},{8,11},{9,8},{10,9... | collective-permute-start | bytes 319496 | tf_op jit(solution)/shard_map/ppermute | solution.py:50
  93.7 5.9 %collective-permute-start.19 = (s16[208,256]{1,0:T(8,128)(2,1)S(1)}, s16[208,256]{1,0:T(8,128)(2,1)S(1)}, u32[]{:S(2)}, u32[]{:S(2)}) collective-permute-start(s16[208,256]{1,0:T(8,128)(2,1)S(1)} %get-tuple-element.72), channel_id=1, source_target_pairs={{0,1},{1,2},{2,3},{3,0},{4,7},{5,4},{6,5},{7,6},{8,9},{9,10},{10,1... | collective-permute-start | bytes 319496 | tf_op jit(solution)/shard_map/ppermute | solution.py:50
  99.8 6.3 %collective-permute-start.20 = (bf16[3,64,256]{2,1,0:T(8,128)(2,1)S(1)}, bf16[3,64,256]{2,1,0:T(8,128)(2,1)S(1)}, u32[]{:S(2)}, u32[]{:S(2)}) collective-permute-start(bf16[3,64,256]{2,1,0:T(8,128)(2,1)S(1)} %fusion.11.s0), channel_id=1, source_target_pairs={{8,0},{124,4},{16,8},{4,12},{24,16},{12,20},{32,24},{20,28},{40,32... | collective-permute-start | bytes 294920 | tf_op jit(solution)/shard_map/ppermute | solution.py:58
  103.1 3.0 %collective-permute-start.23 = (bf16[3,64,256]{2,1,0:T(8,128)(2,1)S(1)}, bf16[3,64,256]{2,1,0:T(8,128)(2,1)S(1)}, u32[]{:S(2)}, u32[]{:S(2)}) collective-permute-start(bf16[3,64,256]{2,1,0:T(8,128)(2,1)S(1)} %fusion.11.s0), channel_id=1, source_target_pairs={{0,4},{4,0},{1,5},{5,1},{2,6},{6,2},{3,7},{7,3},{8,12},{12,8},{9,1... | collective-permute-start | bytes 294920 | tf_op jit(solution)/shard_map/ppermute | solution.py:64
  103.1 7.9 %collective-permute-start.21 = (bf16[3,64,256]{2,1,0:T(8,128)(2,1)S(1)}, bf16[3,64,256]{2,1,0:T(8,128)(2,1)S(1)}, u32[]{:S(2)}, u32[]{:S(2)}) collective-permute-start(bf16[3,64,256]{2,1,0:T(8,128)(2,1)S(1)} %fusion.11.s0), channel_id=1, source_target_pairs={{120,0},{12,4},{0,8},{20,12},{8,16},{28,20},{16,24},{36,28},{24,32... | collective-permute-start | bytes 294920 | tf_op jit(solution)/shard_map/ppermute | solution.py:58
  106.1 4.9 %collective-permute-start.22 = (bf16[3,64,256]{2,1,0:T(8,128)(2,1)S(1)}, bf16[3,64,256]{2,1,0:T(8,128)(2,1)S(1)}, u32[]{:S(2)}, u32[]{:S(2)}) collective-permute-start(bf16[3,64,256]{2,1,0:T(8,128)(2,1)S(1)} %collective-permute-done.20.s2), channel_id=1, source_target_pairs={{0,4},{4,0},{1,5},{5,1},{2,6},{6,2},{3,7},{7,3},{8,12},{12,8},{9,1... | collective-permute-start | bytes 294920 | tf_op jit(solution)/shard_map/ppermute | solution.py:64
  112.4 6.5 %collective-permute-start.24 = (s16[208,256]{1,0:T(8,128)(2,1)S(1)}, s16[208,256]{1,0:T(8,128)(2,1)S(1)}, u32[]{:S(2)}, u32[]{:S(2)}) collective-permute-start(s16[208,256]{1,0:T(8,128)(2,1)S(1)} %spread_far.3), channel_id=1, source_target_pairs={{0,2},{1,3},{2,0},{3,1},{4,6},{5,7},{6,4},{7,5},{8,10},{9,11},{10,... | collective-permute-start | bytes 319496 | tf_op jit(solution)/shard_map/ppermute | solution.py:54
  115.0 5.2 %collective-permute-start.25 = (s16[208,256]{1,0:T(8,128)(2,1)S(1)}, s16[208,256]{1,0:T(8,128)(2,1)S(1)}, u32[]{:S(2)}, u32[]{:S(2)}) collective-permute-start(s16[208,256]{1,0:T(8,128)(2,1)S(1)} %get-tuple-element.75), channel_id=1, source_target_pairs={{0,3},{1,0},{2,1},{3,2},{4,5},{5,6},{6,7},{7,4},{8,11},{9,8},{10,9... | collective-permute-start | bytes 319496 | tf_op jit(solution)/shard_map/ppermute | solution.py:50
  117.0 5.9 %collective-permute-start.26 = (s16[208,256]{1,0:T(8,128)(2,1)S(1)}, s16[208,256]{1,0:T(8,128)(2,1)S(1)}, u32[]{:S(2)}, u32[]{:S(2)}) collective-permute-start(s16[208,256]{1,0:T(8,128)(2,1)S(1)} %get-tuple-element.76), channel_id=1, source_target_pairs={{0,1},{1,2},{2,3},{3,0},{4,7},{5,4},{6,5},{7,6},{8,9},{9,10},{10,1... | collective-permute-start | bytes 319496 | tf_op jit(solution)/shard_map/ppermute | solution.py:50

commit v7 on v5

--- a/solution.py
+++ b/solution.py
@@ -34,6 +34,7 @@
 BEFORE = 250
 LISTS = 256
 STEP = 9
+CODED = 32000.0
 SPARE = NX * BLK
 SUMS = CH + 8
 IDS = 16
@@ -269,13 +270,53 @@
     tiles(3, list_ref, rows, cols, states, w3_ref, sum_ref)
 
 
+def power_of(values):
+    return jnp.ceil(jnp.log2(jnp.maximum(values, 1e-30)))
+
+
+def put_coded(ref, sums, first, degrees=False):
+    row = lax.broadcasted_iota(jnp.int32, (16, ROWS), 0)
+    extra = jnp.zeros((16, ROWS), F32)
+    for i in range(BLK):
+        values = sums[first + i, :CH]
+        power = power_of(jnp.max(jnp.abs(values), axis=0, keepdims=True))
+        coded = jnp.floor(values * (jnp.exp2(-power) * CODED) + 0.5)
+        ref[i * CH : (i + 1) * CH] = coded.astype(jnp.int32).astype(jnp.int16)
+        extra = jnp.where(row == i, power, extra)
+        if degrees:
+            degree = jnp.sum(sums[first + i, CH:], axis=0, keepdims=True)
+            power = power_of(degree)
+            scaled = degree * (jnp.exp2(-power) * CODED)
+            high = jnp.floor(scaled + 0.5)
+            low = jnp.floor((scaled - high) * CODED + 0.5)
+            for at, part in enumerate((power, high, low)):
+                extra = jnp.where(row == (at + 1) * BLK + i, part, extra)
+    ref[BLK * CH :] = extra.astype(jnp.int32).astype(jnp.int16)
+
+
+def uncoded(v):
+    values = v[: BLK * CH].astype(F32).reshape(BLK, CH, ROWS)
+    powers = v[BLK * CH : BLK * CH + BLK].astype(F32)
+    return values * (jnp.exp2(powers) * (1.0 / CODED))[:, None, :]
+
+
+def uncoded_degrees(v):
+    power, high, low = (
+        v[BLK * CH + at * BLK : BLK * CH + (at + 1) * BLK].astype(F32) for at in (1, 2, 3)
+    )
+    return (high + low * (1.0 / CODED)) * (jnp.exp2(power) * (1.0 / CODED))
+
+
 def last_columns(list_ref, rows, c4, given, w_ref, outs, sums, states, first, low, high):
     sums[...] = given[...]
     for j in range(BLK):
         states[j] = c4[BLK * ROWS :, j * ROWS : (j + 1) * ROWS]
     tiles(4, list_ref, rows, c4, states, w_ref, sums, low, high, BASE[4])
     for at, ref in enumerate(outs):
-        ref[...] = sums[(first + at) * BLK : (first + at + 1) * BLK]
+        if first + at:
+            put_coded(ref, sums, (first + at) * BLK, degrees=True)
+        else:
+            ref[...] = sums[:BLK]
 
 
 def build_far(list_ref, rows, c4, given, w_ref, far, sums, states):
@@ -344,7 +385,7 @@
         states[(at + 2) * BLK : (at + 3) * BLK] = ref[...]
     for chunk, w_ref in ((3, w3), (4, w4)):
         add_spread(chunk, list_ref, w_ref, states, sums, list_ref[BEFORE + chunk], list_ref[TOTALS + chunk])
-    far[...] = sums[3 * BLK : SPARE]
+    put_coded(far, sums, 3 * BLK)
 
 
 def spread_rest(near_ref, list_ref, w1, w3, w4, s2, s3, s4, given, own, back, fore, sums, states):
@@ -354,20 +395,22 @@
     add_spread(1, near_ref, w1, states, sums, 0, near_ref[TOTALS + 1])
     for chunk, w_ref in ((3, w3), (4, w4)):
         add_spread(chunk, list_ref, w_ref, states, sums, 0, list_ref[BEFORE + chunk])
-    for at, ref in enumerate((own, back, fore)):
-        ref[...] = sums[at * BLK : (at + 1) * BLK]
+    own[...] = sums[:BLK]
+    put_coded(back, sums, BLK)
+    put_coded(fore, sums, 2 * BLK)
 
 
 def spread(lists, weights, states):
     sums = ((SPARE + 1, CH, ROWS), F32)
     held = ((5 * BLK, CH, ROWS), BF16)
-    part = ((BLK, CH, ROWS), F32)
+    part = ((BLK * CH + 16, ROWS), jnp.int16)
     w0, w1, w2, w3, w4_far, w4 = weights
     (near,) = build(spread_near, 3, [sums], [held], *lists, w0, w2, *states[:2])
     (far,) = build(spread_far, 4, [part], [sums, held], lists[1], w3, w4_far, *states[2:], near)
     near, _ = lax.optimization_barrier((near, far))
     return *build(
-        spread_rest, 4, [part] * (NX - 1), [sums, held], *lists, w1, w3, w4, *states[2:], near
+        spread_rest, 4, [((BLK, CH, ROWS), F32), part, part], [sums, held],
+        *lists, w1, w3, w4, *states[2:], near,
     ), far
 
 
@@ -379,9 +422,13 @@
     return [v, partner, one, other, across]
 
 
-def reduce_rows(own, back, fore, far):
-    first = lax.optimization_barrier(own + across_x(far))
-    return first + along_x(back, -1) + along_x(fore, 1)
+def exchange_rows(back, fore, far):
+    return across_x(far), along_x(back, -1), along_x(fore, 1)
+
+
+def add_rows(own, parts):
+    first = lax.optimization_barrier(own + uncoded(parts[0]))
+    return first + uncoded(parts[1]) + uncoded(parts[2])
 
 
 def local(embeddings, seeds, neighbours):
@@ -421,24 +468,25 @@
         build_2, 4, [weights_of(2), weights_of(3), SUM_BUF, rows_of(12)], [],
         lists, rows, fore_two, far_two, far_one, cols, states, sums,
     )
-    part = ((BLK, SUMS, ROWS), F32)
+    part = ((BLK * CH + 16, ROWS), jnp.int16)
     scratch = [SUM_BUF, ((BLK, CH, ROWS), BF16)]
     w4_far, far = build(build_far, 4, [weights_of(4), part], scratch, lists, rows, beside, sums)
     w4, own, back, fore = build(
-        build_rest, 4, [weights_of(4)] + [part] * (NX - 1), scratch,
+        build_rest, 4, [weights_of(4), ((BLK, SUMS, ROWS), F32), part, part], scratch,
         lists, rows, beside, after(sums, far),
     )
     lists = [near, lists]
     weights = [w0, w1, w2, w3, w4_far, w4]
 
-    total = reduce_rows(own, back, fore, far)
-    scale = ALPHA / jnp.sum(total[:, CH:], axis=1, keepdims=True)
+    parts = exchange_rows(back, fore, far)
+    degree = jnp.sum(own[:, CH:], axis=1) + sum(uncoded_degrees(p) for p in parts)
+    scale = (ALPHA / degree)[:, None, :]
     prior = (1.0 - ALPHA) * seeds_t
-    scores = total[:, :CH] * scale + prior
+    scores = add_rows(own[:, :CH], parts) * scale + prior
     for _ in range(ITERS - 1):
         states = wide_exchange(scores.astype(BF16))
-        total = reduce_rows(*spread(lists, weights, states))
-        scores = total * scale + prior
+        own, *parts = spread(lists, weights, states)
+        scores = add_rows(own, exchange_rows(*parts)) * scale + prior
     return jnp.swapaxes(scores, 1, 2)
 
 

time: 127 us -> 121 us (0.953); the launches traced: 127 us -> 119 us
  starting transfers between devices: 43.3 us -> 35.5 us
  waiting for transfers between devices: 42.8 us -> 41.5 us
    ppermute x6, starting transfers between devices: 18 us -> 12.5 us  [from_wide(): lax.ppermute(v, WIDE, [((i + (2 * sign if i % 2 == 0 else -2 * sign)) % N...]
    ppermute x3, starting transfers between devices: 7.22 us -> 3.37 us  [across_x(): return lax.ppermute(v, 'x', [(x, (x + 2) % NX) for x in range(NX)])]
    ppermute x3, waiting for transfers between devices: 4.61 us -> 2.79 us  [across_x(): return lax.ppermute(v, 'x', [(x, (x + 2) % NX) for x in range(NX)])]
  transfers between devices with their start and end apart: 27 -> 27, of which waited for: 15 -> 14; matrix products, arithmetic and copies ran while one was open for 0% -> 0% of each run, Pallas kernels for 26% -> 28%
where the time goes in v7:
time: 121 us; the launch traced here: 119 us
  waiting for transfers between devices  41.5 us (34%)
  Pallas kernels  39.3 us (32%)
  starting transfers between devices  35.5 us (29%)
  other arithmetic  2.29 us (2%)
    pallas_call x11, Pallas kernels, build(): pl.pallas_call(kernel, out_shape=[jax.ShapeDtypeStruct(*o) for o in outs]...  32.5 us
    ppermute x12, waiting for transfers between devices, along_x(): return lax.ppermute(v, ('c', 'x'), pairs)  23.8 us
    ppermute x12, starting transfers between devices, along_x(): return lax.ppermute(v, ('c', 'x'), pairs)  16.8 us
    ppermute x6, waiting for transfers between devices, from_wide(): lax.ppermute(v, WIDE, [((i + (2 * sign if i % 2 == 0 else -2 * sign)) % N...  14.9 us
    ppermute x6, starting transfers between devices, from_wide(): lax.ppermute(v, WIDE, [((i + (2 * sign if i % 2 == 0 else -2 * sign)) % N...  12.5 us
    pallas_call x2, Pallas kernels, make_plan(): pl.pallas_call(functools.partial(plan_kernel, groups), out_shape=jax.Shap...  4.99 us
    ppermute x3, starting transfers between devices, across_x(): return lax.ppermute(v, 'x', [(x, (x + 2) % NX) for x in range(NX)])  3.37 us
    ppermute x3, waiting for transfers between devices, across_x(): return lax.ppermute(v, 'x', [(x, (x + 2) % NX) for x in range(NX)])  2.79 us
  transfers between devices with their start and end apart: 27, of which 14 were waited for; matrix products, arithmetic and copies ran while one was open for 0% of the time, Pallas kernels for 28%

profile of v7, /device:TPU:0, one launch (start us, length us, event | category | flops | bytes accessed | tf_op | source)
XLA Modules:
  0.0 119.0 jit_solution(2187992356129698070)
XLA Ops:
  0.0 0.7 shift-right-arithmetic_convert_fusion
  0.8 1.7 %prep.1 = (bf16[1552,256]{1,0:T(8,128)(2,1)S(1)}, bf16[832,768]{1,0:T(8,128)(2,1)S(1)}) custom-call(bf16[3,256,768]{2,1,0:T(8,128)(2,1)} %emb_hbm.1, f32[3,64,256]{2,1,0:T(8,128)} %bitcast.24, bf16[16,256]{1,0:T(8,128)(2,1)S(1)} %fusion.23.ids_ref), custom_call_target="tpu_custom_call" | custom-call | flops 1000 | bytes 1000 | tf_op jit(solution)/shard_map/prep/pallas_call | solution.py:88
  2.5 1.6 %collective-permute-start = (bf16[1552,256]{1,0:T(8,128)(2,1)S(1)}, bf16[1552,256]{1,0:T(8,128)(2,1)S(1)}, u32[]{:S(2)}, u32[]{:S(2)}) collective-permute-start(bf16[1552,256]{1,0:T(8,128)(2,1)S(1)} %get-tuple-element.52.r0), channel_id=1, source_target_pairs={{0,1},{1,2},{2,3},{3,0},{4,7},{5,4},{6,5},{7,6},{8,9},{9,10},{10,1... | collective-permute-start | bytes 2383880 | tf_op jit(solution)/shard_map/ppermute | solution.py:50
  4.3 1.6 %collective-permute-start.2 = (bf16[784,256]{1,0:T(8,128)(2,1)S(1)}, bf16[784,256]{1,0:T(8,128)(2,1)S(1)}, u32[]{:S(2)}, u32[]{:S(2)}) collective-permute-start(bf16[784,256]{1,0:T(8,128)(2,1)S(1)} %third.1.r1), channel_id=1, source_target_pairs={{0,1},{1,2},{2,3},{3,0},{4,7},{5,4},{6,5},{7,6},{8,9},{9,10},{10,1... | collective-permute-start | bytes 1204232 | tf_op jit(solution)/shard_map/ppermute | solution.py:50
  5.9 1.7 %collective-permute-start.1 = (bf16[784,256]{1,0:T(8,128)(2,1)S(1)}, bf16[784,256]{1,0:T(8,128)(2,1)S(1)}, u32[]{:S(2)}, u32[]{:S(2)}) collective-permute-start(bf16[784,256]{1,0:T(8,128)(2,1)S(1)} %third.1.r1), channel_id=1, source_target_pairs={{0,3},{1,0},{2,1},{3,2},{4,5},{5,6},{6,7},{7,4},{8,11},{9,8},{10,9... | collective-permute-start | bytes 1204232 | tf_op jit(solution)/shard_map/ppermute | solution.py:50
  7.6 1.6 %collective-permute-start.6 = (bf16[832,768]{1,0:T(8,128)(2,1)S(1)}, bf16[832,768]{1,0:T(8,128)(2,1)S(1)}, u32[]{:S(2)}, u32[]{:S(2)}) collective-permute-start(bf16[832,768]{1,0:T(8,128)(2,1)S(1)} %get-tuple-element.46.full_ref.c0), channel_id=1, source_target_pairs={{120,0},{12,4},{0,8},{20,12},{8,16},{28,20},{16,24},{36,28},{24,32... | collective-permute-start | bytes 3833864 | tf_op jit(solution)/shard_map/ppermute | solution.py:58
  9.2 4.9 %collective-permute-start.5 = (bf16[832,768]{1,0:T(8,128)(2,1)S(1)}, bf16[832,768]{1,0:T(8,128)(2,1)S(1)}, u32[]{:S(2)}, u32[]{:S(2)}) collective-permute-start(bf16[832,768]{1,0:T(8,128)(2,1)S(1)} %get-tuple-element.46.full_ref.c0), channel_id=1, source_target_pairs={{8,0},{124,4},{16,8},{4,12},{24,16},{12,20},{32,24},{20,28},{40,32... | collective-permute-start | bytes 3833864 | tf_op jit(solution)/shard_map/ppermute | solution.py:58
  14.1 10.4 %collective-permute-done.2.r3 = bf16[784,256]{1,0:T(8,128)(2,1)S(1)} collective-permute-done((bf16[784,256]{1,0:T(8,128)(2,1)S(1)}, bf16[784,256]{1,0:T(8,128)(2,1)S(1)}, u32[]{:S(2)}, u32[]{:S(2)}) %collective-permute-start.2) | collective-permute-done | bytes 401440 | tf_op jit(solution)/shard_map/ppermute | solution.py:50
  24.9 2.9 %collective-permute-start.7 = (bf16[1552,256]{1,0:T(8,128)(2,1)S(1)}, bf16[1552,256]{1,0:T(8,128)(2,1)S(1)}, u32[]{:S(2)}, u32[]{:S(2)}) collective-permute-start(bf16[1552,256]{1,0:T(8,128)(2,1)S(1)} %get-tuple-element.52.r0), channel_id=1, source_target_pairs={{0,3},{1,0},{2,1},{3,2},{4,5},{5,6},{6,7},{7,4},{8,11},{9,8},{10,9... | collective-permute-start | bytes 2383880 | tf_op jit(solution)/shard_map/ppermute | solution.py:50
  27.9 3.0 %plan.2.list_ref.refs_1_.near_ref = s32[256]{0:T(256)S(1)} custom-call(s32[3,32]{1,0:T(4,128)S(1)} %get-tuple-element.83.refs_0_, s32[3,32]{1,0:T(4,128)S(1)} %get-tuple-element.84.refs_1_, s32[3,32]{1,0:T(4,128)S(1)} %get-tuple-element.85.refs_2_), custom_call_target="tpu_custom_call" | custom-call | flops 30000001024 | bytes 1000 | tf_op jit(solution)/shard_map/plan/pallas_call | solution.py:194
  31.0 1.3 %collective-permute-start.8 = (bf16[784,256]{1,0:T(8,128)(2,1)S(1)}, bf16[784,256]{1,0:T(8,128)(2,1)S(1)}, u32[]{:S(2)}, u32[]{:S(2)}) collective-permute-start(bf16[784,256]{1,0:T(8,128)(2,1)S(1)} %collective-permute-done.1.r4), channel_id=1, source_target_pairs={{0,3},{1,0},{2,1},{3,2},{4,5},{5,6},{6,7},{7,4},{8,11},{9,8},{10,9... | collective-permute-start | bytes 1204232 | tf_op jit(solution)/shard_map/ppermute | solution.py:50
  32.3 4.0 %build_0.1 = (bf16[44,256,256]{2,1,0:T(8,128)(2,1)S(1)}, f32[13,72,256]{2,1,0:T(8,128)S(1)}, bf16[6912,256]{1,0:T(8,128)(2,1)S(1)}) custom-call(s32[256]{0:T(256)S(1)} %plan.2.list_ref.refs_1_.near_ref, bf16[1552,256]{1,0:T(8,128)(2,1)S(1)} %get-tuple-element.52.r0, bf16[784,256]{1,0:T(8,128)(2,1)S(1)} %third.1.r1, ...), custom_call_target="tpu_custom_call" | custom-call | flops 30000001024 | bytes 1000 | tf_op jit(solution)/shard_map/build_0/pallas_call | solution.py:335
  36.3 4.4 %collective-permute-done.5.c2 = bf16[832,768]{1,0:T(8,128)(2,1)S(1)} collective-permute-done((bf16[832,768]{1,0:T(8,128)(2,1)S(1)}, bf16[832,768]{1,0:T(8,128)(2,1)S(1)}, u32[]{:S(2)}, u32[]{:S(2)}) %collective-permute-start.5) | collective-permute-done | bytes 1277984 | tf_op jit(solution)/shard_map/ppermute | solution.py:58
  40.7 2.2 %collective-permute-start.9 = (bf16[832,768]{1,0:T(8,128)(2,1)S(1)}, bf16[832,768]{1,0:T(8,128)(2,1)S(1)}, u32[]{:S(2)}, u32[]{:S(2)}) collective-permute-start(bf16[832,768]{1,0:T(8,128)(2,1)S(1)} %collective-permute-done.5.c2), channel_id=1, source_target_pairs={{0,4},{4,0},{1,5},{5,1},{2,6},{6,2},{3,7},{7,3},{8,12},{12,8},{9,1... | collective-permute-start | bytes 3833864 | tf_op jit(solution)/shard_map/ppermute | solution.py:64
  42.9 3.9 %build_1.1 = (bf16[44,256,256]{2,1,0:T(8,128)(2,1)S(1)}, f32[13,72,256]{2,1,0:T(8,128)S(1)}, bf16[3072,768]{1,0:T(8,128)(2,1)S(1)}, bf16[12,64,256]{2,1,0:T(8,128)(2,1)S(1)}) custom-call(s32[256]{0:T(256)S(1)} %plan.2.list_ref.refs_1_.near_ref, bf16[6912,256]{1,0:T(8,128)(2,1)S(1)} %get-tuple-element.47.rows.old_rows, ...), custom_call_target="tpu_custom_call" | custom-call | flops 30000001024 | bytes 1000 | tf_op jit(solution)/shard_map/build_1/pallas_call | solution.py:335
  47.0 2.0 %plan.3.list_ref = s32[256]{0:T(256)S(1)} custom-call(s32[3,32]{1,0:T(4,128)S(1)} %fusion.51.refs_0_, s32[256]{0:T(256)S(1)} %plan.2.list_ref.refs_1_.near_ref), custom_call_target="tpu_custom_call" | custom-call | flops 30000001024 | bytes 1000 | tf_op jit(solution)/shard_map/plan/pallas_call | solution.py:194
  48.9 6.9 %build_2.1 = (bf16[36,256,256]{2,1,0:T(8,128)(2,1)S(1)}, bf16[36,256,256]{2,1,0:T(8,128)(2,1)S(1)}, f32[13,72,256]{2,1,0:T(8,128)S(1)}, bf16[9216,256]{1,0:T(8,128)(2,1)S(1)}) custom-call(s32[256]{0:T(256)S(1)} %plan.3.list_ref, bf16[6912,256]{1,0:T(8,128)(2,1)S(1)} %get-tuple-element.47.rows.old_rows, bf16[1552,256]{1,0:T(8,128)(2,1)S(1)} %collective-permute-done.7.r0, ...), custom_call_target="tpu_custom_call" | custom-call | flops 30000001024 | bytes 1000 | tf_op jit(solution)/shard_map/build_2/pallas_call | solution.py:335
  55.9 1.6 %build_far.1 = (bf16[40,256,256]{2,1,0:T(8,128)(2,1)S(1)}, s16[208,256]{1,0:T(8,128)(2,1)S(1)}) custom-call(s32[256]{0:T(256)S(1)} %plan.3.list_ref, bf16[9216,256]{1,0:T(8,128)(2,1)S(1)} %get-tuple-element.57.rows, bf16[832,768]{1,0:T(8,128)(2,1)S(1)} %collective-permute-done.9.c4, f32[13,72,256]{2,1,0:T(8,128)S(1)} %get-tuple-element.61.given), custom_call_target="tpu_custom_call" | custom-call | flops 30000001024 | bytes 1000 | tf_op jit(solution)/shard_map/build_far/pallas_call | solution.py:335
  57.5 1.6 %collective-permute-start.10 = (s16[208,256]{1,0:T(8,128)(2,1)S(1)}, s16[208,256]{1,0:T(8,128)(2,1)S(1)}, u32[]{:S(2)}, u32[]{:S(2)}) collective-permute-start(s16[208,256]{1,0:T(8,128)(2,1)S(1)} %get-tuple-element.60), channel_id=1, source_target_pairs={{0,2},{1,3},{2,0},{3,1},{4,6},{5,7},{6,4},{7,5},{8,10},{9,11},{10,... | collective-permute-start | bytes 319496 | tf_op jit(solution)/shard_map/ppermute | solution.py:54
  59.1 3.1 %build_rest.1 = (bf16[40,256,256]{2,1,0:T(8,128)(2,1)S(1)}, f32[3,72,256]{2,1,0:T(8,128)S(1)}, s16[208,256]{1,0:T(8,128)(2,1)S(1)}, s16[208,256]{1,0:T(8,128)(2,1)S(1)}) custom-call(s32[256]{0:T(256)S(1)} %plan.3.list_ref, bf16[9216,256]{1,0:T(8,128)(2,1)S(1)} %get-tuple-element.57.rows, bf16[832,768]{1,0:T(8,128)(2,1)S(1)} %collective-permute-done.9.c4, ...), custom_call_target="tpu_custom_call" | custom-call | flops 30000001024 | bytes 1000 | tf_op jit(solution)/shard_map/build_rest/pallas_call | solution.py:335
  62.2 2.6 %collective-permute-start.11 = (s16[208,256]{1,0:T(8,128)(2,1)S(1)}, s16[208,256]{1,0:T(8,128)(2,1)S(1)}, u32[]{:S(2)}, u32[]{:S(2)}) collective-permute-start(s16[208,256]{1,0:T(8,128)(2,1)S(1)} %get-tuple-element.64), channel_id=1, source_target_pairs={{0,3},{1,0},{2,1},{3,2},{4,5},{5,6},{6,7},{7,4},{8,11},{9,8},{10,9... | collective-permute-start | bytes 319496 | tf_op jit(solution)/shard_map/ppermute | solution.py:50
  65.2 2.5 %collective-permute-done.11 = s16[208,256]{1,0:T(8,128)(2,1)S(1)} collective-permute-done((s16[208,256]{1,0:T(8,128)(2,1)S(1)}, s16[208,256]{1,0:T(8,128)(2,1)S(1)}, u32[]{:S(2)}, u32[]{:S(2)}) %collective-permute-start.11) | collective-permute-done | bytes 106528 | tf_op jit(solution)/shard_map/ppermute | solution.py:50
  67.7 3.0 %collective-permute-done.12 = s16[208,256]{1,0:T(8,128)(2,1)S(1)} collective-permute-done((s16[208,256]{1,0:T(8,128)(2,1)S(1)}, s16[208,256]{1,0:T(8,128)(2,1)S(1)}, u32[]{:S(2)}, u32[]{:S(2)}) %collective-permute-start.12) | collective-permute-done | bytes 106528 | tf_op jit(solution)/shard_map/ppermute | solution.py:50
  71.0 3.8 %collective-permute-start.13 = (bf16[3,64,256]{2,1,0:T(8,128)(2,1)S(1)}, bf16[3,64,256]{2,1,0:T(8,128)(2,1)S(1)}, u32[]{:S(2)}, u32[]{:S(2)}) collective-permute-start(bf16[3,64,256]{2,1,0:T(8,128)(2,1)S(1)} %fusion.15.s0), channel_id=1, source_target_pairs={{8,0},{124,4},{16,8},{4,12},{24,16},{12,20},{32,24},{20,28},{40,32... | collective-permute-start | bytes 294920 | tf_op jit(solution)/shard_map/ppermute | solution.py:58
  74.7 2.2 %collective-permute-done.13.s2 = bf16[3,64,256]{2,1,0:T(8,128)(2,1)S(1)} collective-permute-done((bf16[3,64,256]{2,1,0:T(8,128)(2,1)S(1)}, bf16[3,64,256]{2,1,0:T(8,128)(2,1)S(1)}, u32[]{:S(2)}, u32[]{:S(2)}) %collective-permute-start.13) | collective-permute-done | bytes 98336 | tf_op jit(solution)/shard_map/ppermute | solution.py:58
  76.9 0.6 collective-permute-start.15
  77.5 2.4 %spread_near.2.given = f32[13,64,256]{2,1,0:T(8,128)S(1)} custom-call(s32[256]{0:T(256)S(1)} %plan.2.list_ref.refs_1_.near_ref, s32[256]{0:T(256)S(1)} %plan.3.list_ref, bf16[44,256,256]{2,1,0:T(8,128)(2,1)S(1)} %get-tuple-element.66.w0, bf16[36,256,256]{2,1,0:T(8,128)(2,1)S(1)} %get-tuple-element.67.w2, bf16[3,64,256]{2,1,0:T(8,128)(2,1)S(1)} %fusion.15.s0, ...), custom_call_target="tpu_custom_call" | custom-call | flops 30000001024 | bytes 1000 | tf_op jit(solution)/shard_map/spread_near/pallas_call | solution.py:335
  79.9 2.8 %collective-permute-done.14.s3 = bf16[3,64,256]{2,1,0:T(8,128)(2,1)S(1)} collective-permute-done((bf16[3,64,256]{2,1,0:T(8,128)(2,1)S(1)}, bf16[3,64,256]{2,1,0:T(8,128)(2,1)S(1)}, u32[]{:S(2)}, u32[]{:S(2)}) %collective-permute-start.14) | collective-permute-done | bytes 98336 | tf_op jit(solution)/shard_map/ppermute | solution.py:58
  82.7 1.3 %spread_far.2 = s16[208,256]{1,0:T(8,128)(2,1)S(1)} custom-call(s32[256]{0:T(256)S(1)} %plan.3.list_ref, bf16[36,256,256]{2,1,0:T(8,128)(2,1)S(1)} %get-tuple-element.56.w3, bf16[40,256,256]{2,1,0:T(8,128)(2,1)S(1)} %get-tuple-element.68.w4, bf16[3,64,256]{2,1,0:T(8,128)(2,1)S(1)} %collective-permute-done.13.s2, ...), custom_call_target="tpu_custom_call" | custom-call | flops 30000001024 | bytes 1000 | tf_op jit(solution)/shard_map/spread_far/pallas_call | solution.py:335
  84.0 1.3 %collective-permute-start.17 = (s16[208,256]{1,0:T(8,128)(2,1)S(1)}, s16[208,256]{1,0:T(8,128)(2,1)S(1)}, u32[]{:S(2)}, u32[]{:S(2)}) collective-permute-start(s16[208,256]{1,0:T(8,128)(2,1)S(1)} %spread_far.2), channel_id=1, source_target_pairs={{0,2},{1,3},{2,0},{3,1},{4,6},{5,7},{6,4},{7,5},{8,10},{9,11},{10,... | collective-permute-start | bytes 319496 | tf_op jit(solution)/shard_map/ppermute | solution.py:54
  85.3 2.7 %spread_rest.2 = (f32[3,64,256]{2,1,0:T(8,128)S(1)}, s16[208,256]{1,0:T(8,128)(2,1)S(1)}, s16[208,256]{1,0:T(8,128)(2,1)S(1)}) custom-call(s32[256]{0:T(256)S(1)} %plan.2.list_ref.refs_1_.near_ref, s32[256]{0:T(256)S(1)} %plan.3.list_ref, bf16[44,256,256]{2,1,0:T(8,128)(2,1)S(1)} %get-tuple-element.51.w1, bf16[36,256,256]{2,1,0:T(8,128)(2,1)S(1)} %get-tuple-element.56.w3, ...), custom_call_target="tpu_custom_call" | custom-call | flops 30000001024 | bytes 1000 | tf_op jit(solution)/shard_map/spread_rest/pallas_call | solution.py:335
  88.0 1.9 %collective-permute-start.18 = (s16[208,256]{1,0:T(8,128)(2,1)S(1)}, s16[208,256]{1,0:T(8,128)(2,1)S(1)}, u32[]{:S(2)}, u32[]{:S(2)}) collective-permute-start(s16[208,256]{1,0:T(8,128)(2,1)S(1)} %get-tuple-element.71), channel_id=1, source_target_pairs={{0,3},{1,0},{2,1},{3,2},{4,5},{5,6},{6,7},{7,4},{8,11},{9,8},{10,9... | collective-permute-start | bytes 319496 | tf_op jit(solution)/shard_map/ppermute | solution.py:50
  90.1 1.2 collective-permute-done.17
  91.4 1.4 %collective-permute-done.18 = s16[208,256]{1,0:T(8,128)(2,1)S(1)} collective-permute-done((s16[208,256]{1,0:T(8,128)(2,1)S(1)}, s16[208,256]{1,0:T(8,128)(2,1)S(1)}, u32[]{:S(2)}, u32[]{:S(2)}) %collective-permute-start.18) | collective-permute-done | bytes 106528 | tf_op jit(solution)/shard_map/ppermute | solution.py:50
  92.8 3.0 %collective-permute-done.19 = s16[208,256]{1,0:T(8,128)(2,1)S(1)} collective-permute-done((s16[208,256]{1,0:T(8,128)(2,1)S(1)}, s16[208,256]{1,0:T(8,128)(2,1)S(1)}, u32[]{:S(2)}, u32[]{:S(2)}) %collective-permute-start.19) | collective-permute-done | bytes 106528 | tf_op jit(solution)/shard_map/ppermute | solution.py:50
  96.0 2.3 %collective-permute-start.20 = (bf16[3,64,256]{2,1,0:T(8,128)(2,1)S(1)}, bf16[3,64,256]{2,1,0:T(8,128)(2,1)S(1)}, u32[]{:S(2)}, u32[]{:S(2)}) collective-permute-start(bf16[3,64,256]{2,1,0:T(8,128)(2,1)S(1)} %fusion.9.s0), channel_id=1, source_target_pairs={{8,0},{124,4},{16,8},{4,12},{24,16},{12,20},{32,24},{20,28},{40,32... | collective-permute-start | bytes 294920 | tf_op jit(solution)/shard_map/ppermute | solution.py:58
  98.2 3.0 %collective-permute-done.20.s2 = bf16[3,64,256]{2,1,0:T(8,128)(2,1)S(1)} collective-permute-done((bf16[3,64,256]{2,1,0:T(8,128)(2,1)S(1)}, bf16[3,64,256]{2,1,0:T(8,128)(2,1)S(1)}, u32[]{:S(2)}, u32[]{:S(2)}) %collective-permute-start.20) | collective-permute-done | bytes 98336 | tf_op jit(solution)/shard_map/ppermute | solution.py:58
  101.3 2.4 %spread_near.3.given = f32[13,64,256]{2,1,0:T(8,128)S(1)} custom-call(s32[256]{0:T(256)S(1)} %plan.2.list_ref.refs_1_.near_ref, s32[256]{0:T(256)S(1)} %plan.3.list_ref, bf16[44,256,256]{2,1,0:T(8,128)(2,1)S(1)} %get-tuple-element.66.w0, bf16[36,256,256]{2,1,0:T(8,128)(2,1)S(1)} %get-tuple-element.67.w2, bf16[3,64,256]{2,1,0:T(8,128)(2,1)S(1)} %fusion.9.s0, ...), custom_call_target="tpu_custom_call" | custom-call | flops 30000001024 | bytes 1000 | tf_op jit(solution)/shard_map/spread_near/pallas_call | solution.py:335
  103.6 2.5 %collective-permute-done.21.s3 = bf16[3,64,256]{2,1,0:T(8,128)(2,1)S(1)} collective-permute-done((bf16[3,64,256]{2,1,0:T(8,128)(2,1)S(1)}, bf16[3,64,256]{2,1,0:T(8,128)(2,1)S(1)}, u32[]{:S(2)}, u32[]{:S(2)}) %collective-permute-start.21) | collective-permute-done | bytes 98336 | tf_op jit(solution)/shard_map/ppermute | solution.py:58
  106.2 1.3 %spread_far.3 = s16[208,256]{1,0:T(8,128)(2,1)S(1)} custom-call(s32[256]{0:T(256)S(1)} %plan.3.list_ref, bf16[36,256,256]{2,1,0:T(8,128)(2,1)S(1)} %get-tuple-element.56.w3, bf16[40,256,256]{2,1,0:T(8,128)(2,1)S(1)} %get-tuple-element.68.w4, bf16[3,64,256]{2,1,0:T(8,128)(2,1)S(1)} %collective-permute-done.20.s2, ...), custom_call_target="tpu_custom_call" | custom-call | flops 30000001024 | bytes 1000 | tf_op jit(solution)/shard_map/spread_far/pallas_call | solution.py:335
  107.5 0.5 collective-permute-start.24
  108.0 2.7 %spread_rest.3 = (f32[3,64,256]{2,1,0:T(8,128)S(1)}, s16[208,256]{1,0:T(8,128)(2,1)S(1)}, s16[208,256]{1,0:T(8,128)(2,1)S(1)}) custom-call(s32[256]{0:T(256)S(1)} %plan.2.list_ref.refs_1_.near_ref, s32[256]{0:T(256)S(1)} %plan.3.list_ref, bf16[44,256,256]{2,1,0:T(8,128)(2,1)S(1)} %get-tuple-element.51.w1, bf16[36,256,256]{2,1,0:T(8,128)(2,1)S(1)} %get-tuple-element.56.w3, ...), custom_call_target="tpu_custom_call" | custom-call | flops 30000001024 | bytes 1000 | tf_op jit(solution)/shard_map/spread_rest/pallas_call | solution.py:335
  110.8 1.6 %collective-permute-start.25 = (s16[208,256]{1,0:T(8,128)(2,1)S(1)}, s16[208,256]{1,0:T(8,128)(2,1)S(1)}, u32[]{:S(2)}, u32[]{:S(2)}) collective-permute-start(s16[208,256]{1,0:T(8,128)(2,1)S(1)} %get-tuple-element.75), channel_id=1, source_target_pairs={{0,3},{1,0},{2,1},{3,2},{4,5},{5,6},{6,7},{7,4},{8,11},{9,8},{10,9... | collective-permute-start | bytes 319496 | tf_op jit(solution)/shard_map/ppermute | solution.py:50
  112.3 0.6 collective-permute-start.26
  112.9 1.6 %collective-permute-done.24 = s16[208,256]{1,0:T(8,128)(2,1)S(1)} collective-permute-done((s16[208,256]{1,0:T(8,128)(2,1)S(1)}, s16[208,256]{1,0:T(8,128)(2,1)S(1)}, u32[]{:S(2)}, u32[]{:S(2)}) %collective-permute-start.24) | collective-permute-done | bytes 106528 | tf_op jit(solution)/shard_map/ppermute | solution.py:54
  114.6 0.9 collective-permute-done.25
  115.6 2.7 %collective-permute-done.26 = s16[208,256]{1,0:T(8,128)(2,1)S(1)} collective-permute-done((s16[208,256]{1,0:T(8,128)(2,1)S(1)}, s16[208,256]{1,0:T(8,128)(2,1)S(1)}, u32[]{:S(2)}, u32[]{:S(2)}) %collective-permute-start.26) | collective-permute-done | bytes 106528 | tf_op jit(solution)/shard_map/ppermute | solution.py:50
  118.3 0.8 fusion.3
  (53 shorter events, 2.1 us)
Async XLA Ops:
  2.5 22.0 %collective-permute-start = (bf16[1552,256]{1,0:T(8,128)(2,1)S(1)}, bf16[1552,256]{1,0:T(8,128)(2,1)S(1)}, u32[]{:S(2)}, u32[]{:S(2)}) collective-permute-start(bf16[1552,256]{1,0:T(8,128)(2,1)S(1)} %get-tuple-element.52.r0), channel_id=1, source_target_pairs={{0,1},{1,2},{2,3},{3,0},{4,7},{5,4},{6,5},{7,6},{8,9},{9,10},{10,1... | collective-permute-start | bytes 2383880 | tf_op jit(solution)/shard_map/ppermute | solution.py:50
  4.3 20.2 %collective-permute-start.2 = (bf16[784,256]{1,0:T(8,128)(2,1)S(1)}, bf16[784,256]{1,0:T(8,128)(2,1)S(1)}, u32[]{:S(2)}, u32[]{:S(2)}) collective-permute-start(bf16[784,256]{1,0:T(8,128)(2,1)S(1)} %third.1.r1), channel_id=1, source_target_pairs={{0,1},{1,2},{2,3},{3,0},{4,7},{5,4},{6,5},{7,6},{8,9},{9,10},{10,1... | collective-permute-start | bytes 1204232 | tf_op jit(solution)/shard_map/ppermute | solution.py:50
  5.9 18.6 %collective-permute-start.1 = (bf16[784,256]{1,0:T(8,128)(2,1)S(1)}, bf16[784,256]{1,0:T(8,128)(2,1)S(1)}, u32[]{:S(2)}, u32[]{:S(2)}) collective-permute-start(bf16[784,256]{1,0:T(8,128)(2,1)S(1)} %third.1.r1), channel_id=1, source_target_pairs={{0,3},{1,0},{2,1},{3,2},{4,5},{5,6},{6,7},{7,4},{8,11},{9,8},{10,9... | collective-permute-start | bytes 1204232 | tf_op jit(solution)/shard_map/ppermute | solution.py:50
  7.6 35.2 %collective-permute-start.6 = (bf16[832,768]{1,0:T(8,128)(2,1)S(1)}, bf16[832,768]{1,0:T(8,128)(2,1)S(1)}, u32[]{:S(2)}, u32[]{:S(2)}) collective-permute-start(bf16[832,768]{1,0:T(8,128)(2,1)S(1)} %get-tuple-element.46.full_ref.c0), channel_id=1, source_target_pairs={{120,0},{12,4},{0,8},{20,12},{8,16},{28,20},{16,24},{36,28},{24,32... | collective-permute-start | bytes 3833864 | tf_op jit(solution)/shard_map/ppermute | solution.py:58
  9.2 31.5 %collective-permute-start.5 = (bf16[832,768]{1,0:T(8,128)(2,1)S(1)}, bf16[832,768]{1,0:T(8,128)(2,1)S(1)}, u32[]{:S(2)}, u32[]{:S(2)}) collective-permute-start(bf16[832,768]{1,0:T(8,128)(2,1)S(1)} %get-tuple-element.46.full_ref.c0), channel_id=1, source_target_pairs={{8,0},{124,4},{16,8},{4,12},{24,16},{12,20},{32,24},{20,28},{40,32... | collective-permute-start | bytes 3833864 | tf_op jit(solution)/shard_map/ppermute | solution.py:58
  24.5 22.3 %collective-permute-start.3 = (bf16[1552,256]{1,0:T(8,128)(2,1)S(1)}, bf16[1552,256]{1,0:T(8,128)(2,1)S(1)}, u32[]{:S(2)}, u32[]{:S(2)}) collective-permute-start(bf16[1552,256]{1,0:T(8,128)(2,1)S(1)} %collective-permute-done.r2), channel_id=1, source_target_pairs={{0,1},{1,2},{2,3},{3,0},{4,7},{5,4},{6,5},{7,6},{8,9},{9,10},{10,1... | collective-permute-start | bytes 2383880 | tf_op jit(solution)/shard_map/ppermute | solution.py:50
  24.9 24.0 %collective-permute-start.7 = (bf16[1552,256]{1,0:T(8,128)(2,1)S(1)}, bf16[1552,256]{1,0:T(8,128)(2,1)S(1)}, u32[]{:S(2)}, u32[]{:S(2)}) collective-permute-start(bf16[1552,256]{1,0:T(8,128)(2,1)S(1)} %get-tuple-element.52.r0), channel_id=1, source_target_pairs={{0,3},{1,0},{2,1},{3,2},{4,5},{5,6},{6,7},{7,4},{8,11},{9,8},{10,9... | collective-permute-start | bytes 2383880 | tf_op jit(solution)/shard_map/ppermute | solution.py:50
  27.8 3.2 %collective-permute-start.4 = (bf16[832,768]{1,0:T(8,128)(2,1)S(1)}, bf16[832,768]{1,0:T(8,128)(2,1)S(1)}, u32[]{:S(2)}, u32[]{:S(2)}) collective-permute-start(bf16[832,768]{1,0:T(8,128)(2,1)S(1)} %get-tuple-element.46.full_ref.c0), channel_id=1, source_target_pairs={{0,4},{4,0},{1,5},{5,1},{2,6},{6,2},{3,7},{7,3},{8,12},{12,8},{9,1... | collective-permute-start | bytes 3833864 | tf_op jit(solution)/shard_map/ppermute | solution.py:64
  31.0 18.0 %collective-permute-start.8 = (bf16[784,256]{1,0:T(8,128)(2,1)S(1)}, bf16[784,256]{1,0:T(8,128)(2,1)S(1)}, u32[]{:S(2)}, u32[]{:S(2)}) collective-permute-start(bf16[784,256]{1,0:T(8,128)(2,1)S(1)} %collective-permute-done.1.r4), channel_id=1, source_target_pairs={{0,3},{1,0},{2,1},{3,2},{4,5},{5,6},{6,7},{7,4},{8,11},{9,8},{10,9... | collective-permute-start | bytes 1204232 | tf_op jit(solution)/shard_map/ppermute | solution.py:50
  40.7 15.2 %collective-permute-start.9 = (bf16[832,768]{1,0:T(8,128)(2,1)S(1)}, bf16[832,768]{1,0:T(8,128)(2,1)S(1)}, u32[]{:S(2)}, u32[]{:S(2)}) collective-permute-start(bf16[832,768]{1,0:T(8,128)(2,1)S(1)} %collective-permute-done.5.c2), channel_id=1, source_target_pairs={{0,4},{4,0},{1,5},{5,1},{2,6},{6,2},{3,7},{7,3},{8,12},{12,8},{9,1... | collective-permute-start | bytes 3833864 | tf_op jit(solution)/shard_map/ppermute | solution.py:64
  57.5 13.3 %copy-start = (f32[3,256,64]{1,2,0:T(8,128)S(1)}, f32[3,256,64]{1,2,0:T(8,128)}, u32[]{:S(2)}) copy-start(f32[3,256,64]{1,2,0:T(8,128)} %param.4) | copy-start | bytes 589828
  57.5 7.7 %collective-permute-start.10 = (s16[208,256]{1,0:T(8,128)(2,1)S(1)}, s16[208,256]{1,0:T(8,128)(2,1)S(1)}, u32[]{:S(2)}, u32[]{:S(2)}) collective-permute-start(s16[208,256]{1,0:T(8,128)(2,1)S(1)} %get-tuple-element.60), channel_id=1, source_target_pairs={{0,2},{1,3},{2,0},{3,1},{4,6},{5,7},{6,4},{7,5},{8,10},{9,11},{10,... | collective-permute-start | bytes 319496 | tf_op jit(solution)/shard_map/ppermute | solution.py:54
  62.2 5.5 %collective-permute-start.11 = (s16[208,256]{1,0:T(8,128)(2,1)S(1)}, s16[208,256]{1,0:T(8,128)(2,1)S(1)}, u32[]{:S(2)}, u32[]{:S(2)}) collective-permute-start(s16[208,256]{1,0:T(8,128)(2,1)S(1)} %get-tuple-element.64), channel_id=1, source_target_pairs={{0,3},{1,0},{2,1},{3,2},{4,5},{5,6},{6,7},{7,4},{8,11},{9,8},{10,9... | collective-permute-start | bytes 319496 | tf_op jit(solution)/shard_map/ppermute | solution.py:50
  64.8 5.9 %collective-permute-start.12 = (s16[208,256]{1,0:T(8,128)(2,1)S(1)}, s16[208,256]{1,0:T(8,128)(2,1)S(1)}, u32[]{:S(2)}, u32[]{:S(2)}) collective-permute-start(s16[208,256]{1,0:T(8,128)(2,1)S(1)} %get-tuple-element.65), channel_id=1, source_target_pairs={{0,1},{1,2},{2,3},{3,0},{4,7},{5,4},{6,5},{7,6},{8,9},{9,10},{10,1... | collective-permute-start | bytes 319496 | tf_op jit(solution)/shard_map/ppermute | solution.py:50
  71.0 6.0 %collective-permute-start.13 = (bf16[3,64,256]{2,1,0:T(8,128)(2,1)S(1)}, bf16[3,64,256]{2,1,0:T(8,128)(2,1)S(1)}, u32[]{:S(2)}, u32[]{:S(2)}) collective-permute-start(bf16[3,64,256]{2,1,0:T(8,128)(2,1)S(1)} %fusion.15.s0), channel_id=1, source_target_pairs={{8,0},{124,4},{16,8},{4,12},{24,16},{12,20},{32,24},{20,28},{40,32... | collective-permute-start | bytes 294920 | tf_op jit(solution)/shard_map/ppermute | solution.py:58
  74.7 2.8 %collective-permute-start.16 = (bf16[3,64,256]{2,1,0:T(8,128)(2,1)S(1)}, bf16[3,64,256]{2,1,0:T(8,128)(2,1)S(1)}, u32[]{:S(2)}, u32[]{:S(2)}) collective-permute-start(bf16[3,64,256]{2,1,0:T(8,128)(2,1)S(1)} %fusion.15.s0), channel_id=1, source_target_pairs={{0,4},{4,0},{1,5},{5,1},{2,6},{6,2},{3,7},{7,3},{8,12},{12,8},{9,1... | collective-permute-start | bytes 294920 | tf_op jit(solution)/shard_map/ppermute | solution.py:64
  74.7 7.9 %collective-permute-start.14 = (bf16[3,64,256]{2,1,0:T(8,128)(2,1)S(1)}, bf16[3,64,256]{2,1,0:T(8,128)(2,1)S(1)}, u32[]{:S(2)}, u32[]{:S(2)}) collective-permute-start(bf16[3,64,256]{2,1,0:T(8,128)(2,1)S(1)} %fusion.15.s0), channel_id=1, source_target_pairs={{120,0},{12,4},{0,8},{20,12},{8,16},{28,20},{16,24},{36,28},{24,32... | collective-permute-start | bytes 294920 | tf_op jit(solution)/shard_map/ppermute | solution.py:58
  76.9 5.7 %collective-permute-start.15 = (bf16[3,64,256]{2,1,0:T(8,128)(2,1)S(1)}, bf16[3,64,256]{2,1,0:T(8,128)(2,1)S(1)}, u32[]{:S(2)}, u32[]{:S(2)}) collective-permute-start(bf16[3,64,256]{2,1,0:T(8,128)(2,1)S(1)} %collective-permute-done.13.s2), channel_id=1, source_target_pairs={{0,4},{4,0},{1,5},{5,1},{2,6},{6,2},{3,7},{7,3},{8,12},{12,8},{9,1... | collective-permute-start | bytes 294920 | tf_op jit(solution)/shard_map/ppermute | solution.py:64
  84.0 7.3 %collective-permute-start.17 = (s16[208,256]{1,0:T(8,128)(2,1)S(1)}, s16[208,256]{1,0:T(8,128)(2,1)S(1)}, u32[]{:S(2)}, u32[]{:S(2)}) collective-permute-start(s16[208,256]{1,0:T(8,128)(2,1)S(1)} %spread_far.2), channel_id=1, source_target_pairs={{0,2},{1,3},{2,0},{3,1},{4,6},{5,7},{6,4},{7,5},{8,10},{9,11},{10,... | collective-permute-start | bytes 319496 | tf_op jit(solution)/shard_map/ppermute | solution.py:54
  88.0 4.8 %collective-permute-start.18 = (s16[208,256]{1,0:T(8,128)(2,1)S(1)}, s16[208,256]{1,0:T(8,128)(2,1)S(1)}, u32[]{:S(2)}, u32[]{:S(2)}) collective-permute-start(s16[208,256]{1,0:T(8,128)(2,1)S(1)} %get-tuple-element.71), channel_id=1, source_target_pairs={{0,3},{1,0},{2,1},{3,2},{4,5},{5,6},{6,7},{7,4},{8,11},{9,8},{10,9... | collective-permute-start | bytes 319496 | tf_op jit(solution)/shard_map/ppermute | solution.py:50
  89.9 5.9 %collective-permute-start.19 = (s16[208,256]{1,0:T(8,128)(2,1)S(1)}, s16[208,256]{1,0:T(8,128)(2,1)S(1)}, u32[]{:S(2)}, u32[]{:S(2)}) collective-permute-start(s16[208,256]{1,0:T(8,128)(2,1)S(1)} %get-tuple-element.72), channel_id=1, source_target_pairs={{0,1},{1,2},{2,3},{3,0},{4,7},{5,4},{6,5},{7,6},{8,9},{9,10},{10,1... | collective-permute-start | bytes 319496 | tf_op jit(solution)/shard_map/ppermute | solution.py:50
  96.0 5.3 %collective-permute-start.20 = (bf16[3,64,256]{2,1,0:T(8,128)(2,1)S(1)}, bf16[3,64,256]{2,1,0:T(8,128)(2,1)S(1)}, u32[]{:S(2)}, u32[]{:S(2)}) collective-permute-start(bf16[3,64,256]{2,1,0:T(8,128)(2,1)S(1)} %fusion.9.s0), channel_id=1, source_target_pairs={{8,0},{124,4},{16,8},{4,12},{24,16},{12,20},{32,24},{20,28},{40,32... | collective-permute-start | bytes 294920 | tf_op jit(solution)/shard_map/ppermute | solution.py:58
  98.2 3.0 %collective-permute-start.23 = (bf16[3,64,256]{2,1,0:T(8,128)(2,1)S(1)}, bf16[3,64,256]{2,1,0:T(8,128)(2,1)S(1)}, u32[]{:S(2)}, u32[]{:S(2)}) collective-permute-start(bf16[3,64,256]{2,1,0:T(8,128)(2,1)S(1)} %fusion.9.s0), channel_id=1, source_target_pairs={{0,4},{4,0},{1,5},{5,1},{2,6},{6,2},{3,7},{7,3},{8,12},{12,8},{9,1... | collective-permute-start | bytes 294920 | tf_op jit(solution)/shard_map/ppermute | solution.py:64
  98.2 7.9 %collective-permute-start.21 = (bf16[3,64,256]{2,1,0:T(8,128)(2,1)S(1)}, bf16[3,64,256]{2,1,0:T(8,128)(2,1)S(1)}, u32[]{:S(2)}, u32[]{:S(2)}) collective-permute-start(bf16[3,64,256]{2,1,0:T(8,128)(2,1)S(1)} %fusion.9.s0), channel_id=1, source_target_pairs={{120,0},{12,4},{0,8},{20,12},{8,16},{28,20},{16,24},{36,28},{24,32... | collective-permute-start | bytes 294920 | tf_op jit(solution)/shard_map/ppermute | solution.py:58
  101.2 4.9 %collective-permute-start.22 = (bf16[3,64,256]{2,1,0:T(8,128)(2,1)S(1)}, bf16[3,64,256]{2,1,0:T(8,128)(2,1)S(1)}, u32[]{:S(2)}, u32[]{:S(2)}) collective-permute-start(bf16[3,64,256]{2,1,0:T(8,128)(2,1)S(1)} %collective-permute-done.20.s2), channel_id=1, source_target_pairs={{0,4},{4,0},{1,5},{5,1},{2,6},{6,2},{3,7},{7,3},{8,12},{12,8},{9,1... | collective-permute-start | bytes 294920 | tf_op jit(solution)/shard_map/ppermute | solution.py:64
  107.5 7.0 %collective-permute-start.24 = (s16[208,256]{1,0:T(8,128)(2,1)S(1)}, s16[208,256]{1,0:T(8,128)(2,1)S(1)}, u32[]{:S(2)}, u32[]{:S(2)}) collective-permute-start(s16[208,256]{1,0:T(8,128)(2,1)S(1)} %spread_far.3), channel_id=1, source_target_pairs={{0,2},{1,3},{2,0},{3,1},{4,6},{5,7},{6,4},{7,5},{8,10},{9,11},{10,... | collective-permute-start | bytes 319496 | tf_op jit(solution)/shard_map/ppermute | solution.py:54
  110.8 4.8 %collective-permute-start.25 = (s16[208,256]{1,0:T(8,128)(2,1)S(1)}, s16[208,256]{1,0:T(8,128)(2,1)S(1)}, u32[]{:S(2)}, u32[]{:S(2)}) collective-permute-start(s16[208,256]{1,0:T(8,128)(2,1)S(1)} %get-tuple-element.75), channel_id=1, source_target_pairs={{0,3},{1,0},{2,1},{3,2},{4,5},{5,6},{6,7},{7,4},{8,11},{9,8},{10,9... | collective-permute-start | bytes 319496 | tf_op jit(solution)/shard_map/ppermute | solution.py:50
  112.3 5.9 %collective-permute-start.26 = (s16[208,256]{1,0:T(8,128)(2,1)S(1)}, s16[208,256]{1,0:T(8,128)(2,1)S(1)}, u32[]{:S(2)}, u32[]{:S(2)}) collective-permute-start(s16[208,256]{1,0:T(8,128)(2,1)S(1)} %get-tuple-element.76), channel_id=1, source_target_pairs={{0,1},{1,2},{2,3},{3,0},{4,7},{5,4},{6,5},{7,6},{8,9},{9,10},{10,1... | collective-permute-start | bytes 319496 | tf_op jit(solution)/shard_map/ppermute | solution.py:50

commit v8 on v7

--- a/solution.py
+++ b/solution.py
@@ -271,7 +271,7 @@
 
 
 def power_of(values):
-    return jnp.ceil(jnp.log2(jnp.maximum(values, 1e-30)))
+    return jnp.ceil(jnp.log2(jnp.maximum(values, 1e-36)))
 
 
 def put_coded(ref, sums, first, degrees=False):
@@ -280,13 +280,13 @@
     for i in range(BLK):
         values = sums[first + i, :CH]
         power = power_of(jnp.max(jnp.abs(values), axis=0, keepdims=True))
-        coded = jnp.floor(values * (jnp.exp2(-power) * CODED) + 0.5)
+        coded = jnp.floor(values * jnp.exp2(-power) * CODED + 0.5)
         ref[i * CH : (i + 1) * CH] = coded.astype(jnp.int32).astype(jnp.int16)
         extra = jnp.where(row == i, power, extra)
         if degrees:
             degree = jnp.sum(sums[first + i, CH:], axis=0, keepdims=True)
             power = power_of(degree)
-            scaled = degree * (jnp.exp2(-power) * CODED)
+            scaled = degree * jnp.exp2(-power) * CODED
             high = jnp.floor(scaled + 0.5)
             low = jnp.floor((scaled - high) * CODED + 0.5)
             for at, part in enumerate((power, high, low)):
@@ -297,14 +297,14 @@
 def uncoded(v):
     values = v[: BLK * CH].astype(F32).reshape(BLK, CH, ROWS)
     powers = v[BLK * CH : BLK * CH + BLK].astype(F32)
-    return values * (jnp.exp2(powers) * (1.0 / CODED))[:, None, :]
+    return values * (1.0 / CODED) * jnp.exp2(powers)[:, None, :]
 
 
 def uncoded_degrees(v):
     power, high, low = (
         v[BLK * CH + at * BLK : BLK * CH + (at + 1) * BLK].astype(F32) for at in (1, 2, 3)
     )
-    return (high + low * (1.0 / CODED)) * (jnp.exp2(power) * (1.0 / CODED))
+    return (high + low * (1.0 / CODED)) * (1.0 / CODED) * jnp.exp2(power)
 
 
 def last_columns(list_ref, rows, c4, given, w_ref, outs, sums, states, first, low, high):

time: 121 us -> 123 us (1.017); the launches traced: 119 us -> 124 us
  waiting for transfers between devices: 41.5 us -> 44.5 us
  starting transfers between devices: 35.5 us -> 37.3 us
    ppermute x6, waiting for transfers between devices: 14.9 us -> 17.7 us  [from_wide(): lax.ppermute(v, WIDE, [((i + (2 * sign if i % 2 == 0 else -2 * sign)) % N...]
    ppermute x6, starting transfers between devices: 12.5 us -> 14.4 us  [from_wide(): lax.ppermute(v, WIDE, [((i + (2 * sign if i % 2 == 0 else -2 * sign)) % N...]
    ppermute x12, waiting for transfers between devices: 23.8 us -> 25.1 us  [along_x(): return lax.ppermute(v, ('c', 'x'), pairs)]
  transfers between devices with their start and end apart: 27 -> 27, of which waited for: 14 -> 13; matrix products, arithmetic and copies ran while one was open for 0% -> 0% of each run, Pallas kernels for 28% -> 26%
where the time goes in v8:
time: 123 us; the launch traced here: 124 us
  waiting for transfers between devices  44.5 us (36%)
  Pallas kernels  39.4 us (32%)
  starting transfers between devices  37.3 us (30%)
  other arithmetic  2.29 us (2%)
    pallas_call x11, Pallas kernels, build(): pl.pallas_call(kernel, out_shape=[jax.ShapeDtypeStruct(*o) for o in outs]...  32.5 us
    ppermute x12, waiting for transfers between devices, along_x(): return lax.ppermute(v, ('c', 'x'), pairs)  25.1 us
    ppermute x6, waiting for transfers between devices, from_wide(): lax.ppermute(v, WIDE, [((i + (2 * sign if i % 2 == 0 else -2 * sign)) % N...  17.7 us
    ppermute x12, starting transfers between devices, along_x(): return lax.ppermute(v, ('c', 'x'), pairs)  17 us
    ppermute x6, starting transfers between devices, from_wide(): lax.ppermute(v, WIDE, [((i + (2 * sign if i % 2 == 0 else -2 * sign)) % N...  14.4 us
    pallas_call x2, Pallas kernels, make_plan(): pl.pallas_call(functools.partial(plan_kernel, groups), out_shape=jax.Shap...  5.01 us
    ppermute x3, starting transfers between devices, across_x(): return lax.ppermute(v, 'x', [(x, (x + 2) % NX) for x in range(NX)])  3.69 us
  transfers between devices with their start and end apart: 27, of which 13 were waited for; matrix products, arithmetic and copies ran while one was open for 0% of the time, Pallas kernels for 26%

profile of v8, /device:TPU:0, one launch (start us, length us, event | category | flops | bytes accessed | tf_op | source)
XLA Modules:
  0.0 123.9 jit_solution(2191480686806069091)
XLA Ops:
  0.0 0.7 shift-right-arithmetic_convert_fusion
  0.8 1.7 %prep.1 = (bf16[1552,256]{1,0:T(8,128)(2,1)S(1)}, bf16[832,768]{1,0:T(8,128)(2,1)S(1)}) custom-call(bf16[3,256,768]{2,1,0:T(8,128)(2,1)} %emb_hbm.1, f32[3,64,256]{2,1,0:T(8,128)} %bitcast.24, bf16[16,256]{1,0:T(8,128)(2,1)S(1)} %fusion.23.ids_ref), custom_call_target="tpu_custom_call" | custom-call | flops 1000 | bytes 1000 | tf_op jit(solution)/shard_map/prep/pallas_call | solution.py:88
  2.5 1.6 %collective-permute-start = (bf16[1552,256]{1,0:T(8,128)(2,1)S(1)}, bf16[1552,256]{1,0:T(8,128)(2,1)S(1)}, u32[]{:S(2)}, u32[]{:S(2)}) collective-permute-start(bf16[1552,256]{1,0:T(8,128)(2,1)S(1)} %get-tuple-element.52.r0), channel_id=1, source_target_pairs={{0,1},{1,2},{2,3},{3,0},{4,7},{5,4},{6,5},{7,6},{8,9},{9,10},{10,1... | collective-permute-start | bytes 2383880 | tf_op jit(solution)/shard_map/ppermute | solution.py:50
  4.2 0.1 third.1.r1
  4.3 1.6 %collective-permute-start.2 = (bf16[784,256]{1,0:T(8,128)(2,1)S(1)}, bf16[784,256]{1,0:T(8,128)(2,1)S(1)}, u32[]{:S(2)}, u32[]{:S(2)}) collective-permute-start(bf16[784,256]{1,0:T(8,128)(2,1)S(1)} %third.1.r1), channel_id=1, source_target_pairs={{0,1},{1,2},{2,3},{3,0},{4,7},{5,4},{6,5},{7,6},{8,9},{9,10},{10,1... | collective-permute-start | bytes 1204232 | tf_op jit(solution)/shard_map/ppermute | solution.py:50
  5.9 1.7 %collective-permute-start.1 = (bf16[784,256]{1,0:T(8,128)(2,1)S(1)}, bf16[784,256]{1,0:T(8,128)(2,1)S(1)}, u32[]{:S(2)}, u32[]{:S(2)}) collective-permute-start(bf16[784,256]{1,0:T(8,128)(2,1)S(1)} %third.1.r1), channel_id=1, source_target_pairs={{0,3},{1,0},{2,1},{3,2},{4,5},{5,6},{6,7},{7,4},{8,11},{9,8},{10,9... | collective-permute-start | bytes 1204232 | tf_op jit(solution)/shard_map/ppermute | solution.py:50
  7.6 1.6 %collective-permute-start.6 = (bf16[832,768]{1,0:T(8,128)(2,1)S(1)}, bf16[832,768]{1,0:T(8,128)(2,1)S(1)}, u32[]{:S(2)}, u32[]{:S(2)}) collective-permute-start(bf16[832,768]{1,0:T(8,128)(2,1)S(1)} %get-tuple-element.46.full_ref.c0), channel_id=1, source_target_pairs={{120,0},{12,4},{0,8},{20,12},{8,16},{28,20},{16,24},{36,28},{24,32... | collective-permute-start | bytes 3833864 | tf_op jit(solution)/shard_map/ppermute | solution.py:58
  9.2 4.9 %collective-permute-start.5 = (bf16[832,768]{1,0:T(8,128)(2,1)S(1)}, bf16[832,768]{1,0:T(8,128)(2,1)S(1)}, u32[]{:S(2)}, u32[]{:S(2)}) collective-permute-start(bf16[832,768]{1,0:T(8,128)(2,1)S(1)} %get-tuple-element.46.full_ref.c0), channel_id=1, source_target_pairs={{8,0},{124,4},{16,8},{4,12},{24,16},{12,20},{32,24},{20,28},{40,32... | collective-permute-start | bytes 3833864 | tf_op jit(solution)/shard_map/ppermute | solution.py:58
  14.1 10.4 %collective-permute-done.2.r3 = bf16[784,256]{1,0:T(8,128)(2,1)S(1)} collective-permute-done((bf16[784,256]{1,0:T(8,128)(2,1)S(1)}, bf16[784,256]{1,0:T(8,128)(2,1)S(1)}, u32[]{:S(2)}, u32[]{:S(2)}) %collective-permute-start.2) | collective-permute-done | bytes 401440 | tf_op jit(solution)/shard_map/ppermute | solution.py:50
  24.5 0.4 collective-permute-start.3
  24.9 2.9 %collective-permute-start.7 = (bf16[1552,256]{1,0:T(8,128)(2,1)S(1)}, bf16[1552,256]{1,0:T(8,128)(2,1)S(1)}, u32[]{:S(2)}, u32[]{:S(2)}) collective-permute-start(bf16[1552,256]{1,0:T(8,128)(2,1)S(1)} %get-tuple-element.52.r0), channel_id=1, source_target_pairs={{0,3},{1,0},{2,1},{3,2},{4,5},{5,6},{6,7},{7,4},{8,11},{9,8},{10,9... | collective-permute-start | bytes 2383880 | tf_op jit(solution)/shard_map/ppermute | solution.py:50
  27.9 3.0 %plan.2.list_ref.refs_1_.near_ref = s32[256]{0:T(256)S(1)} custom-call(s32[3,32]{1,0:T(4,128)S(1)} %get-tuple-element.83.refs_0_, s32[3,32]{1,0:T(4,128)S(1)} %get-tuple-element.84.refs_1_, s32[3,32]{1,0:T(4,128)S(1)} %get-tuple-element.85.refs_2_), custom_call_target="tpu_custom_call" | custom-call | flops 30000001024 | bytes 1000 | tf_op jit(solution)/shard_map/plan/pallas_call | solution.py:194
  31.0 1.3 %collective-permute-start.8 = (bf16[784,256]{1,0:T(8,128)(2,1)S(1)}, bf16[784,256]{1,0:T(8,128)(2,1)S(1)}, u32[]{:S(2)}, u32[]{:S(2)}) collective-permute-start(bf16[784,256]{1,0:T(8,128)(2,1)S(1)} %collective-permute-done.1.r4), channel_id=1, source_target_pairs={{0,3},{1,0},{2,1},{3,2},{4,5},{5,6},{6,7},{7,4},{8,11},{9,8},{10,9... | collective-permute-start | bytes 1204232 | tf_op jit(solution)/shard_map/ppermute | solution.py:50
  32.3 2.6 %build_0.1 = (bf16[44,256,256]{2,1,0:T(8,128)(2,1)S(1)}, f32[13,72,256]{2,1,0:T(8,128)S(1)}, bf16[6912,256]{1,0:T(8,128)(2,1)S(1)}) custom-call(s32[256]{0:T(256)S(1)} %plan.2.list_ref.refs_1_.near_ref, bf16[1552,256]{1,0:T(8,128)(2,1)S(1)} %get-tuple-element.52.r0, bf16[784,256]{1,0:T(8,128)(2,1)S(1)} %third.1.r1, ...), custom_call_target="tpu_custom_call" | custom-call | flops 30000001024 | bytes 1000 | tf_op jit(solution)/shard_map/build_0/pallas_call | solution.py:335
  34.9 5.8 %collective-permute-done.5.c2 = bf16[832,768]{1,0:T(8,128)(2,1)S(1)} collective-permute-done((bf16[832,768]{1,0:T(8,128)(2,1)S(1)}, bf16[832,768]{1,0:T(8,128)(2,1)S(1)}, u32[]{:S(2)}, u32[]{:S(2)}) %collective-permute-start.5) | collective-permute-done | bytes 1277984 | tf_op jit(solution)/shard_map/ppermute | solution.py:58
  40.7 2.2 %collective-permute-start.9 = (bf16[832,768]{1,0:T(8,128)(2,1)S(1)}, bf16[832,768]{1,0:T(8,128)(2,1)S(1)}, u32[]{:S(2)}, u32[]{:S(2)}) collective-permute-start(bf16[832,768]{1,0:T(8,128)(2,1)S(1)} %collective-permute-done.5.c2), channel_id=1, source_target_pairs={{0,4},{4,0},{1,5},{5,1},{2,6},{6,2},{3,7},{7,3},{8,12},{12,8},{9,1... | collective-permute-start | bytes 3833864 | tf_op jit(solution)/shard_map/ppermute | solution.py:64
  42.9 4.7 %build_1.1 = (bf16[44,256,256]{2,1,0:T(8,128)(2,1)S(1)}, f32[13,72,256]{2,1,0:T(8,128)S(1)}, bf16[3072,768]{1,0:T(8,128)(2,1)S(1)}, bf16[12,64,256]{2,1,0:T(8,128)(2,1)S(1)}) custom-call(s32[256]{0:T(256)S(1)} %plan.2.list_ref.refs_1_.near_ref, bf16[6912,256]{1,0:T(8,128)(2,1)S(1)} %get-tuple-element.47.rows.old_rows, ...), custom_call_target="tpu_custom_call" | custom-call | flops 30000001024 | bytes 1000 | tf_op jit(solution)/shard_map/build_1/pallas_call | solution.py:335
  47.7 2.0 %plan.3.list_ref = s32[256]{0:T(256)S(1)} custom-call(s32[3,32]{1,0:T(4,128)S(1)} %fusion.51.refs_0_, s32[256]{0:T(256)S(1)} %plan.2.list_ref.refs_1_.near_ref), custom_call_target="tpu_custom_call" | custom-call | flops 30000001024 | bytes 1000 | tf_op jit(solution)/shard_map/plan/pallas_call | solution.py:194
  49.7 6.9 %build_2.1 = (bf16[36,256,256]{2,1,0:T(8,128)(2,1)S(1)}, bf16[36,256,256]{2,1,0:T(8,128)(2,1)S(1)}, f32[13,72,256]{2,1,0:T(8,128)S(1)}, bf16[9216,256]{1,0:T(8,128)(2,1)S(1)}) custom-call(s32[256]{0:T(256)S(1)} %plan.3.list_ref, bf16[6912,256]{1,0:T(8,128)(2,1)S(1)} %get-tuple-element.47.rows.old_rows, bf16[1552,256]{1,0:T(8,128)(2,1)S(1)} %collective-permute-done.7.r0, ...), custom_call_target="tpu_custom_call" | custom-call | flops 30000001024 | bytes 1000 | tf_op jit(solution)/shard_map/build_2/pallas_call | solution.py:335
  56.6 2.3 %build_far.1 = (bf16[40,256,256]{2,1,0:T(8,128)(2,1)S(1)}, s16[208,256]{1,0:T(8,128)(2,1)S(1)}) custom-call(s32[256]{0:T(256)S(1)} %plan.3.list_ref, bf16[9216,256]{1,0:T(8,128)(2,1)S(1)} %get-tuple-element.57.rows, bf16[832,768]{1,0:T(8,128)(2,1)S(1)} %collective-permute-done.9.c4, f32[13,72,256]{2,1,0:T(8,128)S(1)} %get-tuple-element.61.given), custom_call_target="tpu_custom_call" | custom-call | flops 30000001024 | bytes 1000 | tf_op jit(solution)/shard_map/build_far/pallas_call | solution.py:335
  59.0 1.1 collective-permute-start.10
  60.1 3.1 %build_rest.1 = (bf16[40,256,256]{2,1,0:T(8,128)(2,1)S(1)}, f32[3,72,256]{2,1,0:T(8,128)S(1)}, s16[208,256]{1,0:T(8,128)(2,1)S(1)}, s16[208,256]{1,0:T(8,128)(2,1)S(1)}) custom-call(s32[256]{0:T(256)S(1)} %plan.3.list_ref, bf16[9216,256]{1,0:T(8,128)(2,1)S(1)} %get-tuple-element.57.rows, bf16[832,768]{1,0:T(8,128)(2,1)S(1)} %collective-permute-done.9.c4, ...), custom_call_target="tpu_custom_call" | custom-call | flops 30000001024 | bytes 1000 | tf_op jit(solution)/shard_map/build_rest/pallas_call | solution.py:335
  63.2 2.7 %collective-permute-start.11 = (s16[208,256]{1,0:T(8,128)(2,1)S(1)}, s16[208,256]{1,0:T(8,128)(2,1)S(1)}, u32[]{:S(2)}, u32[]{:S(2)}) collective-permute-start(s16[208,256]{1,0:T(8,128)(2,1)S(1)} %get-tuple-element.64), channel_id=1, source_target_pairs={{0,3},{1,0},{2,1},{3,2},{4,5},{5,6},{6,7},{7,4},{8,11},{9,8},{10,9... | collective-permute-start | bytes 319496 | tf_op jit(solution)/shard_map/ppermute | solution.py:50
  65.9 2.8 %collective-permute-done.11 = s16[208,256]{1,0:T(8,128)(2,1)S(1)} collective-permute-done((s16[208,256]{1,0:T(8,128)(2,1)S(1)}, s16[208,256]{1,0:T(8,128)(2,1)S(1)}, u32[]{:S(2)}, u32[]{:S(2)}) %collective-permute-start.11) | collective-permute-done | bytes 106528 | tf_op jit(solution)/shard_map/ppermute | solution.py:50
  68.7 3.1 %collective-permute-done.12 = s16[208,256]{1,0:T(8,128)(2,1)S(1)} collective-permute-done((s16[208,256]{1,0:T(8,128)(2,1)S(1)}, s16[208,256]{1,0:T(8,128)(2,1)S(1)}, u32[]{:S(2)}, u32[]{:S(2)}) %collective-permute-start.12) | collective-permute-done | bytes 106528 | tf_op jit(solution)/shard_map/ppermute | solution.py:50
  72.1 4.8 %collective-permute-start.13 = (bf16[3,64,256]{2,1,0:T(8,128)(2,1)S(1)}, bf16[3,64,256]{2,1,0:T(8,128)(2,1)S(1)}, u32[]{:S(2)}, u32[]{:S(2)}) collective-permute-start(bf16[3,64,256]{2,1,0:T(8,128)(2,1)S(1)} %fusion.15.s0), channel_id=1, source_target_pairs={{8,0},{124,4},{16,8},{4,12},{24,16},{12,20},{32,24},{20,28},{40,32... | collective-permute-start | bytes 294920 | tf_op jit(solution)/shard_map/ppermute | solution.py:58
  76.8 3.0 %collective-permute-done.13.s2 = bf16[3,64,256]{2,1,0:T(8,128)(2,1)S(1)} collective-permute-done((bf16[3,64,256]{2,1,0:T(8,128)(2,1)S(1)}, bf16[3,64,256]{2,1,0:T(8,128)(2,1)S(1)}, u32[]{:S(2)}, u32[]{:S(2)}) %collective-permute-start.13) | collective-permute-done | bytes 98336 | tf_op jit(solution)/shard_map/ppermute | solution.py:58
  79.9 1.9 %spread_near.2.given = f32[13,64,256]{2,1,0:T(8,128)S(1)} custom-call(s32[256]{0:T(256)S(1)} %plan.2.list_ref.refs_1_.near_ref, s32[256]{0:T(256)S(1)} %plan.3.list_ref, bf16[44,256,256]{2,1,0:T(8,128)(2,1)S(1)} %get-tuple-element.66.w0, bf16[36,256,256]{2,1,0:T(8,128)(2,1)S(1)} %get-tuple-element.67.w2, bf16[3,64,256]{2,1,0:T(8,128)(2,1)S(1)} %fusion.15.s0, ...), custom_call_target="tpu_custom_call" | custom-call | flops 30000001024 | bytes 1000 | tf_op jit(solution)/shard_map/spread_near/pallas_call | solution.py:335
  81.8 3.0 %collective-permute-done.14.s3 = bf16[3,64,256]{2,1,0:T(8,128)(2,1)S(1)} collective-permute-done((bf16[3,64,256]{2,1,0:T(8,128)(2,1)S(1)}, bf16[3,64,256]{2,1,0:T(8,128)(2,1)S(1)}, u32[]{:S(2)}, u32[]{:S(2)}) %collective-permute-start.14) | collective-permute-done | bytes 98336 | tf_op jit(solution)/shard_map/ppermute | solution.py:58
  84.8 1.6 %spread_far.2 = s16[208,256]{1,0:T(8,128)(2,1)S(1)} custom-call(s32[256]{0:T(256)S(1)} %plan.3.list_ref, bf16[36,256,256]{2,1,0:T(8,128)(2,1)S(1)} %get-tuple-element.56.w3, bf16[40,256,256]{2,1,0:T(8,128)(2,1)S(1)} %get-tuple-element.68.w4, bf16[3,64,256]{2,1,0:T(8,128)(2,1)S(1)} %collective-permute-done.13.s2, ...), custom_call_target="tpu_custom_call" | custom-call | flops 30000001024 | bytes 1000 | tf_op jit(solution)/shard_map/spread_far/pallas_call | solution.py:335
  86.4 2.5 %collective-permute-start.17 = (s16[208,256]{1,0:T(8,128)(2,1)S(1)}, s16[208,256]{1,0:T(8,128)(2,1)S(1)}, u32[]{:S(2)}, u32[]{:S(2)}) collective-permute-start(s16[208,256]{1,0:T(8,128)(2,1)S(1)} %spread_far.2), channel_id=1, source_target_pairs={{0,2},{1,3},{2,0},{3,1},{4,6},{5,7},{6,4},{7,5},{8,10},{9,11},{10,... | collective-permute-start | bytes 319496 | tf_op jit(solution)/shard_map/ppermute | solution.py:54
  88.8 3.0 %spread_rest.2 = (f32[3,64,256]{2,1,0:T(8,128)S(1)}, s16[208,256]{1,0:T(8,128)(2,1)S(1)}, s16[208,256]{1,0:T(8,128)(2,1)S(1)}) custom-call(s32[256]{0:T(256)S(1)} %plan.2.list_ref.refs_1_.near_ref, s32[256]{0:T(256)S(1)} %plan.3.list_ref, bf16[44,256,256]{2,1,0:T(8,128)(2,1)S(1)} %get-tuple-element.51.w1, bf16[36,256,256]{2,1,0:T(8,128)(2,1)S(1)} %get-tuple-element.56.w3, ...), custom_call_target="tpu_custom_call" | custom-call | flops 30000001024 | bytes 1000 | tf_op jit(solution)/shard_map/spread_rest/pallas_call | solution.py:335
  91.8 0.9 collective-permute-start.18
  92.7 1.2 collective-permute-start.19
  94.0 2.6 %collective-permute-done.18 = s16[208,256]{1,0:T(8,128)(2,1)S(1)} collective-permute-done((s16[208,256]{1,0:T(8,128)(2,1)S(1)}, s16[208,256]{1,0:T(8,128)(2,1)S(1)}, u32[]{:S(2)}, u32[]{:S(2)}) %collective-permute-start.18) | collective-permute-done | bytes 106528 | tf_op jit(solution)/shard_map/ppermute | solution.py:50
  96.6 2.0 %collective-permute-done.19 = s16[208,256]{1,0:T(8,128)(2,1)S(1)} collective-permute-done((s16[208,256]{1,0:T(8,128)(2,1)S(1)}, s16[208,256]{1,0:T(8,128)(2,1)S(1)}, u32[]{:S(2)}, u32[]{:S(2)}) %collective-permute-start.19) | collective-permute-done | bytes 106528 | tf_op jit(solution)/shard_map/ppermute | solution.py:50
  98.7 0.1 fusion.9.s0
  98.8 3.1 %collective-permute-start.20 = (bf16[3,64,256]{2,1,0:T(8,128)(2,1)S(1)}, bf16[3,64,256]{2,1,0:T(8,128)(2,1)S(1)}, u32[]{:S(2)}, u32[]{:S(2)}) collective-permute-start(bf16[3,64,256]{2,1,0:T(8,128)(2,1)S(1)} %fusion.9.s0), channel_id=1, source_target_pairs={{8,0},{124,4},{16,8},{4,12},{24,16},{12,20},{32,24},{20,28},{40,32... | collective-permute-start | bytes 294920 | tf_op jit(solution)/shard_map/ppermute | solution.py:58
  101.9 3.0 %collective-permute-done.20.s2 = bf16[3,64,256]{2,1,0:T(8,128)(2,1)S(1)} collective-permute-done((bf16[3,64,256]{2,1,0:T(8,128)(2,1)S(1)}, bf16[3,64,256]{2,1,0:T(8,128)(2,1)S(1)}, u32[]{:S(2)}, u32[]{:S(2)}) %collective-permute-start.20) | collective-permute-done | bytes 98336 | tf_op jit(solution)/shard_map/ppermute | solution.py:58
  105.0 1.9 %spread_near.3.given = f32[13,64,256]{2,1,0:T(8,128)S(1)} custom-call(s32[256]{0:T(256)S(1)} %plan.2.list_ref.refs_1_.near_ref, s32[256]{0:T(256)S(1)} %plan.3.list_ref, bf16[44,256,256]{2,1,0:T(8,128)(2,1)S(1)} %get-tuple-element.66.w0, bf16[36,256,256]{2,1,0:T(8,128)(2,1)S(1)} %get-tuple-element.67.w2, bf16[3,64,256]{2,1,0:T(8,128)(2,1)S(1)} %fusion.9.s0, ...), custom_call_target="tpu_custom_call" | custom-call | flops 30000001024 | bytes 1000 | tf_op jit(solution)/shard_map/spread_near/pallas_call | solution.py:335
  106.9 3.0 %collective-permute-done.21.s3 = bf16[3,64,256]{2,1,0:T(8,128)(2,1)S(1)} collective-permute-done((bf16[3,64,256]{2,1,0:T(8,128)(2,1)S(1)}, bf16[3,64,256]{2,1,0:T(8,128)(2,1)S(1)}, u32[]{:S(2)}, u32[]{:S(2)}) %collective-permute-start.21) | collective-permute-done | bytes 98336 | tf_op jit(solution)/shard_map/ppermute | solution.py:58
  109.9 1.6 %spread_far.3 = s16[208,256]{1,0:T(8,128)(2,1)S(1)} custom-call(s32[256]{0:T(256)S(1)} %plan.3.list_ref, bf16[36,256,256]{2,1,0:T(8,128)(2,1)S(1)} %get-tuple-element.56.w3, bf16[40,256,256]{2,1,0:T(8,128)(2,1)S(1)} %get-tuple-element.68.w4, bf16[3,64,256]{2,1,0:T(8,128)(2,1)S(1)} %collective-permute-done.20.s2, ...), custom_call_target="tpu_custom_call" | custom-call | flops 30000001024 | bytes 1000 | tf_op jit(solution)/shard_map/spread_far/pallas_call | solution.py:335
  111.6 3.0 %spread_rest.3 = (f32[3,64,256]{2,1,0:T(8,128)S(1)}, s16[208,256]{1,0:T(8,128)(2,1)S(1)}, s16[208,256]{1,0:T(8,128)(2,1)S(1)}) custom-call(s32[256]{0:T(256)S(1)} %plan.2.list_ref.refs_1_.near_ref, s32[256]{0:T(256)S(1)} %plan.3.list_ref, bf16[44,256,256]{2,1,0:T(8,128)(2,1)S(1)} %get-tuple-element.51.w1, bf16[36,256,256]{2,1,0:T(8,128)(2,1)S(1)} %get-tuple-element.56.w3, ...), custom_call_target="tpu_custom_call" | custom-call | flops 30000001024 | bytes 1000 | tf_op jit(solution)/shard_map/spread_rest/pallas_call | solution.py:335
  114.5 2.7 %collective-permute-start.25 = (s16[208,256]{1,0:T(8,128)(2,1)S(1)}, s16[208,256]{1,0:T(8,128)(2,1)S(1)}, u32[]{:S(2)}, u32[]{:S(2)}) collective-permute-start(s16[208,256]{1,0:T(8,128)(2,1)S(1)} %get-tuple-element.75), channel_id=1, source_target_pairs={{0,3},{1,0},{2,1},{3,2},{4,5},{5,6},{6,7},{7,4},{8,11},{9,8},{10,9... | collective-permute-start | bytes 319496 | tf_op jit(solution)/shard_map/ppermute | solution.py:50
  117.2 1.6 %collective-permute-done.24 = s16[208,256]{1,0:T(8,128)(2,1)S(1)} collective-permute-done((s16[208,256]{1,0:T(8,128)(2,1)S(1)}, s16[208,256]{1,0:T(8,128)(2,1)S(1)}, u32[]{:S(2)}, u32[]{:S(2)}) %collective-permute-start.24) | collective-permute-done | bytes 106528 | tf_op jit(solution)/shard_map/ppermute | solution.py:54
  118.8 0.6 collective-permute-done.25
  119.5 3.6 %collective-permute-done.26 = s16[208,256]{1,0:T(8,128)(2,1)S(1)} collective-permute-done((s16[208,256]{1,0:T(8,128)(2,1)S(1)}, s16[208,256]{1,0:T(8,128)(2,1)S(1)}, u32[]{:S(2)}, u32[]{:S(2)}) %collective-permute-start.26) | collective-permute-done | bytes 106528 | tf_op jit(solution)/shard_map/ppermute | solution.py:50
  123.1 0.8 fusion.3
  (53 shorter events, 0.9 us)
Async XLA Ops:
  2.5 22.0 %collective-permute-start = (bf16[1552,256]{1,0:T(8,128)(2,1)S(1)}, bf16[1552,256]{1,0:T(8,128)(2,1)S(1)}, u32[]{:S(2)}, u32[]{:S(2)}) collective-permute-start(bf16[1552,256]{1,0:T(8,128)(2,1)S(1)} %get-tuple-element.52.r0), channel_id=1, source_target_pairs={{0,1},{1,2},{2,3},{3,0},{4,7},{5,4},{6,5},{7,6},{8,9},{9,10},{10,1... | collective-permute-start | bytes 2383880 | tf_op jit(solution)/shard_map/ppermute | solution.py:50
  4.3 20.2 %collective-permute-start.2 = (bf16[784,256]{1,0:T(8,128)(2,1)S(1)}, bf16[784,256]{1,0:T(8,128)(2,1)S(1)}, u32[]{:S(2)}, u32[]{:S(2)}) collective-permute-start(bf16[784,256]{1,0:T(8,128)(2,1)S(1)} %third.1.r1), channel_id=1, source_target_pairs={{0,1},{1,2},{2,3},{3,0},{4,7},{5,4},{6,5},{7,6},{8,9},{9,10},{10,1... | collective-permute-start | bytes 1204232 | tf_op jit(solution)/shard_map/ppermute | solution.py:50
  5.9 18.6 %collective-permute-start.1 = (bf16[784,256]{1,0:T(8,128)(2,1)S(1)}, bf16[784,256]{1,0:T(8,128)(2,1)S(1)}, u32[]{:S(2)}, u32[]{:S(2)}) collective-permute-start(bf16[784,256]{1,0:T(8,128)(2,1)S(1)} %third.1.r1), channel_id=1, source_target_pairs={{0,3},{1,0},{2,1},{3,2},{4,5},{5,6},{6,7},{7,4},{8,11},{9,8},{10,9... | collective-permute-start | bytes 1204232 | tf_op jit(solution)/shard_map/ppermute | solution.py:50
  7.6 35.2 %collective-permute-start.6 = (bf16[832,768]{1,0:T(8,128)(2,1)S(1)}, bf16[832,768]{1,0:T(8,128)(2,1)S(1)}, u32[]{:S(2)}, u32[]{:S(2)}) collective-permute-start(bf16[832,768]{1,0:T(8,128)(2,1)S(1)} %get-tuple-element.46.full_ref.c0), channel_id=1, source_target_pairs={{120,0},{12,4},{0,8},{20,12},{8,16},{28,20},{16,24},{36,28},{24,32... | collective-permute-start | bytes 3833864 | tf_op jit(solution)/shard_map/ppermute | solution.py:58
  9.2 31.5 %collective-permute-start.5 = (bf16[832,768]{1,0:T(8,128)(2,1)S(1)}, bf16[832,768]{1,0:T(8,128)(2,1)S(1)}, u32[]{:S(2)}, u32[]{:S(2)}) collective-permute-start(bf16[832,768]{1,0:T(8,128)(2,1)S(1)} %get-tuple-element.46.full_ref.c0), channel_id=1, source_target_pairs={{8,0},{124,4},{16,8},{4,12},{24,16},{12,20},{32,24},{20,28},{40,32... | collective-permute-start | bytes 3833864 | tf_op jit(solution)/shard_map/ppermute | solution.py:58
  24.5 23.0 %collective-permute-start.3 = (bf16[1552,256]{1,0:T(8,128)(2,1)S(1)}, bf16[1552,256]{1,0:T(8,128)(2,1)S(1)}, u32[]{:S(2)}, u32[]{:S(2)}) collective-permute-start(bf16[1552,256]{1,0:T(8,128)(2,1)S(1)} %collective-permute-done.r2), channel_id=1, source_target_pairs={{0,1},{1,2},{2,3},{3,0},{4,7},{5,4},{6,5},{7,6},{8,9},{9,10},{10,1... | collective-permute-start | bytes 2383880 | tf_op jit(solution)/shard_map/ppermute | solution.py:50
  24.9 24.7 %collective-permute-start.7 = (bf16[1552,256]{1,0:T(8,128)(2,1)S(1)}, bf16[1552,256]{1,0:T(8,128)(2,1)S(1)}, u32[]{:S(2)}, u32[]{:S(2)}) collective-permute-start(bf16[1552,256]{1,0:T(8,128)(2,1)S(1)} %get-tuple-element.52.r0), channel_id=1, source_target_pairs={{0,3},{1,0},{2,1},{3,2},{4,5},{5,6},{6,7},{7,4},{8,11},{9,8},{10,9... | collective-permute-start | bytes 2383880 | tf_op jit(solution)/shard_map/ppermute | solution.py:50
  27.8 3.2 %collective-permute-start.4 = (bf16[832,768]{1,0:T(8,128)(2,1)S(1)}, bf16[832,768]{1,0:T(8,128)(2,1)S(1)}, u32[]{:S(2)}, u32[]{:S(2)}) collective-permute-start(bf16[832,768]{1,0:T(8,128)(2,1)S(1)} %get-tuple-element.46.full_ref.c0), channel_id=1, source_target_pairs={{0,4},{4,0},{1,5},{5,1},{2,6},{6,2},{3,7},{7,3},{8,12},{12,8},{9,1... | collective-permute-start | bytes 3833864 | tf_op jit(solution)/shard_map/ppermute | solution.py:64
  31.0 18.7 %collective-permute-start.8 = (bf16[784,256]{1,0:T(8,128)(2,1)S(1)}, bf16[784,256]{1,0:T(8,128)(2,1)S(1)}, u32[]{:S(2)}, u32[]{:S(2)}) collective-permute-start(bf16[784,256]{1,0:T(8,128)(2,1)S(1)} %collective-permute-done.1.r4), channel_id=1, source_target_pairs={{0,3},{1,0},{2,1},{3,2},{4,5},{5,6},{6,7},{7,4},{8,11},{9,8},{10,9... | collective-permute-start | bytes 1204232 | tf_op jit(solution)/shard_map/ppermute | solution.py:50
  40.7 15.9 %collective-permute-start.9 = (bf16[832,768]{1,0:T(8,128)(2,1)S(1)}, bf16[832,768]{1,0:T(8,128)(2,1)S(1)}, u32[]{:S(2)}, u32[]{:S(2)}) collective-permute-start(bf16[832,768]{1,0:T(8,128)(2,1)S(1)} %collective-permute-done.5.c2), channel_id=1, source_target_pairs={{0,4},{4,0},{1,5},{5,1},{2,6},{6,2},{3,7},{7,3},{8,12},{12,8},{9,1... | collective-permute-start | bytes 3833864 | tf_op jit(solution)/shard_map/ppermute | solution.py:64
  58.9 13.0 %copy-start = (f32[3,256,64]{1,2,0:T(8,128)S(1)}, f32[3,256,64]{1,2,0:T(8,128)}, u32[]{:S(2)}) copy-start(f32[3,256,64]{1,2,0:T(8,128)} %param.4) | copy-start | bytes 589828
  59.0 7.0 %collective-permute-start.10 = (s16[208,256]{1,0:T(8,128)(2,1)S(1)}, s16[208,256]{1,0:T(8,128)(2,1)S(1)}, u32[]{:S(2)}, u32[]{:S(2)}) collective-permute-start(s16[208,256]{1,0:T(8,128)(2,1)S(1)} %get-tuple-element.60), channel_id=1, source_target_pairs={{0,2},{1,3},{2,0},{3,1},{4,6},{5,7},{6,4},{7,5},{8,10},{9,11},{10,... | collective-permute-start | bytes 319496 | tf_op jit(solution)/shard_map/ppermute | solution.py:54
  63.2 5.5 %collective-permute-start.11 = (s16[208,256]{1,0:T(8,128)(2,1)S(1)}, s16[208,256]{1,0:T(8,128)(2,1)S(1)}, u32[]{:S(2)}, u32[]{:S(2)}) collective-permute-start(s16[208,256]{1,0:T(8,128)(2,1)S(1)} %get-tuple-element.64), channel_id=1, source_target_pairs={{0,3},{1,0},{2,1},{3,2},{4,5},{5,6},{6,7},{7,4},{8,11},{9,8},{10,9... | collective-permute-start | bytes 319496 | tf_op jit(solution)/shard_map/ppermute | solution.py:50
  65.9 5.9 %collective-permute-start.12 = (s16[208,256]{1,0:T(8,128)(2,1)S(1)}, s16[208,256]{1,0:T(8,128)(2,1)S(1)}, u32[]{:S(2)}, u32[]{:S(2)}) collective-permute-start(s16[208,256]{1,0:T(8,128)(2,1)S(1)} %get-tuple-element.65), channel_id=1, source_target_pairs={{0,1},{1,2},{2,3},{3,0},{4,7},{5,4},{6,5},{7,6},{8,9},{9,10},{10,1... | collective-permute-start | bytes 319496 | tf_op jit(solution)/shard_map/ppermute | solution.py:50
  72.1 7.8 %collective-permute-start.13 = (bf16[3,64,256]{2,1,0:T(8,128)(2,1)S(1)}, bf16[3,64,256]{2,1,0:T(8,128)(2,1)S(1)}, u32[]{:S(2)}, u32[]{:S(2)}) collective-permute-start(bf16[3,64,256]{2,1,0:T(8,128)(2,1)S(1)} %fusion.15.s0), channel_id=1, source_target_pairs={{8,0},{124,4},{16,8},{4,12},{24,16},{12,20},{32,24},{20,28},{40,32... | collective-permute-start | bytes 294920 | tf_op jit(solution)/shard_map/ppermute | solution.py:58
  76.8 3.0 %collective-permute-start.16 = (bf16[3,64,256]{2,1,0:T(8,128)(2,1)S(1)}, bf16[3,64,256]{2,1,0:T(8,128)(2,1)S(1)}, u32[]{:S(2)}, u32[]{:S(2)}) collective-permute-start(bf16[3,64,256]{2,1,0:T(8,128)(2,1)S(1)} %fusion.15.s0), channel_id=1, source_target_pairs={{0,4},{4,0},{1,5},{5,1},{2,6},{6,2},{3,7},{7,3},{8,12},{12,8},{9,1... | collective-permute-start | bytes 294920 | tf_op jit(solution)/shard_map/ppermute | solution.py:64
  76.8 7.9 %collective-permute-start.14 = (bf16[3,64,256]{2,1,0:T(8,128)(2,1)S(1)}, bf16[3,64,256]{2,1,0:T(8,128)(2,1)S(1)}, u32[]{:S(2)}, u32[]{:S(2)}) collective-permute-start(bf16[3,64,256]{2,1,0:T(8,128)(2,1)S(1)} %fusion.15.s0), channel_id=1, source_target_pairs={{120,0},{12,4},{0,8},{20,12},{8,16},{28,20},{16,24},{36,28},{24,32... | collective-permute-start | bytes 294920 | tf_op jit(solution)/shard_map/ppermute | solution.py:58
  79.8 4.9 %collective-permute-start.15 = (bf16[3,64,256]{2,1,0:T(8,128)(2,1)S(1)}, bf16[3,64,256]{2,1,0:T(8,128)(2,1)S(1)}, u32[]{:S(2)}, u32[]{:S(2)}) collective-permute-start(bf16[3,64,256]{2,1,0:T(8,128)(2,1)S(1)} %collective-permute-done.13.s2), channel_id=1, source_target_pairs={{0,4},{4,0},{1,5},{5,1},{2,6},{6,2},{3,7},{7,3},{8,12},{12,8},{9,1... | collective-permute-start | bytes 294920 | tf_op jit(solution)/shard_map/ppermute | solution.py:64
  86.4 7.5 %collective-permute-start.17 = (s16[208,256]{1,0:T(8,128)(2,1)S(1)}, s16[208,256]{1,0:T(8,128)(2,1)S(1)}, u32[]{:S(2)}, u32[]{:S(2)}) collective-permute-start(s16[208,256]{1,0:T(8,128)(2,1)S(1)} %spread_far.2), channel_id=1, source_target_pairs={{0,2},{1,3},{2,0},{3,1},{4,6},{5,7},{6,4},{7,5},{8,10},{9,11},{10,... | collective-permute-start | bytes 319496 | tf_op jit(solution)/shard_map/ppermute | solution.py:54
  91.8 4.8 %collective-permute-start.18 = (s16[208,256]{1,0:T(8,128)(2,1)S(1)}, s16[208,256]{1,0:T(8,128)(2,1)S(1)}, u32[]{:S(2)}, u32[]{:S(2)}) collective-permute-start(s16[208,256]{1,0:T(8,128)(2,1)S(1)} %get-tuple-element.71), channel_id=1, source_target_pairs={{0,3},{1,0},{2,1},{3,2},{4,5},{5,6},{6,7},{7,4},{8,11},{9,8},{10,9... | collective-permute-start | bytes 319496 | tf_op jit(solution)/shard_map/ppermute | solution.py:50
  92.7 5.9 %collective-permute-start.19 = (s16[208,256]{1,0:T(8,128)(2,1)S(1)}, s16[208,256]{1,0:T(8,128)(2,1)S(1)}, u32[]{:S(2)}, u32[]{:S(2)}) collective-permute-start(s16[208,256]{1,0:T(8,128)(2,1)S(1)} %get-tuple-element.72), channel_id=1, source_target_pairs={{0,1},{1,2},{2,3},{3,0},{4,7},{5,4},{6,5},{7,6},{8,9},{9,10},{10,1... | collective-permute-start | bytes 319496 | tf_op jit(solution)/shard_map/ppermute | solution.py:50
  98.8 6.2 %collective-permute-start.20 = (bf16[3,64,256]{2,1,0:T(8,128)(2,1)S(1)}, bf16[3,64,256]{2,1,0:T(8,128)(2,1)S(1)}, u32[]{:S(2)}, u32[]{:S(2)}) collective-permute-start(bf16[3,64,256]{2,1,0:T(8,128)(2,1)S(1)} %fusion.9.s0), channel_id=1, source_target_pairs={{8,0},{124,4},{16,8},{4,12},{24,16},{12,20},{32,24},{20,28},{40,32... | collective-permute-start | bytes 294920 | tf_op jit(solution)/shard_map/ppermute | solution.py:58
  101.9 3.0 %collective-permute-start.23 = (bf16[3,64,256]{2,1,0:T(8,128)(2,1)S(1)}, bf16[3,64,256]{2,1,0:T(8,128)(2,1)S(1)}, u32[]{:S(2)}, u32[]{:S(2)}) collective-permute-start(bf16[3,64,256]{2,1,0:T(8,128)(2,1)S(1)} %fusion.9.s0), channel_id=1, source_target_pairs={{0,4},{4,0},{1,5},{5,1},{2,6},{6,2},{3,7},{7,3},{8,12},{12,8},{9,1... | collective-permute-start | bytes 294920 | tf_op jit(solution)/shard_map/ppermute | solution.py:64
  101.9 7.9 %collective-permute-start.21 = (bf16[3,64,256]{2,1,0:T(8,128)(2,1)S(1)}, bf16[3,64,256]{2,1,0:T(8,128)(2,1)S(1)}, u32[]{:S(2)}, u32[]{:S(2)}) collective-permute-start(bf16[3,64,256]{2,1,0:T(8,128)(2,1)S(1)} %fusion.9.s0), channel_id=1, source_target_pairs={{120,0},{12,4},{0,8},{20,12},{8,16},{28,20},{16,24},{36,28},{24,32... | collective-permute-start | bytes 294920 | tf_op jit(solution)/shard_map/ppermute | solution.py:58
  105.0 4.9 %collective-permute-start.22 = (bf16[3,64,256]{2,1,0:T(8,128)(2,1)S(1)}, bf16[3,64,256]{2,1,0:T(8,128)(2,1)S(1)}, u32[]{:S(2)}, u32[]{:S(2)}) collective-permute-start(bf16[3,64,256]{2,1,0:T(8,128)(2,1)S(1)} %collective-permute-done.20.s2), channel_id=1, source_target_pairs={{0,4},{4,0},{1,5},{5,1},{2,6},{6,2},{3,7},{7,3},{8,12},{12,8},{9,1... | collective-permute-start | bytes 294920 | tf_op jit(solution)/shard_map/ppermute | solution.py:64
  111.5 7.3 %collective-permute-start.24 = (s16[208,256]{1,0:T(8,128)(2,1)S(1)}, s16[208,256]{1,0:T(8,128)(2,1)S(1)}, u32[]{:S(2)}, u32[]{:S(2)}) collective-permute-start(s16[208,256]{1,0:T(8,128)(2,1)S(1)} %spread_far.3), channel_id=1, source_target_pairs={{0,2},{1,3},{2,0},{3,1},{4,6},{5,7},{6,4},{7,5},{8,10},{9,11},{10,... | collective-permute-start | bytes 319496 | tf_op jit(solution)/shard_map/ppermute | solution.py:54
  114.5 5.0 %collective-permute-start.25 = (s16[208,256]{1,0:T(8,128)(2,1)S(1)}, s16[208,256]{1,0:T(8,128)(2,1)S(1)}, u32[]{:S(2)}, u32[]{:S(2)}) collective-permute-start(s16[208,256]{1,0:T(8,128)(2,1)S(1)} %get-tuple-element.75), channel_id=1, source_target_pairs={{0,3},{1,0},{2,1},{3,2},{4,5},{5,6},{6,7},{7,4},{8,11},{9,8},{10,9... | collective-permute-start | bytes 319496 | tf_op jit(solution)/shard_map/ppermute | solution.py:50
  117.2 5.9 %collective-permute-start.26 = (s16[208,256]{1,0:T(8,128)(2,1)S(1)}, s16[208,256]{1,0:T(8,128)(2,1)S(1)}, u32[]{:S(2)}, u32[]{:S(2)}) collective-permute-start(s16[208,256]{1,0:T(8,128)(2,1)S(1)} %get-tuple-element.76), channel_id=1, source_target_pairs={{0,1},{1,2},{2,3},{3,0},{4,7},{5,4},{6,5},{7,6},{8,9},{9,10},{10,1... | collective-permute-start | bytes 319496 | tf_op jit(solution)/shard_map/ppermute | solution.py:50

commit v9 on v8

--- a/solution.py
+++ b/solution.py
@@ -255,19 +255,19 @@
     tiles(0, list_ref, rows, cols, states, w_ref, sum_ref)
 
 
-def build_1(list_ref, rows, c0, c1, c2, c3, given, w_ref, sum_ref, cols, states):
-    put_cols(cols, states, (c0, c1, c2, c3))
+def build_1(list_ref, rows, c0, c1, given, w_ref, sum_ref, cols, states):
+    put_cols(cols, states, (c0, c1))
     sum_ref[...] = given[...]
-    tiles(1, list_ref, rows, cols, states, w_ref, sum_ref)
-
-
-def build_2(list_ref, old_rows, r0, r1, r2, cols, states, given, w2_ref, w3_ref, sum_ref, rows):
+    tiles(1, list_ref, rows, cols, states, w_ref, sum_ref, base=BASE[1])
+
+
+def build_2(list_ref, old_rows, r0, r1, r2, cols, states, cols2, states2, given, w2_ref, w3_ref, sum_ref, rows):
     rows[: 6 * D] = old_rows[: 6 * D]
     rows[8 * D : 9 * D] = old_rows[8 * D :]
     put_rows(rows, (r0, r1, r2), ((6, 2), (9, 2), (11, 1)))
     sum_ref[...] = given[...]
     tiles(2, list_ref, rows, cols, states, w2_ref, sum_ref)
-    tiles(3, list_ref, rows, cols, states, w3_ref, sum_ref)
+    tiles(3, list_ref, rows, cols2, states2, w3_ref, sum_ref, base=BASE[3])
 
 
 def power_of(values):
@@ -454,19 +454,18 @@
     near = make_plan(
         (0, 1, 2), [code(neighbours), code(joined_ids(back_two)), code(joined_ids(fore_one))]
     )
-    w0, sums, rows = build(
-        build_0, 6, [weights_of(0), SUM_BUF, rows_of(9)], columns(2),
+    w0, sums, rows, *near_cols = build(
+        build_0, 4, [weights_of(0), SUM_BUF, rows_of(9), *columns(2)], [],
         near, two, one, back_two, back_one, fore_one, full, partner,
     )
     beside = swap_core(after(above, sums))
-    w1, sums, cols, states = build(
-        build_1, 4, [weights_of(1), SUM_BUF, *columns(4)], [],
-        near, rows, full, partner, above, below, sums,
+    w1, sums, *wide_cols = build(
+        build_1, 4, [weights_of(1), SUM_BUF, *columns(2)], [], near, rows, above, below, sums
     )
     lists = make_plan((3,), [code(joined_ids(after(far_two, sums)))], near)
     w2, w3, sums, rows = build(
         build_2, 4, [weights_of(2), weights_of(3), SUM_BUF, rows_of(12)], [],
-        lists, rows, fore_two, far_two, far_one, cols, states, sums,
+        lists, rows, fore_two, far_two, far_one, *near_cols, *wide_cols, sums,
     )
     part = ((BLK * CH + 16, ROWS), jnp.int16)
     scratch = [SUM_BUF, ((BLK, CH, ROWS), BF16)]

time: 123 us -> 122 us (level)
  waiting for transfers between devices: 44.5 us -> 38.3 us
  starting transfers between devices: 37.3 us -> 41.9 us
    ppermute x3, starting transfers between devices: 3.69 us -> 8.21 us  [across_x(): return lax.ppermute(v, 'x', [(x, (x + 2) % NX) for x in range(NX)])]
    ppermute x6, waiting for transfers between devices: 17.7 us -> 14.7 us  [from_wide(): lax.ppermute(v, WIDE, [((i + (2 * sign if i % 2 == 0 else -2 * sign)) % N...]
    ppermute x12, waiting for transfers between devices: 25.1 us -> 23.5 us  [along_x(): return lax.ppermute(v, ('c', 'x'), pairs)]
    ppermute x3, waiting for transfers between devices: 1.59 us -> 0.01 us  [across_x(): return lax.ppermute(v, 'x', [(x, (x + 2) % NX) for x in range(NX)])]
    ppermute x6, starting transfers between devices: 14.4 us -> 15.6 us  [from_wide(): lax.ppermute(v, WIDE, [((i + (2 * sign if i % 2 == 0 else -2 * sign)) % N...]
  transfers between devices with their start and end apart: 27 -> 27, of which waited for: 13 -> 12; matrix products, arithmetic and copies ran while one was open for 0% -> 0% of each run, Pallas kernels for 26% -> 28%
where the time goes in v9:
time: 122 us; the launch traced here: 123 us
  starting transfers between devices  41.9 us (34%)
  Pallas kernels  40.4 us (33%)
  waiting for transfers between devices  38.3 us (31%)
  other arithmetic  2.28 us (2%)
    pallas_call x11, Pallas kernels, build(): pl.pallas_call(kernel, out_shape=[jax.ShapeDtypeStruct(*o) for o in outs]...  33.6 us
    ppermute x12, waiting for transfers between devices, along_x(): return lax.ppermute(v, ('c', 'x'), pairs)  23.5 us
    ppermute x12, starting transfers between devices, along_x(): return lax.ppermute(v, ('c', 'x'), pairs)  15.9 us
    ppermute x6, starting transfers between devices, from_wide(): lax.ppermute(v, WIDE, [((i + (2 * sign if i % 2 == 0 else -2 * sign)) % N...  15.6 us
    ppermute x6, waiting for transfers between devices, from_wide(): lax.ppermute(v, WIDE, [((i + (2 * sign if i % 2 == 0 else -2 * sign)) % N...  14.7 us
    ppermute x3, starting transfers between devices, across_x(): return lax.ppermute(v, 'x', [(x, (x + 2) % NX) for x in range(NX)])  8.21 us
    pallas_call x2, Pallas kernels, make_plan(): pl.pallas_call(functools.partial(plan_kernel, groups), out_shape=jax.Shap...  4.99 us
  transfers between devices with their start and end apart: 27, of which 12 were waited for; matrix products, arithmetic and copies ran while one was open for 0% of the time, Pallas kernels for 28%

profile of v9, /device:TPU:0, one launch (start us, length us, event | category | flops | bytes accessed | tf_op | source)
XLA Modules:
  0.0 123.3 jit_solution(6795272348513657679)
XLA Ops:
  0.0 0.7 shift-right-arithmetic_convert_fusion
  0.8 1.7 %prep.1 = (bf16[1552,256]{1,0:T(8,128)(2,1)S(1)}, bf16[832,768]{1,0:T(8,128)(2,1)S(1)}) custom-call(bf16[3,256,768]{2,1,0:T(8,128)(2,1)} %emb_hbm.1, f32[3,64,256]{2,1,0:T(8,128)} %bitcast.24, bf16[16,256]{1,0:T(8,128)(2,1)S(1)} %fusion.23.ids_ref), custom_call_target="tpu_custom_call" | custom-call | flops 1000 | bytes 1000 | tf_op jit(solution)/shard_map/prep/pallas_call | solution.py:88
  2.5 1.6 %collective-permute-start = (bf16[1552,256]{1,0:T(8,128)(2,1)S(1)}, bf16[1552,256]{1,0:T(8,128)(2,1)S(1)}, u32[]{:S(2)}, u32[]{:S(2)}) collective-permute-start(bf16[1552,256]{1,0:T(8,128)(2,1)S(1)} %get-tuple-element.54.r0), channel_id=1, source_target_pairs={{0,1},{1,2},{2,3},{3,0},{4,7},{5,4},{6,5},{7,6},{8,9},{9,10},{10,1... | collective-permute-start | bytes 2383880 | tf_op jit(solution)/shard_map/ppermute | solution.py:50
  4.2 0.1 third.1.r1
  4.3 1.6 %collective-permute-start.2 = (bf16[784,256]{1,0:T(8,128)(2,1)S(1)}, bf16[784,256]{1,0:T(8,128)(2,1)S(1)}, u32[]{:S(2)}, u32[]{:S(2)}) collective-permute-start(bf16[784,256]{1,0:T(8,128)(2,1)S(1)} %third.1.r1), channel_id=1, source_target_pairs={{0,1},{1,2},{2,3},{3,0},{4,7},{5,4},{6,5},{7,6},{8,9},{9,10},{10,1... | collective-permute-start | bytes 1204232 | tf_op jit(solution)/shard_map/ppermute | solution.py:50
  5.9 1.7 %collective-permute-start.1 = (bf16[784,256]{1,0:T(8,128)(2,1)S(1)}, bf16[784,256]{1,0:T(8,128)(2,1)S(1)}, u32[]{:S(2)}, u32[]{:S(2)}) collective-permute-start(bf16[784,256]{1,0:T(8,128)(2,1)S(1)} %third.1.r1), channel_id=1, source_target_pairs={{0,3},{1,0},{2,1},{3,2},{4,5},{5,6},{6,7},{7,4},{8,11},{9,8},{10,9... | collective-permute-start | bytes 1204232 | tf_op jit(solution)/shard_map/ppermute | solution.py:50
  7.6 1.6 %collective-permute-start.6 = (bf16[832,768]{1,0:T(8,128)(2,1)S(1)}, bf16[832,768]{1,0:T(8,128)(2,1)S(1)}, u32[]{:S(2)}, u32[]{:S(2)}) collective-permute-start(bf16[832,768]{1,0:T(8,128)(2,1)S(1)} %get-tuple-element.48.full_ref.c0), channel_id=1, source_target_pairs={{120,0},{12,4},{0,8},{20,12},{8,16},{28,20},{16,24},{36,28},{24,32... | collective-permute-start | bytes 3833864 | tf_op jit(solution)/shard_map/ppermute | solution.py:58
  9.2 4.9 %collective-permute-start.5 = (bf16[832,768]{1,0:T(8,128)(2,1)S(1)}, bf16[832,768]{1,0:T(8,128)(2,1)S(1)}, u32[]{:S(2)}, u32[]{:S(2)}) collective-permute-start(bf16[832,768]{1,0:T(8,128)(2,1)S(1)} %get-tuple-element.48.full_ref.c0), channel_id=1, source_target_pairs={{8,0},{124,4},{16,8},{4,12},{24,16},{12,20},{32,24},{20,28},{40,32... | collective-permute-start | bytes 3833864 | tf_op jit(solution)/shard_map/ppermute | solution.py:58
  14.1 10.4 %collective-permute-done.2.r3 = bf16[784,256]{1,0:T(8,128)(2,1)S(1)} collective-permute-done((bf16[784,256]{1,0:T(8,128)(2,1)S(1)}, bf16[784,256]{1,0:T(8,128)(2,1)S(1)}, u32[]{:S(2)}, u32[]{:S(2)}) %collective-permute-start.2) | collective-permute-done | bytes 401440 | tf_op jit(solution)/shard_map/ppermute | solution.py:50
  24.5 0.4 collective-permute-start.3
  24.9 2.9 %collective-permute-start.7 = (bf16[1552,256]{1,0:T(8,128)(2,1)S(1)}, bf16[1552,256]{1,0:T(8,128)(2,1)S(1)}, u32[]{:S(2)}, u32[]{:S(2)}) collective-permute-start(bf16[1552,256]{1,0:T(8,128)(2,1)S(1)} %get-tuple-element.54.r0), channel_id=1, source_target_pairs={{0,3},{1,0},{2,1},{3,2},{4,5},{5,6},{6,7},{7,4},{8,11},{9,8},{10,9... | collective-permute-start | bytes 2383880 | tf_op jit(solution)/shard_map/ppermute | solution.py:50
  27.9 3.0 %plan.2.list_ref.refs_1_.near_ref = s32[256]{0:T(256)S(1)} custom-call(s32[3,32]{1,0:T(4,128)S(1)} %get-tuple-element.87.refs_0_, s32[3,32]{1,0:T(4,128)S(1)} %get-tuple-element.88.refs_1_, s32[3,32]{1,0:T(4,128)S(1)} %get-tuple-element.89.refs_2_), custom_call_target="tpu_custom_call" | custom-call | flops 30000001024 | bytes 1000 | tf_op jit(solution)/shard_map/plan/pallas_call | solution.py:194
  31.0 1.3 %collective-permute-start.8 = (bf16[784,256]{1,0:T(8,128)(2,1)S(1)}, bf16[784,256]{1,0:T(8,128)(2,1)S(1)}, u32[]{:S(2)}, u32[]{:S(2)}) collective-permute-start(bf16[784,256]{1,0:T(8,128)(2,1)S(1)} %collective-permute-done.1.r4), channel_id=1, source_target_pairs={{0,3},{1,0},{2,1},{3,2},{4,5},{5,6},{6,7},{7,4},{8,11},{9,8},{10,9... | collective-permute-start | bytes 1204232 | tf_op jit(solution)/shard_map/ppermute | solution.py:50
  32.3 4.7 %build_0.1 = (bf16[44,256,256]{2,1,0:T(8,128)(2,1)S(1)}, f32[13,72,256]{2,1,0:T(8,128)S(1)}, bf16[6912,256]{1,0:T(8,128)(2,1)S(1)}, bf16[1536,768]{1,0:T(8,128)(2,1)S(1)}, bf16[6,64,256]{2,1,0:T(8,128)(2,1)S(1)}) custom-call(s32[256]{0:T(256)S(1)} %plan.2.list_ref.refs_1_.near_ref, bf16[1552,256]{1,0:T(8,128)(2,1)S(1)} %get-tuple-element.54.r0, ...), custom_call_target="tpu_custom_call" | custom-call | flops 30000001024 | bytes 1000 | tf_op jit(solution)/shard_map/build_0/pallas_call | solution.py:335
  37.0 3.7 %collective-permute-done.5.c0 = bf16[832,768]{1,0:T(8,128)(2,1)S(1)} collective-permute-done((bf16[832,768]{1,0:T(8,128)(2,1)S(1)}, bf16[832,768]{1,0:T(8,128)(2,1)S(1)}, u32[]{:S(2)}, u32[]{:S(2)}) %collective-permute-start.5) | collective-permute-done | bytes 1277984 | tf_op jit(solution)/shard_map/ppermute | solution.py:58
  40.7 2.2 %collective-permute-start.9 = (bf16[832,768]{1,0:T(8,128)(2,1)S(1)}, bf16[832,768]{1,0:T(8,128)(2,1)S(1)}, u32[]{:S(2)}, u32[]{:S(2)}) collective-permute-start(bf16[832,768]{1,0:T(8,128)(2,1)S(1)} %collective-permute-done.5.c0), channel_id=1, source_target_pairs={{0,4},{4,0},{1,5},{5,1},{2,6},{6,2},{3,7},{7,3},{8,12},{12,8},{9,1... | collective-permute-start | bytes 3833864 | tf_op jit(solution)/shard_map/ppermute | solution.py:64
  42.9 5.2 %build_1.1 = (bf16[44,256,256]{2,1,0:T(8,128)(2,1)S(1)}, f32[13,72,256]{2,1,0:T(8,128)S(1)}, bf16[1536,768]{1,0:T(8,128)(2,1)S(1)}, bf16[6,64,256]{2,1,0:T(8,128)(2,1)S(1)}) custom-call(s32[256]{0:T(256)S(1)} %plan.2.list_ref.refs_1_.near_ref, bf16[6912,256]{1,0:T(8,128)(2,1)S(1)} %get-tuple-element.49.rows.old_rows, ...), custom_call_target="tpu_custom_call" | custom-call | flops 30000001024 | bytes 1000 | tf_op jit(solution)/shard_map/build_1/pallas_call | solution.py:335
  48.2 2.0 %plan.3.list_ref = s32[256]{0:T(256)S(1)} custom-call(s32[3,32]{1,0:T(4,128)S(1)} %fusion.51.refs_0_, s32[256]{0:T(256)S(1)} %plan.2.list_ref.refs_1_.near_ref), custom_call_target="tpu_custom_call" | custom-call | flops 30000001024 | bytes 1000 | tf_op jit(solution)/shard_map/plan/pallas_call | solution.py:194
  50.2 4.8 %build_2.1 = (bf16[36,256,256]{2,1,0:T(8,128)(2,1)S(1)}, bf16[36,256,256]{2,1,0:T(8,128)(2,1)S(1)}, f32[13,72,256]{2,1,0:T(8,128)S(1)}, bf16[9216,256]{1,0:T(8,128)(2,1)S(1)}) custom-call(s32[256]{0:T(256)S(1)} %plan.3.list_ref, bf16[6912,256]{1,0:T(8,128)(2,1)S(1)} %get-tuple-element.49.rows.old_rows, bf16[1552,256]{1,0:T(8,128)(2,1)S(1)} %collective-permute-done.7.r0, ...), custom_call_target="tpu_custom_call" | custom-call | flops 30000001024 | bytes 1000 | tf_op jit(solution)/shard_map/build_2/pallas_call | solution.py:335
  55.0 1.6 %build_far.1 = (bf16[40,256,256]{2,1,0:T(8,128)(2,1)S(1)}, s16[208,256]{1,0:T(8,128)(2,1)S(1)}) custom-call(s32[256]{0:T(256)S(1)} %plan.3.list_ref, bf16[9216,256]{1,0:T(8,128)(2,1)S(1)} %get-tuple-element.61.rows, bf16[832,768]{1,0:T(8,128)(2,1)S(1)} %collective-permute-done.9.c4, f32[13,72,256]{2,1,0:T(8,128)S(1)} %get-tuple-element.65.given), custom_call_target="tpu_custom_call" | custom-call | flops 30000001024 | bytes 1000 | tf_op jit(solution)/shard_map/build_far/pallas_call | solution.py:335
  56.7 3.8 %collective-permute-start.10 = (s16[208,256]{1,0:T(8,128)(2,1)S(1)}, s16[208,256]{1,0:T(8,128)(2,1)S(1)}, u32[]{:S(2)}, u32[]{:S(2)}) collective-permute-start(s16[208,256]{1,0:T(8,128)(2,1)S(1)} %get-tuple-element.64), channel_id=1, source_target_pairs={{0,2},{1,3},{2,0},{3,1},{4,6},{5,7},{6,4},{7,5},{8,10},{9,11},{10,... | collective-permute-start | bytes 319496 | tf_op jit(solution)/shard_map/ppermute | solution.py:54
  60.5 3.8 %build_rest.1 = (bf16[40,256,256]{2,1,0:T(8,128)(2,1)S(1)}, f32[3,72,256]{2,1,0:T(8,128)S(1)}, s16[208,256]{1,0:T(8,128)(2,1)S(1)}, s16[208,256]{1,0:T(8,128)(2,1)S(1)}) custom-call(s32[256]{0:T(256)S(1)} %plan.3.list_ref, bf16[9216,256]{1,0:T(8,128)(2,1)S(1)} %get-tuple-element.61.rows, bf16[832,768]{1,0:T(8,128)(2,1)S(1)} %collective-permute-done.9.c4, ...), custom_call_target="tpu_custom_call" | custom-call | flops 30000001024 | bytes 1000 | tf_op jit(solution)/shard_map/build_rest/pallas_call | solution.py:335
  64.4 2.0 %collective-permute-start.12 = (s16[208,256]{1,0:T(8,128)(2,1)S(1)}, s16[208,256]{1,0:T(8,128)(2,1)S(1)}, u32[]{:S(2)}, u32[]{:S(2)}) collective-permute-start(s16[208,256]{1,0:T(8,128)(2,1)S(1)} %get-tuple-element.69), channel_id=1, source_target_pairs={{0,1},{1,2},{2,3},{3,0},{4,7},{5,4},{6,5},{7,6},{8,9},{9,10},{10,1... | collective-permute-start | bytes 319496 | tf_op jit(solution)/shard_map/ppermute | solution.py:50
  66.4 2.6 %collective-permute-done.11 = s16[208,256]{1,0:T(8,128)(2,1)S(1)} collective-permute-done((s16[208,256]{1,0:T(8,128)(2,1)S(1)}, s16[208,256]{1,0:T(8,128)(2,1)S(1)}, u32[]{:S(2)}, u32[]{:S(2)}) %collective-permute-start.11) | collective-permute-done | bytes 106528 | tf_op jit(solution)/shard_map/ppermute | solution.py:50
  69.1 1.3 %collective-permute-done.12 = s16[208,256]{1,0:T(8,128)(2,1)S(1)} collective-permute-done((s16[208,256]{1,0:T(8,128)(2,1)S(1)}, s16[208,256]{1,0:T(8,128)(2,1)S(1)}, u32[]{:S(2)}, u32[]{:S(2)}) %collective-permute-start.12) | collective-permute-done | bytes 106528 | tf_op jit(solution)/shard_map/ppermute | solution.py:50
  70.6 6.4 %collective-permute-start.13 = (bf16[3,64,256]{2,1,0:T(8,128)(2,1)S(1)}, bf16[3,64,256]{2,1,0:T(8,128)(2,1)S(1)}, u32[]{:S(2)}, u32[]{:S(2)}) collective-permute-start(bf16[3,64,256]{2,1,0:T(8,128)(2,1)S(1)} %fusion.15.s0), channel_id=1, source_target_pairs={{8,0},{124,4},{16,8},{4,12},{24,16},{12,20},{32,24},{20,28},{40,32... | collective-permute-start | bytes 294920 | tf_op jit(solution)/shard_map/ppermute | solution.py:58
  77.1 3.2 %collective-permute-done.13.s2 = bf16[3,64,256]{2,1,0:T(8,128)(2,1)S(1)} collective-permute-done((bf16[3,64,256]{2,1,0:T(8,128)(2,1)S(1)}, bf16[3,64,256]{2,1,0:T(8,128)(2,1)S(1)}, u32[]{:S(2)}, u32[]{:S(2)}) %collective-permute-start.13) | collective-permute-done | bytes 98336 | tf_op jit(solution)/shard_map/ppermute | solution.py:58
  80.3 2.4 %spread_near.2.given = f32[13,64,256]{2,1,0:T(8,128)S(1)} custom-call(s32[256]{0:T(256)S(1)} %plan.2.list_ref.refs_1_.near_ref, s32[256]{0:T(256)S(1)} %plan.3.list_ref, bf16[44,256,256]{2,1,0:T(8,128)(2,1)S(1)} %get-tuple-element.70.w0, bf16[36,256,256]{2,1,0:T(8,128)(2,1)S(1)} %get-tuple-element.71.w2, bf16[3,64,256]{2,1,0:T(8,128)(2,1)S(1)} %fusion.15.s0, ...), custom_call_target="tpu_custom_call" | custom-call | flops 30000001024 | bytes 1000 | tf_op jit(solution)/shard_map/spread_near/pallas_call | solution.py:335
  82.6 2.4 %collective-permute-done.14.s3 = bf16[3,64,256]{2,1,0:T(8,128)(2,1)S(1)} collective-permute-done((bf16[3,64,256]{2,1,0:T(8,128)(2,1)S(1)}, bf16[3,64,256]{2,1,0:T(8,128)(2,1)S(1)}, u32[]{:S(2)}, u32[]{:S(2)}) %collective-permute-start.14) | collective-permute-done | bytes 98336 | tf_op jit(solution)/shard_map/ppermute | solution.py:58
  85.0 1.1 spread_far.2
  86.1 2.2 %collective-permute-start.17 = (s16[208,256]{1,0:T(8,128)(2,1)S(1)}, s16[208,256]{1,0:T(8,128)(2,1)S(1)}, u32[]{:S(2)}, u32[]{:S(2)}) collective-permute-start(s16[208,256]{1,0:T(8,128)(2,1)S(1)} %spread_far.2), channel_id=1, source_target_pairs={{0,2},{1,3},{2,0},{3,1},{4,6},{5,7},{6,4},{7,5},{8,10},{9,11},{10,... | collective-permute-start | bytes 319496 | tf_op jit(solution)/shard_map/ppermute | solution.py:54
  88.4 3.2 %spread_rest.2 = (f32[3,64,256]{2,1,0:T(8,128)S(1)}, s16[208,256]{1,0:T(8,128)(2,1)S(1)}, s16[208,256]{1,0:T(8,128)(2,1)S(1)}) custom-call(s32[256]{0:T(256)S(1)} %plan.2.list_ref.refs_1_.near_ref, s32[256]{0:T(256)S(1)} %plan.3.list_ref, bf16[44,256,256]{2,1,0:T(8,128)(2,1)S(1)} %get-tuple-element.53.w1, bf16[36,256,256]{2,1,0:T(8,128)(2,1)S(1)} %get-tuple-element.60.w3, ...), custom_call_target="tpu_custom_call" | custom-call | flops 30000001024 | bytes 1000 | tf_op jit(solution)/shard_map/spread_rest/pallas_call | solution.py:335
  91.5 0.5 collective-permute-start.18
  92.1 1.6 %collective-permute-start.19 = (s16[208,256]{1,0:T(8,128)(2,1)S(1)}, s16[208,256]{1,0:T(8,128)(2,1)S(1)}, u32[]{:S(2)}, u32[]{:S(2)}) collective-permute-start(s16[208,256]{1,0:T(8,128)(2,1)S(1)} %get-tuple-element.76), channel_id=1, source_target_pairs={{0,1},{1,2},{2,3},{3,0},{4,7},{5,4},{6,5},{7,6},{8,9},{9,10},{10,1... | collective-permute-start | bytes 319496 | tf_op jit(solution)/shard_map/ppermute | solution.py:50
  93.7 2.6 %collective-permute-done.18 = s16[208,256]{1,0:T(8,128)(2,1)S(1)} collective-permute-done((s16[208,256]{1,0:T(8,128)(2,1)S(1)}, s16[208,256]{1,0:T(8,128)(2,1)S(1)}, u32[]{:S(2)}, u32[]{:S(2)}) %collective-permute-start.18) | collective-permute-done | bytes 106528 | tf_op jit(solution)/shard_map/ppermute | solution.py:50
  96.3 1.7 %collective-permute-done.19 = s16[208,256]{1,0:T(8,128)(2,1)S(1)} collective-permute-done((s16[208,256]{1,0:T(8,128)(2,1)S(1)}, s16[208,256]{1,0:T(8,128)(2,1)S(1)}, u32[]{:S(2)}, u32[]{:S(2)}) %collective-permute-start.19) | collective-permute-done | bytes 106528 | tf_op jit(solution)/shard_map/ppermute | solution.py:50
  98.1 2.7 %collective-permute-start.20 = (bf16[3,64,256]{2,1,0:T(8,128)(2,1)S(1)}, bf16[3,64,256]{2,1,0:T(8,128)(2,1)S(1)}, u32[]{:S(2)}, u32[]{:S(2)}) collective-permute-start(bf16[3,64,256]{2,1,0:T(8,128)(2,1)S(1)} %fusion.9.s0), channel_id=1, source_target_pairs={{8,0},{124,4},{16,8},{4,12},{24,16},{12,20},{32,24},{20,28},{40,32... | collective-permute-start | bytes 294920 | tf_op jit(solution)/shard_map/ppermute | solution.py:58
  100.9 3.0 %collective-permute-done.20.s2 = bf16[3,64,256]{2,1,0:T(8,128)(2,1)S(1)} collective-permute-done((bf16[3,64,256]{2,1,0:T(8,128)(2,1)S(1)}, bf16[3,64,256]{2,1,0:T(8,128)(2,1)S(1)}, u32[]{:S(2)}, u32[]{:S(2)}) %collective-permute-start.20) | collective-permute-done | bytes 98336 | tf_op jit(solution)/shard_map/ppermute | solution.py:58
  103.9 2.4 %spread_near.3.given = f32[13,64,256]{2,1,0:T(8,128)S(1)} custom-call(s32[256]{0:T(256)S(1)} %plan.2.list_ref.refs_1_.near_ref, s32[256]{0:T(256)S(1)} %plan.3.list_ref, bf16[44,256,256]{2,1,0:T(8,128)(2,1)S(1)} %get-tuple-element.70.w0, bf16[36,256,256]{2,1,0:T(8,128)(2,1)S(1)} %get-tuple-element.71.w2, bf16[3,64,256]{2,1,0:T(8,128)(2,1)S(1)} %fusion.9.s0, ...), custom_call_target="tpu_custom_call" | custom-call | flops 30000001024 | bytes 1000 | tf_op jit(solution)/shard_map/spread_near/pallas_call | solution.py:335
  106.3 2.5 %collective-permute-done.21.s3 = bf16[3,64,256]{2,1,0:T(8,128)(2,1)S(1)} collective-permute-done((bf16[3,64,256]{2,1,0:T(8,128)(2,1)S(1)}, bf16[3,64,256]{2,1,0:T(8,128)(2,1)S(1)}, u32[]{:S(2)}, u32[]{:S(2)}) %collective-permute-start.21) | collective-permute-done | bytes 98336 | tf_op jit(solution)/shard_map/ppermute | solution.py:58
  108.8 1.1 spread_far.3
  109.9 2.2 %collective-permute-start.24 = (s16[208,256]{1,0:T(8,128)(2,1)S(1)}, s16[208,256]{1,0:T(8,128)(2,1)S(1)}, u32[]{:S(2)}, u32[]{:S(2)}) collective-permute-start(s16[208,256]{1,0:T(8,128)(2,1)S(1)} %spread_far.3), channel_id=1, source_target_pairs={{0,2},{1,3},{2,0},{3,1},{4,6},{5,7},{6,4},{7,5},{8,10},{9,11},{10,... | collective-permute-start | bytes 319496 | tf_op jit(solution)/shard_map/ppermute | solution.py:54
  112.2 3.2 %spread_rest.3 = (f32[3,64,256]{2,1,0:T(8,128)S(1)}, s16[208,256]{1,0:T(8,128)(2,1)S(1)}, s16[208,256]{1,0:T(8,128)(2,1)S(1)}) custom-call(s32[256]{0:T(256)S(1)} %plan.2.list_ref.refs_1_.near_ref, s32[256]{0:T(256)S(1)} %plan.3.list_ref, bf16[44,256,256]{2,1,0:T(8,128)(2,1)S(1)} %get-tuple-element.53.w1, bf16[36,256,256]{2,1,0:T(8,128)(2,1)S(1)} %get-tuple-element.60.w3, ...), custom_call_target="tpu_custom_call" | custom-call | flops 30000001024 | bytes 1000 | tf_op jit(solution)/shard_map/spread_rest/pallas_call | solution.py:335
  115.3 1.2 %collective-permute-start.25 = (s16[208,256]{1,0:T(8,128)(2,1)S(1)}, s16[208,256]{1,0:T(8,128)(2,1)S(1)}, u32[]{:S(2)}, u32[]{:S(2)}) collective-permute-start(s16[208,256]{1,0:T(8,128)(2,1)S(1)} %get-tuple-element.79), channel_id=1, source_target_pairs={{0,3},{1,0},{2,1},{3,2},{4,5},{5,6},{6,7},{7,4},{8,11},{9,8},{10,9... | collective-permute-start | bytes 319496 | tf_op jit(solution)/shard_map/ppermute | solution.py:50
  116.6 0.8 collective-permute-start.26
  117.5 2.6 %collective-permute-done.25 = s16[208,256]{1,0:T(8,128)(2,1)S(1)} collective-permute-done((s16[208,256]{1,0:T(8,128)(2,1)S(1)}, s16[208,256]{1,0:T(8,128)(2,1)S(1)}, u32[]{:S(2)}, u32[]{:S(2)}) %collective-permute-start.25) | collective-permute-done | bytes 106528 | tf_op jit(solution)/shard_map/ppermute | solution.py:50
  120.1 2.4 %collective-permute-done.26 = s16[208,256]{1,0:T(8,128)(2,1)S(1)} collective-permute-done((s16[208,256]{1,0:T(8,128)(2,1)S(1)}, s16[208,256]{1,0:T(8,128)(2,1)S(1)}, u32[]{:S(2)}, u32[]{:S(2)}) %collective-permute-start.26) | collective-permute-done | bytes 106528 | tf_op jit(solution)/shard_map/ppermute | solution.py:50
  122.5 0.8 fusion.3
  (53 shorter events, 1.0 us)
Async XLA Ops:
  2.5 22.0 %collective-permute-start = (bf16[1552,256]{1,0:T(8,128)(2,1)S(1)}, bf16[1552,256]{1,0:T(8,128)(2,1)S(1)}, u32[]{:S(2)}, u32[]{:S(2)}) collective-permute-start(bf16[1552,256]{1,0:T(8,128)(2,1)S(1)} %get-tuple-element.54.r0), channel_id=1, source_target_pairs={{0,1},{1,2},{2,3},{3,0},{4,7},{5,4},{6,5},{7,6},{8,9},{9,10},{10,1... | collective-permute-start | bytes 2383880 | tf_op jit(solution)/shard_map/ppermute | solution.py:50
  4.3 20.2 %collective-permute-start.2 = (bf16[784,256]{1,0:T(8,128)(2,1)S(1)}, bf16[784,256]{1,0:T(8,128)(2,1)S(1)}, u32[]{:S(2)}, u32[]{:S(2)}) collective-permute-start(bf16[784,256]{1,0:T(8,128)(2,1)S(1)} %third.1.r1), channel_id=1, source_target_pairs={{0,1},{1,2},{2,3},{3,0},{4,7},{5,4},{6,5},{7,6},{8,9},{9,10},{10,1... | collective-permute-start | bytes 1204232 | tf_op jit(solution)/shard_map/ppermute | solution.py:50
  5.9 18.6 %collective-permute-start.1 = (bf16[784,256]{1,0:T(8,128)(2,1)S(1)}, bf16[784,256]{1,0:T(8,128)(2,1)S(1)}, u32[]{:S(2)}, u32[]{:S(2)}) collective-permute-start(bf16[784,256]{1,0:T(8,128)(2,1)S(1)} %third.1.r1), channel_id=1, source_target_pairs={{0,3},{1,0},{2,1},{3,2},{4,5},{5,6},{6,7},{7,4},{8,11},{9,8},{10,9... | collective-permute-start | bytes 1204232 | tf_op jit(solution)/shard_map/ppermute | solution.py:50
  7.6 35.2 %collective-permute-start.6 = (bf16[832,768]{1,0:T(8,128)(2,1)S(1)}, bf16[832,768]{1,0:T(8,128)(2,1)S(1)}, u32[]{:S(2)}, u32[]{:S(2)}) collective-permute-start(bf16[832,768]{1,0:T(8,128)(2,1)S(1)} %get-tuple-element.48.full_ref.c0), channel_id=1, source_target_pairs={{120,0},{12,4},{0,8},{20,12},{8,16},{28,20},{16,24},{36,28},{24,32... | collective-permute-start | bytes 3833864 | tf_op jit(solution)/shard_map/ppermute | solution.py:58
  9.2 31.5 %collective-permute-start.5 = (bf16[832,768]{1,0:T(8,128)(2,1)S(1)}, bf16[832,768]{1,0:T(8,128)(2,1)S(1)}, u32[]{:S(2)}, u32[]{:S(2)}) collective-permute-start(bf16[832,768]{1,0:T(8,128)(2,1)S(1)} %get-tuple-element.48.full_ref.c0), channel_id=1, source_target_pairs={{8,0},{124,4},{16,8},{4,12},{24,16},{12,20},{32,24},{20,28},{40,32... | collective-permute-start | bytes 3833864 | tf_op jit(solution)/shard_map/ppermute | solution.py:58
  24.5 23.6 %collective-permute-start.3 = (bf16[1552,256]{1,0:T(8,128)(2,1)S(1)}, bf16[1552,256]{1,0:T(8,128)(2,1)S(1)}, u32[]{:S(2)}, u32[]{:S(2)}) collective-permute-start(bf16[1552,256]{1,0:T(8,128)(2,1)S(1)} %collective-permute-done.r2), channel_id=1, source_target_pairs={{0,1},{1,2},{2,3},{3,0},{4,7},{5,4},{6,5},{7,6},{8,9},{9,10},{10,1... | collective-permute-start | bytes 2383880 | tf_op jit(solution)/shard_map/ppermute | solution.py:50
  24.9 25.2 %collective-permute-start.7 = (bf16[1552,256]{1,0:T(8,128)(2,1)S(1)}, bf16[1552,256]{1,0:T(8,128)(2,1)S(1)}, u32[]{:S(2)}, u32[]{:S(2)}) collective-permute-start(bf16[1552,256]{1,0:T(8,128)(2,1)S(1)} %get-tuple-element.54.r0), channel_id=1, source_target_pairs={{0,3},{1,0},{2,1},{3,2},{4,5},{5,6},{6,7},{7,4},{8,11},{9,8},{10,9... | collective-permute-start | bytes 2383880 | tf_op jit(solution)/shard_map/ppermute | solution.py:50
  27.8 3.2 %collective-permute-start.4 = (bf16[832,768]{1,0:T(8,128)(2,1)S(1)}, bf16[832,768]{1,0:T(8,128)(2,1)S(1)}, u32[]{:S(2)}, u32[]{:S(2)}) collective-permute-start(bf16[832,768]{1,0:T(8,128)(2,1)S(1)} %get-tuple-element.48.full_ref.c0), channel_id=1, source_target_pairs={{0,4},{4,0},{1,5},{5,1},{2,6},{6,2},{3,7},{7,3},{8,12},{12,8},{9,1... | collective-permute-start | bytes 3833864 | tf_op jit(solution)/shard_map/ppermute | solution.py:64
  31.0 19.2 %collective-permute-start.8 = (bf16[784,256]{1,0:T(8,128)(2,1)S(1)}, bf16[784,256]{1,0:T(8,128)(2,1)S(1)}, u32[]{:S(2)}, u32[]{:S(2)}) collective-permute-start(bf16[784,256]{1,0:T(8,128)(2,1)S(1)} %collective-permute-done.1.r4), channel_id=1, source_target_pairs={{0,3},{1,0},{2,1},{3,2},{4,5},{5,6},{6,7},{7,4},{8,11},{9,8},{10,9... | collective-permute-start | bytes 1204232 | tf_op jit(solution)/shard_map/ppermute | solution.py:50
  40.7 14.3 %collective-permute-start.9 = (bf16[832,768]{1,0:T(8,128)(2,1)S(1)}, bf16[832,768]{1,0:T(8,128)(2,1)S(1)}, u32[]{:S(2)}, u32[]{:S(2)}) collective-permute-start(bf16[832,768]{1,0:T(8,128)(2,1)S(1)} %collective-permute-done.5.c0), channel_id=1, source_target_pairs={{0,4},{4,0},{1,5},{5,1},{2,6},{6,2},{3,7},{7,3},{8,12},{12,8},{9,1... | collective-permute-start | bytes 3833864 | tf_op jit(solution)/shard_map/ppermute | solution.py:64
  56.7 13.8 %copy-start = (f32[3,256,64]{1,2,0:T(8,128)S(1)}, f32[3,256,64]{1,2,0:T(8,128)}, u32[]{:S(2)}) copy-start(f32[3,256,64]{1,2,0:T(8,128)} %param.4) | copy-start | bytes 589828
  56.7 9.7 %collective-permute-start.10 = (s16[208,256]{1,0:T(8,128)(2,1)S(1)}, s16[208,256]{1,0:T(8,128)(2,1)S(1)}, u32[]{:S(2)}, u32[]{:S(2)}) collective-permute-start(s16[208,256]{1,0:T(8,128)(2,1)S(1)} %get-tuple-element.64), channel_id=1, source_target_pairs={{0,2},{1,3},{2,0},{3,1},{4,6},{5,7},{6,4},{7,5},{8,10},{9,11},{10,... | collective-permute-start | bytes 319496 | tf_op jit(solution)/shard_map/ppermute | solution.py:54
  64.3 4.8 %collective-permute-start.11 = (s16[208,256]{1,0:T(8,128)(2,1)S(1)}, s16[208,256]{1,0:T(8,128)(2,1)S(1)}, u32[]{:S(2)}, u32[]{:S(2)}) collective-permute-start(s16[208,256]{1,0:T(8,128)(2,1)S(1)} %get-tuple-element.68), channel_id=1, source_target_pairs={{0,3},{1,0},{2,1},{3,2},{4,5},{5,6},{6,7},{7,4},{8,11},{9,8},{10,9... | collective-permute-start | bytes 319496 | tf_op jit(solution)/shard_map/ppermute | solution.py:50
  64.4 6.0 %collective-permute-start.12 = (s16[208,256]{1,0:T(8,128)(2,1)S(1)}, s16[208,256]{1,0:T(8,128)(2,1)S(1)}, u32[]{:S(2)}, u32[]{:S(2)}) collective-permute-start(s16[208,256]{1,0:T(8,128)(2,1)S(1)} %get-tuple-element.69), channel_id=1, source_target_pairs={{0,1},{1,2},{2,3},{3,0},{4,7},{5,4},{6,5},{7,6},{8,9},{9,10},{10,1... | collective-permute-start | bytes 319496 | tf_op jit(solution)/shard_map/ppermute | solution.py:50
  70.6 9.6 %collective-permute-start.13 = (bf16[3,64,256]{2,1,0:T(8,128)(2,1)S(1)}, bf16[3,64,256]{2,1,0:T(8,128)(2,1)S(1)}, u32[]{:S(2)}, u32[]{:S(2)}) collective-permute-start(bf16[3,64,256]{2,1,0:T(8,128)(2,1)S(1)} %fusion.15.s0), channel_id=1, source_target_pairs={{8,0},{124,4},{16,8},{4,12},{24,16},{12,20},{32,24},{20,28},{40,32... | collective-permute-start | bytes 294920 | tf_op jit(solution)/shard_map/ppermute | solution.py:58
  77.1 3.2 %collective-permute-start.16 = (bf16[3,64,256]{2,1,0:T(8,128)(2,1)S(1)}, bf16[3,64,256]{2,1,0:T(8,128)(2,1)S(1)}, u32[]{:S(2)}, u32[]{:S(2)}) collective-permute-start(bf16[3,64,256]{2,1,0:T(8,128)(2,1)S(1)} %fusion.15.s0), channel_id=1, source_target_pairs={{0,4},{4,0},{1,5},{5,1},{2,6},{6,2},{3,7},{7,3},{8,12},{12,8},{9,1... | collective-permute-start | bytes 294920 | tf_op jit(solution)/shard_map/ppermute | solution.py:64
  77.1 7.9 %collective-permute-start.14 = (bf16[3,64,256]{2,1,0:T(8,128)(2,1)S(1)}, bf16[3,64,256]{2,1,0:T(8,128)(2,1)S(1)}, u32[]{:S(2)}, u32[]{:S(2)}) collective-permute-start(bf16[3,64,256]{2,1,0:T(8,128)(2,1)S(1)} %fusion.15.s0), channel_id=1, source_target_pairs={{120,0},{12,4},{0,8},{20,12},{8,16},{28,20},{16,24},{36,28},{24,32... | collective-permute-start | bytes 294920 | tf_op jit(solution)/shard_map/ppermute | solution.py:58
  80.2 4.8 %collective-permute-start.15 = (bf16[3,64,256]{2,1,0:T(8,128)(2,1)S(1)}, bf16[3,64,256]{2,1,0:T(8,128)(2,1)S(1)}, u32[]{:S(2)}, u32[]{:S(2)}) collective-permute-start(bf16[3,64,256]{2,1,0:T(8,128)(2,1)S(1)} %collective-permute-done.13.s2), channel_id=1, source_target_pairs={{0,4},{4,0},{1,5},{5,1},{2,6},{6,2},{3,7},{7,3},{8,12},{12,8},{9,1... | collective-permute-start | bytes 294920 | tf_op jit(solution)/shard_map/ppermute | solution.py:64
  86.1 7.5 %collective-permute-start.17 = (s16[208,256]{1,0:T(8,128)(2,1)S(1)}, s16[208,256]{1,0:T(8,128)(2,1)S(1)}, u32[]{:S(2)}, u32[]{:S(2)}) collective-permute-start(s16[208,256]{1,0:T(8,128)(2,1)S(1)} %spread_far.2), channel_id=1, source_target_pairs={{0,2},{1,3},{2,0},{3,1},{4,6},{5,7},{6,4},{7,5},{8,10},{9,11},{10,... | collective-permute-start | bytes 319496 | tf_op jit(solution)/shard_map/ppermute | solution.py:54
  91.5 4.8 %collective-permute-start.18 = (s16[208,256]{1,0:T(8,128)(2,1)S(1)}, s16[208,256]{1,0:T(8,128)(2,1)S(1)}, u32[]{:S(2)}, u32[]{:S(2)}) collective-permute-start(s16[208,256]{1,0:T(8,128)(2,1)S(1)} %get-tuple-element.75), channel_id=1, source_target_pairs={{0,3},{1,0},{2,1},{3,2},{4,5},{5,6},{6,7},{7,4},{8,11},{9,8},{10,9... | collective-permute-start | bytes 319496 | tf_op jit(solution)/shard_map/ppermute | solution.py:50
  92.1 5.9 %collective-permute-start.19 = (s16[208,256]{1,0:T(8,128)(2,1)S(1)}, s16[208,256]{1,0:T(8,128)(2,1)S(1)}, u32[]{:S(2)}, u32[]{:S(2)}) collective-permute-start(s16[208,256]{1,0:T(8,128)(2,1)S(1)} %get-tuple-element.76), channel_id=1, source_target_pairs={{0,1},{1,2},{2,3},{3,0},{4,7},{5,4},{6,5},{7,6},{8,9},{9,10},{10,1... | collective-permute-start | bytes 319496 | tf_op jit(solution)/shard_map/ppermute | solution.py:50
  98.1 5.7 %collective-permute-start.20 = (bf16[3,64,256]{2,1,0:T(8,128)(2,1)S(1)}, bf16[3,64,256]{2,1,0:T(8,128)(2,1)S(1)}, u32[]{:S(2)}, u32[]{:S(2)}) collective-permute-start(bf16[3,64,256]{2,1,0:T(8,128)(2,1)S(1)} %fusion.9.s0), channel_id=1, source_target_pairs={{8,0},{124,4},{16,8},{4,12},{24,16},{12,20},{32,24},{20,28},{40,32... | collective-permute-start | bytes 294920 | tf_op jit(solution)/shard_map/ppermute | solution.py:58
  100.8 3.0 %collective-permute-start.23 = (bf16[3,64,256]{2,1,0:T(8,128)(2,1)S(1)}, bf16[3,64,256]{2,1,0:T(8,128)(2,1)S(1)}, u32[]{:S(2)}, u32[]{:S(2)}) collective-permute-start(bf16[3,64,256]{2,1,0:T(8,128)(2,1)S(1)} %fusion.9.s0), channel_id=1, source_target_pairs={{0,4},{4,0},{1,5},{5,1},{2,6},{6,2},{3,7},{7,3},{8,12},{12,8},{9,1... | collective-permute-start | bytes 294920 | tf_op jit(solution)/shard_map/ppermute | solution.py:64
  100.9 7.9 %collective-permute-start.21 = (bf16[3,64,256]{2,1,0:T(8,128)(2,1)S(1)}, bf16[3,64,256]{2,1,0:T(8,128)(2,1)S(1)}, u32[]{:S(2)}, u32[]{:S(2)}) collective-permute-start(bf16[3,64,256]{2,1,0:T(8,128)(2,1)S(1)} %fusion.9.s0), channel_id=1, source_target_pairs={{120,0},{12,4},{0,8},{20,12},{8,16},{28,20},{16,24},{36,28},{24,32... | collective-permute-start | bytes 294920 | tf_op jit(solution)/shard_map/ppermute | solution.py:58
  103.9 4.9 %collective-permute-start.22 = (bf16[3,64,256]{2,1,0:T(8,128)(2,1)S(1)}, bf16[3,64,256]{2,1,0:T(8,128)(2,1)S(1)}, u32[]{:S(2)}, u32[]{:S(2)}) collective-permute-start(bf16[3,64,256]{2,1,0:T(8,128)(2,1)S(1)} %collective-permute-done.20.s2), channel_id=1, source_target_pairs={{0,4},{4,0},{1,5},{5,1},{2,6},{6,2},{3,7},{7,3},{8,12},{12,8},{9,1... | collective-permute-start | bytes 294920 | tf_op jit(solution)/shard_map/ppermute | solution.py:64
  109.9 7.5 %collective-permute-start.24 = (s16[208,256]{1,0:T(8,128)(2,1)S(1)}, s16[208,256]{1,0:T(8,128)(2,1)S(1)}, u32[]{:S(2)}, u32[]{:S(2)}) collective-permute-start(s16[208,256]{1,0:T(8,128)(2,1)S(1)} %spread_far.3), channel_id=1, source_target_pairs={{0,2},{1,3},{2,0},{3,1},{4,6},{5,7},{6,4},{7,5},{8,10},{9,11},{10,... | collective-permute-start | bytes 319496 | tf_op jit(solution)/shard_map/ppermute | solution.py:54
  115.3 4.8 %collective-permute-start.25 = (s16[208,256]{1,0:T(8,128)(2,1)S(1)}, s16[208,256]{1,0:T(8,128)(2,1)S(1)}, u32[]{:S(2)}, u32[]{:S(2)}) collective-permute-start(s16[208,256]{1,0:T(8,128)(2,1)S(1)} %get-tuple-element.79), channel_id=1, source_target_pairs={{0,3},{1,0},{2,1},{3,2},{4,5},{5,6},{6,7},{7,4},{8,11},{9,8},{10,9... | collective-permute-start | bytes 319496 | tf_op jit(solution)/shard_map/ppermute | solution.py:50
  116.6 5.9 %collective-permute-start.26 = (s16[208,256]{1,0:T(8,128)(2,1)S(1)}, s16[208,256]{1,0:T(8,128)(2,1)S(1)}, u32[]{:S(2)}, u32[]{:S(2)}) collective-permute-start(s16[208,256]{1,0:T(8,128)(2,1)S(1)} %get-tuple-element.80), channel_id=1, source_target_pairs={{0,1},{1,2},{2,3},{3,0},{4,7},{5,4},{6,5},{7,6},{8,9},{9,10},{10,1... | collective-permute-start | bytes 319496 | tf_op jit(solution)/shard_map/ppermute | solution.py:50

commit v10 on v9

--- a/solution.py
+++ b/solution.py
@@ -180,7 +180,7 @@
                 return packed + (value >> 4)
 
             packed = sum(counts[c] << (at * STEP) for at, c in enumerate(chunks))
-            packed = lax.fori_loop(0, NBR, body, packed, unroll=8)
+            packed = lax.fori_loop(0, NBR, body, packed, unroll=NBR)
             for at, c in enumerate(chunks):
                 counts[c] = (packed >> (at * STEP)) & ((1 << STEP) - 1)
     for c in range(CHUNKS):

time: 122 us -> 121 us (level)
  Pallas kernels: 40.4 us -> 37 us
  waiting for transfers between devices: 38.3 us -> 40.6 us
    pallas_call x11, Pallas kernels: 33.6 us -> 30.8 us  [build(): pl.pallas_call(kernel, out_shape=[jax.ShapeDtypeStruct(*o) for o in outs]...]
    ppermute x3, waiting for transfers between devices: 0.01 us -> 1.8 us  [across_x(): return lax.ppermute(v, 'x', [(x, (x + 2) % NX) for x in range(NX)])]
    ppermute x6, waiting for transfers between devices: 14.7 us -> 16.4 us  [from_wide(): lax.ppermute(v, WIDE, [((i + (2 * sign if i % 2 == 0 else -2 * sign)) % N...]
    ppermute x12, waiting for transfers between devices: 23.5 us -> 22.2 us  [along_x(): return lax.ppermute(v, ('c', 'x'), pairs)]
  transfers between devices with their start and end apart: 27 -> 27, of which waited for: 12 -> 14; matrix products, arithmetic and copies ran while one was open for 0% -> 0% of each run, Pallas kernels for 28% -> 25%
where the time goes in v10:
time: 121 us; the launch traced here: 122 us
  starting transfers between devices  41.6 us (34%)
  waiting for transfers between devices  40.6 us (34%)
  Pallas kernels  37 us (31%)
  other arithmetic  2.28 us (2%)
    pallas_call x11, Pallas kernels, build(): pl.pallas_call(kernel, out_shape=[jax.ShapeDtypeStruct(*o) for o in outs]...  30.8 us
    ppermute x12, waiting for transfers between devices, along_x(): return lax.ppermute(v, ('c', 'x'), pairs)  22.2 us
    ppermute x6, waiting for transfers between devices, from_wide(): lax.ppermute(v, WIDE, [((i + (2 * sign if i % 2 == 0 else -2 * sign)) % N...  16.4 us
    ppermute x6, starting transfers between devices, from_wide(): lax.ppermute(v, WIDE, [((i + (2 * sign if i % 2 == 0 else -2 * sign)) % N...  16 us
    ppermute x12, starting transfers between devices, along_x(): return lax.ppermute(v, ('c', 'x'), pairs)  15.7 us
    ppermute x3, starting transfers between devices, across_x(): return lax.ppermute(v, 'x', [(x, (x + 2) % NX) for x in range(NX)])  7.68 us
    pallas_call x2, Pallas kernels, make_plan(): pl.pallas_call(functools.partial(plan_kernel, groups), out_shape=jax.Shap...  4.34 us
  transfers between devices with their start and end apart: 27, of which 14 were waited for; matrix products, arithmetic and copies ran while one was open for 0% of the time, Pallas kernels for 25%

profile of v10, /device:TPU:0, one launch (start us, length us, event | category | flops | bytes accessed | tf_op | source)
XLA Modules:
  0.0 121.9 jit_solution(17426302814568132071)
XLA Ops:
  0.0 0.7 shift-right-arithmetic_convert_fusion
  0.8 1.7 %prep.1 = (bf16[1552,256]{1,0:T(8,128)(2,1)S(1)}, bf16[832,768]{1,0:T(8,128)(2,1)S(1)}) custom-call(bf16[3,256,768]{2,1,0:T(8,128)(2,1)} %emb_hbm.1, f32[3,64,256]{2,1,0:T(8,128)} %bitcast.24, bf16[16,256]{1,0:T(8,128)(2,1)S(1)} %fusion.23.ids_ref), custom_call_target="tpu_custom_call" | custom-call | flops 1000 | bytes 1000 | tf_op jit(solution)/shard_map/prep/pallas_call | solution.py:88
  2.5 1.6 %collective-permute-start = (bf16[1552,256]{1,0:T(8,128)(2,1)S(1)}, bf16[1552,256]{1,0:T(8,128)(2,1)S(1)}, u32[]{:S(2)}, u32[]{:S(2)}) collective-permute-start(bf16[1552,256]{1,0:T(8,128)(2,1)S(1)} %get-tuple-element.54.r0), channel_id=1, source_target_pairs={{0,1},{1,2},{2,3},{3,0},{4,7},{5,4},{6,5},{7,6},{8,9},{9,10},{10,1... | collective-permute-start | bytes 2383880 | tf_op jit(solution)/shard_map/ppermute | solution.py:50
  4.2 0.1 third.1.r1
  4.3 1.6 %collective-permute-start.2 = (bf16[784,256]{1,0:T(8,128)(2,1)S(1)}, bf16[784,256]{1,0:T(8,128)(2,1)S(1)}, u32[]{:S(2)}, u32[]{:S(2)}) collective-permute-start(bf16[784,256]{1,0:T(8,128)(2,1)S(1)} %third.1.r1), channel_id=1, source_target_pairs={{0,1},{1,2},{2,3},{3,0},{4,7},{5,4},{6,5},{7,6},{8,9},{9,10},{10,1... | collective-permute-start | bytes 1204232 | tf_op jit(solution)/shard_map/ppermute | solution.py:50
  5.9 1.7 %collective-permute-start.1 = (bf16[784,256]{1,0:T(8,128)(2,1)S(1)}, bf16[784,256]{1,0:T(8,128)(2,1)S(1)}, u32[]{:S(2)}, u32[]{:S(2)}) collective-permute-start(bf16[784,256]{1,0:T(8,128)(2,1)S(1)} %third.1.r1), channel_id=1, source_target_pairs={{0,3},{1,0},{2,1},{3,2},{4,5},{5,6},{6,7},{7,4},{8,11},{9,8},{10,9... | collective-permute-start | bytes 1204232 | tf_op jit(solution)/shard_map/ppermute | solution.py:50
  7.6 1.6 %collective-permute-start.6 = (bf16[832,768]{1,0:T(8,128)(2,1)S(1)}, bf16[832,768]{1,0:T(8,128)(2,1)S(1)}, u32[]{:S(2)}, u32[]{:S(2)}) collective-permute-start(bf16[832,768]{1,0:T(8,128)(2,1)S(1)} %get-tuple-element.48.full_ref.c0), channel_id=1, source_target_pairs={{120,0},{12,4},{0,8},{20,12},{8,16},{28,20},{16,24},{36,28},{24,32... | collective-permute-start | bytes 3833864 | tf_op jit(solution)/shard_map/ppermute | solution.py:58
  9.2 4.9 %collective-permute-start.5 = (bf16[832,768]{1,0:T(8,128)(2,1)S(1)}, bf16[832,768]{1,0:T(8,128)(2,1)S(1)}, u32[]{:S(2)}, u32[]{:S(2)}) collective-permute-start(bf16[832,768]{1,0:T(8,128)(2,1)S(1)} %get-tuple-element.48.full_ref.c0), channel_id=1, source_target_pairs={{8,0},{124,4},{16,8},{4,12},{24,16},{12,20},{32,24},{20,28},{40,32... | collective-permute-start | bytes 3833864 | tf_op jit(solution)/shard_map/ppermute | solution.py:58
  14.1 10.4 %collective-permute-done.2.r3 = bf16[784,256]{1,0:T(8,128)(2,1)S(1)} collective-permute-done((bf16[784,256]{1,0:T(8,128)(2,1)S(1)}, bf16[784,256]{1,0:T(8,128)(2,1)S(1)}, u32[]{:S(2)}, u32[]{:S(2)}) %collective-permute-start.2) | collective-permute-done | bytes 401440 | tf_op jit(solution)/shard_map/ppermute | solution.py:50
  24.5 0.4 collective-permute-start.3
  24.9 2.9 %collective-permute-start.7 = (bf16[1552,256]{1,0:T(8,128)(2,1)S(1)}, bf16[1552,256]{1,0:T(8,128)(2,1)S(1)}, u32[]{:S(2)}, u32[]{:S(2)}) collective-permute-start(bf16[1552,256]{1,0:T(8,128)(2,1)S(1)} %get-tuple-element.54.r0), channel_id=1, source_target_pairs={{0,3},{1,0},{2,1},{3,2},{4,5},{5,6},{6,7},{7,4},{8,11},{9,8},{10,9... | collective-permute-start | bytes 2383880 | tf_op jit(solution)/shard_map/ppermute | solution.py:50
  27.9 2.6 %plan.2.list_ref.refs_1_.near_ref = s32[256]{0:T(256)S(1)} custom-call(s32[3,32]{1,0:T(4,128)S(1)} %get-tuple-element.87.refs_0_, s32[3,32]{1,0:T(4,128)S(1)} %get-tuple-element.88.refs_1_, s32[3,32]{1,0:T(4,128)S(1)} %get-tuple-element.89.refs_2_), custom_call_target="tpu_custom_call" | custom-call | flops 30000001024 | bytes 1000 | tf_op jit(solution)/shard_map/plan/pallas_call | solution.py:194
  30.5 0.3 collective-permute-done.4.c1
  30.8 1.0 collective-permute-start.8
  31.8 4.0 %build_0.1 = (bf16[44,256,256]{2,1,0:T(8,128)(2,1)S(1)}, f32[13,72,256]{2,1,0:T(8,128)S(1)}, bf16[6912,256]{1,0:T(8,128)(2,1)S(1)}, bf16[1536,768]{1,0:T(8,128)(2,1)S(1)}, bf16[6,64,256]{2,1,0:T(8,128)(2,1)S(1)}) custom-call(s32[256]{0:T(256)S(1)} %plan.2.list_ref.refs_1_.near_ref, bf16[1552,256]{1,0:T(8,128)(2,1)S(1)} %get-tuple-element.54.r0, ...), custom_call_target="tpu_custom_call" | custom-call | flops 30000001024 | bytes 1000 | tf_op jit(solution)/shard_map/build_0/pallas_call | solution.py:335
  35.8 4.8 %collective-permute-done.5.c0 = bf16[832,768]{1,0:T(8,128)(2,1)S(1)} collective-permute-done((bf16[832,768]{1,0:T(8,128)(2,1)S(1)}, bf16[832,768]{1,0:T(8,128)(2,1)S(1)}, u32[]{:S(2)}, u32[]{:S(2)}) %collective-permute-start.5) | collective-permute-done | bytes 1277984 | tf_op jit(solution)/shard_map/ppermute | solution.py:58
  40.7 2.2 %collective-permute-start.9 = (bf16[832,768]{1,0:T(8,128)(2,1)S(1)}, bf16[832,768]{1,0:T(8,128)(2,1)S(1)}, u32[]{:S(2)}, u32[]{:S(2)}) collective-permute-start(bf16[832,768]{1,0:T(8,128)(2,1)S(1)} %collective-permute-done.5.c0), channel_id=1, source_target_pairs={{0,4},{4,0},{1,5},{5,1},{2,6},{6,2},{3,7},{7,3},{8,12},{12,8},{9,1... | collective-permute-start | bytes 3833864 | tf_op jit(solution)/shard_map/ppermute | solution.py:64
  42.9 3.8 %build_1.1 = (bf16[44,256,256]{2,1,0:T(8,128)(2,1)S(1)}, f32[13,72,256]{2,1,0:T(8,128)S(1)}, bf16[1536,768]{1,0:T(8,128)(2,1)S(1)}, bf16[6,64,256]{2,1,0:T(8,128)(2,1)S(1)}) custom-call(s32[256]{0:T(256)S(1)} %plan.2.list_ref.refs_1_.near_ref, bf16[6912,256]{1,0:T(8,128)(2,1)S(1)} %get-tuple-element.49.rows.old_rows, ...), custom_call_target="tpu_custom_call" | custom-call | flops 30000001024 | bytes 1000 | tf_op jit(solution)/shard_map/build_1/pallas_call | solution.py:335
  46.8 1.8 %plan.3.list_ref = s32[256]{0:T(256)S(1)} custom-call(s32[3,32]{1,0:T(4,128)S(1)} %fusion.51.refs_0_, s32[256]{0:T(256)S(1)} %plan.2.list_ref.refs_1_.near_ref), custom_call_target="tpu_custom_call" | custom-call | flops 30000001024 | bytes 1000 | tf_op jit(solution)/shard_map/plan/pallas_call | solution.py:194
  48.6 5.6 %build_2.1 = (bf16[36,256,256]{2,1,0:T(8,128)(2,1)S(1)}, bf16[36,256,256]{2,1,0:T(8,128)(2,1)S(1)}, f32[13,72,256]{2,1,0:T(8,128)S(1)}, bf16[9216,256]{1,0:T(8,128)(2,1)S(1)}) custom-call(s32[256]{0:T(256)S(1)} %plan.3.list_ref, bf16[6912,256]{1,0:T(8,128)(2,1)S(1)} %get-tuple-element.49.rows.old_rows, bf16[1552,256]{1,0:T(8,128)(2,1)S(1)} %collective-permute-done.7.r0, ...), custom_call_target="tpu_custom_call" | custom-call | flops 30000001024 | bytes 1000 | tf_op jit(solution)/shard_map/build_2/pallas_call | solution.py:335
  54.2 1.6 %build_far.1 = (bf16[40,256,256]{2,1,0:T(8,128)(2,1)S(1)}, s16[208,256]{1,0:T(8,128)(2,1)S(1)}) custom-call(s32[256]{0:T(256)S(1)} %plan.3.list_ref, bf16[9216,256]{1,0:T(8,128)(2,1)S(1)} %get-tuple-element.61.rows, bf16[832,768]{1,0:T(8,128)(2,1)S(1)} %collective-permute-done.9.c4, f32[13,72,256]{2,1,0:T(8,128)S(1)} %get-tuple-element.65.given), custom_call_target="tpu_custom_call" | custom-call | flops 30000001024 | bytes 1000 | tf_op jit(solution)/shard_map/build_far/pallas_call | solution.py:335
  55.8 3.7 %collective-permute-start.10 = (s16[208,256]{1,0:T(8,128)(2,1)S(1)}, s16[208,256]{1,0:T(8,128)(2,1)S(1)}, u32[]{:S(2)}, u32[]{:S(2)}) collective-permute-start(s16[208,256]{1,0:T(8,128)(2,1)S(1)} %get-tuple-element.64), channel_id=1, source_target_pairs={{0,2},{1,3},{2,0},{3,1},{4,6},{5,7},{6,4},{7,5},{8,10},{9,11},{10,... | collective-permute-start | bytes 319496 | tf_op jit(solution)/shard_map/ppermute | solution.py:54
  59.5 3.3 %build_rest.1 = (bf16[40,256,256]{2,1,0:T(8,128)(2,1)S(1)}, f32[3,72,256]{2,1,0:T(8,128)S(1)}, s16[208,256]{1,0:T(8,128)(2,1)S(1)}, s16[208,256]{1,0:T(8,128)(2,1)S(1)}) custom-call(s32[256]{0:T(256)S(1)} %plan.3.list_ref, bf16[9216,256]{1,0:T(8,128)(2,1)S(1)} %get-tuple-element.61.rows, bf16[832,768]{1,0:T(8,128)(2,1)S(1)} %collective-permute-done.9.c4, ...), custom_call_target="tpu_custom_call" | custom-call | flops 30000001024 | bytes 1000 | tf_op jit(solution)/shard_map/build_rest/pallas_call | solution.py:335
  62.9 2.0 %collective-permute-start.12 = (s16[208,256]{1,0:T(8,128)(2,1)S(1)}, s16[208,256]{1,0:T(8,128)(2,1)S(1)}, u32[]{:S(2)}, u32[]{:S(2)}) collective-permute-start(s16[208,256]{1,0:T(8,128)(2,1)S(1)} %get-tuple-element.69), channel_id=1, source_target_pairs={{0,1},{1,2},{2,3},{3,0},{4,7},{5,4},{6,5},{7,6},{8,9},{9,10},{10,1... | collective-permute-start | bytes 319496 | tf_op jit(solution)/shard_map/ppermute | solution.py:50
  65.0 2.6 %collective-permute-done.11 = s16[208,256]{1,0:T(8,128)(2,1)S(1)} collective-permute-done((s16[208,256]{1,0:T(8,128)(2,1)S(1)}, s16[208,256]{1,0:T(8,128)(2,1)S(1)}, u32[]{:S(2)}, u32[]{:S(2)}) %collective-permute-start.11) | collective-permute-done | bytes 106528 | tf_op jit(solution)/shard_map/ppermute | solution.py:50
  67.6 1.3 %collective-permute-done.12 = s16[208,256]{1,0:T(8,128)(2,1)S(1)} collective-permute-done((s16[208,256]{1,0:T(8,128)(2,1)S(1)}, s16[208,256]{1,0:T(8,128)(2,1)S(1)}, u32[]{:S(2)}, u32[]{:S(2)}) %collective-permute-start.12) | collective-permute-done | bytes 106528 | tf_op jit(solution)/shard_map/ppermute | solution.py:50
  69.2 6.0 %collective-permute-start.13 = (bf16[3,64,256]{2,1,0:T(8,128)(2,1)S(1)}, bf16[3,64,256]{2,1,0:T(8,128)(2,1)S(1)}, u32[]{:S(2)}, u32[]{:S(2)}) collective-permute-start(bf16[3,64,256]{2,1,0:T(8,128)(2,1)S(1)} %fusion.15.s0), channel_id=1, source_target_pairs={{8,0},{124,4},{16,8},{4,12},{24,16},{12,20},{32,24},{20,28},{40,32... | collective-permute-start | bytes 294920 | tf_op jit(solution)/shard_map/ppermute | solution.py:58
  75.2 3.1 %collective-permute-done.13.s2 = bf16[3,64,256]{2,1,0:T(8,128)(2,1)S(1)} collective-permute-done((bf16[3,64,256]{2,1,0:T(8,128)(2,1)S(1)}, bf16[3,64,256]{2,1,0:T(8,128)(2,1)S(1)}, u32[]{:S(2)}, u32[]{:S(2)}) %collective-permute-start.13) | collective-permute-done | bytes 98336 | tf_op jit(solution)/shard_map/ppermute | solution.py:58
  78.3 2.2 %spread_near.2.given = f32[13,64,256]{2,1,0:T(8,128)S(1)} custom-call(s32[256]{0:T(256)S(1)} %plan.2.list_ref.refs_1_.near_ref, s32[256]{0:T(256)S(1)} %plan.3.list_ref, bf16[44,256,256]{2,1,0:T(8,128)(2,1)S(1)} %get-tuple-element.70.w0, bf16[36,256,256]{2,1,0:T(8,128)(2,1)S(1)} %get-tuple-element.71.w2, bf16[3,64,256]{2,1,0:T(8,128)(2,1)S(1)} %fusion.15.s0, ...), custom_call_target="tpu_custom_call" | custom-call | flops 30000001024 | bytes 1000 | tf_op jit(solution)/shard_map/spread_near/pallas_call | solution.py:335
  80.4 2.7 %collective-permute-done.14.s3 = bf16[3,64,256]{2,1,0:T(8,128)(2,1)S(1)} collective-permute-done((bf16[3,64,256]{2,1,0:T(8,128)(2,1)S(1)}, bf16[3,64,256]{2,1,0:T(8,128)(2,1)S(1)}, u32[]{:S(2)}, u32[]{:S(2)}) %collective-permute-start.14) | collective-permute-done | bytes 98336 | tf_op jit(solution)/shard_map/ppermute | solution.py:58
  83.1 1.4 %spread_far.2 = s16[208,256]{1,0:T(8,128)(2,1)S(1)} custom-call(s32[256]{0:T(256)S(1)} %plan.3.list_ref, bf16[36,256,256]{2,1,0:T(8,128)(2,1)S(1)} %get-tuple-element.60.w3, bf16[40,256,256]{2,1,0:T(8,128)(2,1)S(1)} %get-tuple-element.72.w4, bf16[3,64,256]{2,1,0:T(8,128)(2,1)S(1)} %collective-permute-done.13.s2, ...), custom_call_target="tpu_custom_call" | custom-call | flops 30000001024 | bytes 1000 | tf_op jit(solution)/shard_map/spread_far/pallas_call | solution.py:335
  84.5 3.6 %collective-permute-start.17 = (s16[208,256]{1,0:T(8,128)(2,1)S(1)}, s16[208,256]{1,0:T(8,128)(2,1)S(1)}, u32[]{:S(2)}, u32[]{:S(2)}) collective-permute-start(s16[208,256]{1,0:T(8,128)(2,1)S(1)} %spread_far.2), channel_id=1, source_target_pairs={{0,2},{1,3},{2,0},{3,1},{4,6},{5,7},{6,4},{7,5},{8,10},{9,11},{10,... | collective-permute-start | bytes 319496 | tf_op jit(solution)/shard_map/ppermute | solution.py:54
  88.1 2.7 %spread_rest.2 = (f32[3,64,256]{2,1,0:T(8,128)S(1)}, s16[208,256]{1,0:T(8,128)(2,1)S(1)}, s16[208,256]{1,0:T(8,128)(2,1)S(1)}) custom-call(s32[256]{0:T(256)S(1)} %plan.2.list_ref.refs_1_.near_ref, s32[256]{0:T(256)S(1)} %plan.3.list_ref, bf16[44,256,256]{2,1,0:T(8,128)(2,1)S(1)} %get-tuple-element.53.w1, bf16[36,256,256]{2,1,0:T(8,128)(2,1)S(1)} %get-tuple-element.60.w3, ...), custom_call_target="tpu_custom_call" | custom-call | flops 30000001024 | bytes 1000 | tf_op jit(solution)/shard_map/spread_rest/pallas_call | solution.py:335
  90.9 2.0 %collective-permute-start.19 = (s16[208,256]{1,0:T(8,128)(2,1)S(1)}, s16[208,256]{1,0:T(8,128)(2,1)S(1)}, u32[]{:S(2)}, u32[]{:S(2)}) collective-permute-start(s16[208,256]{1,0:T(8,128)(2,1)S(1)} %get-tuple-element.76), channel_id=1, source_target_pairs={{0,1},{1,2},{2,3},{3,0},{4,7},{5,4},{6,5},{7,6},{8,9},{9,10},{10,1... | collective-permute-start | bytes 319496 | tf_op jit(solution)/shard_map/ppermute | solution.py:50
  93.0 2.6 %collective-permute-done.18 = s16[208,256]{1,0:T(8,128)(2,1)S(1)} collective-permute-done((s16[208,256]{1,0:T(8,128)(2,1)S(1)}, s16[208,256]{1,0:T(8,128)(2,1)S(1)}, u32[]{:S(2)}, u32[]{:S(2)}) %collective-permute-start.18) | collective-permute-done | bytes 106528 | tf_op jit(solution)/shard_map/ppermute | solution.py:50
  95.7 1.3 %collective-permute-done.19 = s16[208,256]{1,0:T(8,128)(2,1)S(1)} collective-permute-done((s16[208,256]{1,0:T(8,128)(2,1)S(1)}, s16[208,256]{1,0:T(8,128)(2,1)S(1)}, u32[]{:S(2)}, u32[]{:S(2)}) %collective-permute-start.19) | collective-permute-done | bytes 106528 | tf_op jit(solution)/shard_map/ppermute | solution.py:50
  97.1 3.5 %collective-permute-start.20 = (bf16[3,64,256]{2,1,0:T(8,128)(2,1)S(1)}, bf16[3,64,256]{2,1,0:T(8,128)(2,1)S(1)}, u32[]{:S(2)}, u32[]{:S(2)}) collective-permute-start(bf16[3,64,256]{2,1,0:T(8,128)(2,1)S(1)} %fusion.9.s0), channel_id=1, source_target_pairs={{8,0},{124,4},{16,8},{4,12},{24,16},{12,20},{32,24},{20,28},{40,32... | collective-permute-start | bytes 294920 | tf_op jit(solution)/shard_map/ppermute | solution.py:58
  100.5 3.0 %collective-permute-done.20.s2 = bf16[3,64,256]{2,1,0:T(8,128)(2,1)S(1)} collective-permute-done((bf16[3,64,256]{2,1,0:T(8,128)(2,1)S(1)}, bf16[3,64,256]{2,1,0:T(8,128)(2,1)S(1)}, u32[]{:S(2)}, u32[]{:S(2)}) %collective-permute-start.20) | collective-permute-done | bytes 98336 | tf_op jit(solution)/shard_map/ppermute | solution.py:58
  103.5 2.2 %spread_near.3.given = f32[13,64,256]{2,1,0:T(8,128)S(1)} custom-call(s32[256]{0:T(256)S(1)} %plan.2.list_ref.refs_1_.near_ref, s32[256]{0:T(256)S(1)} %plan.3.list_ref, bf16[44,256,256]{2,1,0:T(8,128)(2,1)S(1)} %get-tuple-element.70.w0, bf16[36,256,256]{2,1,0:T(8,128)(2,1)S(1)} %get-tuple-element.71.w2, bf16[3,64,256]{2,1,0:T(8,128)(2,1)S(1)} %fusion.9.s0, ...), custom_call_target="tpu_custom_call" | custom-call | flops 30000001024 | bytes 1000 | tf_op jit(solution)/shard_map/spread_near/pallas_call | solution.py:335
  105.7 2.7 %collective-permute-done.21.s3 = bf16[3,64,256]{2,1,0:T(8,128)(2,1)S(1)} collective-permute-done((bf16[3,64,256]{2,1,0:T(8,128)(2,1)S(1)}, bf16[3,64,256]{2,1,0:T(8,128)(2,1)S(1)}, u32[]{:S(2)}, u32[]{:S(2)}) %collective-permute-start.21) | collective-permute-done | bytes 98336 | tf_op jit(solution)/shard_map/ppermute | solution.py:58
  108.5 1.4 %spread_far.3 = s16[208,256]{1,0:T(8,128)(2,1)S(1)} custom-call(s32[256]{0:T(256)S(1)} %plan.3.list_ref, bf16[36,256,256]{2,1,0:T(8,128)(2,1)S(1)} %get-tuple-element.60.w3, bf16[40,256,256]{2,1,0:T(8,128)(2,1)S(1)} %get-tuple-element.72.w4, bf16[3,64,256]{2,1,0:T(8,128)(2,1)S(1)} %collective-permute-done.20.s2, ...), custom_call_target="tpu_custom_call" | custom-call | flops 30000001024 | bytes 1000 | tf_op jit(solution)/shard_map/spread_far/pallas_call | solution.py:335
  109.8 0.3 collective-permute-start.24
  110.2 2.7 %spread_rest.3 = (f32[3,64,256]{2,1,0:T(8,128)S(1)}, s16[208,256]{1,0:T(8,128)(2,1)S(1)}, s16[208,256]{1,0:T(8,128)(2,1)S(1)}) custom-call(s32[256]{0:T(256)S(1)} %plan.2.list_ref.refs_1_.near_ref, s32[256]{0:T(256)S(1)} %plan.3.list_ref, bf16[44,256,256]{2,1,0:T(8,128)(2,1)S(1)} %get-tuple-element.53.w1, bf16[36,256,256]{2,1,0:T(8,128)(2,1)S(1)} %get-tuple-element.60.w3, ...), custom_call_target="tpu_custom_call" | custom-call | flops 30000001024 | bytes 1000 | tf_op jit(solution)/shard_map/spread_rest/pallas_call | solution.py:335
  112.9 2.3 %collective-permute-start.25 = (s16[208,256]{1,0:T(8,128)(2,1)S(1)}, s16[208,256]{1,0:T(8,128)(2,1)S(1)}, u32[]{:S(2)}, u32[]{:S(2)}) collective-permute-start(s16[208,256]{1,0:T(8,128)(2,1)S(1)} %get-tuple-element.79), channel_id=1, source_target_pairs={{0,3},{1,0},{2,1},{3,2},{4,5},{5,6},{6,7},{7,4},{8,11},{9,8},{10,9... | collective-permute-start | bytes 319496 | tf_op jit(solution)/shard_map/ppermute | solution.py:50
  115.2 1.8 %collective-permute-done.24 = s16[208,256]{1,0:T(8,128)(2,1)S(1)} collective-permute-done((s16[208,256]{1,0:T(8,128)(2,1)S(1)}, s16[208,256]{1,0:T(8,128)(2,1)S(1)}, u32[]{:S(2)}, u32[]{:S(2)}) %collective-permute-start.24) | collective-permute-done | bytes 106528 | tf_op jit(solution)/shard_map/ppermute | solution.py:54
  117.0 0.6 collective-permute-done.25
  117.7 3.4 %collective-permute-done.26 = s16[208,256]{1,0:T(8,128)(2,1)S(1)} collective-permute-done((s16[208,256]{1,0:T(8,128)(2,1)S(1)}, s16[208,256]{1,0:T(8,128)(2,1)S(1)}, u32[]{:S(2)}, u32[]{:S(2)}) %collective-permute-start.26) | collective-permute-done | bytes 106528 | tf_op jit(solution)/shard_map/ppermute | solution.py:50
  121.1 0.8 fusion.3
  (53 shorter events, 1.1 us)
Async XLA Ops:
  2.5 22.0 %collective-permute-start = (bf16[1552,256]{1,0:T(8,128)(2,1)S(1)}, bf16[1552,256]{1,0:T(8,128)(2,1)S(1)}, u32[]{:S(2)}, u32[]{:S(2)}) collective-permute-start(bf16[1552,256]{1,0:T(8,128)(2,1)S(1)} %get-tuple-element.54.r0), channel_id=1, source_target_pairs={{0,1},{1,2},{2,3},{3,0},{4,7},{5,4},{6,5},{7,6},{8,9},{9,10},{10,1... | collective-permute-start | bytes 2383880 | tf_op jit(solution)/shard_map/ppermute | solution.py:50
  4.3 20.2 %collective-permute-start.2 = (bf16[784,256]{1,0:T(8,128)(2,1)S(1)}, bf16[784,256]{1,0:T(8,128)(2,1)S(1)}, u32[]{:S(2)}, u32[]{:S(2)}) collective-permute-start(bf16[784,256]{1,0:T(8,128)(2,1)S(1)} %third.1.r1), channel_id=1, source_target_pairs={{0,1},{1,2},{2,3},{3,0},{4,7},{5,4},{6,5},{7,6},{8,9},{9,10},{10,1... | collective-permute-start | bytes 1204232 | tf_op jit(solution)/shard_map/ppermute | solution.py:50
  5.9 18.6 %collective-permute-start.1 = (bf16[784,256]{1,0:T(8,128)(2,1)S(1)}, bf16[784,256]{1,0:T(8,128)(2,1)S(1)}, u32[]{:S(2)}, u32[]{:S(2)}) collective-permute-start(bf16[784,256]{1,0:T(8,128)(2,1)S(1)} %third.1.r1), channel_id=1, source_target_pairs={{0,3},{1,0},{2,1},{3,2},{4,5},{5,6},{6,7},{7,4},{8,11},{9,8},{10,9... | collective-permute-start | bytes 1204232 | tf_op jit(solution)/shard_map/ppermute | solution.py:50
  7.6 35.2 %collective-permute-start.6 = (bf16[832,768]{1,0:T(8,128)(2,1)S(1)}, bf16[832,768]{1,0:T(8,128)(2,1)S(1)}, u32[]{:S(2)}, u32[]{:S(2)}) collective-permute-start(bf16[832,768]{1,0:T(8,128)(2,1)S(1)} %get-tuple-element.48.full_ref.c0), channel_id=1, source_target_pairs={{120,0},{12,4},{0,8},{20,12},{8,16},{28,20},{16,24},{36,28},{24,32... | collective-permute-start | bytes 3833864 | tf_op jit(solution)/shard_map/ppermute | solution.py:58
  9.2 31.5 %collective-permute-start.5 = (bf16[832,768]{1,0:T(8,128)(2,1)S(1)}, bf16[832,768]{1,0:T(8,128)(2,1)S(1)}, u32[]{:S(2)}, u32[]{:S(2)}) collective-permute-start(bf16[832,768]{1,0:T(8,128)(2,1)S(1)} %get-tuple-element.48.full_ref.c0), channel_id=1, source_target_pairs={{8,0},{124,4},{16,8},{4,12},{24,16},{12,20},{32,24},{20,28},{40,32... | collective-permute-start | bytes 3833864 | tf_op jit(solution)/shard_map/ppermute | solution.py:58
  24.5 22.2 %collective-permute-start.3 = (bf16[1552,256]{1,0:T(8,128)(2,1)S(1)}, bf16[1552,256]{1,0:T(8,128)(2,1)S(1)}, u32[]{:S(2)}, u32[]{:S(2)}) collective-permute-start(bf16[1552,256]{1,0:T(8,128)(2,1)S(1)} %collective-permute-done.r2), channel_id=1, source_target_pairs={{0,1},{1,2},{2,3},{3,0},{4,7},{5,4},{6,5},{7,6},{8,9},{9,10},{10,1... | collective-permute-start | bytes 2383880 | tf_op jit(solution)/shard_map/ppermute | solution.py:50
  24.9 23.6 %collective-permute-start.7 = (bf16[1552,256]{1,0:T(8,128)(2,1)S(1)}, bf16[1552,256]{1,0:T(8,128)(2,1)S(1)}, u32[]{:S(2)}, u32[]{:S(2)}) collective-permute-start(bf16[1552,256]{1,0:T(8,128)(2,1)S(1)} %get-tuple-element.54.r0), channel_id=1, source_target_pairs={{0,3},{1,0},{2,1},{3,2},{4,5},{5,6},{6,7},{7,4},{8,11},{9,8},{10,9... | collective-permute-start | bytes 2383880 | tf_op jit(solution)/shard_map/ppermute | solution.py:50
  27.8 3.0 %collective-permute-start.4 = (bf16[832,768]{1,0:T(8,128)(2,1)S(1)}, bf16[832,768]{1,0:T(8,128)(2,1)S(1)}, u32[]{:S(2)}, u32[]{:S(2)}) collective-permute-start(bf16[832,768]{1,0:T(8,128)(2,1)S(1)} %get-tuple-element.48.full_ref.c0), channel_id=1, source_target_pairs={{0,4},{4,0},{1,5},{5,1},{2,6},{6,2},{3,7},{7,3},{8,12},{12,8},{9,1... | collective-permute-start | bytes 3833864 | tf_op jit(solution)/shard_map/ppermute | solution.py:64
  30.8 17.8 %collective-permute-start.8 = (bf16[784,256]{1,0:T(8,128)(2,1)S(1)}, bf16[784,256]{1,0:T(8,128)(2,1)S(1)}, u32[]{:S(2)}, u32[]{:S(2)}) collective-permute-start(bf16[784,256]{1,0:T(8,128)(2,1)S(1)} %collective-permute-done.1.r4), channel_id=1, source_target_pairs={{0,3},{1,0},{2,1},{3,2},{4,5},{5,6},{6,7},{7,4},{8,11},{9,8},{10,9... | collective-permute-start | bytes 1204232 | tf_op jit(solution)/shard_map/ppermute | solution.py:50
  40.7 13.5 %collective-permute-start.9 = (bf16[832,768]{1,0:T(8,128)(2,1)S(1)}, bf16[832,768]{1,0:T(8,128)(2,1)S(1)}, u32[]{:S(2)}, u32[]{:S(2)}) collective-permute-start(bf16[832,768]{1,0:T(8,128)(2,1)S(1)} %collective-permute-done.5.c0), channel_id=1, source_target_pairs={{0,4},{4,0},{1,5},{5,1},{2,6},{6,2},{3,7},{7,3},{8,12},{12,8},{9,1... | collective-permute-start | bytes 3833864 | tf_op jit(solution)/shard_map/ppermute | solution.py:64
  55.8 13.2 %copy-start = (f32[3,256,64]{1,2,0:T(8,128)S(1)}, f32[3,256,64]{1,2,0:T(8,128)}, u32[]{:S(2)}) copy-start(f32[3,256,64]{1,2,0:T(8,128)} %param.4) | copy-start | bytes 589828
  55.8 9.1 %collective-permute-start.10 = (s16[208,256]{1,0:T(8,128)(2,1)S(1)}, s16[208,256]{1,0:T(8,128)(2,1)S(1)}, u32[]{:S(2)}, u32[]{:S(2)}) collective-permute-start(s16[208,256]{1,0:T(8,128)(2,1)S(1)} %get-tuple-element.64), channel_id=1, source_target_pairs={{0,2},{1,3},{2,0},{3,1},{4,6},{5,7},{6,4},{7,5},{8,10},{9,11},{10,... | collective-permute-start | bytes 319496 | tf_op jit(solution)/shard_map/ppermute | solution.py:54
  62.9 4.8 %collective-permute-start.11 = (s16[208,256]{1,0:T(8,128)(2,1)S(1)}, s16[208,256]{1,0:T(8,128)(2,1)S(1)}, u32[]{:S(2)}, u32[]{:S(2)}) collective-permute-start(s16[208,256]{1,0:T(8,128)(2,1)S(1)} %get-tuple-element.68), channel_id=1, source_target_pairs={{0,3},{1,0},{2,1},{3,2},{4,5},{5,6},{6,7},{7,4},{8,11},{9,8},{10,9... | collective-permute-start | bytes 319496 | tf_op jit(solution)/shard_map/ppermute | solution.py:50
  62.9 6.0 %collective-permute-start.12 = (s16[208,256]{1,0:T(8,128)(2,1)S(1)}, s16[208,256]{1,0:T(8,128)(2,1)S(1)}, u32[]{:S(2)}, u32[]{:S(2)}) collective-permute-start(s16[208,256]{1,0:T(8,128)(2,1)S(1)} %get-tuple-element.69), channel_id=1, source_target_pairs={{0,1},{1,2},{2,3},{3,0},{4,7},{5,4},{6,5},{7,6},{8,9},{9,10},{10,1... | collective-permute-start | bytes 319496 | tf_op jit(solution)/shard_map/ppermute | solution.py:50
  69.2 9.1 %collective-permute-start.13 = (bf16[3,64,256]{2,1,0:T(8,128)(2,1)S(1)}, bf16[3,64,256]{2,1,0:T(8,128)(2,1)S(1)}, u32[]{:S(2)}, u32[]{:S(2)}) collective-permute-start(bf16[3,64,256]{2,1,0:T(8,128)(2,1)S(1)} %fusion.15.s0), channel_id=1, source_target_pairs={{8,0},{124,4},{16,8},{4,12},{24,16},{12,20},{32,24},{20,28},{40,32... | collective-permute-start | bytes 294920 | tf_op jit(solution)/shard_map/ppermute | solution.py:58
  75.2 3.1 %collective-permute-start.16 = (bf16[3,64,256]{2,1,0:T(8,128)(2,1)S(1)}, bf16[3,64,256]{2,1,0:T(8,128)(2,1)S(1)}, u32[]{:S(2)}, u32[]{:S(2)}) collective-permute-start(bf16[3,64,256]{2,1,0:T(8,128)(2,1)S(1)} %fusion.15.s0), channel_id=1, source_target_pairs={{0,4},{4,0},{1,5},{5,1},{2,6},{6,2},{3,7},{7,3},{8,12},{12,8},{9,1... | collective-permute-start | bytes 294920 | tf_op jit(solution)/shard_map/ppermute | solution.py:64
  75.2 7.9 %collective-permute-start.14 = (bf16[3,64,256]{2,1,0:T(8,128)(2,1)S(1)}, bf16[3,64,256]{2,1,0:T(8,128)(2,1)S(1)}, u32[]{:S(2)}, u32[]{:S(2)}) collective-permute-start(bf16[3,64,256]{2,1,0:T(8,128)(2,1)S(1)} %fusion.15.s0), channel_id=1, source_target_pairs={{120,0},{12,4},{0,8},{20,12},{8,16},{28,20},{16,24},{36,28},{24,32... | collective-permute-start | bytes 294920 | tf_op jit(solution)/shard_map/ppermute | solution.py:58
  78.3 4.9 %collective-permute-start.15 = (bf16[3,64,256]{2,1,0:T(8,128)(2,1)S(1)}, bf16[3,64,256]{2,1,0:T(8,128)(2,1)S(1)}, u32[]{:S(2)}, u32[]{:S(2)}) collective-permute-start(bf16[3,64,256]{2,1,0:T(8,128)(2,1)S(1)} %collective-permute-done.13.s2), channel_id=1, source_target_pairs={{0,4},{4,0},{1,5},{5,1},{2,6},{6,2},{3,7},{7,3},{8,12},{12,8},{9,1... | collective-permute-start | bytes 294920 | tf_op jit(solution)/shard_map/ppermute | solution.py:64
  84.5 8.5 %collective-permute-start.17 = (s16[208,256]{1,0:T(8,128)(2,1)S(1)}, s16[208,256]{1,0:T(8,128)(2,1)S(1)}, u32[]{:S(2)}, u32[]{:S(2)}) collective-permute-start(s16[208,256]{1,0:T(8,128)(2,1)S(1)} %spread_far.2), channel_id=1, source_target_pairs={{0,2},{1,3},{2,0},{3,1},{4,6},{5,7},{6,4},{7,5},{8,10},{9,11},{10,... | collective-permute-start | bytes 319496 | tf_op jit(solution)/shard_map/ppermute | solution.py:54
  90.9 4.8 %collective-permute-start.18 = (s16[208,256]{1,0:T(8,128)(2,1)S(1)}, s16[208,256]{1,0:T(8,128)(2,1)S(1)}, u32[]{:S(2)}, u32[]{:S(2)}) collective-permute-start(s16[208,256]{1,0:T(8,128)(2,1)S(1)} %get-tuple-element.75), channel_id=1, source_target_pairs={{0,3},{1,0},{2,1},{3,2},{4,5},{5,6},{6,7},{7,4},{8,11},{9,8},{10,9... | collective-permute-start | bytes 319496 | tf_op jit(solution)/shard_map/ppermute | solution.py:50
  90.9 6.0 %collective-permute-start.19 = (s16[208,256]{1,0:T(8,128)(2,1)S(1)}, s16[208,256]{1,0:T(8,128)(2,1)S(1)}, u32[]{:S(2)}, u32[]{:S(2)}) collective-permute-start(s16[208,256]{1,0:T(8,128)(2,1)S(1)} %get-tuple-element.76), channel_id=1, source_target_pairs={{0,1},{1,2},{2,3},{3,0},{4,7},{5,4},{6,5},{7,6},{8,9},{9,10},{10,1... | collective-permute-start | bytes 319496 | tf_op jit(solution)/shard_map/ppermute | solution.py:50
  97.1 6.5 %collective-permute-start.20 = (bf16[3,64,256]{2,1,0:T(8,128)(2,1)S(1)}, bf16[3,64,256]{2,1,0:T(8,128)(2,1)S(1)}, u32[]{:S(2)}, u32[]{:S(2)}) collective-permute-start(bf16[3,64,256]{2,1,0:T(8,128)(2,1)S(1)} %fusion.9.s0), channel_id=1, source_target_pairs={{8,0},{124,4},{16,8},{4,12},{24,16},{12,20},{32,24},{20,28},{40,32... | collective-permute-start | bytes 294920 | tf_op jit(solution)/shard_map/ppermute | solution.py:58
  100.5 3.0 %collective-permute-start.23 = (bf16[3,64,256]{2,1,0:T(8,128)(2,1)S(1)}, bf16[3,64,256]{2,1,0:T(8,128)(2,1)S(1)}, u32[]{:S(2)}, u32[]{:S(2)}) collective-permute-start(bf16[3,64,256]{2,1,0:T(8,128)(2,1)S(1)} %fusion.9.s0), channel_id=1, source_target_pairs={{0,4},{4,0},{1,5},{5,1},{2,6},{6,2},{3,7},{7,3},{8,12},{12,8},{9,1... | collective-permute-start | bytes 294920 | tf_op jit(solution)/shard_map/ppermute | solution.py:64
  100.5 7.9 %collective-permute-start.21 = (bf16[3,64,256]{2,1,0:T(8,128)(2,1)S(1)}, bf16[3,64,256]{2,1,0:T(8,128)(2,1)S(1)}, u32[]{:S(2)}, u32[]{:S(2)}) collective-permute-start(bf16[3,64,256]{2,1,0:T(8,128)(2,1)S(1)} %fusion.9.s0), channel_id=1, source_target_pairs={{120,0},{12,4},{0,8},{20,12},{8,16},{28,20},{16,24},{36,28},{24,32... | collective-permute-start | bytes 294920 | tf_op jit(solution)/shard_map/ppermute | solution.py:58
  103.5 4.9 %collective-permute-start.22 = (bf16[3,64,256]{2,1,0:T(8,128)(2,1)S(1)}, bf16[3,64,256]{2,1,0:T(8,128)(2,1)S(1)}, u32[]{:S(2)}, u32[]{:S(2)}) collective-permute-start(bf16[3,64,256]{2,1,0:T(8,128)(2,1)S(1)} %collective-permute-done.20.s2), channel_id=1, source_target_pairs={{0,4},{4,0},{1,5},{5,1},{2,6},{6,2},{3,7},{7,3},{8,12},{12,8},{9,1... | collective-permute-start | bytes 294920 | tf_op jit(solution)/shard_map/ppermute | solution.py:64
  109.8 7.1 %collective-permute-start.24 = (s16[208,256]{1,0:T(8,128)(2,1)S(1)}, s16[208,256]{1,0:T(8,128)(2,1)S(1)}, u32[]{:S(2)}, u32[]{:S(2)}) collective-permute-start(s16[208,256]{1,0:T(8,128)(2,1)S(1)} %spread_far.3), channel_id=1, source_target_pairs={{0,2},{1,3},{2,0},{3,1},{4,6},{5,7},{6,4},{7,5},{8,10},{9,11},{10,... | collective-permute-start | bytes 319496 | tf_op jit(solution)/shard_map/ppermute | solution.py:54
  112.9 4.8 %collective-permute-start.25 = (s16[208,256]{1,0:T(8,128)(2,1)S(1)}, s16[208,256]{1,0:T(8,128)(2,1)S(1)}, u32[]{:S(2)}, u32[]{:S(2)}) collective-permute-start(s16[208,256]{1,0:T(8,128)(2,1)S(1)} %get-tuple-element.79), channel_id=1, source_target_pairs={{0,3},{1,0},{2,1},{3,2},{4,5},{5,6},{6,7},{7,4},{8,11},{9,8},{10,9... | collective-permute-start | bytes 319496 | tf_op jit(solution)/shard_map/ppermute | solution.py:50
  115.2 5.9 %collective-permute-start.26 = (s16[208,256]{1,0:T(8,128)(2,1)S(1)}, s16[208,256]{1,0:T(8,128)(2,1)S(1)}, u32[]{:S(2)}, u32[]{:S(2)}) collective-permute-start(s16[208,256]{1,0:T(8,128)(2,1)S(1)} %get-tuple-element.80), channel_id=1, source_target_pairs={{0,1},{1,2},{2,3},{3,0},{4,7},{5,4},{6,5},{7,6},{8,9},{9,10},{10,1... | collective-permute-start | bytes 319496 | tf_op jit(solution)/shard_map/ppermute | solution.py:50
